TPU v7x, 32 devices: a whole 2x2x4 slice. The times are simulated.
32 devices in a mesh: fsdp: 8 (over y, x, core), tp: 4 (over z).
Axes of the slice: x: 2, y: 2, z: 4, core: 2. Of those that a mesh axis runs over, the one named last changes fastest.
Arguments:
- tokens: bfloat16 [7168, 2048], P('fsdp', 'tp'), may hold values from -6 to 6
- cotangent: bfloat16 [7168, 2048], P('fsdp', 'tp'), may hold values from -6 to 6
- w_query: bfloat16 [2048, 2048], P('fsdp', 'tp'), may hold values from -0.25 to 0.25
- w_key: bfloat16 [2048, 2048], P('fsdp', 'tp'), may hold values from -0.125 to 0.125
- w_value: bfloat16 [2048, 2048], P('fsdp', 'tp'), may hold values from -0.125 to 0.125
- w_out: bfloat16 [2048, 2048], P(('tp', 'fsdp')), may hold values from -0.75 to 0.75
- w_gate: bfloat16 [2048, 8192], P('fsdp', 'tp'), may hold values from -0.125 to 0.125
- w_up: bfloat16 [2048, 8192], P('fsdp', 'tp'), may hold values from -0.125 to 0.125
- w_down: bfloat16 [8192, 2048], P(('tp', 'fsdp')), may hold values from -0.0625 to 0.0625
- seq_lengths: int32 [8, 4], replicated, may hold values from 0 to 1024, as said below
- deal: int32 [8], replicated, may hold values from 0 to 7, as said below
- row_dest: int32 [7168], P('fsdp'), may hold values from 0 to 8191, as said below
Outputs:
- output: bfloat16 [7168, 2048], P('fsdp', 'tp')
- input_grad: bfloat16 [7168, 2048], P('fsdp', 'tp')
- grad_query: float32 [2048, 2048], P('fsdp', 'tp')
- grad_key: float32 [2048, 2048], P('fsdp', 'tp')
- grad_value: float32 [2048, 2048], P('fsdp', 'tp')
- grad_out: float32 [2048, 2048], P(('tp', 'fsdp'))
- grad_gate: float32 [2048, 8192], P('fsdp', 'tp')
- grad_up: float32 [2048, 8192], P('fsdp', 'tp')
- grad_down: float32 [8192, 2048], P(('tp', 'fsdp'))
Inputs may be any that keep to these rules, and one draw needn't show every extreme that they name: `seq_lengths`: row k lists, in buffer order, the lengths of the sequences of the group deal[k], zero for an absent sequence. Each row sums to a multiple of 32 of at most 1024; in every draw one row is a single sequence of exactly 1024. `deal`: every group appears exactly once. `row_dest`: A value g * 1024 + j names slot j of group g's buffer; no slot is named twice, and the named slots of group g are its first ones, as many as its list of lengths sums to. The 896 given rows of one index of fsdp name at most 128 slots of one group; in every draw some group receives exactly 128 rows from every index of fsdp.
All inputs are finite; a program needn't handle non-finite values.
Results may differ from a plain program's by a relative error of at most 0.018.
Values may be sent and summed in bfloat16 or wider, within the bound.
No kernel may reach another device: no remote copies, remote signals or barrier semaphores. Data moves between devices by JAX's collectives and lax.ppermute only.
A program may use at most 256 MiB of HBM per device.

v0:
```python
import jax
import jax.numpy as jnp
from jax import lax
from jax.sharding import PartitionSpec as P

HEAD_DIM = 128
GROUP_CAP = 1024
SEQ_SLOTS = 4


norm_eps = 1e-05
rope_base = 10000.0


def matmul(left, right):
    return jnp.dot(left, right, preferred_element_type=jnp.float32)


def times_transposed(left, right):
    return lax.dot_general(
        left, right, (((1,), (1,)), ((), ())), preferred_element_type=jnp.float32
    )


def transposed_times(left, right):
    return lax.dot_general(
        left, right, (((0,), (0,)), ((), ())), preferred_element_type=jnp.float32
    )


def layer_norm(values_in):
    row_mean = jnp.mean(values_in, axis=-1, keepdims=True)
    centered = values_in - row_mean
    variance = jnp.mean(centered * centered, axis=-1, keepdims=True)
    return centered * lax.rsqrt(variance + norm_eps)


def norm_back(values_in, grad_in):
    row_mean = jnp.mean(values_in, axis=-1, keepdims=True)
    centered = values_in - row_mean
    inverse = lax.rsqrt(jnp.mean(centered * centered, axis=-1, keepdims=True) + norm_eps)
    unit_rows = centered * inverse
    return inverse * (
        grad_in
        - jnp.mean(grad_in, axis=-1, keepdims=True)
        - unit_rows * jnp.mean(grad_in * unit_rows, axis=-1, keepdims=True)
    )


def rope_tables(position, head_dim):
    half_dim = head_dim // 2
    frequency = rope_base ** (-(jnp.arange(half_dim, dtype=jnp.float32) * 2.0) / head_dim)
    angles = position.astype(jnp.float32)[:, None] * frequency[None, :]
    return (jnp.cos(angles), jnp.sin(angles))


def rotate(values_in, cosine, sine_table):
    half_dim = values_in.shape[-1] // 2
    first_half = values_in[..., :half_dim]
    second_half = values_in[..., half_dim:]
    cos_rows = cosine[:, None, :]
    sin_rows = sine_table[:, None, :]
    return jnp.concatenate(
        [
            first_half * cos_rows - second_half * sin_rows,
            second_half * cos_rows + first_half * sin_rows,
        ],
        axis=-1,
    )


def rotate_back(grad_in, cosine, sine_table):
    half_dim = grad_in.shape[-1] // 2
    first_half = grad_in[..., :half_dim]
    second_half = grad_in[..., half_dim:]
    cos_rows = cosine[:, None, :]
    sin_rows = sine_table[:, None, :]
    return jnp.concatenate(
        [
            first_half * cos_rows + second_half * sin_rows,
            second_half * cos_rows - first_half * sin_rows,
        ],
        axis=-1,
    )


def segments(lengths):
    load_ends = jnp.cumsum(lengths)
    row_index = jnp.arange(GROUP_CAP, dtype=jnp.int32)
    segment = jnp.sum((row_index[:, None] >= load_ends[None, :]).astype(jnp.int32), axis=1)
    seg_starts = jnp.concatenate([jnp.zeros((1,), jnp.int32), load_ends])
    slot_ids = jnp.arange(SEQ_SLOTS + 1, dtype=jnp.int32)
    begin_row = jnp.sum(
        jnp.where(segment[:, None] == slot_ids[None, :], seg_starts[None, :], 0), axis=1
    )
    return (segment, row_index - begin_row)


def on_device(
    tokens,
    cotangent,
    w_query,
    w_key,
    w_value,
    w_out,
    w_gate,
    w_up,
    w_down,
    seq_lengths,
    deal,
    row_dest,
):
    groups = lax.axis_size("fsdp")
    shards = lax.axis_size("tp")
    own_group = lax.axis_index("fsdp")
    own_shard = lax.axis_index("tp")
    capacity = GROUP_CAP
    per_pair = capacity // groups
    quarter = capacity // shards
    head_dim = HEAD_DIM
    target = row_dest // capacity
    within = row_dest - target * capacity
    hit_table = (target[:, None] == jnp.arange(groups, dtype=jnp.int32)[None, :]).astype(jnp.int32)
    rank_rows = jnp.sum(hit_table * (jnp.cumsum(hit_table, axis=0) - 1), axis=1)
    slot_of = target * per_pair + rank_rows
    send_rows = jnp.zeros((capacity, tokens.shape[1]), jnp.bfloat16).at[slot_of].set(tokens)
    send_grads = jnp.zeros((capacity, tokens.shape[1]), jnp.bfloat16).at[slot_of].set(cotangent)
    send_place = jnp.full((capacity,), capacity, jnp.int32).at[slot_of].set(within)
    recv_rows, recv_grads, recv_place = (
        lax.all_to_all(send_rows, "fsdp", split_axis=0, concat_axis=0, tiled=True),
        lax.all_to_all(send_grads, "fsdp", split_axis=0, concat_axis=0, tiled=True),
        lax.all_to_all(send_place, "fsdp", split_axis=0, concat_axis=0, tiled=True),
    )
    buffer_rows = jnp.zeros_like(recv_rows).at[recv_place].set(recv_rows, mode="drop")
    buffer_grads = jnp.zeros_like(recv_grads).at[recv_place].set(recv_grads, mode="drop")
    full_rows, full_grads = (
        lax.all_gather(buffer_rows, "tp", axis=1, tiled=True),
        lax.all_gather(buffer_grads, "tp", axis=1, tiled=True),
    )
    full_query, full_key, full_value, full_out, full_gate, full_up, full_down = (
        lax.all_gather(w_query, "fsdp", axis=0, tiled=True),
        lax.all_gather(w_key, "fsdp", axis=0, tiled=True),
        lax.all_gather(w_value, "fsdp", axis=0, tiled=True),
        lax.all_gather(w_out, "fsdp", axis=0, tiled=True),
        lax.all_gather(w_gate, "fsdp", axis=0, tiled=True),
        lax.all_gather(w_up, "fsdp", axis=0, tiled=True),
        lax.all_gather(w_down, "fsdp", axis=0, tiled=True),
    )
    list_index = jnp.sum(jnp.where(deal == own_group, jnp.arange(groups, dtype=jnp.int32), 0))
    lengths = lax.dynamic_index_in_dim(seq_lengths, list_index, 0, keepdims=False)
    segment, position = segments(lengths)
    row_start = own_shard * quarter
    input_here = lax.dynamic_slice_in_dim(full_rows, row_start, quarter, 0).astype(jnp.float32)
    grad_here = lax.dynamic_slice_in_dim(full_grads, row_start, quarter, 0).astype(jnp.float32)
    normed_one = layer_norm(full_rows.astype(jnp.float32)).astype(jnp.bfloat16)
    cosine, sine_table = rope_tables(position, head_dim)
    local_heads = full_query.shape[1] // head_dim
    query_pre = matmul(normed_one, full_query).reshape(capacity, local_heads, head_dim)
    key_pre = matmul(normed_one, full_key).reshape(capacity, local_heads, head_dim)
    value_rows = (
        matmul(normed_one, full_value).astype(jnp.bfloat16).reshape(capacity, local_heads, head_dim)
    )
    queries = rotate(query_pre, cosine, sine_table).astype(jnp.bfloat16)
    key_rows = rotate(key_pre, cosine, sine_table).astype(jnp.bfloat16)
    block_rows = min(512, capacity)
    score_scale = head_dim ** (-0.5)
    row_index = jnp.arange(capacity, dtype=jnp.int32)
    outputs = []
    log_parts = []
    for row_first in range(0, capacity, block_rows):
        q_rows = queries[row_first : row_first + block_rows]
        allowed = (segment[row_first : row_first + block_rows, None] == segment[None, :]) & (
            row_index[None, :] <= row_index[row_first : row_first + block_rows, None]
        )
        scores = (
            jnp.einsum("qhd,khd->hqk", q_rows, key_rows, preferred_element_type=jnp.float32)
            * score_scale
        )
        scores = jnp.where(allowed[None], scores, -1e30)
        row_max = jnp.max(scores, axis=-1, keepdims=True)
        exponent = jnp.exp(scores - row_max)
        row_total = jnp.sum(exponent, axis=-1, keepdims=True)
        prob_low = (exponent / row_total).astype(jnp.bfloat16)
        outputs.append(
            jnp.einsum(
                "hqk,khd->qhd", prob_low, value_rows, preferred_element_type=jnp.float32
            ).astype(jnp.bfloat16)
        )
        log_parts.append(row_max + jnp.log(row_total))
    attended = jnp.concatenate(outputs, axis=0).reshape(capacity, local_heads * head_dim)
    attn_here = lax.psum_scatter(matmul(attended, full_out), "tp", scatter_dimension=0, tiled=True)
    hidden_here = input_here + attn_here
    normed_two = lax.all_gather(
        layer_norm(hidden_here).astype(jnp.bfloat16), "tp", axis=0, tiled=True
    )
    gate_pre = matmul(normed_two, full_gate)
    up_pre = matmul(normed_two, full_up)
    activated = (jax.nn.silu(gate_pre) * up_pre).astype(jnp.bfloat16)
    mlp_here = lax.psum_scatter(
        matmul(activated, full_down).astype(jnp.bfloat16), "tp", scatter_dimension=0, tiled=True
    ).astype(jnp.float32)
    output_here = hidden_here + mlp_here
    down_grad = times_transposed(full_grads, full_down)
    sigmoid_gate = jax.nn.sigmoid(gate_pre)
    gate_grad = (
        down_grad * up_pre * sigmoid_gate * (1.0 + gate_pre * (1.0 - sigmoid_gate))
    ).astype(jnp.bfloat16)
    up_grad = (down_grad * gate_pre * sigmoid_gate).astype(jnp.bfloat16)
    grad_down = transposed_times(activated, full_grads)
    grad_gate = transposed_times(normed_two, gate_grad)
    grad_up = transposed_times(normed_two, up_grad)
    normed_two_grad = lax.psum_scatter(
        times_transposed(gate_grad, full_gate) + times_transposed(up_grad, full_up),
        "tp",
        scatter_dimension=0,
        tiled=True,
    )
    hidden_grad = grad_here + norm_back(hidden_here, normed_two_grad)
    hidden_grad_full = lax.all_gather(hidden_grad.astype(jnp.bfloat16), "tp", axis=0, tiled=True)
    attended_grad = (
        times_transposed(hidden_grad_full, full_out)
        .astype(jnp.bfloat16)
        .reshape(capacity, local_heads, head_dim)
    )
    grad_out = transposed_times(attended, hidden_grad_full)
    query_parts = []
    key_sum = jnp.zeros((capacity, local_heads, head_dim), jnp.float32)
    value_sum = jnp.zeros((capacity, local_heads, head_dim), jnp.float32)
    for part_index, row_first in enumerate(range(0, capacity, block_rows)):
        q_rows = queries[row_first : row_first + block_rows]
        grad_rows = attended_grad[row_first : row_first + block_rows]
        allowed = (segment[row_first : row_first + block_rows, None] == segment[None, :]) & (
            row_index[None, :] <= row_index[row_first : row_first + block_rows, None]
        )
        scores = (
            jnp.einsum("qhd,khd->hqk", q_rows, key_rows, preferred_element_type=jnp.float32)
            * score_scale
        )
        probs = jnp.where(allowed[None], jnp.exp(scores - log_parts[part_index]), 0.0)
        prob_low = probs.astype(jnp.bfloat16)
        prob_grad = jnp.einsum(
            "qhd,khd->hqk", grad_rows, value_rows, preferred_element_type=jnp.float32
        )
        row_delta = jnp.sum(prob_grad * probs, axis=-1, keepdims=True)
        score_grad = (probs * (prob_grad - row_delta)).astype(jnp.bfloat16)
        query_parts.append(
            jnp.einsum("hqk,khd->qhd", score_grad, key_rows, preferred_element_type=jnp.float32)
            * score_scale
        )
        key_sum = (
            key_sum
            + jnp.einsum("hqk,qhd->khd", score_grad, q_rows, preferred_element_type=jnp.float32)
            * score_scale
        )
        value_sum = value_sum + jnp.einsum(
            "hqk,qhd->khd", prob_low, grad_rows, preferred_element_type=jnp.float32
        )
    query_grad = (
        rotate_back(jnp.concatenate(query_parts, axis=0), cosine, sine_table)
        .astype(jnp.bfloat16)
        .reshape(capacity, local_heads * head_dim)
    )
    key_grad = (
        rotate_back(key_sum, cosine, sine_table)
        .astype(jnp.bfloat16)
        .reshape(capacity, local_heads * head_dim)
    )
    value_grad = value_sum.astype(jnp.bfloat16).reshape(capacity, local_heads * head_dim)
    grad_query = transposed_times(normed_one, query_grad)
    grad_key = transposed_times(normed_one, key_grad)
    grad_value = transposed_times(normed_one, value_grad)
    normed_one_grad = lax.psum_scatter(
        (
            times_transposed(query_grad, full_query)
            + times_transposed(key_grad, full_key)
            + times_transposed(value_grad, full_value)
        ).astype(jnp.bfloat16),
        "tp",
        scatter_dimension=0,
        tiled=True,
    ).astype(jnp.float32)
    input_grad = hidden_grad + norm_back(input_here, normed_one_grad)
    sum_query, sum_key, sum_value, sum_out, sum_gate, sum_up, sum_down = (
        lax.psum_scatter(
            grad_query.astype(jnp.bfloat16), "fsdp", scatter_dimension=0, tiled=True
        ).astype(jnp.float32),
        lax.psum_scatter(
            grad_key.astype(jnp.bfloat16), "fsdp", scatter_dimension=0, tiled=True
        ).astype(jnp.float32),
        lax.psum_scatter(
            grad_value.astype(jnp.bfloat16), "fsdp", scatter_dimension=0, tiled=True
        ).astype(jnp.float32),
        lax.psum_scatter(
            grad_out.astype(jnp.bfloat16), "fsdp", scatter_dimension=0, tiled=True
        ).astype(jnp.float32),
        lax.psum_scatter(
            grad_gate.astype(jnp.bfloat16), "fsdp", scatter_dimension=0, tiled=True
        ).astype(jnp.float32),
        lax.psum_scatter(
            grad_up.astype(jnp.bfloat16), "fsdp", scatter_dimension=0, tiled=True
        ).astype(jnp.float32),
        lax.psum_scatter(
            grad_down.astype(jnp.bfloat16), "fsdp", scatter_dimension=0, tiled=True
        ).astype(jnp.float32),
    )
    back_rows, back_grads = (
        lax.all_to_all(
            output_here.astype(jnp.bfloat16), "tp", split_axis=1, concat_axis=0, tiled=True
        ),
        lax.all_to_all(
            input_grad.astype(jnp.bfloat16), "tp", split_axis=1, concat_axis=0, tiled=True
        ),
    )
    place_read = jnp.minimum(recv_place, capacity - 1)
    home_rows, home_grads = (
        lax.all_to_all(back_rows[place_read], "fsdp", split_axis=0, concat_axis=0, tiled=True),
        lax.all_to_all(back_grads[place_read], "fsdp", split_axis=0, concat_axis=0, tiled=True),
    )
    return (
        home_rows[slot_of],
        home_grads[slot_of],
        sum_query,
        sum_key,
        sum_value,
        sum_out,
        sum_gate,
        sum_up,
        sum_down,
    )


def solution(mesh):
    in_specs = (
        P("fsdp", "tp"),
        P("fsdp", "tp"),
        P("fsdp", "tp"),
        P("fsdp", "tp"),
        P("fsdp", "tp"),
        P(("tp", "fsdp"), None),
        P("fsdp", "tp"),
        P("fsdp", "tp"),
        P(("tp", "fsdp"), None),
        P(),
        P(),
        P("fsdp"),
    )
    out_specs = (
        P("fsdp", "tp"),
        P("fsdp", "tp"),
        P("fsdp", "tp"),
        P("fsdp", "tp"),
        P("fsdp", "tp"),
        P(("tp", "fsdp"), None),
        P("fsdp", "tp"),
        P("fsdp", "tp"),
        P(("tp", "fsdp"), None),
    )
    return jax.shard_map(
        on_device, mesh=mesh, in_specs=in_specs, out_specs=out_specs, check_vma=False
    )
```

profile of v0, /device:TPU:16, one launch (start us, length us, event | category | flops | bytes accessed | tf_op | source)
XLA Modules:
  0.0 1681.5 jit_solution(4581085192667695403)
XLA Ops:
  20.7 7.0 scatter_custom_fusion.1
  32.6 14.8 all-to-all-done.1
  47.4 6.1 scatter_custom_fusion.2
  64.1 68.1 %all-gather.12.cloned.1.call-done = bf16[1024,2048]{1,0:T(8,128)(2,1)} async-done(((bf16[1024,512]{1,0:T(8,128)(2,1)}), bf16[1024,2048]{1,0:T(8,128)(2,1)}) %all-gather.12.cloned.1.call-update) | async-done | bytes 4194320 | tf_op jit(solution)/shard_map/all_gather | solution.py:137
  139.5 22.5 %all-gather.18.cloned.1.call-done = bf16[2048,512]{1,0:T(8,128)(2,1)} async-done(((bf16[256,512]{1,0:T(8,128)(2,1)}), bf16[2048,512]{1,0:T(8,128)(2,1)}) %all-gather.18.cloned.1.call-update) | async-done | bytes 2097168 | tf_op jit(solution)/shard_map/all_gather | solution.py:142
  171.2 20.6 %all-gather.16.cloned.1.call-done = bf16[2048,512]{1,0:T(8,128)(2,1)} async-done(((bf16[256,512]{1,0:T(8,128)(2,1)}), bf16[2048,512]{1,0:T(8,128)(2,1)}) %all-gather.16.cloned.1.call-update) | async-done | bytes 2097168 | tf_op jit(solution)/shard_map/all_gather | solution.py:141
  212.2 14.3 fusion.5
  251.1 7.2 fusion.80
  260.7 143.1 %reduce-scatter.12.cloned.1.call-done = f32[256,2048]{1,0:T(8,128)} async-done(((f32[1024,2048]{1,0:T(8,128)}), f32[256,2048]{1,0:T(8,128)}) %reduce-scatter.12.cloned.1.call-update) | async-done | bytes 2097168 | tf_op jit(solution)/shard_map/reduce_scatter | solution.py:191
  409.3 6.3 scatter_custom_fusion.3
  415.6 24.0 %all_to_all.98 = bf16[8,128,512]{2,1,0:T(8,128)(2,1)} all-to-all(bf16[8,128,512]{2,1,0:T(8,128)(2,1)S(1)} %bitcast.142), channel_id=1, replica_groups=mesh['fsdp'=8,'tp'=4] {'fsdp'}, dimensions={0} | all-to-all | bytes 2097152 | tf_op jit(solution)/shard_map/all_to_all | solution.py:131
  439.6 6.6 scatter_custom_fusion.4
  447.0 24.3 %all-gather.26.cloned.1.call-done = bf16[2048,2048]{1,0:T(8,128)(2,1)} async-done(((bf16[256,2048]{1,0:T(8,128)(2,1)}), bf16[2048,2048]{1,0:T(8,128)(2,1)}) %all-gather.26.cloned.1.call-update) | async-done | bytes 8388624 | tf_op jit(solution)/shard_map/all_gather | solution.py:146
  471.3 81.5 %all-gather.22.cloned.1.call-done = bf16[1024,2048]{1,0:T(8,128)(2,1)} async-done(((bf16[256,2048]{1,0:T(8,128)(2,1)}), bf16[1024,2048]{1,0:T(8,128)(2,1)}) %all-gather.22.cloned.1.call-update) | async-done | bytes 4194320 | tf_op jit(solution)/shard_map/all_gather | solution.py:193
  552.8 14.8 fusion.82
  567.6 41.5 %all-gather.24.cloned.1.call-done = bf16[2048,2048]{1,0:T(8,128)(2,1)} async-done(((bf16[256,2048]{1,0:T(8,128)(2,1)}), bf16[2048,2048]{1,0:T(8,128)(2,1)}) %all-gather.24.cloned.1.call-update) | async-done | bytes 8388624 | tf_op jit(solution)/shard_map/all_gather | solution.py:145
  609.1 14.4 fusion.81
  623.5 66.9 %all-gather.30.cloned.1.call-done = bf16[1024,2048]{1,0:T(8,128)(2,1)} async-done(((bf16[1024,512]{1,0:T(8,128)(2,1)}), bf16[1024,2048]{1,0:T(8,128)(2,1)}) %all-gather.30.cloned.1.call-update) | async-done | bytes 4194320 | tf_op jit(solution)/shard_map/all_gather | solution.py:138
  690.4 56.3 %all-gather.28.cloned.1.call-done = bf16[2048,2048]{1,0:T(8,128)(2,1)} async-done(((bf16[256,2048]{1,0:T(8,128)(2,1)}), bf16[2048,2048]{1,0:T(8,128)(2,1)}) %all-gather.28.cloned.1.call-update) | async-done | bytes 8388624 | tf_op jit(solution)/shard_map/all_gather | solution.py:147
  746.7 21.9 %multiply_convert_fusion.2 = (bf16[1024,2048]{1,0:T(8,128)(2,1)}, bf16[1024,2048]{1,0:T(8,128)(2,1)}, bf16[1024,2048]{1,0:T(8,128)(2,1)}) fusion(f32[1024,2048]{1,0:T(8,128)} %fusion.81, f32[1024,2048]{1,0:T(8,128)} %fusion.82, bf16[1024,2048]{1,0:T(8,128)(2,1)} %all-gather.30.cloned.1.call-done, bf16[2048,2048]{1,0:T(8,128)(2,1)} %all-gather.28.cloned.1.call-done), kind=kOutput, calls=%fused_computation.22 | convolution fusion | flops 8623489024 | bytes 41943040 | tf_op jit(solution)/shard_map/dot_general | solution.py:20
  768.6 12.9 fusion.83
  781.5 13.5 convolution_add_fusion
  795.1 13.9 convolution_convert_fusion.3
  809.0 131.4 %reduce-scatter.16.cloned.1.call-done = f32[256,2048]{1,0:T(8,128)} async-done(((f32[1024,2048]{1,0:T(8,128)}), f32[256,2048]{1,0:T(8,128)}) %reduce-scatter.16.cloned.1.call-update) | async-done | bytes 2097168 | tf_op jit(solution)/shard_map/reduce_scatter | solution.py:212
  942.6 77.4 %reduce-scatter.14.cloned.1.call-done = bf16[256,2048]{1,0:T(8,128)(2,1)} async-done(((bf16[1024,2048]{1,0:T(8,128)(2,1)}), bf16[256,2048]{1,0:T(8,128)(2,1)}) %reduce-scatter.14.cloned.1.call-update) | async-done | bytes 1048592 | tf_op jit(solution)/shard_map/reduce_scatter | solution.py:199
  1025.3 79.3 %all-gather.32.cloned.1.call-done = bf16[1024,2048]{1,0:T(8,128)(2,1)} async-done(((bf16[256,2048]{1,0:T(8,128)(2,1)}), bf16[1024,2048]{1,0:T(8,128)(2,1)}) %all-gather.32.cloned.1.call-update) | async-done | bytes 4194320 | tf_op jit(solution)/shard_map/all_gather | solution.py:219
  1110.0 7.0 fusion.8
  1117.0 6.4 multiply_reduce_fusion
  1129.2 8.7 multiply_convert_fusion
  1169.3 14.3 convolution_convert_fusion
  1183.7 14.1 convolution_convert_fusion.1
  1197.9 14.5 convolution_convert_fusion.2
  1213.7 5.9 convolution_convert_fusion.4
  1219.7 6.1 convolution_convert_fusion.5
  1225.9 6.1 convolution_convert_fusion.7
  1238.7 12.2 reduce-scatter.18.cloned.1.call-done
  1256.6 8.9 all-to-all-done.2
  1265.4 6.8 all-to-all-start.5
  1272.2 5.9 convolution_convert_fusion.6
  1283.3 11.9 all-to-all-done.5
  1303.9 12.2 all-to-all-done.3
  1319.7 17.7 %reduce-scatter.32.cloned.1.call-done = bf16[256,2048]{1,0:T(8,128)(2,1)} async-done(((bf16[2048,2048]{1,0:T(8,128)(2,1)}), bf16[256,2048]{1,0:T(8,128)(2,1)}) %reduce-scatter.32.cloned.1.call-update) | async-done | bytes 1048592 | tf_op jit(solution)/shard_map/reduce_scatter | solution.py:302
  1340.2 75.2 %reduce-scatter.30.cloned.1.call-done = bf16[256,2048]{1,0:T(8,128)(2,1)} async-done(((bf16[2048,2048]{1,0:T(8,128)(2,1)}), bf16[256,2048]{1,0:T(8,128)(2,1)}) %reduce-scatter.30.cloned.1.call-update) | async-done | bytes 1048592 | tf_op jit(solution)/shard_map/reduce_scatter | solution.py:299
  1418.2 71.8 %reduce-scatter.28.cloned.1.call-done = bf16[256,2048]{1,0:T(8,128)(2,1)} async-done(((bf16[2048,2048]{1,0:T(8,128)(2,1)}), bf16[256,2048]{1,0:T(8,128)(2,1)}) %reduce-scatter.28.cloned.1.call-update) | async-done | bytes 1048592 | tf_op jit(solution)/shard_map/reduce_scatter | solution.py:296
  1496.8 38.1 %reduce-scatter.26.cloned.1.call-done = bf16[64,2048]{1,0:T(8,128)(2,1)} async-done(((bf16[512,2048]{1,0:T(8,128)(2,1)}), bf16[64,2048]{1,0:T(8,128)(2,1)}) %reduce-scatter.26.cloned.1.call-update) | async-done | bytes 262160 | tf_op jit(solution)/shard_map/reduce_scatter | solution.py:293
  1536.6 42.6 %reduce-scatter.24.cloned.1.call-done = bf16[256,512]{1,0:T(8,128)(2,1)} async-done(((bf16[2048,512]{1,0:T(8,128)(2,1)}), bf16[256,512]{1,0:T(8,128)(2,1)}) %reduce-scatter.24.cloned.1.call-update) | async-done | bytes 262160 | tf_op jit(solution)/shard_map/reduce_scatter | solution.py:290
  1581.0 43.1 %reduce-scatter.20.cloned.1.call-done = bf16[256,512]{1,0:T(8,128)(2,1)} async-done(((bf16[2048,512]{1,0:T(8,128)(2,1)}), bf16[256,512]{1,0:T(8,128)(2,1)}) %reduce-scatter.20.cloned.1.call-update) | async-done | bytes 262160 | tf_op jit(solution)/shard_map/reduce_scatter | solution.py:284
  1625.9 42.7 %reduce-scatter.22.cloned.1.call-done = bf16[256,512]{1,0:T(8,128)(2,1)} async-done(((bf16[2048,512]{1,0:T(8,128)(2,1)}), bf16[256,512]{1,0:T(8,128)(2,1)}) %reduce-scatter.22.cloned.1.call-update) | async-done | bytes 262160 | tf_op jit(solution)/shard_map/reduce_scatter | solution.py:287
  (259 shorter events, 201.2 us)
Async XLA Ops:
  7.2 52.0 %copy-start = (s32[8,4]{0,1:T(4,128)S(1)}, s32[8,4]{0,1:T(4,128)}, u32[]{:S(2)}) copy-start(s32[8,4]{0,1:T(4,128)} %param.21) | copy-start | bytes 388
  7.2 49.4 %copy-start.46 = (s32[8]{0:T(128)S(1)}, s32[8]{0:T(128)}, u32[]{:S(2)}) copy-start(s32[8]{0:T(128)} %param.22) | copy-start | bytes 100
  11.2 398.1 %copy-start.40 = (s32[896]{0:T(1024)}, s32[896]{0:T(1024)S(1)}, u32[]{:S(2)}) copy-start(s32[896]{0:T(1024)S(1)} %get-tuple-element.49) | copy-start | bytes 10756
  17.0 10.8 all-to-all-start
  27.8 19.6 %all-to-all-start.1 = ((bf16[8,128,512]{2,1,0:T(8,128)(2,1)}), bf16[8,128,512]{2,1,0:T(8,128)(2,1)S(1)}, u32[]{:S(2)}, u32[]{:S(2)}) async-start(bf16[8,128,512]{2,1,0:T(8,128)(2,1)} %bitcast.8), calls=%async_computation.1 | async-start | bytes 2097152 | tf_op jit(solution)/shard_map/all_to_all | solution.py:130
  32.0 100.2 %all-gather.12.cloned.1.call-start = ((), (), s32[]{:S(2)}) async-start(), calls=%async_computation.18 | async-start | bytes 5242880 | tf_op jit(solution)/shard_map/all_gather | solution.py:137
  53.5 108.5 %all-gather.18.cloned.1.call-start = ((), (), s32[]{:S(2)}) async-start(), calls=%async_computation.21 | async-start | bytes 2359296 | tf_op jit(solution)/shard_map/all_gather | solution.py:142
  54.2 137.6 %all-gather.16.cloned.1.call-start = ((), (), s32[]{:S(2)}) async-start(), calls=%async_computation.20 | async-start | bytes 2359296 | tf_op jit(solution)/shard_map/all_gather | solution.py:141
  55.0 171.5 %all-gather.14.cloned.1.call-start = ((), (), s32[]{:S(2)}) async-start(), calls=%async_computation.19 | async-start | bytes 2359296 | tf_op jit(solution)/shard_map/all_gather | solution.py:143
  55.5 195.6 %all-gather.20.cloned.1.call-start = ((), (), s32[]{:S(2)}) async-start(), calls=%async_computation.22 | async-start | bytes 2359296 | tf_op jit(solution)/shard_map/all_gather | solution.py:144
  56.1 347.6 %reduce-scatter.12.cloned.1.call-start = ((), (), s32[]{:S(2)}) async-start(), calls=%async_computation.23 | async-start | bytes 10485760 | tf_op jit(solution)/shard_map/reduce_scatter | solution.py:191
  64.1 172.4 %copy-start.13 = (pred[512,1024]{1,0:T(8,128)(4,1)}, pred[512,1024]{1,0:T(8,128)(4,1)S(1)}, u32[]{:S(2)}) copy-start(pred[512,1024]{1,0:T(8,128)(4,1)S(1)} %get-tuple-element.45) | copy-start | bytes 1572868
  64.1 179.8 %copy-start.10 = (pred[512,1024]{1,0:T(8,128)(4,1)}, pred[512,1024]{1,0:T(8,128)(4,1)S(1)}, u32[]{:S(2)}) copy-start(pred[512,1024]{1,0:T(8,128)(4,1)S(1)} %get-tuple-element.44) | copy-start | bytes 1572868
  206.1 25.7 %copy-start.7 = (bf16[1024,4,64]{2,0,1:T(8,128)(2,1)}, bf16[1024,4,64]{2,0,1:T(8,128)(2,1)S(1)}, u32[]{:S(2)}) copy-start(bf16[1024,4,64]{2,0,1:T(8,128)(2,1)S(1)} %get-tuple-element.38) | copy-start | bytes 1572868
  206.1 25.7 %copy-start.9 = (bf16[1024,4,64]{2,0,1:T(8,128)(2,1)}, bf16[1024,4,64]{2,0,1:T(8,128)(2,1)S(1)}, u32[]{:S(2)}) copy-start(bf16[1024,4,64]{2,0,1:T(8,128)(2,1)S(1)} %get-tuple-element.39) | copy-start | bytes 1572868
  208.9 27.7 %copy-start.35 = (f32[4,512]{1,0:T(4,128)}, f32[4,512]{1,0:T(4,128)S(1)}, u32[]{:S(2)}) copy-start(f32[4,512]{1,0:T(4,128)S(1)} %get-tuple-element.52) | copy-start | bytes 24580
  231.8 12.2 copy-start.24
  258.4 212.9 %all-gather.26.cloned.1.call-start = ((), (), s32[]{:S(2)}) async-start(), calls=%async_computation.26 | async-start | bytes 9437184 | tf_op jit(solution)/shard_map/all_gather | solution.py:146
  259.1 293.6 %all-gather.22.cloned.1.call-start = ((), (), s32[]{:S(2)}) async-start(), calls=%async_computation.24 | async-start | bytes 5242880 | tf_op jit(solution)/shard_map/all_gather | solution.py:193
  260.7 146.2 %copy-start.42 = (f32[256]{0:T(256)}, f32[256]{0:T(256)S(1)}, u32[]{:S(2)}) copy-start(f32[256]{0:T(256)S(1)} %broadcast_multiply_fusion.3) | copy-start | bytes 3076
  408.5 200.6 %all-gather.24.cloned.1.call-start = ((), (), s32[]{:S(2)}) async-start(), calls=%async_computation.25 | async-start | bytes 9437184 | tf_op jit(solution)/shard_map/all_gather | solution.py:145
  409.2 281.2 %all-gather.30.cloned.1.call-start = ((), (), s32[]{:S(2)}) async-start(), calls=%async_computation.29 | async-start | bytes 5242880 | tf_op jit(solution)/shard_map/all_gather | solution.py:138
  446.2 300.5 %all-gather.28.cloned.1.call-start = ((), (), s32[]{:S(2)}) async-start(), calls=%async_computation.27 | async-start | bytes 9437184 | tf_op jit(solution)/shard_map/all_gather | solution.py:147
  447.0 493.4 %reduce-scatter.16.cloned.1.call-start = ((), (), s32[]{:S(2)}) async-start(), calls=%async_computation.30 | async-start | bytes 10485760 | tf_op jit(solution)/shard_map/reduce_scatter | solution.py:212
  768.6 12.9 copy-start.48
  795.0 225.0 %reduce-scatter.14.cloned.1.call-start = ((), (), s32[]{:S(2)}) async-start(), calls=%async_computation.28 | async-start | bytes 5242880 | tf_op jit(solution)/shard_map/reduce_scatter | solution.py:199
  809.0 295.7 %all-gather.32.cloned.1.call-start = ((), (), s32[]{:S(2)}) async-start(), calls=%async_computation.31 | async-start | bytes 5242880 | tf_op jit(solution)/shard_map/all_gather | solution.py:219
  942.6 82.7 %copy-start.36 = (f32[4,512]{1,0:T(4,128)S(1)}, f32[4,512]{1,0:T(4,128)}, u32[]{:S(2)}) copy-start(f32[4,512]{1,0:T(4,128)} %copy-done.35) | copy-start | bytes 24580
  942.6 82.7 %copy-start.38 = (f32[4,512]{1,0:T(4,128)S(1)}, f32[4,512]{1,0:T(4,128)}, u32[]{:S(2)}) copy-start(f32[4,512]{1,0:T(4,128)} %copy-done.37) | copy-start | bytes 24580
  1025.2 225.7 %reduce-scatter.18.cloned.1.call-start = ((), (), s32[]{:S(2)}) async-start(), calls=%async_computation.32 | async-start | bytes 5242880 | tf_op jit(solution)/shard_map/reduce_scatter | solution.py:272
  1025.3 84.7 %copy-start.14 = (pred[512,1024]{1,0:T(8,128)(4,1)S(1)}, pred[512,1024]{1,0:T(8,128)(4,1)}, u32[]{:S(2)}) copy-start(pred[512,1024]{1,0:T(8,128)(4,1)} %copy-done.13) | copy-start | bytes 1572868
  1110.0 13.5 copy-start.27
  1110.0 13.4 slice-start
  1169.2 168.1 %reduce-scatter.32.cloned.1.call-start = ((), (), s32[]{:S(2)}) async-start(), calls=%async_computation.39 | async-start | bytes 9437184 | tf_op jit(solution)/shard_map/reduce_scatter | solution.py:302
  1183.7 231.7 %reduce-scatter.30.cloned.1.call-start = ((), (), s32[]{:S(2)}) async-start(), calls=%async_computation.38 | async-start | bytes 9437184 | tf_op jit(solution)/shard_map/reduce_scatter | solution.py:299
  1197.9 292.1 %reduce-scatter.28.cloned.1.call-start = ((), (), s32[]{:S(2)}) async-start(), calls=%async_computation.37 | async-start | bytes 9437184 | tf_op jit(solution)/shard_map/reduce_scatter | solution.py:296
  1212.5 322.4 %reduce-scatter.26.cloned.1.call-start = ((), (), s32[]{:S(2)}) async-start(), calls=%async_computation.36 | async-start | bytes 2359296 | tf_op jit(solution)/shard_map/reduce_scatter | solution.py:293
  1219.6 359.6 %reduce-scatter.24.cloned.1.call-start = ((), (), s32[]{:S(2)}) async-start(), calls=%async_computation.35 | async-start | bytes 2359296 | tf_op jit(solution)/shard_map/reduce_scatter | solution.py:290
  1225.8 398.3 %reduce-scatter.20.cloned.1.call-start = ((), (), s32[]{:S(2)}) async-start(), calls=%async_computation.33 | async-start | bytes 2359296 | tf_op jit(solution)/shard_map/reduce_scatter | solution.py:284
  1232.0 18.9 %copy-start.43 = (f32[256]{0:T(256)S(1)}, f32[256]{0:T(256)}, u32[]{:S(2)}) copy-start(f32[256]{0:T(256)} %copy-done.42) | copy-start | bytes 3076
  1232.0 21.2 %copy-start.18 = (f32[256,2048]{1,0:T(8,128)S(1)}, f32[256,2048]{1,0:T(8,128)}, u32[]{:S(2)}) copy-start(f32[256,2048]{1,0:T(8,128)} %get-tuple-element.14) | copy-start | bytes 6291460
  1233.1 32.3 %all-to-all-start.2 = ((bf16[256,4,512]{2,0,1:T(8,128)(2,1)}), bf16[256,4,512]{2,0,1:T(8,128)(2,1)S(1)}, u32[]{:S(2)}, u32[]{:S(2)}) async-start(bf16[256,4,512]{2,0,1:T(8,128)(2,1)} %bitcast.141), calls=%async_computation.4 | async-start | bytes 2097152 | tf_op jit(solution)/shard_map/all_to_all | solution.py:307
  1255.5 16.7 copy-start.32
  1265.4 29.8 %all-to-all-start.5 = ((bf16[256,4,512]{2,0,1:T(8,128)(2,1)}), bf16[256,4,512]{2,0,1:T(8,128)(2,1)S(1)}, u32[]{:S(2)}, u32[]{:S(2)}) async-start(bf16[256,4,512]{2,0,1:T(8,128)(2,1)} %bitcast.122), calls=%async_computation.9 | async-start | bytes 2097152 | tf_op jit(solution)/shard_map/all_to_all | solution.py:310
  1272.2 396.5 %reduce-scatter.22.cloned.1.call-start = ((), (), s32[]{:S(2)}) async-start(), calls=%async_computation.34 | async-start | bytes 2359296 | tf_op jit(solution)/shard_map/reduce_scatter | solution.py:287
  1295.2 20.9 %all-to-all-start.3 = ((bf16[8,128,512]{2,1,0:T(8,128)(2,1)}), bf16[8,128,512]{2,1,0:T(8,128)(2,1)S(1)}, u32[]{:S(2)}, u32[]{:S(2)}) async-start(bf16[8,128,512]{2,1,0:T(8,128)(2,1)} %bitcast.140), calls=%async_computation.5 | async-start | bytes 2097152 | tf_op jit(solution)/shard_map/all_to_all | solution.py:316
  1298.9 20.8 %copy-start.41 = (s32[896]{0:T(1024)S(1)}, s32[896]{0:T(1024)}, u32[]{:S(2)}) copy-start(s32[896]{0:T(1024)} %copy-done.40) | copy-start | bytes 10756
  1316.1 354.4 %all-to-all-start.6 = ((bf16[8,128,512]{2,1,0:T(8,128)(2,1)}), bf16[8,128,512]{2,1,0:T(8,128)(2,1)S(1)}, u32[]{:S(2)}, u32[]{:S(2)}) async-start(bf16[8,128,512]{2,1,0:T(8,128)(2,1)} %bitcast.139), calls=%async_computation.10 | async-start | bytes 2097152 | tf_op jit(solution)/shard_map/all_to_all | solution.py:317
  (33 other events, 161.7 us)
Sparse Core Ops, SparseCore 0:
  53.6 78.5 all-gather.11
  134.1 27.8 all-gather.17
  163.9 27.8 all-gather.15
  193.5 27.8 all-gather.13
  223.2 27.8 all-gather.19
  258.5 145.1 reduce-scatter.11
  405.6 65.6 all-gather.25
  473.4 79.2 all-gather.21
  554.7 54.3 all-gather.23
  611.1 79.2 all-gather.29
  692.3 54.3 all-gather.27
  795.1 145.2 reduce-scatter.15
  942.7 77.2 reduce-scatter.13
  1025.3 79.2 all-gather.31
  1169.4 81.4 reduce-scatter.17
  1254.2 83.1 reduce-scatter.31
  1341.1 74.2 reduce-scatter.29
  1418.7 71.2 reduce-scatter.27
  1493.6 41.1 reduce-scatter.25
  1538.0 41.1 reduce-scatter.23
  1582.9 41.2 reduce-scatter.19
  1627.4 41.1 reduce-scatter.21
where the time goes:
time: 1690 us; the launch traced here: 1680 us
  waiting for transfers between devices  1210 us (72%)
  matrix products  241 us (14%)
  other arithmetic  84.7 us (5%)
  local copies, waits for them, and re-layouts  72.9 us (4%)
  starting transfers between devices  28.7 us (2%)
  blocking collectives  24 us (1%)
  between operations  17.5 us (1%)
    reduce_scatter x1, waiting for transfers between devices, on_device(): lax.psum_scatter(matmul(attended, full_out), 'tp', scatter_dimension=0, t...  143 us
    reduce_scatter x1, waiting for transfers between devices, on_device(): lax.psum_scatter(times_transposed(gate_grad, full_gate) + times_transpose...  131 us
    all_gather x1, waiting for transfers between devices, on_device(): lax.all_gather(layer_norm(hidden_here).astype(jnp.bfloat16), 'tp', axis=0...  81.5 us
    all_gather x1, waiting for transfers between devices, on_device(): lax.all_gather(hidden_grad.astype(jnp.bfloat16), 'tp', axis=0, tiled=True)  79.3 us
    reduce_scatter x1, waiting for transfers between devices, on_device(): lax.psum_scatter(matmul(activated, full_down).astype(jnp.bfloat16), 'tp',...  77.4 us
    reduce_scatter x1, waiting for transfers between devices, on_device(): lax.psum_scatter(grad_up.astype(jnp.bfloat16), 'fsdp', scatter_dimension=...  75.2 us
    reduce_scatter x1, waiting for transfers between devices, on_device(): lax.psum_scatter(grad_gate.astype(jnp.bfloat16), 'fsdp', scatter_dimensio...  71.8 us
    all_gather x1, waiting for transfers between devices, on_device(): lax.all_gather(buffer_rows, 'tp', axis=1, tiled=True)  68.1 us
  transfers between devices with their start and end apart: 28, of which 25 were waited for; matrix products, arithmetic and copies ran while one was open for 15% of the time, Pallas kernels for 0%

commit v1 on v0

v1 whole, which is shorter than its diff:
```python
import jax
import jax.numpy as jnp
from jax import lax
from jax.sharding import PartitionSpec as P

HEAD_DIM = 128
GROUP_CAP = 1024
SEQ_SLOTS = 4

norm_eps = 1e-05
rope_base = 10000.0
bf16 = jnp.bfloat16
f32 = jnp.float32


def matmul(left, right):
    return jnp.dot(left, right, preferred_element_type=f32)


def times_transposed(left, right):
    return lax.dot_general(
        left, right, (((1,), (1,)), ((), ())), preferred_element_type=f32
    )


def transposed_times(left, right):
    return lax.dot_general(
        left, right, (((0,), (0,)), ((), ())), preferred_element_type=f32
    )


def norm_parts(values_in):
    row_mean = jnp.mean(values_in, axis=-1, keepdims=True)
    centered = values_in - row_mean
    variance = jnp.mean(centered * centered, axis=-1, keepdims=True)
    inverse = lax.rsqrt(variance + norm_eps)
    return centered * inverse, inverse


def norm_back(values_in, grad_in):
    unit_rows, inverse = norm_parts(values_in)
    return inverse * (
        grad_in
        - jnp.mean(grad_in, axis=-1, keepdims=True)
        - unit_rows * jnp.mean(grad_in * unit_rows, axis=-1, keepdims=True)
    )


def rope_tables(position, head_dim):
    half_dim = head_dim // 2
    frequency = rope_base ** (-(jnp.arange(half_dim, dtype=f32) * 2.0) / head_dim)
    angles = position.astype(f32)[:, None] * frequency[None, :]
    return (jnp.cos(angles), jnp.sin(angles))


def rotate(values_in, cosine, sine_table):
    half_dim = values_in.shape[-1] // 2
    first_half = values_in[..., :half_dim]
    second_half = values_in[..., half_dim:]
    cos_rows = cosine[:, None, :]
    sin_rows = sine_table[:, None, :]
    return jnp.concatenate(
        [
            first_half * cos_rows - second_half * sin_rows,
            second_half * cos_rows + first_half * sin_rows,
        ],
        axis=-1,
    )


def rotate_back(grad_in, cosine, sine_table):
    return rotate(grad_in, cosine, -sine_table)


def segments(lengths):
    row_index = jnp.arange(GROUP_CAP, dtype=jnp.int32)
    slot_ids = jnp.arange(SEQ_SLOTS, dtype=jnp.int32)
    ends = jnp.sum(
        jnp.where(slot_ids[:, None] <= slot_ids[None, :], lengths[:, None], 0), axis=0
    )
    passed = row_index[:, None] >= ends[None, :]
    segment = jnp.sum(passed.astype(jnp.int32), axis=1)
    begin_row = jnp.max(jnp.where(passed, ends[None, :], 0), axis=1)
    return (segment, row_index - begin_row)


def chain_gather(block, axis, size):
    me = lax.axis_index(axis)
    from_low, from_high = [block], [block]
    for step in range(1, size):
        up = [(i, i + 1) for i in range(step - 1, size - 1)]
        down = [(i, i - 1) for i in range(size - step, 0, -1)]
        from_low.append(lax.ppermute(from_low[-1], axis, up))
        from_high.append(lax.ppermute(from_high[-1], axis, down))
    whole = []
    for owner in range(size):
        piece = block
        for step in range(1, size):
            if owner + step < size:
                piece = jnp.where(me == owner + step, from_low[step], piece)
            if owner - step >= 0:
                piece = jnp.where(me == owner - step, from_high[step], piece)
        whole.append(piece)
    return whole


def direct_scatter(pieces_of, axis, size):
    me = lax.axis_index(axis)
    total = None
    order = sorted(range(1, size), key=lambda step: -min(step, size - step))
    for step in order:
        term = pieces_of(lax.rem(me + step, size)).astype(bf16)
        came = lax.ppermute(term, axis, [(i, (i + step) % size) for i in range(size)])
        total = came.astype(f32) if total is None else total + came.astype(f32)
    return total + pieces_of(me)


def on_device(
    tokens,
    cotangent,
    w_query,
    w_key,
    w_value,
    w_out,
    w_gate,
    w_up,
    w_down,
    seq_lengths,
    deal,
    row_dest,
):
    groups = lax.axis_size("fsdp")
    shards = lax.axis_size("tp")
    own_group = lax.axis_index("fsdp")
    own_shard = lax.axis_index("tp")
    capacity = GROUP_CAP
    per_pair = capacity // groups
    quarter = capacity // shards
    head_dim = HEAD_DIM
    given = tokens.shape[0]
    width = tokens.shape[1]
    model = width * shards

    full_qkv = lax.all_gather(
        jnp.concatenate([w_query, w_key, w_value], axis=1), "fsdp", axis=0, tiled=True
    )
    out_rows = jnp.stack(chain_gather(w_out, "tp", shards))
    full_out = lax.all_gather(out_rows, "fsdp", axis=1, tiled=True).reshape(model, model)
    full_gate, full_up, full_down = lax.all_gather(
        jnp.stack([w_gate, w_up, w_down]), "fsdp", axis=1, tiled=True
    )

    target = row_dest // capacity
    within = row_dest - target * capacity
    given_index = jnp.arange(given, dtype=jnp.int32)
    earlier = (target[:, None] == target[None, :]) & (
        given_index[None, :] < given_index[:, None]
    )
    slot_of = target * per_pair + jnp.sum(earlier.astype(jnp.int32), axis=1)
    slots = jnp.arange(capacity, dtype=jnp.int32)
    deal_hit = slots[:, None] == slot_of[None, :]
    deal_out = deal_hit.astype(bf16)
    send_place = jnp.sum(jnp.where(deal_hit, within[None, :] + 1, 0), axis=1) - 1
    recv_place = lax.all_to_all(send_place, "fsdp", split_axis=0, concat_axis=0, tiled=True)
    place_in = (slots[:, None] == recv_place[None, :]).astype(bf16)

    def to_group(rows):
        sent = matmul(deal_out, rows).astype(bf16)
        came = lax.all_to_all(sent, "fsdp", split_axis=0, concat_axis=0, tiled=True)
        return matmul(place_in, came).astype(bf16)

    def to_home(rows):
        sent = transposed_times(place_in, rows).astype(bf16)
        came = lax.all_to_all(sent, "fsdp", split_axis=0, concat_axis=0, tiled=True)
        return transposed_times(deal_out, came).astype(bf16)

    buffer_rows = to_group(tokens)
    buffer_grads = to_group(cotangent)
    full_rows = jnp.concatenate(chain_gather(buffer_rows, "tp", shards), axis=1)

    list_index = jnp.sum(jnp.where(deal == own_group, jnp.arange(groups, dtype=jnp.int32), 0))
    lengths = lax.dynamic_index_in_dim(seq_lengths, list_index, 0, keepdims=False)
    segment, position = segments(lengths)
    row_start = own_shard * quarter

    normed_one = norm_parts(full_rows.astype(f32))[0].astype(bf16)
    cosine, sine_table = rope_tables(position, head_dim)
    local_width = w_query.shape[1]
    local_heads = local_width // head_dim
    qkv = matmul(normed_one, full_qkv)
    query_pre = qkv[:, :local_width].reshape(capacity, local_heads, head_dim)
    key_pre = qkv[:, local_width : 2 * local_width].reshape(capacity, local_heads, head_dim)
    value_rows = qkv[:, 2 * local_width :].astype(bf16).reshape(capacity, local_heads, head_dim)
    queries = rotate(query_pre, cosine, sine_table).astype(bf16)
    key_rows = rotate(key_pre, cosine, sine_table).astype(bf16)
    block_rows = min(512, capacity)
    score_scale = head_dim ** (-0.5)
    row_index = jnp.arange(capacity, dtype=jnp.int32)
    outputs = []
    log_parts = []
    for row_first in range(0, capacity, block_rows):
        q_rows = queries[row_first : row_first + block_rows]
        allowed = (segment[row_first : row_first + block_rows, None] == segment[None, :]) & (
            row_index[None, :] <= row_index[row_first : row_first + block_rows, None]
        )
        scores = (
            jnp.einsum("qhd,khd->hqk", q_rows, key_rows, preferred_element_type=f32)
            * score_scale
        )
        scores = jnp.where(allowed[None], scores, -1e30)
        row_max = jnp.max(scores, axis=-1, keepdims=True)
        exponent = jnp.exp(scores - row_max)
        row_total = jnp.sum(exponent, axis=-1, keepdims=True)
        prob_low = (exponent / row_total).astype(bf16)
        outputs.append(
            jnp.einsum(
                "hqk,khd->qhd", prob_low, value_rows, preferred_element_type=f32
            ).astype(bf16)
        )
        log_parts.append(row_max + jnp.log(row_total))
    attended = jnp.concatenate(outputs, axis=0).reshape(capacity, local_width)

    full_attended = jnp.concatenate(chain_gather(attended, "tp", shards), axis=1)
    full_grads = jnp.concatenate(chain_gather(buffer_grads, "tp", shards), axis=1)
    hidden = full_rows.astype(f32) + matmul(full_attended, full_out)
    normed_two = norm_parts(hidden)[0].astype(bf16)
    gate_pre = matmul(normed_two, full_gate)
    up_pre = matmul(normed_two, full_up)
    activated = (jax.nn.silu(gate_pre) * up_pre).astype(bf16)
    down_grad = times_transposed(full_grads, full_down)
    sigmoid_gate = jax.nn.sigmoid(gate_pre)
    gate_grad = (
        down_grad * up_pre * sigmoid_gate * (1.0 + gate_pre * (1.0 - sigmoid_gate))
    ).astype(bf16)
    up_grad = (down_grad * gate_pre * sigmoid_gate).astype(bf16)

    normed_two_grad = (
        times_transposed(gate_grad, full_gate) + times_transposed(up_grad, full_up)
    ).astype(bf16)
    two_grad_here = direct_scatter(
        lambda owner: lax.dynamic_slice_in_dim(
            normed_two_grad, owner * quarter, quarter, 0
        ).astype(f32),
        "tp",
        shards,
    )

    def own_rows(rows):
        return lax.dynamic_slice_in_dim(rows, row_start, quarter, 0)

    hidden_grad = own_rows(full_grads).astype(f32) + norm_back(own_rows(hidden), two_grad_here)
    hidden_grad_low = hidden_grad.astype(bf16)
    att_grad_here = times_transposed(hidden_grad_low, full_out).astype(bf16)
    attended_grad = lax.all_to_all(
        att_grad_here, "tp", split_axis=1, concat_axis=0, tiled=True
    ).reshape(capacity, local_heads, head_dim)

    grad_mlp = jnp.stack(
        [
            transposed_times(normed_two, gate_grad).astype(bf16),
            transposed_times(normed_two, up_grad).astype(bf16),
            transposed_times(activated, full_grads).astype(bf16),
        ]
    )
    sum_gate, sum_up, sum_down = lax.psum_scatter(
        grad_mlp, "fsdp", scatter_dimension=1, tiled=True
    ).astype(f32)

    mlp_part = matmul(activated, full_down).astype(bf16)

    def own_features(rows, owner):
        return lax.dynamic_slice_in_dim(rows, owner * width, width, 1)

    mlp_here = direct_scatter(
        lambda owner: own_features(mlp_part, owner).astype(f32), "tp", shards
    )
    output_here = (own_features(hidden, own_shard) + mlp_here).astype(bf16)
    output = to_home(output_here)

    grad_out = transposed_times(own_rows(full_attended), hidden_grad_low).astype(bf16)
    hidden_grad_features = lax.all_to_all(
        hidden_grad_low, "tp", split_axis=1, concat_axis=0, tiled=True
    )

    query_parts = []
    key_sum = jnp.zeros((capacity, local_heads, head_dim), f32)
    value_sum = jnp.zeros((capacity, local_heads, head_dim), f32)
    for part_index, row_first in enumerate(range(0, capacity, block_rows)):
        q_rows = queries[row_first : row_first + block_rows]
        grad_rows = attended_grad[row_first : row_first + block_rows]
        allowed = (segment[row_first : row_first + block_rows, None] == segment[None, :]) & (
            row_index[None, :] <= row_index[row_first : row_first + block_rows, None]
        )
        scores = (
            jnp.einsum("qhd,khd->hqk", q_rows, key_rows, preferred_element_type=f32)
            * score_scale
        )
        probs = jnp.where(allowed[None], jnp.exp(scores - log_parts[part_index]), 0.0)
        prob_low = probs.astype(bf16)
        prob_grad = jnp.einsum("qhd,khd->hqk", grad_rows, value_rows, preferred_element_type=f32)
        row_delta = jnp.sum(prob_grad * probs, axis=-1, keepdims=True)
        score_grad = (probs * (prob_grad - row_delta)).astype(bf16)
        query_parts.append(
            jnp.einsum("hqk,khd->qhd", score_grad, key_rows, preferred_element_type=f32)
            * score_scale
        )
        key_sum = (
            key_sum
            + jnp.einsum("hqk,qhd->khd", score_grad, q_rows, preferred_element_type=f32)
            * score_scale
        )
        value_sum = value_sum + jnp.einsum(
            "hqk,qhd->khd", prob_low, grad_rows, preferred_element_type=f32
        )
    query_grad = rotate_back(jnp.concatenate(query_parts, axis=0), cosine, sine_table)
    key_grad = rotate_back(key_sum, cosine, sine_table)
    qkv_grad = jnp.concatenate(
        [
            part.astype(bf16).reshape(capacity, local_width)
            for part in (query_grad, key_grad, value_sum)
        ],
        axis=1,
    )

    normed_one_grad = times_transposed(qkv_grad, full_qkv)
    unit_one, inverse_one = norm_parts(full_rows.astype(f32))
    row_sums = jnp.stack(
        [jnp.sum(normed_one_grad, axis=1), jnp.sum(normed_one_grad * unit_one, axis=1)]
    )
    sums_here = row_sums
    for step in range(1, shards):
        sums_here = sums_here + lax.ppermute(
            row_sums, "tp", [(i, (i + step) % shards) for i in range(shards)]
        )
    one_grad_low = normed_one_grad.astype(bf16)
    one_grad_here = direct_scatter(
        lambda owner: own_features(one_grad_low, owner).astype(f32), "tp", shards
    )
    means = sums_here / model
    back_here = inverse_one * (
        one_grad_here
        - means[0][:, None]
        - own_features(unit_one, own_shard) * means[1][:, None]
    )
    input_grad = to_home((hidden_grad_features.astype(f32) + back_here).astype(bf16))

    grad_qkv = transposed_times(normed_one, qkv_grad).astype(bf16)
    sum_qkv = lax.psum_scatter(grad_qkv, "fsdp", scatter_dimension=0, tiled=True)
    out_part = lax.psum_scatter(
        grad_out.reshape(shards, model // shards, model), "fsdp", scatter_dimension=1, tiled=True
    )
    sum_out = direct_scatter(
        lambda owner: lax.dynamic_index_in_dim(out_part, owner, 0, keepdims=False).astype(f32),
        "tp",
        shards,
    )
    sum_qkv = sum_qkv.astype(f32)
    return (
        output,
        input_grad,
        sum_qkv[:, :local_width],
        sum_qkv[:, local_width : 2 * local_width],
        sum_qkv[:, 2 * local_width :],
        sum_out,
        sum_gate,
        sum_up,
        sum_down,
    )


def solution(mesh):
    in_specs = (
        P("fsdp", "tp"),
        P("fsdp", "tp"),
        P("fsdp", "tp"),
        P("fsdp", "tp"),
        P("fsdp", "tp"),
        P(("tp", "fsdp"), None),
        P("fsdp", "tp"),
        P("fsdp", "tp"),
        P(("tp", "fsdp"), None),
        P(),
        P(),
        P("fsdp"),
    )
    out_specs = (
        P("fsdp", "tp"),
        P("fsdp", "tp"),
        P("fsdp", "tp"),
        P("fsdp", "tp"),
        P("fsdp", "tp"),
        P(("tp", "fsdp"), None),
        P("fsdp", "tp"),
        P("fsdp", "tp"),
        P(("tp", "fsdp"), None),
    )
    return jax.shard_map(
        on_device, mesh=mesh, in_specs=in_specs, out_specs=out_specs, check_vma=False
    )
```

time: 1690 us -> 963 us (0.57)
  waiting for transfers between devices: 1210 us -> 345 us
  starting transfers between devices: 28.7 us -> 163 us
  local copies, waits for them, and re-layouts: 72.9 us -> 51.7 us
  matrix products: 241 us -> 258 us
    reduce_scatter x11 -> x3, waiting for transfers between devices: 695 us -> 0.01 us  [the longest x1 0.01 us: on_device(): lax.psum_scatter(grad_out.reshape(shards, model // shards, model), 'fsdp'...]
    all_gather x11 -> x3, waiting for transfers between devices: 464 us -> 0.02 us  [the longest x1 0.02 us: on_device(): lax.all_gather(jnp.concatenate([w_query, w_key, w_value], axis=1), 'fsdp'...]
    ppermute x0 -> x39, waiting for transfers between devices: none -> 261 us  [the longest x12 112 us: direct_scatter(): lax.ppermute(term, axis, [(i, (i + step) % size) for i in range(size)])]
    ppermute x0 -> x39, starting transfers between devices: none -> 129 us  [the longest x12 43.6 us: chain_gather(): from_low.append(lax.ppermute(from_low[-1], axis, up))]
    all_to_all x5, waiting for transfers between devices: 47.7 us -> 80.4 us  [the longest x1 47.7 us: on_device(): lax.all_to_all(hidden_grad_low, 'tp', split_axis=1, concat_axis=0, tiled=...]
    scatter x5 -> x0, local copies, waits for them, and re-layouts: 31.8 us -> none  [the longest x1 7.02 us: on_device(): jnp.zeros((capacity, tokens.shape[1]), jnp.bfloat16).at[slot_of].set(tokens)]
    convert_element_type x14 -> x5, other arithmetic: 35.8 us -> 17.1 us  [the longest x1 9.59 us: on_device(): score_grad = (probs * (prob_grad - row_delta)).astype(bf16)]
    gather x4 -> x0, local copies, waits for them, and re-layouts: 18.1 us -> none  [the longest x1 5.08 us: on_device(): back_rows[place_read]]
  transfers between devices with their start and end apart: 28 -> 51, of which waited for: 25 -> 23; matrix products, arithmetic and copies ran while one was open for 15% -> 31% of each run, Pallas kernels for 0% -> 0%
where the time goes in v1:
time: 963 us; the launch traced here: 948 us
  waiting for transfers between devices  345 us (36%)
  matrix products  258 us (27%)
  starting transfers between devices  163 us (17%)
  other arithmetic  94.9 us (10%)
  local copies, waits for them, and re-layouts  51.7 us (5%)
  between operations  18.2 us (2%)
  blocking collectives  17.8 us (2%)
    ppermute x12, waiting for transfers between devices, direct_scatter(): lax.ppermute(term, axis, [(i, (i + step) % size) for i in range(size)])  112 us
    ppermute x12, waiting for transfers between devices, chain_gather(): from_low.append(lax.ppermute(from_low[-1], axis, up))  110 us
    dot_general x9, matrix products, matmul(): return jnp.dot(left, right, preferred_element_type=f32)  77.8 us
    dot_general x9, matrix products, transposed_times(): lax.dot_general(left, right, (((0,), (0,)), ((), ())), preferred_element_...  67.8 us
    dot_general x5, matrix products, times_transposed(): lax.dot_general(left, right, (((1,), (1,)), ((), ())), preferred_element_...  66.7 us
    all_to_all x1, waiting for transfers between devices, on_device(): lax.all_to_all(hidden_grad_low, 'tp', split_axis=1, concat_axis=0, tiled=...  47.7 us
    ppermute x12, starting transfers between devices, chain_gather(): from_low.append(lax.ppermute(from_low[-1], axis, up))  43.6 us
    ppermute x12, starting transfers between devices, chain_gather(): from_high.append(lax.ppermute(from_high[-1], axis, down))  40.4 us
  transfers between devices with their start and end apart: 51, of which 23 were waited for; matrix products, arithmetic and copies ran while one was open for 31% of the time, Pallas kernels for 0%

profile of v1, /device:TPU:16, one launch (start us, length us, event | category | flops | bytes accessed | tf_op | source)
XLA Modules:
  0.0 948.4 jit_solution(17302214853028301147)
XLA Ops:
  52.3 17.8 %all_to_all.83 = bf16[8,128,512]{2,1,0:T(8,128)(2,1)S(1)} all-to-all(bf16[8,128,512]{2,1,0:T(8,128)(2,1)S(1)} %bitcast.179), channel_id=1, replica_groups=mesh['fsdp'=8,'tp'=4] {'fsdp'}, dimensions={0} | all-to-all | bytes 2097152 | tf_op jit(solution)/shard_map/all_to_all | solution.py:169
  80.0 19.2 %collective-permute-done = bf16[1024,512]{0,1:T(8,128)(2,1)S(1)} collective-permute-done((bf16[1024,512]{0,1:T(8,128)(2,1)S(1)}, bf16[1024,512]{0,1:T(8,128)(2,1)S(1)}, u32[]{:S(2)}, u32[]{:S(2)}) %collective-permute-start) | collective-permute-done | bytes 1048608 | tf_op jit(solution)/shard_map/ppermute | solution.py:93
  102.1 6.2 collective-permute-start.4
  117.8 7.2 collective-permute-done.1
  139.6 6.6 collective-permute-start.24
  156.2 10.4 %fusion.42 = f32[1024,1536]{1,0:T(8,128)S(1)} fusion(bf16[2048,1536]{1,0:T(8,128)(2,1)} %all-gather.4.cloned.1.call-done, f32[1024]{0:T(1024)S(1)} %add_rsqrt_fusion.1, f32[1024]{0:T(1024)S(1)} %broadcast_multiply_fusion.1, bf16[1024,512]{0,1:T(8,128)(2,1)} %copy-done.15, bf16[1024,512]{0,1:T(8,128)(2,1)} %copy-done.13, ...), kind=kOutput, calls=%fused_computation.80 | convolution fusion | flops 6465519616 | bytes 16785408 | tf_op jit(solution)/shard_map/dot_general | solution.py:17
  213.3 15.6 %collective-permute-done.6 = bf16[1024,512]{0,1:T(8,128)(2,1)S(1)} collective-permute-done((bf16[1024,512]{0,1:T(8,128)(2,1)S(1)}, bf16[1024,512]{0,1:T(8,128)(2,1)S(1)}, u32[]{:S(2)}, u32[]{:S(2)}) %collective-permute-start.6) | collective-permute-done | bytes 1048608 | tf_op jit(solution)/shard_map/ppermute | solution.py:93
  236.7 14.7 %collective-permute-done.22 = bf16[1024,512]{0,1:T(8,128)(2,1)S(1)} collective-permute-done((bf16[1024,512]{0,1:T(8,128)(2,1)}, bf16[1024,512]{0,1:T(8,128)(2,1)S(1)}, u32[]{:S(2)}, u32[]{:S(2)}) %collective-permute-start.22) | collective-permute-done | bytes 1048608 | tf_op jit(solution)/shard_map/ppermute | solution.py:93
  257.0 15.5 %collective-permute-done.7 = bf16[1024,512]{0,1:T(8,128)(2,1)} collective-permute-done((bf16[1024,512]{0,1:T(8,128)(2,1)S(1)}, bf16[1024,512]{0,1:T(8,128)(2,1)}, u32[]{:S(2)}, u32[]{:S(2)}) %collective-permute-start.7) | collective-permute-done | bytes 1048608 | tf_op jit(solution)/shard_map/ppermute | solution.py:93
  272.4 5.5 collective-permute-start.8
  279.7 15.2 %collective-permute-done.23 = bf16[1024,512]{0,1:T(8,128)(2,1)} collective-permute-done((bf16[1024,512]{0,1:T(8,128)(2,1)S(1)}, bf16[1024,512]{0,1:T(8,128)(2,1)}, u32[]{:S(2)}, u32[]{:S(2)}) %collective-permute-start.23) | collective-permute-done | bytes 1048608 | tf_op jit(solution)/shard_map/ppermute | solution.py:93
  298.6 9.6 %collective-permute-done.8 = bf16[1024,512]{0,1:T(8,128)(2,1)} collective-permute-done((bf16[1024,512]{0,1:T(8,128)(2,1)}, bf16[1024,512]{0,1:T(8,128)(2,1)}, u32[]{:S(2)}, u32[]{:S(2)}) %collective-permute-start.8) | collective-permute-done | bytes 1048608 | tf_op jit(solution)/shard_map/ppermute | solution.py:93
  312.1 15.9 %fusion.123 = (f32[1024]{0:T(1024)S(1)}, f32[1024,2048]{0,1:T(8,128)}) fusion(bf16[2048,2048]{1,0:T(8,128)(2,1)} %bitcast.195, bf16[1024,512]{0,1:T(8,128)(2,1)} %get-tuple-element.48, bf16[1024,512]{0,1:T(8,128)(2,1)} %get-tuple-element.47, bf16[1024,512]{0,1:T(8,128)(2,1)} %get-tuple-element.46, bf16[1024,512]{0,1:T(8,128)(2,1)} %get-tuple-element.45, ...), kind=kOutput, calls=%fused_computation.251 | convolution fusion | flops 8627682304 | bytes 25169920 | tf_op jit(solution)/shard_map/dot_general | solution.py:17
  337.3 16.1 %fusion.4 = f32[1024,2048]{1,0:T(8,128)} fusion(bf16[1024,2048]{0,1:T(8,128)(2,1)} %multiply_convert_fusion.5, bf16[3,2048,2048]{2,1,0:T(8,128)(2,1)} %all-gather.8.cloned.1.call-done), kind=kOutput, calls=%fused_computation.36 | convolution fusion | flops 8589934592 | bytes 20971520 | tf_op jit(solution)/shard_map/dot_general | solution.py:17
  353.4 13.9 %fusion.6 = f32[1024,2048]{1,0:T(8,128)} fusion(bf16[1024,2048]{0,1:T(8,128)(2,1)S(1)} %copy-done.36, bf16[3,2048,2048]{2,1,0:T(8,128)(2,1)} %all-gather.8.cloned.1.call-done), kind=kOutput, calls=%fused_computation.38 | convolution fusion | flops 8589934592 | bytes 20971520 | tf_op jit(solution)/shard_map/dot_general | solution.py:17
  367.3 20.5 %multiply_convert_fusion.2 = (bf16[1024,2048]{1,0:T(8,128)(2,1)}, bf16[1024,2048]{1,0:T(8,128)(2,1)}, bf16[1024,2048]{1,0:T(8,128)(2,1)}) fusion(f32[1024,2048]{1,0:T(8,128)} %fusion.4, f32[1024,2048]{1,0:T(8,128)} %fusion.6, bf16[3,2048,2048]{2,1,0:T(8,128)(2,1)} %all-gather.8.cloned.1.call-done, bf16[1024,512]{0,1:T(8,128)(2,1)S(1)} %copy-done.41, ...), kind=kOutput, calls=%fused_computation.21 | convolution fusion | flops 8640266240 | bytes 41943040 | tf_op jit(solution)/shard_map/dot_general | solution.py:21
  387.8 14.7 %fusion.3 = f32[1024,2048]{0,1:T(8,128)} fusion(bf16[1024,2048]{1,0:T(8,128)(2,1)} %get-tuple-element.14, bf16[3,2048,2048]{2,1,0:T(8,128)(2,1)} %all-gather.8.cloned.1.call-done), kind=kOutput, calls=%fused_computation.35 | convolution fusion | flops 8589934592 | bytes 20971520 | tf_op jit(solution)/shard_map/dot_general | solution.py:21
  402.5 12.8 %add_convert_fusion = bf16[1024,2048]{0,1:T(8,128)(2,1)S(1)} fusion(f32[1024,2048]{0,1:T(8,128)} %fusion.3, bf16[1024,2048]{1,0:T(8,128)(2,1)S(1)} %copy-done.85, bf16[3,2048,2048]{2,1,0:T(8,128)(2,1)} %all-gather.8.cloned.1.call-done), kind=kOutput, calls=%fused_computation.20 | convolution fusion | flops 8594128896 | bytes 25165824 | tf_op jit(solution)/shard_map/dot_general | solution.py:21
  426.8 58.7 %collective-permute-done.29 = bf16[256,2048]{0,1:T(8,128)(2,1)S(1)} collective-permute-done((bf16[256,2048]{0,1:T(8,128)(2,1)S(1)}, bf16[256,2048]{0,1:T(8,128)(2,1)S(1)}, u32[]{:S(2)}, u32[]{:S(2)}) %collective-permute-start.29) | collective-permute-done | bytes 1048608 | tf_op jit(solution)/shard_map/ppermute | solution.py:113
  485.6 11.2 %collective-permute-done.27 = bf16[256,2048]{0,1:T(8,128)(2,1)S(1)} collective-permute-done((bf16[256,2048]{0,1:T(8,128)(2,1)S(1)}, bf16[256,2048]{0,1:T(8,128)(2,1)S(1)}, u32[]{:S(2)}, u32[]{:S(2)}) %collective-permute-start.27) | collective-permute-done | bytes 1048608 | tf_op jit(solution)/shard_map/ppermute | solution.py:113
  499.0 5.6 convolution_convert_fusion
  504.6 5.8 convolution_convert_fusion.2
  511.5 7.5 all-to-all-start.5
  519.1 19.4 %all-to-all-done.5 = bf16[256,4,512]{2,0,1:T(8,128)(2,1)S(1)} async-done(((bf16[256,4,512]{2,0,1:T(8,128)(2,1)}), bf16[256,4,512]{2,0,1:T(8,128)(2,1)S(1)}, u32[]{:S(2)}, u32[]{:S(2)}) %all-to-all-start.5) | async-done | bytes 1048608 | tf_op jit(solution)/shard_map/all_to_all | solution.py:254
  541.6 7.4 multiply_reduce_fusion.1
  549.0 8.7 multiply_reduce_fusion.2
  557.9 9.6 %multiply_convert_fusion = (bf16[4,512,1024]{2,1,0:T(8,128)(2,1)}, bf16[4,512,1024]{2,1,0:T(8,128)(2,1)}) fusion(f32[4,512,1024]{2,1,0:T(8,128)S(1)} %get-tuple-element.91, f32[4,512,1024]{2,1,0:T(8,128)S(1)} %bitcast.160, f32[4,512]{1,0:T(4,128)S(1)} %get-tuple-element.90, f32[4,512]{1,0:T(4,128)S(1)} %log_add_fusion, pred[512,1024]{1,0:T(8,128)(4,1)S(1)} %copy-done.24, ...), kind=kLoop, calls=%fused_computation.14 | loop fusion | flops 25165824 | bytes 43024384 | tf_op jit(solution)/shard_map/convert_element_type | solution.py:302
  590.5 5.7 add_convert_fusion.2
  597.3 12.6 %convolution_convert_fusion.1 = bf16[2048,1536]{1,0:T(8,128)(2,1)} fusion(f32[1024]{0:T(1024)S(1)} %copy-done.75, f32[1024]{0:T(1024)S(1)} %copy-done.71, bf16[1024,512]{0,1:T(8,128)(2,1)S(1)} %bitcast.197, bf16[1024,512]{0,1:T(8,128)(2,1)S(1)} %bitcast.173, bf16[1024,512]{0,1:T(8,128)(2,1)S(1)} %bitcast.175, bf16[1024,512]{0,1:T(8,128)(2,1)S(1)} %copy-done.16, ...), kind=kOutput, calls=%fused_computation.34 | convolution fusion | flops 6478102528 | bytes 13639680 | tf_op jit(solution)/shard_map/dot_general | solution.py:27
  609.9 12.3 %convert_bitcast_fusion = bf16[1,2048,2048]{2,1,0:T(8,128)(2,1)S(1)} fusion(bf16[1024,2048]{1,0:T(8,128)(2,1)} %get-tuple-element.15, bf16[1024,512]{0,1:T(8,128)(2,1)} %get-tuple-element.44, bf16[1024,512]{0,1:T(8,128)(2,1)} %get-tuple-element.43, bf16[1024,512]{0,1:T(8,128)(2,1)} %get-tuple-element.42, bf16[1024,512]{0,1:T(8,128)(2,1)} %get-tuple-element.41), kind=kOutput, calls=%fused_computation.10 | convolution fusion | flops 8610906112 | bytes 16777216 | tf_op jit(solution)/shard_map/dot_general | solution.py:27
  622.2 11.4 %convert_bitcast_fusion.1 = bf16[1,2048,2048]{2,1,0:T(8,128)(2,1)S(1)} fusion(bf16[1024,2048]{0,1:T(8,128)(2,1)S(1)} %copy-done.37, bf16[1024,2048]{1,0:T(8,128)(2,1)} %get-tuple-element.13), kind=kOutput, calls=%fused_computation.11 | convolution fusion | flops 8594128896 | bytes 16777216 | tf_op jit(solution)/shard_map/dot_general | solution.py:27
  633.6 10.9 %convert_bitcast_fusion.2 = bf16[1,2048,2048]{2,1,0:T(8,128)(2,1)} fusion(bf16[1024,2048]{0,1:T(8,128)(2,1)S(1)} %copy-done.37, bf16[1024,2048]{1,0:T(8,128)(2,1)S(1)} %copy-done.86), kind=kOutput, calls=%fused_computation.12 | convolution fusion | flops 8594128896 | bytes 16777216 | tf_op jit(solution)/shard_map/dot_general | solution.py:27
  644.6 14.1 %pad_maximum_fusion = bf16[3,2048,2048]{2,1,0:T(8,128)(2,1)} fusion(bf16[1,2048,2048]{2,1,0:T(8,128)(2,1)S(1)} %convert_bitcast_fusion, bf16[1,2048,2048]{2,1,0:T(8,128)(2,1)S(1)} %convert_bitcast_fusion.1, bf16[1,2048,2048]{2,1,0:T(8,128)(2,1)} %convert_bitcast_fusion.2), kind=kLoop, calls=%fused_computation | loop fusion | flops 25165824 | bytes 50331648 | tf_op jit(solution)/shard_map/stack | solution.py:258
  658.7 12.7 %fusion.30 = bf16[1024,2048]{0,1:T(8,128)(2,1)S(1)} fusion(bf16[1024,2048]{1,0:T(8,128)(2,1)} %get-tuple-element.15, bf16[3,2048,2048]{2,1,0:T(8,128)(2,1)} %all-gather.8.cloned.1.call-done), kind=kOutput, calls=%fused_computation.64 | convolution fusion | flops 8592031744 | bytes 16777216 | tf_op jit(solution)/shard_map/dot_general | solution.py:17
  680.0 5.5 all-to-all-start.4
  685.5 13.0 %fusion.124 = (f32[1024]{0:T(1024)S(1)}, f32[1024,2048]{1,0:T(8,128)}) fusion(bf16[2048,1536]{1,0:T(8,128)(2,1)} %all-gather.4.cloned.1.call-done, bf16[1024,512]{0,1:T(8,128)(2,1)} %bitcast.198, bf16[1024,512]{0,1:T(8,128)(2,1)} %bitcast.172, bf16[1024,512]{0,1:T(8,128)(2,1)} %bitcast.174), kind=kOutput, calls=%fused_computation.252 | convolution fusion | flops 6453984256 | bytes 17829888 | tf_op jit(solution)/shard_map/dot_general | solution.py:21
  698.6 10.4 %copy.136 = f32[1024,2048]{0,1:T(8,128)} copy(f32[1024,2048]{1,0:T(8,128)} %get-tuple-element.95) | data formatting | bytes 16777216 | tf_op jit(solution)/shard_map/dot_general | solution.py:21
  709.0 14.4 %multiply_reduce_fusion = (f32[1024]{0:T(1024)S(1)}, bf16[1024,2048]{0,1:T(8,128)(2,1)S(1)}, f32[1024,2048]{0,1:T(8,128)}) fusion(f32[1024,2048]{0,1:T(8,128)} %copy.136, f32[1024]{0:T(1024)S(1)} %copy-done.75, f32[1024]{0:T(1024)S(1)} %copy-done.71, bf16[1024,512]{0,1:T(8,128)(2,1)} %copy-done.15, bf16[1024,512]{0,1:T(8,128)(2,1)} %copy-done.13, ...), kind=kLoop, calls=%fused_computation.13 | loop fusion | flops 27261952 | bytes 25178112 | tf_op jit(solution)/shard_map/reduce_sum | solution.py:328
  729.2 22.6 %collective-permute-start.35 = (f32[2,1024]{1,0:T(2,128)S(1)}, f32[2,1024]{1,0:T(2,128)S(1)}, u32[]{:S(2)}, u32[]{:S(2)}) collective-permute-start(f32[2,1024]{1,0:T(2,128)S(1)} %pad_maximum_fusion.16), channel_id=1, source_target_pairs={{0,3},{1,0},{2,1},{3,2},{4,7},{5,4},{6,5},{7,6},{8,11},{9,8},{10,9... | collective-permute-start | bytes 24584 | tf_op jit(solution)/shard_map/ppermute | solution.py:332
  751.8 26.6 %collective-permute-done.18 = bf16[1024,512]{0,1:T(8,128)(2,1)} collective-permute-done((bf16[1024,512]{0,1:T(8,128)(2,1)}, bf16[1024,512]{0,1:T(8,128)(2,1)}, u32[]{:S(2)}, u32[]{:S(2)}) %collective-permute-start.18) | collective-permute-done | bytes 1048608 | tf_op jit(solution)/shard_map/ppermute | solution.py:113
  778.4 5.2 fusion.56
  787.0 47.7 %all-to-all-done.4 = bf16[256,4,512]{0,2,1:T(8,128)(2,1)} async-done(((bf16[256,4,512]{0,2,1:T(8,128)(2,1)}), bf16[256,4,512]{0,2,1:T(8,128)(2,1)}, u32[]{:S(2)}, u32[]{:S(2)}) %all-to-all-start.4) | async-done | bytes 1048608 | tf_op jit(solution)/shard_map/all_to_all | solution.py:281
  834.8 7.2 all-to-all-start.2
  842.0 36.6 %collective-permute-done.35 = f32[2,1024]{1,0:T(2,128)S(1)} collective-permute-done((f32[2,1024]{1,0:T(2,128)S(1)}, f32[2,1024]{1,0:T(2,128)S(1)}, u32[]{:S(2)}, u32[]{:S(2)}) %collective-permute-start.35) | collective-permute-done | bytes 8224 | tf_op jit(solution)/shard_map/ppermute | solution.py:332
  882.8 5.6 fusion.59
  888.4 5.5 all-to-all-start.6
  896.0 13.2 %all-to-all-done.6 = bf16[8,128,512]{2,1,0:T(8,128)(2,1)S(1)} async-done(((bf16[8,128,512]{2,1,0:T(8,128)(2,1)}), bf16[8,128,512]{2,1,0:T(8,128)(2,1)S(1)}, u32[]{:S(2)}, u32[]{:S(2)}) %all-to-all-start.6) | async-done | bytes 1048608 | tf_op jit(solution)/shard_map/all_to_all | solution.py:174
  918.6 12.2 %collective-permute-done.38 = bf16[64,2048]{1,0:T(8,128)(2,1)S(1)} collective-permute-done((bf16[64,2048]{1,0:T(8,128)(2,1)S(1)}, bf16[64,2048]{1,0:T(8,128)(2,1)S(1)}, u32[]{:S(2)}, u32[]{:S(2)}) %collective-permute-start.38) | collective-permute-done | bytes 262176 | tf_op jit(solution)/shard_map/ppermute | solution.py:113
  (374 shorter events, 253.4 us)
Async XLA Ops:
  7.2 149.0 %all-gather.4.cloned.1.call-start = ((), (), s32[]{:S(2)}) async-start(), calls=%async_computation.10 | async-start | bytes 7077888 | tf_op jit(solution)/shard_map/all_gather | solution.py:144
  9.5 302.6 %all-gather.6.cloned.1.call-start = ((), (), s32[]{:S(2)}) async-start(), calls=%async_computation.11 | async-start | bytes 9437184 | tf_op jit(solution)/shard_map/all_gather | solution.py:148
  9.5 10.2 %collective-permute-start.12 = (bf16[64,2048]{1,0:T(8,128)(2,1)}, bf16[64,2048]{1,0:T(8,128)(2,1)S(1)}, u32[]{:S(2)}, u32[]{:S(2)}) collective-permute-start(bf16[64,2048]{1,0:T(8,128)(2,1)} %param.17), channel_id=1, source_target_pairs={{0,1},{1,2},{2,3},{4,5},{5,6},{6,7},{8,9},{9,10},{10,11},{12,13},{... | collective-permute-start | bytes 786440 | tf_op jit(solution)/shard_map/ppermute | solution.py:93
  13.0 10.1 %collective-permute-start.15 = (bf16[64,2048]{1,0:T(8,128)(2,1)}, bf16[64,2048]{1,0:T(8,128)(2,1)S(1)}, u32[]{:S(2)}, u32[]{:S(2)}) collective-permute-start(bf16[64,2048]{1,0:T(8,128)(2,1)} %param.17), channel_id=1, source_target_pairs={{3,2},{2,1},{1,0},{7,6},{6,5},{5,4},{11,10},{10,9},{9,8},{15,14},{... | collective-permute-start | bytes 786440 | tf_op jit(solution)/shard_map/ppermute | solution.py:94
  19.7 9.2 collective-permute-start.13
  23.2 9.9 %collective-permute-start.16 = (bf16[64,2048]{1,0:T(8,128)(2,1)S(1)}, bf16[64,2048]{1,0:T(8,128)(2,1)}, u32[]{:S(2)}, u32[]{:S(2)}) collective-permute-start(bf16[64,2048]{1,0:T(8,128)(2,1)S(1)} %collective-permute-done.15), channel_id=1, source_target_pairs={{2,1},{1,0},{6,5},{5,4},{10,9},{9,8},{14,13},{13,12},{18,17},{17,1... | collective-permute-start | bytes 786440 | tf_op jit(solution)/shard_map/ppermute | solution.py:94
  39.1 298.1 %all-gather.8.cloned.1.call-start = ((), (), s32[]{:S(2)}) async-start(), calls=%async_computation.12 | async-start | bytes 28311552 | tf_op jit(solution)/shard_map/all_gather | solution.py:149
  44.0 8.3 all-to-all-start
  71.5 27.6 %collective-permute-start = (bf16[1024,512]{0,1:T(8,128)(2,1)S(1)}, bf16[1024,512]{0,1:T(8,128)(2,1)S(1)}, u32[]{:S(2)}, u32[]{:S(2)}) collective-permute-start(bf16[1024,512]{0,1:T(8,128)(2,1)S(1)} %fusion.64), channel_id=1, source_target_pairs={{0,1},{1,2},{2,3},{4,5},{5,6},{6,7},{8,9},{9,10},{10,11},{12,13},{... | collective-permute-start | bytes 3145736 | tf_op jit(solution)/shard_map/ppermute | solution.py:93
  75.9 26.1 %collective-permute-start.3 = (bf16[1024,512]{0,1:T(8,128)(2,1)S(1)}, bf16[1024,512]{0,1:T(8,128)(2,1)S(1)}, u32[]{:S(2)}, u32[]{:S(2)}) collective-permute-start(bf16[1024,512]{0,1:T(8,128)(2,1)S(1)} %fusion.64), channel_id=1, source_target_pairs={{3,2},{2,1},{1,0},{7,6},{6,5},{5,4},{11,10},{10,9},{9,8},{15,14},{... | collective-permute-start | bytes 3145736 | tf_op jit(solution)/shard_map/ppermute | solution.py:94
  99.2 25.9 %collective-permute-start.1 = (bf16[1024,512]{0,1:T(8,128)(2,1)S(1)}, bf16[1024,512]{0,1:T(8,128)(2,1)}, u32[]{:S(2)}, u32[]{:S(2)}) collective-permute-start(bf16[1024,512]{0,1:T(8,128)(2,1)S(1)} %collective-permute-done), channel_id=1, source_target_pairs={{1,2},{2,3},{5,6},{6,7},{9,10},{10,11},{13,14},{14,15},{17,18},{18... | collective-permute-start | bytes 3145736 | tf_op jit(solution)/shard_map/ppermute | solution.py:93
  102.1 25.4 %collective-permute-start.4 = (bf16[1024,512]{0,1:T(8,128)(2,1)S(1)}, bf16[1024,512]{0,1:T(8,128)(2,1)}, u32[]{:S(2)}, u32[]{:S(2)}) collective-permute-start(bf16[1024,512]{0,1:T(8,128)(2,1)S(1)} %collective-permute-done.3), channel_id=1, source_target_pairs={{2,1},{1,0},{6,5},{5,4},{10,9},{9,8},{14,13},{13,12},{18,17},{17,1... | collective-permute-start | bytes 3145736 | tf_op jit(solution)/shard_map/ppermute | solution.py:94
  110.5 23.1 %all-to-all-start.3 = ((bf16[8,128,512]{2,1,0:T(8,128)(2,1)}), bf16[8,128,512]{2,1,0:T(8,128)(2,1)}, u32[]{:S(2)}, u32[]{:S(2)}) async-start(bf16[8,128,512]{2,1,0:T(8,128)(2,1)} %bitcast.177), calls=%async_computation.3 | async-start | bytes 2097152 | tf_op jit(solution)/shard_map/all_to_all | solution.py:169
  114.8 796.6 %reduce-scatter.6.cloned.1.call-start = ((), (), s32[]{:S(2)}) async-start(), calls=%async_computation.14 | async-start | bytes 9437184 | tf_op jit(solution)/shard_map/reduce_scatter | solution.py:349
  125.0 26.3 %collective-permute-start.2 = (bf16[1024,512]{0,1:T(8,128)(2,1)}, bf16[1024,512]{0,1:T(8,128)(2,1)S(1)}, u32[]{:S(2)}, u32[]{:S(2)}) collective-permute-start(bf16[1024,512]{0,1:T(8,128)(2,1)} %collective-permute-done.1), channel_id=1, source_target_pairs={{2,3},{6,7},{10,11},{14,15},{18,19},{22,23},{26,27},{30,31}} | collective-permute-start | bytes 3145736 | tf_op jit(solution)/shard_map/ppermute | solution.py:93
  127.5 24.8 %collective-permute-start.5 = (bf16[1024,512]{0,1:T(8,128)(2,1)}, bf16[1024,512]{0,1:T(8,128)(2,1)}, u32[]{:S(2)}, u32[]{:S(2)}) collective-permute-start(bf16[1024,512]{0,1:T(8,128)(2,1)} %collective-permute-done.4), channel_id=1, source_target_pairs={{1,0},{5,4},{9,8},{13,12},{17,16},{21,20},{25,24},{29,28}} | collective-permute-start | bytes 3145736 | tf_op jit(solution)/shard_map/ppermute | solution.py:94
  137.6 69.1 %collective-permute-start.21 = (bf16[1024,512]{0,1:T(8,128)(2,1)}, bf16[1024,512]{0,1:T(8,128)(2,1)}, u32[]{:S(2)}, u32[]{:S(2)}) collective-permute-start(bf16[1024,512]{0,1:T(8,128)(2,1)} %fusion.65), channel_id=1, source_target_pairs={{0,1},{1,2},{2,3},{4,5},{5,6},{6,7},{8,9},{9,10},{10,11},{12,13},{... | collective-permute-start | bytes 3145736 | tf_op jit(solution)/shard_map/ppermute | solution.py:93
  139.6 70.3 %collective-permute-start.24 = (bf16[1024,512]{0,1:T(8,128)(2,1)}, bf16[1024,512]{0,1:T(8,128)(2,1)}, u32[]{:S(2)}, u32[]{:S(2)}) collective-permute-start(bf16[1024,512]{0,1:T(8,128)(2,1)} %fusion.65), channel_id=1, source_target_pairs={{3,2},{2,1},{1,0},{7,6},{6,5},{5,4},{11,10},{10,9},{9,8},{15,14},{... | collective-permute-start | bytes 3145736 | tf_op jit(solution)/shard_map/ppermute | solution.py:94
  198.7 30.1 %collective-permute-start.6 = (bf16[1024,512]{0,1:T(8,128)(2,1)S(1)}, bf16[1024,512]{0,1:T(8,128)(2,1)S(1)}, u32[]{:S(2)}, u32[]{:S(2)}) collective-permute-start(bf16[1024,512]{0,1:T(8,128)(2,1)S(1)} %bitcast.167), channel_id=1, source_target_pairs={{0,1},{1,2},{2,3},{4,5},{5,6},{6,7},{8,9},{9,10},{10,11},{12,13},{... | collective-permute-start | bytes 3145736 | tf_op jit(solution)/shard_map/ppermute | solution.py:93
  203.9 28.0 %collective-permute-start.9 = (bf16[1024,512]{0,1:T(8,128)(2,1)S(1)}, bf16[1024,512]{0,1:T(8,128)(2,1)S(1)}, u32[]{:S(2)}, u32[]{:S(2)}) collective-permute-start(bf16[1024,512]{0,1:T(8,128)(2,1)S(1)} %bitcast.168), channel_id=1, source_target_pairs={{3,2},{2,1},{1,0},{7,6},{6,5},{5,4},{11,10},{10,9},{9,8},{15,14},{... | collective-permute-start | bytes 3145736 | tf_op jit(solution)/shard_map/ppermute | solution.py:94
  206.8 44.6 %collective-permute-start.22 = (bf16[1024,512]{0,1:T(8,128)(2,1)}, bf16[1024,512]{0,1:T(8,128)(2,1)S(1)}, u32[]{:S(2)}, u32[]{:S(2)}) collective-permute-start(bf16[1024,512]{0,1:T(8,128)(2,1)} %collective-permute-done.21), channel_id=1, source_target_pairs={{1,2},{2,3},{5,6},{6,7},{9,10},{10,11},{13,14},{14,15},{17,18},{18... | collective-permute-start | bytes 3145736 | tf_op jit(solution)/shard_map/ppermute | solution.py:93
  209.9 45.5 %collective-permute-start.25 = (bf16[1024,512]{0,1:T(8,128)(2,1)}, bf16[1024,512]{0,1:T(8,128)(2,1)S(1)}, u32[]{:S(2)}, u32[]{:S(2)}) collective-permute-start(bf16[1024,512]{0,1:T(8,128)(2,1)} %collective-permute-done.24), channel_id=1, source_target_pairs={{2,1},{1,0},{6,5},{5,4},{10,9},{9,8},{14,13},{13,12},{18,17},{17,1... | collective-permute-start | bytes 3145736 | tf_op jit(solution)/shard_map/ppermute | solution.py:94
  228.9 43.6 %collective-permute-start.7 = (bf16[1024,512]{0,1:T(8,128)(2,1)S(1)}, bf16[1024,512]{0,1:T(8,128)(2,1)}, u32[]{:S(2)}, u32[]{:S(2)}) collective-permute-start(bf16[1024,512]{0,1:T(8,128)(2,1)S(1)} %collective-permute-done.6), channel_id=1, source_target_pairs={{1,2},{2,3},{5,6},{6,7},{9,10},{10,11},{13,14},{14,15},{17,18},{18... | collective-permute-start | bytes 3145736 | tf_op jit(solution)/shard_map/ppermute | solution.py:93
  231.9 46.0 %collective-permute-start.10 = (bf16[1024,512]{0,1:T(8,128)(2,1)S(1)}, bf16[1024,512]{0,1:T(8,128)(2,1)}, u32[]{:S(2)}, u32[]{:S(2)}) collective-permute-start(bf16[1024,512]{0,1:T(8,128)(2,1)S(1)} %collective-permute-done.9), channel_id=1, source_target_pairs={{2,1},{1,0},{6,5},{5,4},{10,9},{9,8},{14,13},{13,12},{18,17},{17,1... | collective-permute-start | bytes 3145736 | tf_op jit(solution)/shard_map/ppermute | solution.py:94
  251.3 43.6 %collective-permute-start.23 = (bf16[1024,512]{0,1:T(8,128)(2,1)S(1)}, bf16[1024,512]{0,1:T(8,128)(2,1)}, u32[]{:S(2)}, u32[]{:S(2)}) collective-permute-start(bf16[1024,512]{0,1:T(8,128)(2,1)S(1)} %collective-permute-done.22), channel_id=1, source_target_pairs={{2,3},{6,7},{10,11},{14,15},{18,19},{22,23},{26,27},{30,31}} | collective-permute-start | bytes 3145736 | tf_op jit(solution)/shard_map/ppermute | solution.py:93
  255.3 39.6 %collective-permute-start.26 = (bf16[1024,512]{0,1:T(8,128)(2,1)S(1)}, bf16[1024,512]{0,1:T(8,128)(2,1)}, u32[]{:S(2)}, u32[]{:S(2)}) collective-permute-start(bf16[1024,512]{0,1:T(8,128)(2,1)S(1)} %collective-permute-done.25), channel_id=1, source_target_pairs={{1,0},{5,4},{9,8},{13,12},{17,16},{21,20},{25,24},{29,28}} | collective-permute-start | bytes 3145736 | tf_op jit(solution)/shard_map/ppermute | solution.py:94
  272.4 35.7 %collective-permute-start.8 = (bf16[1024,512]{0,1:T(8,128)(2,1)}, bf16[1024,512]{0,1:T(8,128)(2,1)}, u32[]{:S(2)}, u32[]{:S(2)}) collective-permute-start(bf16[1024,512]{0,1:T(8,128)(2,1)} %collective-permute-done.7), channel_id=1, source_target_pairs={{2,3},{6,7},{10,11},{14,15},{18,19},{22,23},{26,27},{30,31}} | collective-permute-start | bytes 3145736 | tf_op jit(solution)/shard_map/ppermute | solution.py:93
  277.9 30.2 %collective-permute-start.11 = (bf16[1024,512]{0,1:T(8,128)(2,1)}, bf16[1024,512]{0,1:T(8,128)(2,1)}, u32[]{:S(2)}, u32[]{:S(2)}) collective-permute-start(bf16[1024,512]{0,1:T(8,128)(2,1)} %collective-permute-done.10), channel_id=1, source_target_pairs={{1,0},{5,4},{9,8},{13,12},{17,16},{21,20},{25,24},{29,28}} | collective-permute-start | bytes 3145736 | tf_op jit(solution)/shard_map/ppermute | solution.py:94
  415.7 69.9 %collective-permute-start.29 = (bf16[256,2048]{0,1:T(8,128)(2,1)S(1)}, bf16[256,2048]{0,1:T(8,128)(2,1)S(1)}, u32[]{:S(2)}, u32[]{:S(2)}) collective-permute-start(bf16[256,2048]{0,1:T(8,128)(2,1)S(1)} %get-tuple-element.32), channel_id=1, source_target_pairs={{0,3},{1,0},{2,1},{3,2},{4,7},{5,4},{6,5},{7,6},{8,11},{9,8},{10,9... | collective-permute-start | bytes 3145736 | tf_op jit(solution)/shard_map/ppermute | solution.py:113
  418.3 67.3 %collective-permute-start.28 = (bf16[256,2048]{0,1:T(8,128)(2,1)S(1)}, bf16[256,2048]{0,1:T(8,128)(2,1)S(1)}, u32[]{:S(2)}, u32[]{:S(2)}) collective-permute-start(bf16[256,2048]{0,1:T(8,128)(2,1)S(1)} %get-tuple-element.33), channel_id=1, source_target_pairs={{0,1},{1,2},{2,3},{3,0},{4,5},{5,6},{6,7},{7,4},{8,9},{9,10},{10,1... | collective-permute-start | bytes 3145736 | tf_op jit(solution)/shard_map/ppermute | solution.py:113
  418.6 78.2 %collective-permute-start.27 = (bf16[256,2048]{0,1:T(8,128)(2,1)S(1)}, bf16[256,2048]{0,1:T(8,128)(2,1)S(1)}, u32[]{:S(2)}, u32[]{:S(2)}) collective-permute-start(bf16[256,2048]{0,1:T(8,128)(2,1)S(1)} %get-tuple-element.31), channel_id=1, source_target_pairs={{0,2},{1,3},{2,0},{3,1},{4,6},{5,7},{6,4},{7,5},{8,10},{9,11},{10,... | collective-permute-start | bytes 3145736 | tf_op jit(solution)/shard_map/ppermute | solution.py:113
  511.5 27.0 %all-to-all-start.5 = ((bf16[256,4,512]{2,0,1:T(8,128)(2,1)}), bf16[256,4,512]{2,0,1:T(8,128)(2,1)S(1)}, u32[]{:S(2)}, u32[]{:S(2)}) async-start(bf16[256,4,512]{2,0,1:T(8,128)(2,1)} %bitcast.170), calls=%async_computation.5 | async-start | bytes 2097152 | tf_op jit(solution)/shard_map/all_to_all | solution.py:254
  519.0 397.3 %reduce-scatter.4.cloned.1.call-start = ((), (), s32[]{:S(2)}) async-start(), calls=%async_computation.13 | async-start | bytes 7077888 | tf_op jit(solution)/shard_map/reduce_scatter | solution.py:348
  609.9 325.6 %reduce-scatter.8.cloned.1.call-start = ((), (), s32[]{:S(2)}) async-start(), calls=%async_computation.15 | async-start | bytes 28311552 | tf_op jit(solution)/shard_map/reduce_scatter | solution.py:265
  675.2 52.1 %collective-permute-start.20 = (bf16[1024,512]{0,1:T(8,128)(2,1)}, bf16[1024,512]{0,1:T(8,128)(2,1)}, u32[]{:S(2)}, u32[]{:S(2)}) collective-permute-start(bf16[1024,512]{0,1:T(8,128)(2,1)} %get-tuple-element.35), channel_id=1, source_target_pairs={{0,3},{1,0},{2,1},{3,2},{4,7},{5,4},{6,5},{7,6},{8,11},{9,8},{10,9... | collective-permute-start | bytes 3145736 | tf_op jit(solution)/shard_map/ppermute | solution.py:113
  675.8 53.5 %collective-permute-start.19 = (bf16[1024,512]{0,1:T(8,128)(2,1)}, bf16[1024,512]{0,1:T(8,128)(2,1)}, u32[]{:S(2)}, u32[]{:S(2)}) collective-permute-start(bf16[1024,512]{0,1:T(8,128)(2,1)} %get-tuple-element.36), channel_id=1, source_target_pairs={{0,1},{1,2},{2,3},{3,0},{4,5},{5,6},{6,7},{7,4},{8,9},{9,10},{10,1... | collective-permute-start | bytes 3145736 | tf_op jit(solution)/shard_map/ppermute | solution.py:113
  677.3 101.1 %collective-permute-start.18 = (bf16[1024,512]{0,1:T(8,128)(2,1)}, bf16[1024,512]{0,1:T(8,128)(2,1)}, u32[]{:S(2)}, u32[]{:S(2)}) collective-permute-start(bf16[1024,512]{0,1:T(8,128)(2,1)} %get-tuple-element.34), channel_id=1, source_target_pairs={{0,2},{1,3},{2,0},{3,1},{4,6},{5,7},{6,4},{7,5},{8,10},{9,11},{10,... | collective-permute-start | bytes 3145736 | tf_op jit(solution)/shard_map/ppermute | solution.py:113
  680.0 154.8 %all-to-all-start.4 = ((bf16[256,4,512]{0,2,1:T(8,128)(2,1)}), bf16[256,4,512]{0,2,1:T(8,128)(2,1)}, u32[]{:S(2)}, u32[]{:S(2)}) async-start(bf16[256,4,512]{0,2,1:T(8,128)(2,1)} %bitcast.166), calls=%async_computation.4 | async-start | bytes 2097152 | tf_op jit(solution)/shard_map/all_to_all | solution.py:281
  725.2 157.5 %collective-permute-start.32 = (bf16[1024,512]{0,1:T(8,128)(2,1)}, bf16[1024,512]{0,1:T(8,128)(2,1)}, u32[]{:S(2)}, u32[]{:S(2)}) collective-permute-start(bf16[1024,512]{0,1:T(8,128)(2,1)} %get-tuple-element.29), channel_id=1, source_target_pairs={{0,3},{1,0},{2,1},{3,2},{4,7},{5,4},{6,5},{7,6},{8,11},{9,8},{10,9... | collective-permute-start | bytes 3145736 | tf_op jit(solution)/shard_map/ppermute | solution.py:113
  727.2 155.5 %collective-permute-start.31 = (bf16[1024,512]{0,1:T(8,128)(2,1)}, bf16[1024,512]{0,1:T(8,128)(2,1)}, u32[]{:S(2)}, u32[]{:S(2)}) collective-permute-start(bf16[1024,512]{0,1:T(8,128)(2,1)} %get-tuple-element.30), channel_id=1, source_target_pairs={{0,1},{1,2},{2,3},{3,0},{4,5},{5,6},{6,7},{7,4},{8,9},{9,10},{10,1... | collective-permute-start | bytes 3145736 | tf_op jit(solution)/shard_map/ppermute | solution.py:113
  727.3 155.5 %collective-permute-start.30 = (bf16[1024,512]{0,1:T(8,128)(2,1)S(1)}, bf16[1024,512]{0,1:T(8,128)(2,1)}, u32[]{:S(2)}, u32[]{:S(2)}) collective-permute-start(bf16[1024,512]{0,1:T(8,128)(2,1)S(1)} %get-tuple-element.28), channel_id=1, source_target_pairs={{0,2},{1,3},{2,0},{3,1},{4,6},{5,7},{6,4},{7,5},{8,10},{9,11},{10,... | collective-permute-start | bytes 3145736 | tf_op jit(solution)/shard_map/ppermute | solution.py:113
  729.2 149.4 %collective-permute-start.35 = (f32[2,1024]{1,0:T(2,128)S(1)}, f32[2,1024]{1,0:T(2,128)S(1)}, u32[]{:S(2)}, u32[]{:S(2)}) collective-permute-start(f32[2,1024]{1,0:T(2,128)S(1)} %pad_maximum_fusion.16), channel_id=1, source_target_pairs={{0,3},{1,0},{2,1},{3,2},{4,7},{5,4},{6,5},{7,6},{8,11},{9,8},{10,9... | collective-permute-start | bytes 24584 | tf_op jit(solution)/shard_map/ppermute | solution.py:332
  783.6 96.6 %collective-permute-start.34 = (f32[2,1024]{1,0:T(2,128)S(1)}, f32[2,1024]{1,0:T(2,128)S(1)}, u32[]{:S(2)}, u32[]{:S(2)}) collective-permute-start(f32[2,1024]{1,0:T(2,128)S(1)} %pad_maximum_fusion.16), channel_id=1, source_target_pairs={{0,2},{1,3},{2,0},{3,1},{4,6},{5,7},{6,4},{7,5},{8,10},{9,11},{10,... | collective-permute-start | bytes 24584 | tf_op jit(solution)/shard_map/ppermute | solution.py:332
  834.8 53.6 %all-to-all-start.2 = ((bf16[8,128,512]{2,1,0:T(8,128)(2,1)}), bf16[8,128,512]{2,1,0:T(8,128)(2,1)S(1)}, u32[]{:S(2)}, u32[]{:S(2)}) async-start(bf16[8,128,512]{2,1,0:T(8,128)(2,1)} %bitcast.19), calls=%async_computation.2 | async-start | bytes 2097152 | tf_op jit(solution)/shard_map/all_to_all | solution.py:174
  888.4 20.9 %all-to-all-start.6 = ((bf16[8,128,512]{2,1,0:T(8,128)(2,1)}), bf16[8,128,512]{2,1,0:T(8,128)(2,1)S(1)}, u32[]{:S(2)}, u32[]{:S(2)}) async-start(bf16[8,128,512]{2,1,0:T(8,128)(2,1)} %bitcast.37), calls=%async_computation.6 | async-start | bytes 2097152 | tf_op jit(solution)/shard_map/all_to_all | solution.py:174
  912.6 18.2 %collective-permute-start.38 = (bf16[64,2048]{1,0:T(8,128)(2,1)S(1)}, bf16[64,2048]{1,0:T(8,128)(2,1)S(1)}, u32[]{:S(2)}, u32[]{:S(2)}) collective-permute-start(bf16[64,2048]{1,0:T(8,128)(2,1)S(1)} %get-tuple-element.58), channel_id=1, source_target_pairs={{0,3},{1,0},{2,1},{3,2},{4,7},{5,4},{6,5},{7,6},{8,11},{9,8},{10,9... | collective-permute-start | bytes 786440 | tf_op jit(solution)/shard_map/ppermute | solution.py:113
  913.9 17.7 %collective-permute-start.37 = (bf16[64,2048]{1,0:T(8,128)(2,1)S(1)}, bf16[64,2048]{1,0:T(8,128)(2,1)S(1)}, u32[]{:S(2)}, u32[]{:S(2)}) collective-permute-start(bf16[64,2048]{1,0:T(8,128)(2,1)S(1)} %get-tuple-element.59), channel_id=1, source_target_pairs={{0,1},{1,2},{2,3},{3,0},{4,5},{5,6},{6,7},{7,4},{8,9},{9,10},{10,1... | collective-permute-start | bytes 786440 | tf_op jit(solution)/shard_map/ppermute | solution.py:113
  914.6 18.9 %collective-permute-start.36 = (bf16[64,2048]{1,0:T(8,128)(2,1)S(1)}, bf16[64,2048]{1,0:T(8,128)(2,1)S(1)}, u32[]{:S(2)}, u32[]{:S(2)}) collective-permute-start(bf16[64,2048]{1,0:T(8,128)(2,1)S(1)} %get-tuple-element.57), channel_id=1, source_target_pairs={{0,2},{1,3},{2,0},{3,1},{4,6},{5,7},{6,4},{7,5},{8,10},{9,11},{10,... | collective-permute-start | bytes 786440 | tf_op jit(solution)/shard_map/ppermute | solution.py:113
  (98 other events, 1377.5 us)
Sparse Core Ops, SparseCore 0:
  10.5 46.6 all-gather.3
  59.7 54.4 all-gather.5
  116.1 129.2 all-gather.7
  504.8 77.4 reduce-scatter.5
  610.0 66.7 reduce-scatter.3
  680.2 156.8 reduce-scatter.7

commit v2 on v1

v2 whole, which is shorter than its diff:
```python
import jax
import jax.numpy as jnp
from jax import lax
from jax.experimental import pallas as pl
from jax.experimental.pallas import tpu as pltpu
from jax.sharding import PartitionSpec as P

HEAD_DIM = 128
GROUP_CAP = 1024
SEQ_SLOTS = 4

norm_eps = 1e-05
rope_base = 10000.0
bf16 = jnp.bfloat16
f32 = jnp.float32


def matmul(left, right):
    return jnp.dot(left, right, preferred_element_type=f32)


def times_transposed(left, right):
    return lax.dot_general(
        left, right, (((1,), (1,)), ((), ())), preferred_element_type=f32
    )


def transposed_times(left, right):
    return lax.dot_general(
        left, right, (((0,), (0,)), ((), ())), preferred_element_type=f32
    )


def norm_parts(values_in):
    row_mean = jnp.mean(values_in, axis=-1, keepdims=True)
    centered = values_in - row_mean
    variance = jnp.mean(centered * centered, axis=-1, keepdims=True)
    inverse = lax.rsqrt(variance + norm_eps)
    return centered * inverse, inverse


def rope_tables(position, head_dim):
    half_dim = head_dim // 2
    frequency = rope_base ** (-(jnp.arange(half_dim, dtype=f32) * 2.0) / head_dim)
    angles = position.astype(f32)[:, None] * frequency[None, :]
    cosine, sine = jnp.cos(angles), jnp.sin(angles)
    return (
        jnp.concatenate([cosine, cosine], axis=1),
        jnp.concatenate([-sine, sine], axis=1),
    )


def segments(lengths):
    row_index = jnp.arange(GROUP_CAP, dtype=jnp.int32)
    slot_ids = jnp.arange(SEQ_SLOTS, dtype=jnp.int32)
    ends = jnp.sum(
        jnp.where(slot_ids[:, None] <= slot_ids[None, :], lengths[:, None], 0), axis=0
    )
    passed = row_index[:, None] >= ends[None, :]
    segment = jnp.sum(passed.astype(jnp.int32), axis=1)
    begin_row = jnp.max(jnp.where(passed, ends[None, :], 0), axis=1)
    return (segment, row_index - begin_row)


VMEM_LIMIT = 58 * 1024 * 1024
BLOCK = 256


def params():
    return pltpu.CompilerParams(vmem_limit_bytes=VMEM_LIMIT)


def cost(flops, read, transcendentals=0):
    return pl.CostEstimate(
        flops=int(flops), bytes_accessed=int(read), transcendentals=int(transcendentals)
    )


def half_turn(values_in):
    return pltpu.roll(values_in, HEAD_DIM // 2, 1)


def qkv_kernel(rows_ref, weight_ref, cos_ref, sin_ref, out_ref):
    for first in range(0, rows_ref.shape[0], BLOCK):
        rows = pl.ds(first, BLOCK)
        pre = matmul(rows_ref[rows, :], weight_ref[...])
        for part in range(3):
            piece = pre[:, part * HEAD_DIM : (part + 1) * HEAD_DIM]
            if part < 2:
                piece = piece * cos_ref[rows, :] + half_turn(piece) * sin_ref[rows, :]
            out_ref[rows, part * HEAD_DIM : (part + 1) * HEAD_DIM] = piece.astype(bf16)


def project_qkv(rows, weight, cosine, sine):
    count, model = rows.shape
    columns = weight.shape[1]
    step = 3 * HEAD_DIM
    whole = lambda h: (0, 0)
    return pl.pallas_call(
        qkv_kernel,
        grid=(columns // step,),
        in_specs=[
            pl.BlockSpec((count, model), whole),
            pl.BlockSpec((model, step), lambda h: (0, h)),
            pl.BlockSpec((count, HEAD_DIM), whole),
            pl.BlockSpec((count, HEAD_DIM), whole),
        ],
        out_specs=pl.BlockSpec((count, step), lambda h: (0, h)),
        out_shape=jax.ShapeDtypeStruct((count, columns), bf16),
        compiler_params=params(),
        cost_estimate=cost(2 * count * model * columns, 2 * model * (count + columns)),
        name="qkv",
    )(rows, weight, cosine, sine)


def masked_softmax(q_rows, k_rows, seg_column, seg_row, row_first):
    scores = times_transposed(q_rows, k_rows) * HEAD_DIM ** (-0.5)
    row = lax.broadcasted_iota(jnp.int32, scores.shape, 0) + row_first
    column = lax.broadcasted_iota(jnp.int32, scores.shape, 1)
    allowed = (seg_column == seg_row) & (column <= row)
    scores = jnp.where(allowed, scores, -1e30)
    exponent = jnp.exp(scores - jnp.max(scores, axis=-1, keepdims=True))
    return exponent * (1.0 / jnp.sum(exponent, axis=-1, keepdims=True))


def attend_kernel(q_ref, k_ref, v_ref, column_ref, row_ref, out_ref):
    block = pl.program_id(1)
    for index in range(k_ref.shape[0] // BLOCK):

        @pl.when(block == index)
        def _(index=index):
            seen = (index + 1) * BLOCK
            prob = masked_softmax(
                q_ref[...], k_ref[:seen, :], column_ref[...], row_ref[:, :seen], index * BLOCK
            )
            out_ref[...] = matmul(prob.astype(bf16), v_ref[:seen, :]).astype(bf16)


def attend(qkv, segment):
    count = qkv.shape[0]
    heads = qkv.shape[1] // (3 * HEAD_DIM)
    return pl.pallas_call(
        attend_kernel,
        grid=(heads, count // BLOCK),
        in_specs=[
            pl.BlockSpec((BLOCK, HEAD_DIM), lambda h, i: (i, 3 * h)),
            pl.BlockSpec((count, HEAD_DIM), lambda h, i: (0, 3 * h + 1)),
            pl.BlockSpec((count, HEAD_DIM), lambda h, i: (0, 3 * h + 2)),
            pl.BlockSpec((BLOCK, 1), lambda h, i: (i, 0)),
            pl.BlockSpec((1, count), lambda h, i: (0, 0)),
        ],
        out_specs=pl.BlockSpec((BLOCK, HEAD_DIM), lambda h, i: (i, h)),
        out_shape=jax.ShapeDtypeStruct((count, heads * HEAD_DIM), bf16),
        compiler_params=params(),
        cost_estimate=cost(
            4 * heads * count * count * HEAD_DIM, 8 * count * heads * HEAD_DIM, heads * count * count
        ),
        name="attend",
    )(qkv, qkv, qkv, segment[:, None], segment[None, :])


def attend_back_kernel(
    q_ref, k_ref, v_ref, grad_ref, column_ref, row_ref, cos_ref, sin_ref, out_ref, total
):
    block = pl.program_id(1)
    scale = HEAD_DIM ** (-0.5)
    blocks = k_ref.shape[0] // BLOCK

    @pl.when(block == 0)
    def _():
        total[...] = jnp.zeros_like(total)

    for index in range(blocks):

        @pl.when(block == index)
        def _(index=index):
            seen = (index + 1) * BLOCK
            q_rows, k_rows, grad = q_ref[...], k_ref[:seen, :], grad_ref[...]
            prob = masked_softmax(
                q_rows, k_rows, column_ref[...], row_ref[:, :seen], index * BLOCK
            )
            prob_grad = times_transposed(grad, v_ref[:seen, :])
            delta = jnp.sum(prob_grad * prob, axis=-1, keepdims=True)
            score_grad = (prob * (prob_grad - delta)).astype(bf16)
            total[0, index * BLOCK : seen, :] = matmul(score_grad, k_rows) * scale
            total[1, :seen, :] += transposed_times(score_grad, q_rows) * scale
            total[2, :seen, :] += transposed_times(prob.astype(bf16), grad)

    @pl.when(block == blocks - 1)
    def _():
        for part in range(3):
            piece = total[part]
            if part < 2:
                piece = piece * cos_ref[...] - half_turn(piece) * sin_ref[...]
            out_ref[:, part * HEAD_DIM : (part + 1) * HEAD_DIM] = piece.astype(bf16)


def attend_back(qkv, grad, segment, cosine, sine):
    count = qkv.shape[0]
    heads = qkv.shape[1] // (3 * HEAD_DIM)
    return pl.pallas_call(
        attend_back_kernel,
        grid=(heads, count // BLOCK),
        in_specs=[
            pl.BlockSpec((BLOCK, HEAD_DIM), lambda h, i: (i, 3 * h)),
            pl.BlockSpec((count, HEAD_DIM), lambda h, i: (0, 3 * h + 1)),
            pl.BlockSpec((count, HEAD_DIM), lambda h, i: (0, 3 * h + 2)),
            pl.BlockSpec((BLOCK, HEAD_DIM), lambda h, i: (i, h)),
            pl.BlockSpec((BLOCK, 1), lambda h, i: (i, 0)),
            pl.BlockSpec((1, count), lambda h, i: (0, 0)),
            pl.BlockSpec((count, HEAD_DIM), lambda h, i: (0, 0)),
            pl.BlockSpec((count, HEAD_DIM), lambda h, i: (0, 0)),
        ],
        out_specs=pl.BlockSpec((count, 3 * HEAD_DIM), lambda h, i: (0, h)),
        out_shape=jax.ShapeDtypeStruct(qkv.shape, bf16),
        scratch_shapes=[pltpu.VMEM((3, count, HEAD_DIM), f32)],
        compiler_params=params(),
        cost_estimate=cost(
            10 * heads * count * count * HEAD_DIM, 14 * count * heads * HEAD_DIM, heads * count * count
        ),
        name="attend_back",
    )(qkv, qkv, qkv, grad, segment[:, None], segment[None, :], cosine, sine)


def hidden_kernel(att_ref, weight_ref, rows_ref, hidden_ref, normed_ref):
    hidden = rows_ref[...].astype(f32) + matmul(att_ref[...], weight_ref[...])
    hidden_ref[...] = hidden
    normed_ref[...] = norm_parts(hidden)[0].astype(bf16)


def hidden_and_norm(attended, weight, rows):
    count, model = rows.shape
    here = lambda i: (i, 0)
    return pl.pallas_call(
        hidden_kernel,
        grid=(count // BLOCK,),
        in_specs=[
            pl.BlockSpec((BLOCK, model), here),
            pl.BlockSpec((model, model), lambda i: (0, 0)),
            pl.BlockSpec((BLOCK, model), here),
        ],
        out_specs=[pl.BlockSpec((BLOCK, model), here)] * 2,
        out_shape=[
            jax.ShapeDtypeStruct((count, model), f32),
            jax.ShapeDtypeStruct((count, model), bf16),
        ],
        compiler_params=params(),
        cost_estimate=cost(2 * count * model * model, 2 * model * model + 10 * count * model),
        name="hidden",
    )(attended, weight, rows)


def up_kernel(rows_ref, gate_ref, up_ref, gate_out, up_out, act_ref):
    for first in range(0, rows_ref.shape[0], BLOCK):
        rows = pl.ds(first, BLOCK)
        gate = matmul(rows_ref[rows, :], gate_ref[0])
        up = matmul(rows_ref[rows, :], up_ref[0])
        gate_out[rows, :] = gate
        up_out[rows, :] = up
        act_ref[rows, :] = (gate / (1.0 + jnp.exp(-gate)) * up).astype(bf16)


def mlp_up(rows, weights):
    count, model = rows.shape
    hidden_units = weights.shape[2]
    wide = jax.ShapeDtypeStruct((count, hidden_units), f32)
    return pl.pallas_call(
        up_kernel,
        grid=(hidden_units // BLOCK,),
        in_specs=[
            pl.BlockSpec((count, model), lambda j: (0, 0)),
            pl.BlockSpec((1, model, BLOCK), lambda j: (0, 0, j)),
            pl.BlockSpec((1, model, BLOCK), lambda j: (1, 0, j)),
        ],
        out_specs=[pl.BlockSpec((count, BLOCK), lambda j: (0, j))] * 3,
        out_shape=[wide, wide, jax.ShapeDtypeStruct((count, hidden_units), bf16)],
        compiler_params=params(),
        cost_estimate=cost(
            4 * count * model * hidden_units,
            4 * model * hidden_units + 2 * count * model + 10 * count * hidden_units,
            count * hidden_units,
        ),
        name="mlp_up",
    )(rows, weights, weights)


def down_back_kernel(grad_ref, down_ref, gate_in, up_in, dgate_ref, dup_ref):
    for first in range(0, grad_ref.shape[0], BLOCK):
        rows = pl.ds(first, BLOCK)
        down = times_transposed(grad_ref[rows, :], down_ref[0])
        gate = gate_in[rows, :]
        sigmoid = 1.0 / (1.0 + jnp.exp(-gate))
        silu = gate * sigmoid
        dgate_ref[rows, :] = (
            down * up_in[rows, :] * (sigmoid + silu * (1.0 - sigmoid))
        ).astype(bf16)
        dup_ref[rows, :] = (down * silu).astype(bf16)


def mlp_down_back(grads, weights, gate, up):
    count, model = grads.shape
    hidden_units = weights.shape[2]
    part = pl.BlockSpec((count, BLOCK), lambda j: (0, j))
    out = jax.ShapeDtypeStruct((count, hidden_units), bf16)
    return pl.pallas_call(
        down_back_kernel,
        grid=(hidden_units // BLOCK,),
        in_specs=[
            pl.BlockSpec((count, model), lambda j: (0, 0)),
            pl.BlockSpec((1, BLOCK, model), lambda j: (2, j, 0)),
            part,
            part,
        ],
        out_specs=[part] * 2,
        out_shape=[out] * 2,
        compiler_params=params(),
        cost_estimate=cost(
            2 * count * model * hidden_units,
            2 * model * hidden_units + 2 * count * model + 12 * count * hidden_units,
            count * hidden_units,
        ),
        name="mlp_down_back",
    )(grads, weights, gate, up)


def norm_back(values_in, grad_in):
    unit_rows, inverse = norm_parts(values_in)
    return inverse * (
        grad_in
        - jnp.mean(grad_in, axis=-1, keepdims=True)
        - unit_rows * jnp.mean(grad_in * unit_rows, axis=-1, keepdims=True)
    )


def two_grad_kernel(order_ref, *refs):
    *row_refs, gate_ref, up_ref, out_ref, total = refs
    step = pl.program_id(0)
    columns = pl.ds(pl.multiple_of(step * BLOCK, BLOCK), BLOCK)
    pieces = out_ref.shape[0]
    for piece in range(pieces):
        total[piece, :, columns] = times_transposed(
            row_refs[3 * piece][...], gate_ref[0]
        ) + times_transposed(row_refs[3 * piece + 1][...], up_ref[0])

    @pl.when(step == pl.num_programs(0) - 1)
    def _():
        for piece in range(pieces):
            out_ref[piece] = norm_back(row_refs[3 * piece + 2][...], total[piece]).astype(bf16)


def two_grad_pieces(order, dgate, dup, weights, hidden, quarter):
    pieces = order.shape[0]
    hidden_units = dgate.shape[1]
    model = weights.shape[1]
    rows = []
    for p in range(pieces):
        here = lambda j, order, p=p: (order[p], 0)
        rows += [pl.BlockSpec((quarter, hidden_units), here)] * 2
        rows += [pl.BlockSpec((quarter, model), here, pipeline_mode=pl.Buffered(1))]
    return pl.pallas_call(
        two_grad_kernel,
        grid_spec=pltpu.PrefetchScalarGridSpec(
            num_scalar_prefetch=1,
            grid=(model // BLOCK,),
            in_specs=[
                *rows,
                pl.BlockSpec((1, BLOCK, hidden_units), lambda j, order: (0, j, 0)),
                pl.BlockSpec((1, BLOCK, hidden_units), lambda j, order: (1, j, 0)),
            ],
            out_specs=pl.BlockSpec((pieces, quarter, model), lambda j, order: (0, 0, 0)),
            scratch_shapes=[pltpu.VMEM((pieces, quarter, model), f32)],
        ),
        out_shape=jax.ShapeDtypeStruct((pieces, quarter, model), bf16),
        compiler_params=params(),
        cost_estimate=cost(
            4 * pieces * quarter * model * hidden_units, 4 * model * hidden_units
        ),
        name="two_grad",
    )(order, *([dgate, dup, hidden] * pieces), weights, weights)


def one_grad_kernel(place_ref, grad_ref, weight_ref, rows_ref, out_ref):
    grad = norm_back(
        rows_ref[...].astype(f32), times_transposed(grad_ref[...], weight_ref[...])
    ).astype(bf16)
    width = out_ref.shape[2]
    for piece in range(out_ref.shape[0]):
        out_ref[place_ref[piece]] = grad[:, piece * width : (piece + 1) * width]


def one_grad_pieces(place, qkv_grad, weight, rows):
    count, columns = qkv_grad.shape
    pieces = place.shape[0]
    model = rows.shape[1]
    here = lambda i, place: (i, 0)
    return pl.pallas_call(
        one_grad_kernel,
        grid_spec=pltpu.PrefetchScalarGridSpec(
            num_scalar_prefetch=1,
            grid=(count // BLOCK,),
            in_specs=[
                pl.BlockSpec((BLOCK, columns), here),
                pl.BlockSpec((model, columns), lambda i, place: (0, 0)),
                pl.BlockSpec((BLOCK, model), here),
            ],
            out_specs=pl.BlockSpec(
                (pieces, BLOCK, model // pieces), lambda i, place: (0, i, 0)
            ),
        ),
        out_shape=jax.ShapeDtypeStruct((pieces, count, model // pieces), bf16),
        compiler_params=params(),
        cost_estimate=cost(
            2 * count * model * columns, 2 * columns * model + 6 * count * columns
        ),
        name="one_grad",
    )(place, qkv_grad, weight, rows)


def att_grads_kernel(normed_ref, qkv_ref, att_ref, hidden_ref, out_ref):
    owner = pl.program_id(0)
    columns = qkv_ref.shape[1]
    out_ref[0, :, :columns] = transposed_times(normed_ref[...], qkv_ref[...]).astype(bf16)
    model = hidden_ref.shape[1]
    rest = model - columns
    pieces = model // rest
    height = out_ref.shape[1] // pieces
    per_tile = HEAD_DIM // height
    product = transposed_times(att_ref[...], hidden_ref[...]).astype(bf16)
    for place in range(per_tile):

        @pl.when(lax.rem(owner, per_tile) == place)
        def _(place=place):
            for piece in range(pieces):
                out_ref[0, piece * height : (piece + 1) * height, columns:] = product[
                    place * height : (place + 1) * height, piece * rest : (piece + 1) * rest
                ]


def att_grads(normed, qkv_grad, attended, hidden_grad, groups):
    count, model = normed.shape
    columns = qkv_grad.shape[1]
    local = attended.shape[1]
    tall = model // groups
    per_tile = HEAD_DIM // (local // groups)
    once = pl.Buffered(1)
    whole = lambda i: (0, 0)
    if tall % HEAD_DIM == 0:
        normed_spec = pl.BlockSpec((count, tall), lambda i: (0, i))
        operand = normed
    else:
        normed_spec = pl.BlockSpec((None, count, tall), lambda i: (i, 0, 0))
        operand = normed.reshape(count, groups, tall).swapaxes(0, 1)
    return pl.pallas_call(
        att_grads_kernel,
        grid=(groups,),
        in_specs=[
            normed_spec,
            pl.BlockSpec((count, columns), whole, pipeline_mode=once),
            pl.BlockSpec((count, HEAD_DIM), lambda i: (0, i // per_tile)),
            pl.BlockSpec((count, model), whole, pipeline_mode=once),
        ],
        out_specs=pl.BlockSpec((1, tall, model), lambda i: (i, 0, 0)),
        out_shape=jax.ShapeDtypeStruct((groups, tall, model), bf16),
        compiler_params=params(),
        cost_estimate=cost(
            2 * count * model * columns + 2 * count * groups * HEAD_DIM * model,
            2 * model * model + 4 * count * model + 2 * count * columns,
        ),
        name="att_grads",
    )(operand, qkv_grad, attended, hidden_grad)


def mlp_grads_kernel(left_ref, act_ref, dgate_ref, dup_ref, grad_ref, out_ref):
    which = pl.program_id(0)
    for index, (left, right) in enumerate(
        ((left_ref, dgate_ref), (left_ref, dup_ref), (act_ref, grad_ref))
    ):

        @pl.when(which == index)
        def _(left=left, right=right):
            out_ref[0] = transposed_times(left[...], right[...]).astype(bf16)


def mlp_grads(normed, act, dgate, dup, grads):
    count, model = normed.shape
    hidden_units = act.shape[1]
    whole = lambda w, i: (0, 0)
    once = pl.Buffered(1)
    return pl.pallas_call(
        mlp_grads_kernel,
        grid=(3, model // BLOCK),
        in_specs=[
            pl.BlockSpec((count, BLOCK), lambda w, i: (0, jnp.where(w < 2, i, 0))),
            pl.BlockSpec((count, BLOCK), lambda w, i: (0, jnp.where(w < 2, 0, i))),
            pl.BlockSpec((count, hidden_units), whole, pipeline_mode=once),
            pl.BlockSpec((count, hidden_units), whole, pipeline_mode=once),
            pl.BlockSpec((count, model), whole, pipeline_mode=once),
        ],
        out_specs=pl.BlockSpec((1, BLOCK, hidden_units), lambda w, i: (w, i, 0)),
        out_shape=jax.ShapeDtypeStruct((3, model, hidden_units), bf16),
        compiler_params=params(),
        cost_estimate=cost(
            6 * count * model * hidden_units, 6 * model * hidden_units + 10 * count * model
        ),
        name="mlp_grads",
    )(normed, act, dgate, dup, grads)


def after(value, *others):
    return lax.optimization_barrier((value, *others))[0]


def line_step(block, axis, size, step):
    from_low, from_high = block
    up = [(i, i + 1) for i in range(step - 1, size - 1)]
    down = [(i, i - 1) for i in range(size - step, 0, -1)]
    return lax.ppermute(from_low, axis, up), lax.ppermute(from_high, axis, down)


def line_whole(own, arrived, axis, size):
    me = lax.axis_index(axis)
    whole = []
    for owner in range(size):
        piece = own
        for step in range(1, size):
            if owner + step < size:
                piece = jnp.where(me == owner + step, arrived[step - 1][0], piece)
            if owner - step >= 0:
                piece = jnp.where(me == owner - step, arrived[step - 1][1], piece)
        whole.append(piece)
    return whole


def chain_gather(block, axis, size, begun=None):
    arrived = list(begun or [])
    for step in range(len(arrived) + 1, size):
        arrived.append(line_step(arrived[-1] if arrived else (block, block), axis, size, step))
    return line_whole(block, arrived, axis, size)


def far_first(size):
    return sorted(range(1, size), key=lambda step: -min(step, size - step))


def sent_on(term, axis, size, step):
    return lax.ppermute(term, axis, [(i, (i + step) % size) for i in range(size)])


def added(own, came):
    for piece in came:
        own = own + piece.astype(f32)
    return own


def on_device(
    tokens,
    cotangent,
    w_query,
    w_key,
    w_value,
    w_out,
    w_gate,
    w_up,
    w_down,
    seq_lengths,
    deal,
    row_dest,
):
    groups = lax.axis_size("fsdp")
    shards = lax.axis_size("tp")
    own_group = lax.axis_index("fsdp")
    own_shard = lax.axis_index("tp")
    capacity = GROUP_CAP
    per_pair = capacity // groups
    quarter = capacity // shards
    head_dim = HEAD_DIM
    given, width = tokens.shape
    model = width * shards
    local_width = w_query.shape[1]
    heads = local_width // head_dim
    shard_rows = w_query.shape[0]

    steps = far_first(shards)
    order = jnp.stack([lax.rem(own_shard + step, shards) for step in (*steps, 0)])
    place_of = [0] * shards
    for index, step in enumerate((*steps, 0)):
        place_of[step] = index
    place = jnp.stack(
        [
            sum(
                jnp.where(lax.rem(own_shard + step, shards) == j, place_of[step], 0)
                for step in range(shards)
            )
            for j in range(shards)
        ]
    )

    target = row_dest // capacity
    within = row_dest - target * capacity
    given_index = jnp.arange(given, dtype=jnp.int32)
    earlier = (target[:, None] == target[None, :]) & (
        given_index[None, :] < given_index[:, None]
    )
    slot_of = target * per_pair + jnp.sum(earlier.astype(jnp.int32), axis=1)
    slots = jnp.arange(capacity, dtype=jnp.int32)
    deal_hit = slots[:, None] == slot_of[None, :]
    deal_out = deal_hit.astype(bf16)
    place_high, place_low = (within + 1) // 32, (within + 1) % 32
    lane = jnp.arange(HEAD_DIM, dtype=jnp.int32)[None, :]
    place_columns = jnp.where(
        lane == 0, place_high[:, None], jnp.where(lane == 1, place_low[:, None], 0)
    ).astype(bf16)

    def over_fsdp(rows):
        return lax.all_to_all(rows, "fsdp", split_axis=0, concat_axis=0, tiled=True)

    def to_home(rows):
        sent = transposed_times(place_in, rows).astype(bf16)
        return transposed_times(deal_out, over_fsdp(sent)).astype(bf16)

    sent_rows = matmul(deal_out, jnp.concatenate([tokens, place_columns], axis=1)).astype(bf16)
    sent_grads = matmul(deal_out, cotangent).astype(bf16)

    qkv_shard = jnp.stack(
        [w.reshape(shard_rows, heads, head_dim) for w in (w_query, w_key, w_value)], axis=2
    ).reshape(shard_rows, 3 * local_width)
    full_qkv = lax.all_gather(qkv_shard, "fsdp", axis=0, tiled=True)
    out_came = [sent_on(w_out, "tp", shards, step) for step in range(1, shards)]
    came_rows = over_fsdp(sent_rows)
    *out_came, came_rows, sent_grads = lax.optimization_barrier(
        (*out_came, came_rows, sent_grads)
    )
    came_place = came_rows[:, width : width + 2].astype(jnp.int32)
    recv_place = came_place[:, 0] * 32 + came_place[:, 1] - 1
    place_in = (slots[:, None] == recv_place[None, :]).astype(bf16)
    out_came = [w_out] + out_came
    out_rows = []
    for owner in range(shards):
        piece = w_out
        for step in range(1, shards):
            piece = jnp.where(own_shard == (owner + step) % shards, out_came[step], piece)
        out_rows.append(piece)
    out_rows = jnp.stack(out_rows)
    full_out = lax.all_gather(out_rows, "fsdp", axis=1, tiled=True).reshape(model, model)
    full_mlp = lax.all_gather(
        jnp.stack([w_gate, w_up, w_down]), "fsdp", axis=1, tiled=True
    )

    buffer_rows = matmul(place_in, came_rows[:, :width]).astype(bf16)
    buffer_grads = matmul(place_in, over_fsdp(after(sent_grads, buffer_rows))).astype(bf16)
    full_rows = jnp.concatenate(chain_gather(buffer_rows, "tp", shards), axis=1)
    full_rows, first_grads = lax.optimization_barrier((full_rows, buffer_grads))

    list_index = jnp.sum(jnp.where(deal == own_group, jnp.arange(groups, dtype=jnp.int32), 0))
    lengths = lax.dynamic_index_in_dim(seq_lengths, list_index, 0, keepdims=False)
    segment, position = segments(lengths)
    cosine, sine = rope_tables(position, head_dim)

    normed_one = norm_parts(full_rows.astype(f32))[0].astype(bf16)
    grads_begun = line_step((first_grads, first_grads), "tp", shards, 1)
    qkv = project_qkv(normed_one, full_qkv, cosine, sine)
    attended = attend(qkv, segment)
    attended, *grads_begun = lax.optimization_barrier((attended, *grads_begun))
    full_attended = jnp.concatenate(chain_gather(attended, "tp", shards), axis=1)
    *grads_begun, full_attended = lax.optimization_barrier((*grads_begun, full_attended))
    grads_begun = [grads_begun, line_step(grads_begun, "tp", shards, 2)]
    hidden, normed_two = hidden_and_norm(full_attended, full_out, full_rows)
    *grads_begun[1], normed_two = lax.optimization_barrier((*grads_begun[1], normed_two))
    grads_begun.append(line_step(grads_begun[1], "tp", shards, 3))
    gate, up, activated = mlp_up(normed_two, full_mlp)
    *grads_begun[2], activated = lax.optimization_barrier((*grads_begun[2], activated))
    full_grads = jnp.concatenate(
        chain_gather(first_grads, "tp", shards, grads_begun), axis=1
    )

    def rows_of(rows, owner):
        return lax.dynamic_slice_in_dim(rows, owner * quarter, quarter, 0)

    def features_of(rows, owner):
        return lax.dynamic_slice_in_dim(rows, owner * width, width, 1)

    mlp_part = matmul(activated, full_mlp[2]).astype(bf16)
    mlp_terms = [features_of(mlp_part, order[index]) for index in range(shards)]
    full_grads, *mlp_terms = lax.optimization_barrier((full_grads, *mlp_terms))
    mlp_first = sent_on(mlp_terms[0], "tp", shards, steps[0])
    gate_grad, up_grad = mlp_down_back(full_grads, full_mlp, gate, up)
    two_first = two_grad_pieces(order[:1], gate_grad, up_grad, full_mlp, hidden, quarter)
    two_first, mlp_first, up_late = lax.optimization_barrier((two_first, mlp_first, up_grad))
    two_rest = two_grad_pieces(order[1:], gate_grad, up_late, full_mlp, hidden, quarter)
    two_came = [sent_on(two_first[0], "tp", shards, steps[0])] + [
        sent_on(two_rest[index], "tp", shards, step) for index, step in enumerate(steps[1:])
    ]
    grad_mlp = mlp_grads(normed_two, activated, gate_grad, up_grad, full_grads)
    *two_came, grad_mlp = lax.optimization_barrier((*two_came, grad_mlp))
    sum_mlp = lax.psum_scatter(grad_mlp, "fsdp", scatter_dimension=1, tiled=True)

    hidden_grad = added(
        rows_of(full_grads, own_shard).astype(f32) + two_rest[-1].astype(f32), two_came
    )
    hidden_grad_low = hidden_grad.astype(bf16)
    full_hidden_grad = jnp.concatenate(
        chain_gather(hidden_grad_low, "tp", shards), axis=0
    )
    own_out = lax.dynamic_slice_in_dim(full_out, own_shard * local_width, local_width, 0)
    attended_grad = times_transposed(full_hidden_grad, own_out).astype(bf16)

    *mlp_terms, full_hidden_grad = lax.optimization_barrier((*mlp_terms, full_hidden_grad))
    mlp_came = [mlp_first] + [
        sent_on(mlp_terms[index], "tp", shards, step)
        for index, step in enumerate(steps)
        if index
    ]
    qkv_grad = attend_back(qkv, attended_grad, segment, cosine, sine)
    *mlp_came, qkv_grad = lax.optimization_barrier((*mlp_came, qkv_grad))
    one_terms = one_grad_pieces(place, qkv_grad, full_qkv, full_rows)
    one_came = [
        sent_on(one_terms[index], "tp", shards, step) for index, step in enumerate(steps)
    ]
    grad_att = att_grads(
        normed_one, after(qkv_grad, one_terms), attended, full_hidden_grad, groups
    )
    sum_mlp, grad_att = lax.optimization_barrier((sum_mlp, grad_att))
    sum_att = lax.psum_scatter(grad_att, "fsdp", scatter_dimension=0, tiled=False)

    output_here = added(
        features_of(hidden, own_shard) + mlp_terms[-1].astype(f32), mlp_came
    )
    output = to_home(output_here.astype(bf16))

    back_here = added(one_terms[-1].astype(f32), one_came)
    input_grad = to_home(
        (features_of(full_hidden_grad, own_shard).astype(f32) + back_here).astype(bf16)
    )

    sum_att = sum_att.astype(f32)
    sum_qkv = sum_att[:, : 3 * local_width].reshape(shard_rows, heads, 3, head_dim)
    out_part = sum_att[:, 3 * local_width :]
    out_pieces = model // out_part.shape[1]
    out_height = shard_rows // out_pieces
    sum_out = jnp.concatenate(
        [out_part[i * out_height : (i + 1) * out_height] for i in range(out_pieces)], axis=1
    )
    sum_gate, sum_up, sum_down = sum_mlp.astype(f32)
    return (
        output,
        input_grad,
        sum_qkv[:, :, 0].reshape(shard_rows, local_width),
        sum_qkv[:, :, 1].reshape(shard_rows, local_width),
        sum_qkv[:, :, 2].reshape(shard_rows, local_width),
        sum_out,
        sum_gate,
        sum_up,
        sum_down,
    )


def solution(mesh):
    in_specs = (
        P("fsdp", "tp"),
        P("fsdp", "tp"),
        P("fsdp", "tp"),
        P("fsdp", "tp"),
        P("fsdp", "tp"),
        P(("tp", "fsdp"), None),
        P("fsdp", "tp"),
        P("fsdp", "tp"),
        P(("tp", "fsdp"), None),
        P(),
        P(),
        P("fsdp"),
    )
    out_specs = (
        P("fsdp", "tp"),
        P("fsdp", "tp"),
        P("fsdp", "tp"),
        P("fsdp", "tp"),
        P("fsdp", "tp"),
        P(("tp", "fsdp"), None),
        P("fsdp", "tp"),
        P("fsdp", "tp"),
        P(("tp", "fsdp"), None),
    )
    return jax.shard_map(
        on_device, mesh=mesh, in_specs=in_specs, out_specs=out_specs, check_vma=False
    )
```

time: 963 us -> 780 us (0.81)
  Pallas kernels: 0 us -> 224 us
  matrix products: 258 us -> 41.8 us
  other arithmetic: 94.9 us -> 40.4 us
  starting transfers between devices: 163 us -> 111 us
  waiting for transfers between devices: 345 us -> 308 us
  local copies, waits for them, and re-layouts: 51.7 us -> 28.3 us
  blocking collectives: 17.8 us -> 0 us
    pallas_call x0 -> x11, Pallas kernels: none -> 224 us  [the longest x2 40 us: two_grad_pieces(): pl.pallas_call(two_grad_kernel, grid_spec=pltpu.PrefetchScalarGridSpec(nu...]
    dot_general x5 -> x1, matrix products: 66.7 us -> 7.72 us  [times_transposed(): lax.dot_general(left, right, (((1,), (1,)), ((), ())), preferred_element_...]
    dot_general x9 -> x5, matrix products: 77.8 us -> 20.4 us  [matmul(): return jnp.dot(left, right, preferred_element_type=f32)]
    dot_general x9 -> x4, matrix products: 67.8 us -> 13.6 us  [transposed_times(): lax.dot_general(left, right, (((0,), (0,)), ((), ())), preferred_element_...]
    all_to_all x6 -> x4, waiting for transfers between devices: 83.8 us -> 34.5 us  [over_fsdp(): return lax.all_to_all(rows, 'fsdp', split_axis=0, concat_axis=0, tiled=True)]
    ppermute x39 -> x36, starting transfers between devices: 129 us -> 84 us  [the longest x12 41.8 us: line_step(): lax.ppermute(from_low, axis, up)]
    dot_general x12 -> x0, matrix products: 45.3 us -> none  [the longest x2 16.1 us: on_device(): jnp.einsum('qhd,khd->hqk', grad_rows, value_rows, preferred_element_type=...]
    reduce_sum x5 -> x0, other arithmetic: 21.1 us -> none  [the longest x1 14.4 us: on_device(): jnp.sum(normed_one_grad * unit_one, axis=1)]
  transfers between devices with their start and end apart: 51 -> 45, of which waited for: 23 -> 22; matrix products, arithmetic and copies ran while one was open for 31% -> 10% of each run, Pallas kernels for 0% -> 29%
where the time goes in v2:
time: 780 us; the launch traced here: 770 us
  waiting for transfers between devices  308 us (39%)
  Pallas kernels  224 us (29%)
  starting transfers between devices  111 us (14%)
  matrix products  41.8 us (5%)
  other arithmetic  40.4 us (5%)
  local copies, waits for them, and re-layouts  28.3 us (4%)
  between operations  16.9 us (2%)
    ppermute x12, waiting for transfers between devices, sent_on(): lax.ppermute(term, axis, [(i, (i + step) % size) for i in range(size)])  112 us
    ppermute x12, waiting for transfers between devices, line_step(): lax.ppermute(from_high, axis, down)  101 us
    ppermute x12, waiting for transfers between devices, line_step(): lax.ppermute(from_low, axis, up)  60.3 us
    ppermute x12, starting transfers between devices, line_step(): lax.ppermute(from_low, axis, up)  41.8 us
    pallas_call x2, Pallas kernels, two_grad_pieces(): pl.pallas_call(two_grad_kernel, grid_spec=pltpu.PrefetchScalarGridSpec(nu...  40 us
    pallas_call x1, Pallas kernels, mlp_grads(): pl.pallas_call(mlp_grads_kernel, grid=(3, model // BLOCK), in_specs=[pl.B...  38.8 us
    all_to_all x4, waiting for transfers between devices, over_fsdp(): return lax.all_to_all(rows, 'fsdp', split_axis=0, concat_axis=0, tiled=True)  34.5 us
    ppermute x12, starting transfers between devices, line_step(): lax.ppermute(from_high, axis, down)  27.5 us
  transfers between devices with their start and end apart: 45, of which 22 were waited for; matrix products, arithmetic and copies ran while one was open for 10% of the time, Pallas kernels for 29%

profile of v2, /device:TPU:16, one launch (start us, length us, event | category | flops | bytes accessed | tf_op | source)
XLA Modules:
  0.0 770.3 jit_solution(9535088892896305830)
XLA Ops:
  15.6 3.7 all-to-all-start
  24.7 21.2 %all-to-all-done = bf16[8,128,640]{2,1,0:T(8,128)(2,1)S(1)} async-done(((bf16[8,128,640]{2,1,0:T(8,128)(2,1)}), bf16[8,128,640]{2,1,0:T(8,128)(2,1)S(1)}, u32[]{:S(2)}, u32[]{:S(2)}) %all-to-all-start) | async-done | bytes 1310752 | tf_op jit(solution)/shard_map/all_to_all | solution.py:615
  56.5 3.6 collective-permute-start.3
  60.0 20.9 %collective-permute-done.6 = bf16[1024,512]{1,0:T(8,128)(2,1)S(1)} collective-permute-done((bf16[1024,512]{1,0:T(8,128)(2,1)S(1)}, bf16[1024,512]{1,0:T(8,128)(2,1)S(1)}, u32[]{:S(2)}, u32[]{:S(2)}) %collective-permute-start.6) | collective-permute-done | bytes 1048608 | tf_op jit(solution)/shard_map/ppermute | solution.py:517
  89.3 4.2 all-to-all-start.1
  94.8 9.6 %collective-permute-done.7 = bf16[1024,512]{1,0:T(8,128)(2,1)} collective-permute-done((bf16[1024,512]{1,0:T(8,128)(2,1)S(1)}, bf16[1024,512]{1,0:T(8,128)(2,1)}, u32[]{:S(2)}, u32[]{:S(2)}) %collective-permute-start.7) | collective-permute-done | bytes 1048608 | tf_op jit(solution)/shard_map/ppermute | solution.py:517
  106.1 3.5 collective-permute-done.4
  109.6 3.8 collective-permute-start.5
  119.5 13.3 %collective-permute-done.5 = bf16[1024,512]{1,0:T(8,128)(2,1)} collective-permute-done((bf16[1024,512]{1,0:T(8,128)(2,1)}, bf16[1024,512]{1,0:T(8,128)(2,1)}, u32[]{:S(2)}, u32[]{:S(2)}) %collective-permute-start.5) | collective-permute-done | bytes 1048608 | tf_op jit(solution)/shard_map/ppermute | solution.py:517
  137.2 4.2 collective-permute-start.9
  146.3 14.4 %qkv.1.q_ref.k_ref.v_ref = bf16[1024,1536]{1,0:T(8,128)(2,1)} custom-call(bf16[1024,2048]{1,0:T(8,128)(2,1)} %fusion.3.rows_ref.normed_ref, bf16[2048,1536]{1,0:T(8,128)(2,1)} %all-gather.4.cloned.1.call-done.weight_ref, f32[1024,128]{1,0:T(8,128)} %get-tuple-element.176.cos_ref, f32[1024,128]{1,0:T(8,128)} %get-tuple-element.177.sin_ref), custom_call_target="tpu_custom_call" | custom-call | flops 6442450944 | bytes 10485760 | tf_op jit(solution)/shard_map/qkv/pallas_call | solution.py:99
  160.8 15.5 %attend.1.att_ref = bf16[1024,512]{1,0:T(8,128)(2,1)} custom-call(bf16[1024,1536]{1,0:T(8,128)(2,1)} %qkv.1.q_ref.k_ref.v_ref, bf16[1024,1536]{1,0:T(8,128)(2,1)} %qkv.1.q_ref.k_ref.v_ref, bf16[1024,1536]{1,0:T(8,128)(2,1)} %qkv.1.q_ref.k_ref.v_ref, s32[1024,1]{1,0:T(8,128)} %copy.43.column_ref, s32[1,1024]{1,0:T(1,128)} %bitcast.98), custom_call_target="tpu_custom_call" | custom-call | flops 2147483648 | bytes 4194304 | tf_op jit(solution)/shard_map/attend/pallas_call | solution.py:142
  178.2 4.0 collective-permute-start.11
  182.2 17.3 %collective-permute-done.14 = bf16[1024,512]{1,0:T(8,128)(2,1)S(1)} collective-permute-done((bf16[1024,512]{1,0:T(8,128)(2,1)}, bf16[1024,512]{1,0:T(8,128)(2,1)S(1)}, u32[]{:S(2)}, u32[]{:S(2)}) %collective-permute-start.14) | collective-permute-done | bytes 1048608 | tf_op jit(solution)/shard_map/ppermute | solution.py:517
  201.8 3.8 collective-permute-start.12
  205.7 14.2 %collective-permute-done.15 = bf16[1024,512]{1,0:T(8,128)(2,1)S(1)} collective-permute-done((bf16[1024,512]{1,0:T(8,128)(2,1)S(1)}, bf16[1024,512]{1,0:T(8,128)(2,1)S(1)}, u32[]{:S(2)}, u32[]{:S(2)}) %collective-permute-start.15) | collective-permute-done | bytes 1048608 | tf_op jit(solution)/shard_map/ppermute | solution.py:517
  220.9 3.5 collective-permute-done.12
  224.5 4.4 collective-permute-start.13
  228.9 16.8 %collective-permute-done.13 = bf16[1024,512]{1,0:T(8,128)(2,1)S(1)} collective-permute-done((bf16[1024,512]{1,0:T(8,128)(2,1)S(1)}, bf16[1024,512]{1,0:T(8,128)(2,1)S(1)}, u32[]{:S(2)}, u32[]{:S(2)}) %collective-permute-start.13) | collective-permute-done | bytes 1048608 | tf_op jit(solution)/shard_map/ppermute | solution.py:517
  249.6 4.4 collective-permute-start.17
  258.1 16.8 %hidden.1 = (f32[1024,2048]{1,0:T(8,128)}, bf16[1024,2048]{1,0:T(8,128)(2,1)}) custom-call(bf16[1024,2048]{1,0:T(8,128)(2,1)} %pad_maximum_fusion.1.att_ref, bf16[2048,2048]{1,0:T(8,128)(2,1)} %bitcast.104, bf16[1024,2048]{1,0:T(8,128)(2,1)} %copy-done.2), custom_call_target="tpu_custom_call" | custom-call | flops 8589934592 | bytes 29360128 | tf_op jit(solution)/shard_map/hidden/pallas_call | solution.py:234
  278.8 24.1 %mlp_up.1 = (f32[1024,2048]{1,0:T(8,128)}, f32[1024,2048]{1,0:T(8,128)}, bf16[1024,2048]{1,0:T(8,128)(2,1)}) custom-call(bf16[1024,2048]{1,0:T(8,128)(2,1)} %get-tuple-element.77.rows_ref.left_ref, bf16[3,2048,2048]{2,1,0:T(8,128)(2,1)} %all-gather.8.cloned.1.call-done.gate_ref.up_ref.down_ref.refs_3_.refs_4_.refs_9_.refs_10_, ...), custom_call_target="tpu_custom_call" | custom-call | flops 17179869184 | bytes 41943040 | tf_op jit(solution)/shard_map/mlp_up/pallas_call | solution.py:267
  308.8 11.3 %fusion.9 = bf16[1024,2048]{1,0:T(8,128)(2,1)S(1)} fusion(bf16[1024,2048]{1,0:T(8,128)(2,1)S(1)} %copy-done.25, bf16[3,2048,2048]{2,1,0:T(8,128)(2,1)} %all-gather.8.cloned.1.call-done.gate_ref.up_ref.down_ref.refs_3_.refs_4_.refs_9_.refs_10_), kind=kOutput, calls=%fused_computation.17 | convolution fusion | flops 8592031744 | bytes 16777216 | tf_op jit(solution)/shard_map/dot_general | solution.py:19
  321.9 19.4 %mlp_down_back.1 = (bf16[1024,2048]{1,0:T(8,128)(2,1)}, bf16[1024,2048]{1,0:T(8,128)(2,1)}) custom-call(bf16[1024,2048]{1,0:T(8,128)(2,1)} %pad_maximum_fusion.2.grad_ref, bf16[3,2048,2048]{2,1,0:T(8,128)(2,1)} %all-gather.8.cloned.1.call-done.gate_ref.up_ref.down_ref.refs_3_.refs_4_.refs_9_.refs_10_, f32[1024,2048]{1,0:T(8,128)} %get-tuple-element.87.gate_in, ...), custom_call_target="tpu_custom_call" | custom-call | flops 8589934592 | bytes 37748736 | tf_op jit(solution)/shard_map/mlp_down_back/pallas_call | solution.py:305
  341.3 13.8 %two_grad.2 = bf16[1,256,2048]{2,1,0:T(8,128)(2,1)} custom-call(s32[1]{0:T(128)} %bitcast.23.order_ref, bf16[1024,2048]{1,0:T(8,128)(2,1)} %get-tuple-element.89.refs_0_.refs_3_.refs_6_.dgate_ref, bf16[1024,2048]{1,0:T(8,128)(2,1)} %get-tuple-element.91.refs_1_.refs_4_.refs_7_.dup_ref, f32[1024,2048]{1,0:T(8,128)} %get-tuple-element.71.refs_2_.refs_5_.refs_8_, ...), custom_call_target="tpu_custom_call" | custom-call | flops 4294967296 | bytes 16777216 | tf_op jit(solution)/shard_map/two_grad/pallas_call | solution.py:360
  355.2 4.6 collective-permute-done.21
  363.2 26.2 %two_grad.3 = bf16[3,256,2048]{2,1,0:T(8,128)(2,1)} custom-call(s32[3]{0:T(128)} %pad_add_fusion.order_ref, bf16[1024,2048]{1,0:T(8,128)(2,1)} %get-tuple-element.89.refs_0_.refs_3_.refs_6_.dgate_ref, bf16[1024,2048]{1,0:T(8,128)(2,1)} %get-tuple-element.91.refs_1_.refs_4_.refs_7_.dup_ref, f32[1024,2048]{1,0:T(8,128)} %get-tuple-element.71.refs_2_.refs_5_.refs_8_, ...), custom_call_target="tpu_custom_call" | custom-call | flops 12884901888 | bytes 16777216 | tf_op jit(solution)/shard_map/two_grad/pallas_call | solution.py:360
  394.5 38.8 %mlp_grads.1 = bf16[3,2048,2048]{2,1,0:T(8,128)(2,1)} custom-call(bf16[1024,2048]{1,0:T(8,128)(2,1)} %get-tuple-element.77.rows_ref.left_ref, bf16[1024,2048]{1,0:T(8,128)(2,1)} %get-tuple-element.81.act_ref, bf16[1024,2048]{1,0:T(8,128)(2,1)} %get-tuple-element.89.refs_0_.refs_3_.refs_6_.dgate_ref, ...), custom_call_target="tpu_custom_call" | custom-call | flops 25769803776 | bytes 46137344 | tf_op jit(solution)/shard_map/mlp_grads/pallas_call | solution.py:489
  433.3 16.5 %collective-permute-done.24 = bf16[256,2048]{1,0:T(8,128)(2,1)} collective-permute-done((bf16[256,2048]{1,0:T(8,128)(2,1)}, bf16[256,2048]{1,0:T(8,128)(2,1)}, u32[]{:S(2)}, u32[]{:S(2)}) %collective-permute-start.24) | collective-permute-done | bytes 1048608 | tf_op jit(solution)/shard_map/ppermute | solution.py:546
  457.7 3.7 collective-permute-start.25
  461.4 20.1 %collective-permute-done.28 = bf16[256,2048]{1,0:T(8,128)(2,1)S(1)} collective-permute-done((bf16[256,2048]{1,0:T(8,128)(2,1)S(1)}, bf16[256,2048]{1,0:T(8,128)(2,1)S(1)}, u32[]{:S(2)}, u32[]{:S(2)}) %collective-permute-start.28) | collective-permute-done | bytes 1048608 | tf_op jit(solution)/shard_map/ppermute | solution.py:517
  481.5 4.2 collective-permute-start.29
  487.6 18.8 %collective-permute-done.29 = bf16[256,2048]{1,0:T(8,128)(2,1)} collective-permute-done((bf16[256,2048]{1,0:T(8,128)(2,1)S(1)}, bf16[256,2048]{1,0:T(8,128)(2,1)}, u32[]{:S(2)}, u32[]{:S(2)}) %collective-permute-start.29) | collective-permute-done | bytes 1048608 | tf_op jit(solution)/shard_map/ppermute | solution.py:517
  508.0 3.6 collective-permute-done.26
  515.4 19.6 %collective-permute-done.27 = bf16[256,2048]{1,0:T(8,128)(2,1)} collective-permute-done((bf16[256,2048]{1,0:T(8,128)(2,1)}, bf16[256,2048]{1,0:T(8,128)(2,1)}, u32[]{:S(2)}, u32[]{:S(2)}) %collective-permute-start.27) | collective-permute-done | bytes 1048608 | tf_op jit(solution)/shard_map/ppermute | solution.py:517
  542.9 7.7 %fusion.34.grad_ref = bf16[1024,512]{1,0:T(8,128)(2,1)} fusion(bf16[2048,2048]{1,0:T(8,128)(2,1)} %bitcast.105, s32[]{:T(128)S(6)} %select_n.423, bf16[256,2048]{1,0:T(8,128)(2,1)S(1)} %get-tuple-element.142, bf16[256,2048]{1,0:T(8,128)(2,1)S(1)} %get-tuple-element.141, bf16[256,2048]{1,0:T(8,128)(2,1)S(1)} %get-tuple-element.140, ...), kind=kOutput, calls=%fused_computation.52 | convolution fusion | flops 2164785152 | bytes 7340036 | tf_op jit(solution)/shard_map/dot_general | solution.py:23
  550.6 21.8 %attend_back.1.grad_ref.qkv_ref = bf16[1024,1536]{1,0:T(8,128)(2,1)} custom-call(bf16[1024,1536]{1,0:T(8,128)(2,1)} %qkv.1.q_ref.k_ref.v_ref, bf16[1024,1536]{1,0:T(8,128)(2,1)} %qkv.1.q_ref.k_ref.v_ref, bf16[1024,1536]{1,0:T(8,128)(2,1)} %qkv.1.q_ref.k_ref.v_ref, bf16[1024,512]{1,0:T(8,128)(2,1)} %fusion.34.grad_ref, s32[1024,1]{1,0:T(8,128)} %copy.43.column_ref, ...), custom_call_target="tpu_custom_call" | custom-call | flops 5368709120 | bytes 7340032 | tf_op jit(solution)/shard_map/attend_back/pallas_call | solution.py:201
  572.5 12.4 %collective-permute-done.31 = bf16[1024,512]{1,0:T(8,128)(2,1)S(1)} collective-permute-done((bf16[1024,512]{1,0:T(8,128)(2,1)S(1)}, bf16[1024,512]{1,0:T(8,128)(2,1)S(1)}, u32[]{:S(2)}, u32[]{:S(2)}) %collective-permute-start.31) | collective-permute-done | bytes 1048608 | tf_op jit(solution)/shard_map/ppermute | solution.py:546
  585.7 16.1 %one_grad.1 = bf16[4,1024,512]{2,1,0:T(8,128)(2,1)} custom-call(s32[4]{0:T(128)} %pad_add_fusion.1.place_ref, bf16[1024,1536]{1,0:T(8,128)(2,1)} %attend_back.1.grad_ref.qkv_ref, bf16[2048,1536]{1,0:T(8,128)(2,1)} %all-gather.4.cloned.1.call-done.weight_ref, bf16[1024,2048]{1,0:T(8,128)(2,1)} %copy-done.2), custom_call_target="tpu_custom_call" | custom-call | flops 6442450944 | bytes 15728640 | tf_op jit(solution)/shard_map/one_grad/pallas_call | solution.py:396
  601.8 17.4 %att_grads.1 = bf16[8,256,2048]{2,1,0:T(8,128)(2,1)} custom-call(bf16[1024,2048]{1,0:T(8,128)(2,1)} %fusion.3.rows_ref.normed_ref, bf16[1024,1536]{1,0:T(8,128)(2,1)} %attend_back.1.grad_ref.qkv_ref, bf16[1024,512]{1,0:T(8,128)(2,1)} %attend.1.att_ref, bf16[1024,2048]{1,0:T(8,128)(2,1)} %pad_maximum_fusion.3.hidden_ref), custom_call_target="tpu_custom_call" | custom-call | flops 10737418240 | bytes 19922944 | tf_op jit(solution)/shard_map/att_grads/pallas_call | solution.py:453
  619.2 3.7 slice_bitcast_fusion.9
  626.1 4.4 fusion.40
  630.5 9.5 %all-to-all-start.2 = ((bf16[8,128,512]{2,1,0:T(8,128)(2,1)}), bf16[8,128,512]{2,1,0:T(8,128)(2,1)S(1)}, u32[]{:S(2)}, u32[]{:S(2)}) async-start(bf16[8,128,512]{2,1,0:T(8,128)(2,1)} %bitcast.89), calls=%async_computation.2 | async-start | bytes 2097152 | tf_op jit(solution)/shard_map/all_to_all | solution.py:615
  640.0 29.8 %collective-permute-done.33 = bf16[1024,512]{1,0:T(8,128)(2,1)} collective-permute-done((bf16[1024,512]{1,0:T(8,128)(2,1)}, bf16[1024,512]{1,0:T(8,128)(2,1)}, u32[]{:S(2)}, u32[]{:S(2)}) %collective-permute-start.33) | collective-permute-done | bytes 1048608 | tf_op jit(solution)/shard_map/ppermute | solution.py:546
  669.8 42.6 %collective-permute-done.35 = bf16[1024,512]{1,0:T(8,128)(2,1)} collective-permute-done((bf16[1024,512]{1,0:T(8,128)(2,1)}, bf16[1024,512]{1,0:T(8,128)(2,1)}, u32[]{:S(2)}, u32[]{:S(2)}) %collective-permute-start.35) | collective-permute-done | bytes 1048608 | tf_op jit(solution)/shard_map/ppermute | solution.py:546
  715.4 5.0 fusion.41
  720.4 9.3 %all-to-all-start.3 = ((bf16[8,128,512]{2,1,0:T(8,128)(2,1)}), bf16[8,128,512]{2,1,0:T(8,128)(2,1)S(1)}, u32[]{:S(2)}, u32[]{:S(2)}) async-start(bf16[8,128,512]{2,1,0:T(8,128)(2,1)} %bitcast.38), calls=%async_computation.3 | async-start | bytes 2097152 | tf_op jit(solution)/shard_map/all_to_all | solution.py:615
  731.8 13.3 %all-to-all-done.3 = bf16[8,128,512]{2,1,0:T(8,128)(2,1)S(1)} async-done(((bf16[8,128,512]{2,1,0:T(8,128)(2,1)}), bf16[8,128,512]{2,1,0:T(8,128)(2,1)S(1)}, u32[]{:S(2)}, u32[]{:S(2)}) %all-to-all-start.3) | async-done | bytes 1048608 | tf_op jit(solution)/shard_map/all_to_all | solution.py:615
  (175 shorter events, 132.6 us)
Async XLA Ops:
  7.2 139.1 %all-gather.4.cloned.1.call-start = ((), (), s32[]{:S(2)}) async-start(), calls=%async_computation.6 | async-start | bytes 7077888 | tf_op jit(solution)/shard_map/all_gather | solution.py:627
  15.6 30.3 %all-to-all-start = ((bf16[8,128,640]{2,1,0:T(8,128)(2,1)}), bf16[8,128,640]{2,1,0:T(8,128)(2,1)S(1)}, u32[]{:S(2)}, u32[]{:S(2)}) async-start(bf16[8,128,640]{2,1,0:T(8,128)(2,1)} %bitcast), calls=%async_computation | async-start | bytes 2621440 | tf_op jit(solution)/shard_map/all_to_all | solution.py:615
  19.3 238.8 %all-gather.6.cloned.1.call-start = ((), (), s32[]{:S(2)}) async-start(), calls=%async_computation.7 | async-start | bytes 9437184 | tf_op jit(solution)/shard_map/all_gather | solution.py:644
  19.4 27.2 %collective-permute-start.1 = (bf16[64,2048]{1,0:T(8,128)(2,1)}, bf16[64,2048]{1,0:T(8,128)(2,1)}, u32[]{:S(2)}, u32[]{:S(2)}) collective-permute-start(bf16[64,2048]{1,0:T(8,128)(2,1)} %param.17), channel_id=1, source_target_pairs={{0,2},{1,3},{2,0},{3,1},{4,6},{5,7},{6,4},{7,5},{8,10},{9,11},{10,... | collective-permute-start | bytes 786440 | tf_op jit(solution)/shard_map/ppermute | solution.py:546
  19.8 26.8 %collective-permute-start = (bf16[64,2048]{1,0:T(8,128)(2,1)}, bf16[64,2048]{1,0:T(8,128)(2,1)}, u32[]{:S(2)}, u32[]{:S(2)}) collective-permute-start(bf16[64,2048]{1,0:T(8,128)(2,1)} %param.17), channel_id=1, source_target_pairs={{0,1},{1,2},{2,3},{3,0},{4,5},{5,6},{6,7},{7,4},{8,9},{9,10},{10,1... | collective-permute-start | bytes 786440 | tf_op jit(solution)/shard_map/ppermute | solution.py:546
  21.4 25.3 %collective-permute-start.2 = (bf16[64,2048]{1,0:T(8,128)(2,1)}, bf16[64,2048]{1,0:T(8,128)(2,1)}, u32[]{:S(2)}, u32[]{:S(2)}) collective-permute-start(bf16[64,2048]{1,0:T(8,128)(2,1)} %param.17), channel_id=1, source_target_pairs={{0,3},{1,0},{2,1},{3,2},{4,7},{5,4},{6,5},{7,6},{8,11},{9,8},{10,9... | collective-permute-start | bytes 786440 | tf_op jit(solution)/shard_map/ppermute | solution.py:546
  49.2 229.7 %all-gather.8.cloned.1.call-start = ((), (), s32[]{:S(2)}) async-start(), calls=%async_computation.8 | async-start | bytes 28311552 | tf_op jit(solution)/shard_map/all_gather | solution.py:645
  52.8 63.9 %copy-start.18 = (s32[1024,1]{0,1:T(1,128)}, s32[1024,1]{0,1:T(1,128)S(1)}, u32[]{:S(2)}) copy-start(s32[1024,1]{0,1:T(1,128)S(1)} %fusion.52) | copy-start | bytes 12292
  52.8 36.3 %copy-start.20 = (s32[8,4]{0,1:T(4,128)S(1)}, s32[8,4]{0,1:T(4,128)}, u32[]{:S(2)}) copy-start(s32[8,4]{0,1:T(4,128)} %param.21) | copy-start | bytes 388
  54.1 26.8 %collective-permute-start.6 = (bf16[1024,512]{1,0:T(8,128)(2,1)S(1)}, bf16[1024,512]{1,0:T(8,128)(2,1)S(1)}, u32[]{:S(2)}, u32[]{:S(2)}) collective-permute-start(bf16[1024,512]{1,0:T(8,128)(2,1)S(1)} %fusion.38), channel_id=1, source_target_pairs={{3,2},{2,1},{1,0},{7,6},{6,5},{5,4},{11,10},{10,9},{9,8},{15,14},{... | collective-permute-start | bytes 3145736 | tf_op jit(solution)/shard_map/ppermute | solution.py:517
  56.5 27.6 %collective-permute-start.3 = (bf16[1024,512]{1,0:T(8,128)(2,1)S(1)}, bf16[1024,512]{1,0:T(8,128)(2,1)S(1)}, u32[]{:S(2)}, u32[]{:S(2)}) collective-permute-start(bf16[1024,512]{1,0:T(8,128)(2,1)S(1)} %fusion.38), channel_id=1, source_target_pairs={{0,1},{1,2},{2,3},{4,5},{5,6},{6,7},{8,9},{9,10},{10,11},{12,13},{... | collective-permute-start | bytes 3145736 | tf_op jit(solution)/shard_map/ppermute | solution.py:517
  80.9 23.5 %collective-permute-start.7 = (bf16[1024,512]{1,0:T(8,128)(2,1)S(1)}, bf16[1024,512]{1,0:T(8,128)(2,1)}, u32[]{:S(2)}, u32[]{:S(2)}) collective-permute-start(bf16[1024,512]{1,0:T(8,128)(2,1)S(1)} %collective-permute-done.6), channel_id=1, source_target_pairs={{2,1},{1,0},{6,5},{5,4},{10,9},{9,8},{14,13},{13,12},{18,17},{17,1... | collective-permute-start | bytes 3145736 | tf_op jit(solution)/shard_map/ppermute | solution.py:517
  84.1 25.6 %collective-permute-start.4 = (bf16[1024,512]{1,0:T(8,128)(2,1)S(1)}, bf16[1024,512]{1,0:T(8,128)(2,1)}, u32[]{:S(2)}, u32[]{:S(2)}) collective-permute-start(bf16[1024,512]{1,0:T(8,128)(2,1)S(1)} %collective-permute-done.3), channel_id=1, source_target_pairs={{1,2},{2,3},{5,6},{6,7},{9,10},{10,11},{13,14},{14,15},{17,18},{18... | collective-permute-start | bytes 3145736 | tf_op jit(solution)/shard_map/ppermute | solution.py:517
  89.3 27.4 %all-to-all-start.1 = ((bf16[8,128,512]{2,1,0:T(8,128)(2,1)}), bf16[8,128,512]{2,1,0:T(8,128)(2,1)}, u32[]{:S(2)}, u32[]{:S(2)}) async-start(bf16[8,128,512]{2,1,0:T(8,128)(2,1)} %bitcast.87), calls=%async_computation.1 | async-start | bytes 2097152 | tf_op jit(solution)/shard_map/all_to_all | solution.py:615
  93.6 525.6 %reduce-scatter.3.cloned.1.call-start = ((), (), s32[]{:S(2)}) async-start(), calls=%async_computation.9 | async-start | bytes 28311552 | tf_op jit(solution)/shard_map/reduce_scatter | solution.py:695
  104.4 15.1 %collective-permute-start.8 = (bf16[1024,512]{1,0:T(8,128)(2,1)}, bf16[1024,512]{1,0:T(8,128)(2,1)}, u32[]{:S(2)}, u32[]{:S(2)}) collective-permute-start(bf16[1024,512]{1,0:T(8,128)(2,1)} %collective-permute-done.7), channel_id=1, source_target_pairs={{1,0},{5,4},{9,8},{13,12},{17,16},{21,20},{25,24},{29,28}} | collective-permute-start | bytes 3145736 | tf_op jit(solution)/shard_map/ppermute | solution.py:517
  109.6 23.2 %collective-permute-start.5 = (bf16[1024,512]{1,0:T(8,128)(2,1)}, bf16[1024,512]{1,0:T(8,128)(2,1)}, u32[]{:S(2)}, u32[]{:S(2)}) collective-permute-start(bf16[1024,512]{1,0:T(8,128)(2,1)} %collective-permute-done.4), channel_id=1, source_target_pairs={{2,3},{6,7},{10,11},{14,15},{18,19},{22,23},{26,27},{30,31}} | collective-permute-start | bytes 3145736 | tf_op jit(solution)/shard_map/ppermute | solution.py:517
  135.2 41.1 %collective-permute-start.10 = (bf16[1024,512]{1,0:T(8,128)(2,1)S(1)}, bf16[1024,512]{1,0:T(8,128)(2,1)S(1)}, u32[]{:S(2)}, u32[]{:S(2)}) collective-permute-start(bf16[1024,512]{1,0:T(8,128)(2,1)S(1)} %fusion.39), channel_id=1, source_target_pairs={{3,2},{2,1},{1,0},{7,6},{6,5},{5,4},{11,10},{10,9},{9,8},{15,14},{... | collective-permute-start | bytes 3145736 | tf_op jit(solution)/shard_map/ppermute | solution.py:517
  137.2 39.1 %collective-permute-start.9 = (bf16[1024,512]{1,0:T(8,128)(2,1)S(1)}, bf16[1024,512]{1,0:T(8,128)(2,1)}, u32[]{:S(2)}, u32[]{:S(2)}) collective-permute-start(bf16[1024,512]{1,0:T(8,128)(2,1)S(1)} %fusion.39), channel_id=1, source_target_pairs={{0,1},{1,2},{2,3},{4,5},{5,6},{6,7},{8,9},{9,10},{10,11},{12,13},{... | collective-permute-start | bytes 3145736 | tf_op jit(solution)/shard_map/ppermute | solution.py:517
  176.3 23.2 %collective-permute-start.14 = (bf16[1024,512]{1,0:T(8,128)(2,1)}, bf16[1024,512]{1,0:T(8,128)(2,1)S(1)}, u32[]{:S(2)}, u32[]{:S(2)}) collective-permute-start(bf16[1024,512]{1,0:T(8,128)(2,1)} %attend.1.att_ref), channel_id=1, source_target_pairs={{3,2},{2,1},{1,0},{7,6},{6,5},{5,4},{11,10},{10,9},{9,8},{15,14},{... | collective-permute-start | bytes 3145736 | tf_op jit(solution)/shard_map/ppermute | solution.py:517
  178.2 23.6 %collective-permute-start.11 = (bf16[1024,512]{1,0:T(8,128)(2,1)}, bf16[1024,512]{1,0:T(8,128)(2,1)S(1)}, u32[]{:S(2)}, u32[]{:S(2)}) collective-permute-start(bf16[1024,512]{1,0:T(8,128)(2,1)} %attend.1.att_ref), channel_id=1, source_target_pairs={{0,1},{1,2},{2,3},{4,5},{5,6},{6,7},{8,9},{9,10},{10,11},{12,13},{... | collective-permute-start | bytes 3145736 | tf_op jit(solution)/shard_map/ppermute | solution.py:517
  199.5 20.3 %collective-permute-start.15 = (bf16[1024,512]{1,0:T(8,128)(2,1)S(1)}, bf16[1024,512]{1,0:T(8,128)(2,1)S(1)}, u32[]{:S(2)}, u32[]{:S(2)}) collective-permute-start(bf16[1024,512]{1,0:T(8,128)(2,1)S(1)} %collective-permute-done.14), channel_id=1, source_target_pairs={{2,1},{1,0},{6,5},{5,4},{10,9},{9,8},{14,13},{13,12},{18,17},{17,1... | collective-permute-start | bytes 3145736 | tf_op jit(solution)/shard_map/ppermute | solution.py:517
  201.8 22.7 %collective-permute-start.12 = (bf16[1024,512]{1,0:T(8,128)(2,1)S(1)}, bf16[1024,512]{1,0:T(8,128)(2,1)S(1)}, u32[]{:S(2)}, u32[]{:S(2)}) collective-permute-start(bf16[1024,512]{1,0:T(8,128)(2,1)S(1)} %collective-permute-done.11), channel_id=1, source_target_pairs={{1,2},{2,3},{5,6},{6,7},{9,10},{10,11},{13,14},{14,15},{17,18},{18... | collective-permute-start | bytes 3145736 | tf_op jit(solution)/shard_map/ppermute | solution.py:517
  219.8 9.1 %collective-permute-start.16 = (bf16[1024,512]{1,0:T(8,128)(2,1)S(1)}, bf16[1024,512]{1,0:T(8,128)(2,1)S(1)}, u32[]{:S(2)}, u32[]{:S(2)}) collective-permute-start(bf16[1024,512]{1,0:T(8,128)(2,1)S(1)} %collective-permute-done.15), channel_id=1, source_target_pairs={{1,0},{5,4},{9,8},{13,12},{17,16},{21,20},{25,24},{29,28}} | collective-permute-start | bytes 3145736 | tf_op jit(solution)/shard_map/ppermute | solution.py:517
  224.5 21.2 %collective-permute-start.13 = (bf16[1024,512]{1,0:T(8,128)(2,1)S(1)}, bf16[1024,512]{1,0:T(8,128)(2,1)S(1)}, u32[]{:S(2)}, u32[]{:S(2)}) collective-permute-start(bf16[1024,512]{1,0:T(8,128)(2,1)S(1)} %collective-permute-done.12), channel_id=1, source_target_pairs={{2,3},{6,7},{10,11},{14,15},{18,19},{22,23},{26,27},{30,31}} | collective-permute-start | bytes 3145736 | tf_op jit(solution)/shard_map/ppermute | solution.py:517
  249.6 25.3 %collective-permute-start.17 = (bf16[1024,512]{1,0:T(8,128)(2,1)}, bf16[1024,512]{1,0:T(8,128)(2,1)}, u32[]{:S(2)}, u32[]{:S(2)}) collective-permute-start(bf16[1024,512]{1,0:T(8,128)(2,1)} %collective-permute-done.9), channel_id=1, source_target_pairs={{1,2},{2,3},{5,6},{6,7},{9,10},{10,11},{13,14},{14,15},{17,18},{18... | collective-permute-start | bytes 3145736 | tf_op jit(solution)/shard_map/ppermute | solution.py:517
  254.0 20.9 %collective-permute-start.18 = (bf16[1024,512]{1,0:T(8,128)(2,1)S(1)}, bf16[1024,512]{1,0:T(8,128)(2,1)}, u32[]{:S(2)}, u32[]{:S(2)}) collective-permute-start(bf16[1024,512]{1,0:T(8,128)(2,1)S(1)} %collective-permute-done.10), channel_id=1, source_target_pairs={{2,1},{1,0},{6,5},{5,4},{10,9},{9,8},{14,13},{13,12},{18,17},{17,1... | collective-permute-start | bytes 3145736 | tf_op jit(solution)/shard_map/ppermute | solution.py:517
  274.9 28.1 %collective-permute-start.19 = (bf16[1024,512]{1,0:T(8,128)(2,1)}, bf16[1024,512]{1,0:T(8,128)(2,1)}, u32[]{:S(2)}, u32[]{:S(2)}) collective-permute-start(bf16[1024,512]{1,0:T(8,128)(2,1)} %collective-permute-done.17), channel_id=1, source_target_pairs={{2,3},{6,7},{10,11},{14,15},{18,19},{22,23},{26,27},{30,31}} | collective-permute-start | bytes 3145736 | tf_op jit(solution)/shard_map/ppermute | solution.py:517
  277.2 25.8 %collective-permute-start.20 = (bf16[1024,512]{1,0:T(8,128)(2,1)}, bf16[1024,512]{1,0:T(8,128)(2,1)}, u32[]{:S(2)}, u32[]{:S(2)}) collective-permute-start(bf16[1024,512]{1,0:T(8,128)(2,1)} %collective-permute-done.18), channel_id=1, source_target_pairs={{1,0},{5,4},{9,8},{13,12},{17,16},{21,20},{25,24},{29,28}} | collective-permute-start | bytes 3145736 | tf_op jit(solution)/shard_map/ppermute | solution.py:517
  321.9 37.9 %collective-permute-start.21 = (bf16[1024,512]{1,0:T(8,128)(2,1)S(1)}, bf16[1024,512]{1,0:T(8,128)(2,1)S(1)}, u32[]{:S(2)}, u32[]{:S(2)}) collective-permute-start(bf16[1024,512]{1,0:T(8,128)(2,1)S(1)} %get-tuple-element.82), channel_id=1, source_target_pairs={{0,2},{1,3},{2,0},{3,1},{4,6},{5,7},{6,4},{7,5},{8,10},{9,11},{10,... | collective-permute-start | bytes 3145736 | tf_op jit(solution)/shard_map/ppermute | solution.py:546
  359.8 73.5 %collective-permute-start.22 = (bf16[256,2048]{1,0:T(8,128)(2,1)}, bf16[256,2048]{1,0:T(8,128)(2,1)S(1)}, u32[]{:S(2)}, u32[]{:S(2)}) collective-permute-start(bf16[256,2048]{1,0:T(8,128)(2,1)} %bitcast.86), channel_id=1, source_target_pairs={{0,2},{1,3},{2,0},{3,1},{4,6},{5,7},{6,4},{7,5},{8,10},{9,11},{10,... | collective-permute-start | bytes 3145736 | tf_op jit(solution)/shard_map/ppermute | solution.py:546
  392.4 57.4 %collective-permute-start.24 = (bf16[256,2048]{1,0:T(8,128)(2,1)}, bf16[256,2048]{1,0:T(8,128)(2,1)}, u32[]{:S(2)}, u32[]{:S(2)}) collective-permute-start(bf16[256,2048]{1,0:T(8,128)(2,1)} %get-tuple-element.143), channel_id=1, source_target_pairs={{0,3},{1,0},{2,1},{3,2},{4,7},{5,4},{6,5},{7,6},{8,11},{9,8},{10,9... | collective-permute-start | bytes 3145736 | tf_op jit(solution)/shard_map/ppermute | solution.py:546
  392.8 59.2 %collective-permute-start.23 = (bf16[256,2048]{1,0:T(8,128)(2,1)}, bf16[256,2048]{1,0:T(8,128)(2,1)}, u32[]{:S(2)}, u32[]{:S(2)}) collective-permute-start(bf16[256,2048]{1,0:T(8,128)(2,1)} %get-tuple-element.144), channel_id=1, source_target_pairs={{0,1},{1,2},{2,3},{3,0},{4,5},{5,6},{6,7},{7,4},{8,9},{9,10},{10,1... | collective-permute-start | bytes 3145736 | tf_op jit(solution)/shard_map/ppermute | solution.py:546
  452.0 298.9 %reduce-scatter.5.cloned.1.call-start = ((), (), s32[]{:S(2)}) async-start(), calls=%async_computation.10 | async-start | bytes 9437184 | tf_op jit(solution)/shard_map/reduce_scatter | solution.py:723
  455.5 26.0 %collective-permute-start.28 = (bf16[256,2048]{1,0:T(8,128)(2,1)S(1)}, bf16[256,2048]{1,0:T(8,128)(2,1)S(1)}, u32[]{:S(2)}, u32[]{:S(2)}) collective-permute-start(bf16[256,2048]{1,0:T(8,128)(2,1)S(1)} %fusion.22), channel_id=1, source_target_pairs={{3,2},{2,1},{1,0},{7,6},{6,5},{5,4},{11,10},{10,9},{9,8},{15,14},{... | collective-permute-start | bytes 3145736 | tf_op jit(solution)/shard_map/ppermute | solution.py:517
  457.7 28.0 %collective-permute-start.25 = (bf16[256,2048]{1,0:T(8,128)(2,1)S(1)}, bf16[256,2048]{1,0:T(8,128)(2,1)S(1)}, u32[]{:S(2)}, u32[]{:S(2)}) collective-permute-start(bf16[256,2048]{1,0:T(8,128)(2,1)S(1)} %fusion.22), channel_id=1, source_target_pairs={{0,1},{1,2},{2,3},{4,5},{5,6},{6,7},{8,9},{9,10},{10,11},{12,13},{... | collective-permute-start | bytes 3145736 | tf_op jit(solution)/shard_map/ppermute | solution.py:517
  481.5 24.9 %collective-permute-start.29 = (bf16[256,2048]{1,0:T(8,128)(2,1)S(1)}, bf16[256,2048]{1,0:T(8,128)(2,1)}, u32[]{:S(2)}, u32[]{:S(2)}) collective-permute-start(bf16[256,2048]{1,0:T(8,128)(2,1)S(1)} %collective-permute-done.28), channel_id=1, source_target_pairs={{2,1},{1,0},{6,5},{5,4},{10,9},{9,8},{14,13},{13,12},{18,17},{17,1... | collective-permute-start | bytes 3145736 | tf_op jit(solution)/shard_map/ppermute | solution.py:517
  485.7 25.9 %collective-permute-start.26 = (bf16[256,2048]{1,0:T(8,128)(2,1)S(1)}, bf16[256,2048]{1,0:T(8,128)(2,1)}, u32[]{:S(2)}, u32[]{:S(2)}) collective-permute-start(bf16[256,2048]{1,0:T(8,128)(2,1)S(1)} %collective-permute-done.25), channel_id=1, source_target_pairs={{1,2},{2,3},{5,6},{6,7},{9,10},{10,11},{13,14},{14,15},{17,18},{18... | collective-permute-start | bytes 3145736 | tf_op jit(solution)/shard_map/ppermute | solution.py:517
  506.4 9.0 %collective-permute-start.30 = (bf16[256,2048]{1,0:T(8,128)(2,1)}, bf16[256,2048]{1,0:T(8,128)(2,1)}, u32[]{:S(2)}, u32[]{:S(2)}) collective-permute-start(bf16[256,2048]{1,0:T(8,128)(2,1)} %collective-permute-done.29), channel_id=1, source_target_pairs={{1,0},{5,4},{9,8},{13,12},{17,16},{21,20},{25,24},{29,28}} | collective-permute-start | bytes 3145736 | tf_op jit(solution)/shard_map/ppermute | solution.py:517
  511.7 23.3 %collective-permute-start.27 = (bf16[256,2048]{1,0:T(8,128)(2,1)}, bf16[256,2048]{1,0:T(8,128)(2,1)}, u32[]{:S(2)}, u32[]{:S(2)}) collective-permute-start(bf16[256,2048]{1,0:T(8,128)(2,1)} %collective-permute-done.26), channel_id=1, source_target_pairs={{2,3},{6,7},{10,11},{14,15},{18,19},{22,23},{26,27},{30,31}} | collective-permute-start | bytes 3145736 | tf_op jit(solution)/shard_map/ppermute | solution.py:517
  539.8 45.0 %collective-permute-start.31 = (bf16[1024,512]{1,0:T(8,128)(2,1)S(1)}, bf16[1024,512]{1,0:T(8,128)(2,1)S(1)}, u32[]{:S(2)}, u32[]{:S(2)}) collective-permute-start(bf16[1024,512]{1,0:T(8,128)(2,1)S(1)} %copy-done.5), channel_id=1, source_target_pairs={{0,1},{1,2},{2,3},{3,0},{4,5},{5,6},{6,7},{7,4},{8,9},{9,10},{10,1... | collective-permute-start | bytes 3145736 | tf_op jit(solution)/shard_map/ppermute | solution.py:546
  542.9 42.8 %collective-permute-start.32 = (bf16[1024,512]{1,0:T(8,128)(2,1)S(1)}, bf16[1024,512]{1,0:T(8,128)(2,1)}, u32[]{:S(2)}, u32[]{:S(2)}) collective-permute-start(bf16[1024,512]{1,0:T(8,128)(2,1)S(1)} %copy-done.4), channel_id=1, source_target_pairs={{0,3},{1,0},{2,1},{3,2},{4,7},{5,4},{6,5},{7,6},{8,11},{9,8},{10,9... | collective-permute-start | bytes 3145736 | tf_op jit(solution)/shard_map/ppermute | solution.py:546
  622.9 46.9 %collective-permute-start.33 = (bf16[1024,512]{1,0:T(8,128)(2,1)}, bf16[1024,512]{1,0:T(8,128)(2,1)}, u32[]{:S(2)}, u32[]{:S(2)}) collective-permute-start(bf16[1024,512]{1,0:T(8,128)(2,1)} %get-tuple-element.132), channel_id=1, source_target_pairs={{0,2},{1,3},{2,0},{3,1},{4,6},{5,7},{6,4},{7,5},{8,10},{9,11},{10,... | collective-permute-start | bytes 3145736 | tf_op jit(solution)/shard_map/ppermute | solution.py:546
  623.4 89.0 %collective-permute-start.35 = (bf16[1024,512]{1,0:T(8,128)(2,1)}, bf16[1024,512]{1,0:T(8,128)(2,1)}, u32[]{:S(2)}, u32[]{:S(2)}) collective-permute-start(bf16[1024,512]{1,0:T(8,128)(2,1)} %get-tuple-element.133), channel_id=1, source_target_pairs={{0,3},{1,0},{2,1},{3,2},{4,7},{5,4},{6,5},{7,6},{8,11},{9,8},{10,9... | collective-permute-start | bytes 3145736 | tf_op jit(solution)/shard_map/ppermute | solution.py:546
  626.0 89.4 %collective-permute-start.34 = (bf16[1024,512]{1,0:T(8,128)(2,1)}, bf16[1024,512]{1,0:T(8,128)(2,1)}, u32[]{:S(2)}, u32[]{:S(2)}) collective-permute-start(bf16[1024,512]{1,0:T(8,128)(2,1)} %get-tuple-element.134), channel_id=1, source_target_pairs={{0,1},{1,2},{2,3},{3,0},{4,5},{5,6},{6,7},{7,4},{8,9},{9,10},{10,1... | collective-permute-start | bytes 3145736 | tf_op jit(solution)/shard_map/ppermute | solution.py:546
  630.5 90.0 %all-to-all-start.2 = ((bf16[8,128,512]{2,1,0:T(8,128)(2,1)}), bf16[8,128,512]{2,1,0:T(8,128)(2,1)S(1)}, u32[]{:S(2)}, u32[]{:S(2)}) async-start(bf16[8,128,512]{2,1,0:T(8,128)(2,1)} %bitcast.89), calls=%async_computation.2 | async-start | bytes 2097152 | tf_op jit(solution)/shard_map/all_to_all | solution.py:615
  639.9 89.8 %copy-start.17 = (s32[896]{0:T(1024)S(1)}, s32[896]{0:T(1024)}, u32[]{:S(2)}) copy-start(s32[896]{0:T(1024)} %copy-done.16) | copy-start | bytes 10756
  720.4 24.7 %all-to-all-start.3 = ((bf16[8,128,512]{2,1,0:T(8,128)(2,1)}), bf16[8,128,512]{2,1,0:T(8,128)(2,1)S(1)}, u32[]{:S(2)}, u32[]{:S(2)}) async-start(bf16[8,128,512]{2,1,0:T(8,128)(2,1)} %bitcast.38), calls=%async_computation.3 | async-start | bytes 2097152 | tf_op jit(solution)/shard_map/all_to_all | solution.py:615
  (23 other events, 282.1 us)
Sparse Core Ops, SparseCore 0:
  12.0 59.3 all-gather.3
  74.0 61.2 all-gather.5
  137.2 125.3 all-gather.7
  452.2 165.4 reduce-scatter.2
  621.0 80.3 reduce-scatter.4

commit v3 on v2

v3 whole, which is shorter than its diff:
```python
import jax
import jax.numpy as jnp
from jax import lax
from jax.experimental import pallas as pl
from jax.experimental.pallas import tpu as pltpu
from jax.sharding import PartitionSpec as P

HEAD_DIM = 128
GROUP_CAP = 1024
SEQ_SLOTS = 4

norm_eps = 1e-05
rope_base = 10000.0
bf16 = jnp.bfloat16
f32 = jnp.float32


def matmul(left, right):
    return jnp.dot(left, right, preferred_element_type=f32)


def times_transposed(left, right):
    return lax.dot_general(
        left, right, (((1,), (1,)), ((), ())), preferred_element_type=f32
    )


def transposed_times(left, right):
    return lax.dot_general(
        left, right, (((0,), (0,)), ((), ())), preferred_element_type=f32
    )


def norm_parts(values_in):
    row_mean = jnp.mean(values_in, axis=-1, keepdims=True)
    centered = values_in - row_mean
    variance = jnp.mean(centered * centered, axis=-1, keepdims=True)
    inverse = lax.rsqrt(variance + norm_eps)
    return centered * inverse, inverse


def rope_tables(position, head_dim):
    half_dim = head_dim // 2
    frequency = rope_base ** (-(jnp.arange(half_dim, dtype=f32) * 2.0) / head_dim)
    angles = position.astype(f32)[:, None] * frequency[None, :]
    cosine, sine = jnp.cos(angles), jnp.sin(angles)
    return (
        jnp.concatenate([cosine, cosine], axis=1),
        jnp.concatenate([-sine, sine], axis=1),
    )


def segments(lengths):
    row_index = jnp.arange(GROUP_CAP, dtype=jnp.int32)
    slot_ids = jnp.arange(SEQ_SLOTS, dtype=jnp.int32)
    ends = jnp.sum(
        jnp.where(slot_ids[:, None] <= slot_ids[None, :], lengths[:, None], 0), axis=0
    )
    passed = row_index[:, None] >= ends[None, :]
    segment = jnp.sum(passed.astype(jnp.int32), axis=1)
    begin_row = jnp.max(jnp.where(passed, ends[None, :], 0), axis=1)
    return (segment, row_index - begin_row)


VMEM_LIMIT = 58 * 1024 * 1024
BLOCK = 256
WIDE = 512


def params():
    return pltpu.CompilerParams(vmem_limit_bytes=VMEM_LIMIT)


def cost(flops, read, transcendentals=0):
    return pl.CostEstimate(
        flops=int(flops), bytes_accessed=int(read), transcendentals=int(transcendentals)
    )


def half_turn(values_in):
    return pltpu.roll(values_in, HEAD_DIM // 2, 1)


def pick(me, owner, own, low, high):
    piece = own
    for step, (lower, higher) in enumerate(zip(low, high), start=1):
        piece = jnp.where(me == owner + step, lower, piece)
        piece = jnp.where(me == owner - step, higher, piece)
    return piece


def flat(own, arrived):
    return [own, *[low for low, _ in arrived], *[high for _, high in arrived]]


def picked(me, owner, refs):
    steps = len(refs) // 2
    blocks = [ref[...] for ref in refs]
    return pick(me, owner, blocks[0], blocks[1 : 1 + steps], blocks[1 + steps :])


def norm_kernel(me_ref, *refs):
    *come_refs, rows_ref, normed_ref = refs
    size = len(come_refs) // 2 + 1
    rows = jnp.concatenate([picked(me_ref[0], j, come_refs) for j in range(size)], axis=1)
    rows_ref[...] = rows
    normed_ref[...] = norm_parts(rows.astype(f32))[0].astype(bf16)


def gathered_norm(me, own, arrived):
    count, width = own.shape
    operands = flat(own, arrived)
    model = width * (len(operands) // 2 + 1)
    here = lambda i, me: (i, 0)
    out = jax.ShapeDtypeStruct((count, model), bf16)
    return pl.pallas_call(
        norm_kernel,
        grid_spec=pltpu.PrefetchScalarGridSpec(
            num_scalar_prefetch=1,
            grid=(count // BLOCK,),
            in_specs=[pl.BlockSpec((BLOCK, width), here)] * len(operands),
            out_specs=[pl.BlockSpec((BLOCK, model), here)] * 2,
        ),
        out_shape=[out, out],
        compiler_params=params(),
        cost_estimate=cost(20 * count * model, 8 * count * model),
        name="gathered_norm",
    )(me, *operands)


def qkv_kernel(rows_ref, wq_ref, wk_ref, wv_ref, cos_ref, sin_ref, *out_refs):
    weight = jnp.concatenate([wq_ref[...], wk_ref[...], wv_ref[...]], axis=1)
    for first in range(0, rows_ref.shape[0], BLOCK):
        rows = pl.ds(first, BLOCK)
        pre = matmul(rows_ref[rows, :], weight)
        for part in range(3):
            piece = pre[:, part * HEAD_DIM : (part + 1) * HEAD_DIM]
            if part < 2:
                piece = piece * cos_ref[rows, :] + half_turn(piece) * sin_ref[rows, :]
            out_refs[part][rows, :] = piece.astype(bf16)


def head_specs(model, heads):
    return [
        pl.BlockSpec((model, HEAD_DIM), lambda h, part=part: (0, part * heads + h))
        for part in range(3)
    ]


def project_qkv(rows, weight, cosine, sine):
    count, model = rows.shape
    columns = weight.shape[1]
    heads = columns // (3 * HEAD_DIM)
    whole = lambda h: (0, 0)
    return pl.pallas_call(
        qkv_kernel,
        grid=(heads,),
        in_specs=[
            pl.BlockSpec((count, model), whole),
            *head_specs(model, heads),
            pl.BlockSpec((count, HEAD_DIM), whole),
            pl.BlockSpec((count, HEAD_DIM), whole),
        ],
        out_specs=[pl.BlockSpec((count, HEAD_DIM), lambda h: (0, h))] * 3,
        out_shape=[jax.ShapeDtypeStruct((count, heads * HEAD_DIM), bf16)] * 3,
        compiler_params=params(),
        cost_estimate=cost(2 * count * model * columns, 2 * model * (count + columns)),
        name="qkv",
    )(rows, weight, weight, weight, cosine, sine)


def masked_softmax(q_rows, k_rows, seg_column, seg_row, row_first):
    scores = times_transposed(q_rows, k_rows) * HEAD_DIM ** (-0.5)
    row = lax.broadcasted_iota(jnp.int32, scores.shape, 0) + row_first
    column = lax.broadcasted_iota(jnp.int32, scores.shape, 1)
    allowed = (seg_column == seg_row) & (column <= row)
    scores = jnp.where(allowed, scores, -1e30)
    exponent = jnp.exp(scores - jnp.max(scores, axis=-1, keepdims=True))
    return exponent * (1.0 / jnp.sum(exponent, axis=-1, keepdims=True))


def attend_kernel(q_ref, k_ref, v_ref, column_ref, row_ref, out_ref):
    block = pl.program_id(1)
    for index in range(k_ref.shape[0] // BLOCK):

        @pl.when(block == index)
        def _(index=index):
            seen = (index + 1) * BLOCK
            prob = masked_softmax(
                q_ref[...], k_ref[:seen, :], column_ref[...], row_ref[:, :seen], index * BLOCK
            )
            out_ref[...] = matmul(prob.astype(bf16), v_ref[:seen, :]).astype(bf16)


def attend(qkv, segment):
    count = qkv[0].shape[0]
    heads = qkv[0].shape[1] // HEAD_DIM
    return pl.pallas_call(
        attend_kernel,
        grid=(heads, count // BLOCK),
        in_specs=[
            pl.BlockSpec((BLOCK, HEAD_DIM), lambda h, i: (i, h)),
            pl.BlockSpec((count, HEAD_DIM), lambda h, i: (0, h)),
            pl.BlockSpec((count, HEAD_DIM), lambda h, i: (0, h)),
            pl.BlockSpec((BLOCK, 1), lambda h, i: (i, 0)),
            pl.BlockSpec((1, count), lambda h, i: (0, 0)),
        ],
        out_specs=pl.BlockSpec((BLOCK, HEAD_DIM), lambda h, i: (i, h)),
        out_shape=jax.ShapeDtypeStruct((count, heads * HEAD_DIM), bf16),
        compiler_params=params(),
        cost_estimate=cost(
            4 * heads * count * count * HEAD_DIM, 8 * count * heads * HEAD_DIM, heads * count * count
        ),
        name="attend",
    )(*qkv, segment[:, None], segment[None, :])


def attend_back_kernel(
    q_ref, k_ref, v_ref, grad_ref, column_ref, row_ref, cos_ref, sin_ref, dq_ref, dk_ref, dv_ref, total
):
    block = pl.program_id(1)
    scale = HEAD_DIM ** (-0.5)
    blocks = k_ref.shape[0] // BLOCK

    @pl.when(block == 0)
    def _():
        total[...] = jnp.zeros_like(total)

    for index in range(blocks):

        @pl.when(block == index)
        def _(index=index):
            seen = (index + 1) * BLOCK
            q_rows, k_rows, grad = q_ref[...], k_ref[:seen, :], grad_ref[...]
            prob = masked_softmax(
                q_rows, k_rows, column_ref[...], row_ref[:, :seen], index * BLOCK
            )
            prob_grad = times_transposed(grad, v_ref[:seen, :])
            delta = jnp.sum(prob_grad * prob, axis=-1, keepdims=True)
            score_grad = (prob * (prob_grad - delta)).astype(bf16)
            total[0, index * BLOCK : seen, :] = matmul(score_grad, k_rows) * scale
            total[1, :seen, :] += transposed_times(score_grad, q_rows) * scale
            total[2, :seen, :] += transposed_times(prob.astype(bf16), grad)

    @pl.when(block == blocks - 1)
    def _():
        for part, out_ref in enumerate((dq_ref, dk_ref, dv_ref)):
            piece = total[part]
            if part < 2:
                piece = piece * cos_ref[...] - half_turn(piece) * sin_ref[...]
            out_ref[...] = piece.astype(bf16)


def attend_back(qkv, grad, segment, cosine, sine):
    count = qkv[0].shape[0]
    heads = qkv[0].shape[1] // HEAD_DIM
    return pl.pallas_call(
        attend_back_kernel,
        grid=(heads, count // BLOCK),
        in_specs=[
            pl.BlockSpec((BLOCK, HEAD_DIM), lambda h, i: (i, h)),
            pl.BlockSpec((count, HEAD_DIM), lambda h, i: (0, h)),
            pl.BlockSpec((count, HEAD_DIM), lambda h, i: (0, h)),
            pl.BlockSpec((BLOCK, HEAD_DIM), lambda h, i: (i, h)),
            pl.BlockSpec((BLOCK, 1), lambda h, i: (i, 0)),
            pl.BlockSpec((1, count), lambda h, i: (0, 0)),
            pl.BlockSpec((count, HEAD_DIM), lambda h, i: (0, 0)),
            pl.BlockSpec((count, HEAD_DIM), lambda h, i: (0, 0)),
        ],
        out_specs=[pl.BlockSpec((count, HEAD_DIM), lambda h, i: (0, h))] * 3,
        out_shape=[jax.ShapeDtypeStruct(qkv[0].shape, bf16)] * 3,
        scratch_shapes=[pltpu.VMEM((3, count, HEAD_DIM), f32)],
        compiler_params=params(),
        cost_estimate=cost(1000, 1000),
        name="attend_back",
    )(*qkv, grad, segment[:, None], segment[None, :], cosine, sine)


def hidden_kernel(me_ref, weight_ref, rows_ref, *refs):
    *come_refs, hidden_ref, normed_ref = refs
    size = len(come_refs) // 2 + 1
    attended = jnp.concatenate([picked(me_ref[0], j, come_refs) for j in range(size)], axis=1)
    hidden = rows_ref[...].astype(f32) + matmul(attended, weight_ref[...])
    hidden_ref[...] = hidden
    normed_ref[...] = norm_parts(hidden)[0].astype(bf16)


def hidden_and_norm(me, own, arrived, weight, rows):
    count, model = rows.shape
    operands = flat(own, arrived)
    here = lambda i, me: (i, 0)
    return pl.pallas_call(
        hidden_kernel,
        grid_spec=pltpu.PrefetchScalarGridSpec(
            num_scalar_prefetch=1,
            grid=(count // BLOCK,),
            in_specs=[
                pl.BlockSpec((model, model), lambda i, me: (0, 0), pipeline_mode=pl.Buffered(1)),
                pl.BlockSpec((BLOCK, model), here),
                *[pl.BlockSpec((BLOCK, own.shape[1]), here)] * len(operands),
            ],
            out_specs=[pl.BlockSpec((BLOCK, model), here)] * 2,
        ),
        out_shape=[
            jax.ShapeDtypeStruct((count, model), f32),
            jax.ShapeDtypeStruct((count, model), bf16),
        ],
        compiler_params=params(),
        cost_estimate=cost(2 * count * model * model, 2 * model * model + 10 * count * model),
        name="hidden",
    )(me, weight, rows, *operands)


def up_kernel(rows_ref, gate_ref, up_ref, gate_out, up_out, act_ref):
    for first in range(0, rows_ref.shape[0], BLOCK):
        rows = pl.ds(first, BLOCK)
        gate = matmul(rows_ref[rows, :], gate_ref[0])
        up = matmul(rows_ref[rows, :], up_ref[0])
        sigmoid = 1.0 / (1.0 + jnp.exp(-gate))
        silu = gate * sigmoid
        gate_out[rows, :] = (up * (sigmoid + silu * (1.0 - sigmoid))).astype(bf16)
        up_out[rows, :] = silu.astype(bf16)
        act_ref[rows, :] = (silu * up).astype(bf16)


def mlp_up(rows, weights):
    count, model = rows.shape
    hidden_units = weights.shape[2]
    out = jax.ShapeDtypeStruct((count, hidden_units), bf16)
    return pl.pallas_call(
        up_kernel,
        grid=(hidden_units // WIDE,),
        in_specs=[
            pl.BlockSpec((count, model), lambda j: (0, 0)),
            pl.BlockSpec((1, model, WIDE), lambda j: (0, 0, j)),
            pl.BlockSpec((1, model, WIDE), lambda j: (1, 0, j)),
        ],
        out_specs=[pl.BlockSpec((count, WIDE), lambda j: (0, j))] * 3,
        out_shape=[out] * 3,
        compiler_params=params(),
        cost_estimate=cost(
            4 * count * model * hidden_units,
            4 * model * hidden_units + 2 * count * model + 10 * count * hidden_units,
            count * hidden_units,
        ),
        name="mlp_up",
    )(rows, weights, weights)


def down_back_kernel(me_ref, down_ref, gate_in, up_in, *refs):
    *come_refs, grad_ref, dgate_ref, dup_ref = refs
    size = len(come_refs) // 2 + 1
    width = come_refs[0].shape[1]

    @pl.when(pl.program_id(0) == 0)
    def _():
        for owner in range(size):
            grad_ref[:, owner * width : (owner + 1) * width] = picked(
                me_ref[0], owner, come_refs
            )

    for first in range(0, grad_ref.shape[0], BLOCK):
        rows = pl.ds(first, BLOCK)
        down = times_transposed(grad_ref[rows, :], down_ref[0])
        dgate_ref[rows, :] = (down * gate_in[rows, :].astype(f32)).astype(bf16)
        dup_ref[rows, :] = (down * up_in[rows, :].astype(f32)).astype(bf16)


def mlp_down_back(me, own, arrived, weights, gate, up):
    operands = flat(own, arrived)
    count, width = own.shape
    model = width * (len(operands) // 2 + 1)
    hidden_units = weights.shape[2]
    part = pl.BlockSpec((count, WIDE), lambda j, me: (0, j))
    whole = lambda j, me: (0, 0)
    out = jax.ShapeDtypeStruct((count, hidden_units), bf16)
    return pl.pallas_call(
        down_back_kernel,
        grid_spec=pltpu.PrefetchScalarGridSpec(
            num_scalar_prefetch=1,
            grid=(hidden_units // WIDE,),
            in_specs=[
                pl.BlockSpec((1, WIDE, model), lambda j, me: (2, j, 0)),
                part,
                part,
                *[pl.BlockSpec((count, width), whole, pipeline_mode=pl.Buffered(1))]
                * len(operands),
            ],
            out_specs=[pl.BlockSpec((count, model), whole), part, part],
        ),
        out_shape=[jax.ShapeDtypeStruct((count, model), bf16), out, out],
        compiler_params=params(),
        cost_estimate=cost(
            2 * count * model * hidden_units,
            2 * model * hidden_units + 2 * count * model + 12 * count * hidden_units,
            count * hidden_units,
        ),
        name="mlp_down_back",
    )(me, weights, gate, up, *operands)


def mlp_piece_kernel(order_ref, act_ref, down_ref, *out_refs):
    for piece, out_ref in enumerate(out_refs):

        @pl.when(pl.program_id(0) == piece)
        def _(out_ref=out_ref):
            for first in range(0, act_ref.shape[0], BLOCK):
                rows = pl.ds(first, BLOCK)
                out_ref[rows, :] = matmul(act_ref[rows, :], down_ref[0]).astype(bf16)


def mlp_pieces(order, act, weights, width):
    count, hidden_units = act.shape
    pieces = order.shape[0]
    whole = lambda g, order: (0, 0)
    return pl.pallas_call(
        mlp_piece_kernel,
        grid_spec=pltpu.PrefetchScalarGridSpec(
            num_scalar_prefetch=1,
            grid=(pieces,),
            in_specs=[
                pl.BlockSpec((count, hidden_units), whole, pipeline_mode=pl.Buffered(1)),
                pl.BlockSpec((1, hidden_units, width), lambda g, order: (2, 0, order[g])),
            ],
            out_specs=[pl.BlockSpec((count, width), whole)] * pieces,
        ),
        out_shape=[jax.ShapeDtypeStruct((count, width), bf16)] * pieces,
        compiler_params=params(),
        cost_estimate=cost(
            2 * pieces * count * width * hidden_units, 2 * pieces * width * hidden_units
        ),
        name="mlp_piece",
    )(order, act, weights)


def norm_back(values_in, grad_in):
    unit_rows, inverse = norm_parts(values_in)
    return inverse * (
        grad_in
        - jnp.mean(grad_in, axis=-1, keepdims=True)
        - unit_rows * jnp.mean(grad_in * unit_rows, axis=-1, keepdims=True)
    )


def put_at(place, value, refs):
    for index, ref in enumerate(refs):

        @pl.when(place == index)
        def _(ref=ref):
            ref[...] = value


def two_grad_kernel(order_ref, *refs):
    pieces = (len(refs) - 3) // 4
    row_refs = refs[: 3 * pieces]
    gate_ref, up_ref = refs[3 * pieces : 3 * pieces + 2]
    out_refs, total = refs[3 * pieces + 2 : -1], refs[-1]
    step = pl.program_id(0)
    columns = pl.ds(pl.multiple_of(step * WIDE, WIDE), WIDE)
    for piece in range(pieces):
        total[piece, :, columns] = times_transposed(
            row_refs[3 * piece][...], gate_ref[0]
        ) + times_transposed(row_refs[3 * piece + 1][...], up_ref[0])

    @pl.when(step == pl.num_programs(0) - 1)
    def _():
        for piece in range(pieces):
            out_refs[piece][...] = norm_back(
                row_refs[3 * piece + 2][...], total[piece]
            ).astype(bf16)


def two_grad_pieces(order, dgate, dup, weights, hidden, quarter):
    pieces = order.shape[0]
    hidden_units = dgate.shape[1]
    model = weights.shape[1]
    rows = []
    for p in range(pieces):
        here = lambda j, order, p=p: (order[p], 0)
        rows += [pl.BlockSpec((quarter, hidden_units), here)] * 2
        rows += [pl.BlockSpec((quarter, model), here, pipeline_mode=pl.Buffered(1))]
    return pl.pallas_call(
        two_grad_kernel,
        grid_spec=pltpu.PrefetchScalarGridSpec(
            num_scalar_prefetch=1,
            grid=(model // WIDE,),
            in_specs=[
                *rows,
                pl.BlockSpec((1, WIDE, hidden_units), lambda j, order: (0, j, 0)),
                pl.BlockSpec((1, WIDE, hidden_units), lambda j, order: (1, j, 0)),
            ],
            out_specs=[pl.BlockSpec((quarter, model), lambda j, order: (0, 0))] * pieces,
            scratch_shapes=[pltpu.VMEM((pieces, quarter, model), f32)],
        ),
        out_shape=[jax.ShapeDtypeStruct((quarter, model), bf16)] * pieces,
        compiler_params=params(),
        cost_estimate=cost(
            4 * pieces * quarter * model * hidden_units, 4 * model * hidden_units
        ),
        name="two_grad",
    )(order, *([dgate, dup, hidden] * pieces), weights, weights)


def att_grad_kernel(me_ref, weight_ref, *refs):
    *come_refs, whole_ref, out_ref = refs
    rows = picked(me_ref[0], pl.program_id(0), come_refs)
    whole_ref[...] = rows
    out_ref[...] = times_transposed(rows, weight_ref[...]).astype(bf16)


def att_grad_rows(me, own, arrived, weight, local):
    operands = flat(own, arrived)
    share, model = own.shape
    size = len(operands) // 2 + 1
    here = lambda i, me: (i, 0)
    once = pl.Buffered(1)
    return pl.pallas_call(
        att_grad_kernel,
        grid_spec=pltpu.PrefetchScalarGridSpec(
            num_scalar_prefetch=1,
            grid=(size,),
            in_specs=[
                pl.BlockSpec((local, model), lambda i, me: (me[0], 0), pipeline_mode=once),
                *[pl.BlockSpec((share, model), lambda i, me: (0, 0), pipeline_mode=once)]
                * len(operands),
            ],
            out_specs=[
                pl.BlockSpec((share, model), here),
                pl.BlockSpec((share, local), here),
            ],
        ),
        out_shape=[
            jax.ShapeDtypeStruct((share * size, model), bf16),
            jax.ShapeDtypeStruct((share * size, local), bf16),
        ],
        compiler_params=params(),
        cost_estimate=cost(1000, 1000),
        name="att_grad",
    )(me, weight, *operands)


def one_grad_kernel(place_ref, dq_ref, dk_ref, dv_ref, weight_ref, rows_ref, *out_refs):
    columns = jnp.concatenate([dq_ref[...], dk_ref[...], dv_ref[...]], axis=1)
    grad = norm_back(
        rows_ref[...].astype(f32), times_transposed(columns, weight_ref[...])
    ).astype(bf16)
    width = out_refs[0].shape[1]
    for piece in range(len(out_refs)):
        put_at(place_ref[piece], grad[:, piece * width : (piece + 1) * width], out_refs)


def one_grad_pieces(place, grads, weight, rows):
    count, local = grads[0].shape
    columns = 3 * local
    pieces = place.shape[0]
    model = rows.shape[1]
    here = lambda i, place: (i, 0)
    return pl.pallas_call(
        one_grad_kernel,
        grid_spec=pltpu.PrefetchScalarGridSpec(
            num_scalar_prefetch=1,
            grid=(count // BLOCK,),
            in_specs=[
                *[pl.BlockSpec((BLOCK, local), here)] * 3,
                pl.BlockSpec(
                    (model, columns), lambda i, place: (0, 0), pipeline_mode=pl.Buffered(1)
                ),
                pl.BlockSpec((BLOCK, model), here),
            ],
            out_specs=[pl.BlockSpec((BLOCK, model // pieces), here)] * pieces,
        ),
        out_shape=[jax.ShapeDtypeStruct((count, model // pieces), bf16)] * pieces,
        compiler_params=params(),
        cost_estimate=cost(
            2 * count * model * columns, 2 * columns * model + 6 * count * columns
        ),
        name="one_grad",
    )(place, *grads, weight, rows)


def att_grads_kernel(normed_ref, dq_ref, dk_ref, dv_ref, att_ref, hidden_ref, out_ref):
    owner = pl.program_id(0)
    columns = 3 * dq_ref.shape[1]
    grads = jnp.concatenate([dq_ref[...], dk_ref[...], dv_ref[...]], axis=1)
    out_ref[0, :, :columns] = transposed_times(normed_ref[...], grads).astype(bf16)
    model = hidden_ref.shape[1]
    rest = model - columns
    pieces = model // rest
    height = out_ref.shape[1] // pieces
    per_tile = HEAD_DIM // height
    product = transposed_times(att_ref[...], hidden_ref[...]).astype(bf16)
    for place in range(per_tile):

        @pl.when(lax.rem(owner, per_tile) == place)
        def _(place=place):
            for piece in range(pieces):
                out_ref[0, piece * height : (piece + 1) * height, columns:] = product[
                    place * height : (place + 1) * height, piece * rest : (piece + 1) * rest
                ]


def att_grads(normed, qkv_grad, attended, hidden_grad, groups):
    count, model = normed.shape
    local = attended.shape[1]
    columns = 3 * local
    tall = model // groups
    per_tile = HEAD_DIM // (local // groups)
    once = pl.Buffered(1)
    whole = lambda i: (0, 0)
    if tall % HEAD_DIM == 0:
        normed_spec = pl.BlockSpec((count, tall), lambda i: (0, i))
        operand = normed
    else:
        normed_spec = pl.BlockSpec((None, count, tall), lambda i: (i, 0, 0))
        operand = normed.reshape(count, groups, tall).swapaxes(0, 1)
    return pl.pallas_call(
        att_grads_kernel,
        grid=(groups,),
        in_specs=[
            normed_spec,
            *[pl.BlockSpec((count, local), whole, pipeline_mode=once)] * 3,
            pl.BlockSpec((count, HEAD_DIM), lambda i: (0, i // per_tile)),
            pl.BlockSpec((count, model), whole, pipeline_mode=once),
        ],
        out_specs=pl.BlockSpec((1, tall, model), lambda i: (i, 0, 0)),
        out_shape=jax.ShapeDtypeStruct((groups, tall, model), bf16),
        compiler_params=params(),
        cost_estimate=cost(1000, 1000),
        name="att_grads",
    )(operand, *qkv_grad, attended, hidden_grad)


def mlp_grads_kernel(*refs):
    *operands, out_ref = refs
    count = len(operands) // 2
    total = transposed_times(operands[0][...], operands[count][...])
    for part in range(1, count):
        total += transposed_times(operands[part][...], operands[count + part][...])
    out_ref[0] = total.astype(bf16)


def mlp_grads(which, left, right, before=None):
    rows = left[0].shape[0]
    model, hidden_units = left[0].shape[1], right[0].shape[1]
    once = pl.Buffered(1)
    specs = [pl.BlockSpec((rows, BLOCK), lambda i: (0, i)) for _ in left]
    specs += [
        pl.BlockSpec((rows, hidden_units), lambda i: (0, 0), pipeline_mode=once) for _ in right
    ]
    operands = [*left, *right]
    body = mlp_grads_kernel
    aliases = {}
    if before is not None:
        aliases = {len(operands): 0}
        specs.append(pl.BlockSpec(memory_space=pl.ANY))
        operands.append(before)
        body = lambda *refs: mlp_grads_kernel(*refs[:-2], refs[-1])
    count = rows * len(left)
    return pl.pallas_call(
        body,
        grid=(model // BLOCK,),
        in_specs=specs,
        out_specs=pl.BlockSpec((1, BLOCK, hidden_units), lambda i: (which, i, 0)),
        out_shape=jax.ShapeDtypeStruct((3, model, hidden_units), bf16),
        input_output_aliases=aliases,
        compiler_params=params(),
        cost_estimate=cost(
            2 * count * model * hidden_units, 2 * model * hidden_units + 4 * count * model
        ),
        name="mlp_grads",
    )(*operands)


def after(value, *others):
    return lax.optimization_barrier((value, *others))[0]


def line_step(block, axis, size, step):
    from_low, from_high = block
    up = [(i, i + 1) for i in range(step - 1, size - 1)]
    down = [(i, i - 1) for i in range(size - step, 0, -1)]
    return lax.ppermute(from_low, axis, up), lax.ppermute(from_high, axis, down)


def chain_gather(block, axis, size, begun=None):
    arrived = list(begun or [])
    for step in range(len(arrived) + 1, size):
        arrived.append(line_step(arrived[-1] if arrived else (block, block), axis, size, step))
    return arrived


def far_first(size):
    return sorted(range(1, size), key=lambda step: -min(step, size - step))


def sent_on(term, axis, size, step):
    return lax.ppermute(term, axis, [(i, (i + step) % size) for i in range(size)])


def added(own, came):
    for piece in came:
        own = own + piece.astype(f32)
    return own


def on_device(
    tokens,
    cotangent,
    w_query,
    w_key,
    w_value,
    w_out,
    w_gate,
    w_up,
    w_down,
    seq_lengths,
    deal,
    row_dest,
):
    groups = lax.axis_size("fsdp")
    shards = lax.axis_size("tp")
    own_group = lax.axis_index("fsdp")
    own_shard = lax.axis_index("tp")
    capacity = GROUP_CAP
    per_pair = capacity // groups
    quarter = capacity // shards
    head_dim = HEAD_DIM
    given, width = tokens.shape
    model = width * shards
    local_width = w_query.shape[1]
    shard_rows = w_query.shape[0]

    steps = far_first(shards)
    order = jnp.stack([lax.rem(own_shard + step, shards) for step in (*steps, 0)])
    around = jnp.stack([lax.rem(own_shard + step, shards) for step in range(shards)])
    place_of = [0] * shards
    for index, step in enumerate((*steps, 0)):
        place_of[step] = index
    place = jnp.stack(
        [
            sum(
                jnp.where(lax.rem(own_shard + step, shards) == j, place_of[step], 0)
                for step in range(shards)
            )
            for j in range(shards)
        ]
    )

    target = row_dest // capacity
    within = row_dest - target * capacity
    given_index = jnp.arange(given, dtype=jnp.int32)
    earlier = (target[:, None] == target[None, :]) & (
        given_index[None, :] < given_index[:, None]
    )
    slot_of = target * per_pair + jnp.sum(earlier.astype(jnp.int32), axis=1)
    slots = jnp.arange(capacity, dtype=jnp.int32)
    deal_hit = slots[:, None] == slot_of[None, :]
    deal_out = deal_hit.astype(bf16)
    place_high, place_low = (within + 1) // 32, (within + 1) % 32
    lane = jnp.arange(HEAD_DIM, dtype=jnp.int32)[None, :]
    place_columns = jnp.where(
        lane == 0, place_high[:, None], jnp.where(lane == 1, place_low[:, None], 0)
    ).astype(bf16)

    def over_fsdp(rows):
        return lax.all_to_all(rows, "fsdp", split_axis=0, concat_axis=0, tiled=True)

    sent_rows = matmul(deal_out, jnp.concatenate([tokens, place_columns], axis=1)).astype(bf16)
    sent_grads = matmul(deal_out, cotangent).astype(bf16)

    qkv_shard = jnp.concatenate([w_query, w_key, w_value], axis=1)
    full_qkv = lax.all_gather(qkv_shard, "fsdp", axis=0, tiled=True)
    out_came = [sent_on(w_out, "tp", shards, step) for step in range(1, shards)]
    came_rows = over_fsdp(sent_rows)
    mlp_shard = jnp.stack([w_gate, w_up, w_down])
    *out_came, came_rows, sent_grads, mlp_shard = lax.optimization_barrier(
        (*out_came, came_rows, sent_grads, mlp_shard)
    )
    came_place = came_rows[:, width : width + 2].astype(jnp.int32)
    recv_place = came_place[:, 0] * 32 + came_place[:, 1] - 1
    place_in = (slots[:, None] == recv_place[None, :]).astype(bf16)
    out_came = [w_out] + out_came
    out_rows = []
    for owner in range(shards):
        piece = w_out
        for step in range(1, shards):
            piece = jnp.where(own_shard == (owner + step) % shards, out_came[step], piece)
        out_rows.append(piece)
    out_rows = jnp.stack(out_rows)
    full_out = lax.all_gather(out_rows, "fsdp", axis=1, tiled=True).reshape(model, model)

    full_mlp = lax.all_gather(mlp_shard, "fsdp", axis=1, tiled=True)
    buffer_rows = matmul(place_in, came_rows[:, :width]).astype(bf16)
    buffer_grads = matmul(place_in, over_fsdp(after(sent_grads, buffer_rows))).astype(bf16)
    rows_come = chain_gather(buffer_rows, "tp", shards)
    *last, first_grads = lax.optimization_barrier((*rows_come[-1], buffer_grads))
    rows_come[-1] = tuple(last)
    me = own_shard[None].astype(jnp.int32)

    list_index = jnp.sum(jnp.where(deal == own_group, jnp.arange(groups, dtype=jnp.int32), 0))
    lengths = lax.dynamic_index_in_dim(seq_lengths, list_index, 0, keepdims=False)
    segment, position = segments(lengths)
    cosine, sine = rope_tables(position, head_dim)

    full_rows, normed_one = gathered_norm(me, buffer_rows, rows_come)
    first_grads, normed_one = lax.optimization_barrier((first_grads, normed_one))
    grads_begun = line_step((first_grads, first_grads), "tp", shards, 1)
    qkv = project_qkv(normed_one, full_qkv, cosine, sine)
    attended = attend(qkv, segment)
    attended, *grads_begun = lax.optimization_barrier((attended, *grads_begun))
    att_come = chain_gather(attended, "tp", shards)
    *grads_begun, last_low, last_high = lax.optimization_barrier((*grads_begun, *att_come[-1]))
    att_come[-1] = (last_low, last_high)
    grads_come = [grads_begun, line_step(grads_begun, "tp", shards, 2)]
    hidden, normed_two = hidden_and_norm(me, attended, att_come, full_out, full_rows)
    *grads_come[1], normed_two = lax.optimization_barrier((*grads_come[1], normed_two))
    grads_come = chain_gather(first_grads, "tp", shards, grads_come)
    gate, up, activated = mlp_up(normed_two, full_mlp)
    def features_of(rows, owner):
        return lax.dynamic_slice_in_dim(rows, owner * width, width, 1)

    *last, activated = lax.optimization_barrier((*grads_come[-1], activated))
    grads_come[-1] = tuple(last)
    full_grads, gate_grad, up_grad = mlp_down_back(
        me, first_grads, grads_come, full_mlp, gate, up
    )

    def rows_of(rows, owner):
        return lax.dynamic_slice_in_dim(rows, owner * quarter, quarter, 0)

    near = [steps[1], steps[0], *steps[2:], 0]
    near_order = jnp.stack([lax.rem(own_shard + step, shards) for step in near])
    two_first = two_grad_pieces(
        near_order[:1], gate_grad, up_grad, full_mlp, hidden, quarter
    )
    two_rest = two_grad_pieces(
        near_order[1:], gate_grad, after(up_grad, *two_first), full_mlp, hidden, quarter
    )
    two_came = [
        sent_on(term, "tp", shards, step)
        for term, step in zip((*two_first, *two_rest), near[:-1])
    ]
    grad_mlp = mlp_grads(0, [normed_two], [after(gate_grad, *two_rest)])
    grad_mlp = mlp_grads(1, [normed_two], [up_grad], grad_mlp)
    grad_mlp = mlp_grads(2, [activated], [full_grads], grad_mlp)
    *two_came, grad_mlp = lax.optimization_barrier((*two_came, grad_mlp))
    sum_mlp = lax.psum_scatter(grad_mlp, "fsdp", scatter_dimension=1, tiled=True)
    back_low = added(
        rows_of(full_grads, own_shard).astype(f32) + two_rest[-1].astype(f32), two_came
    ).astype(bf16)
    back_come = [line_step((back_low, back_low), "tp", shards, 1)]
    terms = mlp_pieces(around, after(activated, grad_mlp, back_low), full_mlp, width)
    mlp_come = []
    for step in range(1, shards):
        back_come[-1], mlp_come, terms = lax.optimization_barrier(
            (back_come[-1], mlp_come, terms)
        )
        if step < shards - 1:
            back_come.append(line_step(back_come[-1], "tp", shards, step + 1))
        low, high = terms[shards - step], terms[step]
        if mlp_come:
            low, high = (
                (term.astype(f32) + came.astype(f32)).astype(bf16)
                for term, came in zip((low, high), mlp_come)
            )
        up = [(i, i + 1) for i in range(step)]
        down = [(i, i - 1) for i in range(shards - 1, shards - 1 - step, -1)]
        mlp_come = [lax.ppermute(low, "tp", up), lax.ppermute(high, "tp", down)]
    full_hidden_grad, attended_grad = att_grad_rows(
        me, back_low, back_come, full_out, local_width
    )
    qkv_grad = attend_back(qkv, attended_grad, segment, cosine, sine)
    one_terms = one_grad_pieces(place, qkv_grad, full_qkv, full_rows)
    one_came = [sent_on(term, "tp", shards, step) for term, step in zip(one_terms, steps)]
    *mlp_come, late_grad, _ = lax.optimization_barrier(
        (*mlp_come, tuple(qkv_grad), tuple(one_terms[:3]))
    )
    grad_att = att_grads(
        normed_one, late_grad, attended, full_hidden_grad, groups
    )
    sum_mlp, grad_att = lax.optimization_barrier((sum_mlp, grad_att))
    sum_att = lax.psum_scatter(grad_att, "fsdp", scatter_dimension=0, tiled=False)

    output_here = added(
        features_of(hidden, own_shard) + terms[0].astype(f32), mlp_come
    )
    sum_att = sum_att.astype(f32)
    out_part = sum_att[:, 3 * local_width :]
    out_pieces = model // out_part.shape[1]
    out_height = shard_rows // out_pieces
    sum_out = jnp.concatenate(
        [out_part[i * out_height : (i + 1) * out_height] for i in range(out_pieces)], axis=1
    )
    sum_gate, sum_up, sum_down = sum_mlp.astype(f32)
    back_here = added(one_terms[-1].astype(f32), one_came)
    input_here = features_of(full_hidden_grad, own_shard).astype(f32) + back_here
    here = jnp.concatenate([output_here.astype(bf16), input_here.astype(bf16)], axis=1)
    sent_back = transposed_times(place_in, here).astype(bf16)
    sums = (
        sum_att[:, : local_width],
        sum_att[:, local_width : 2 * local_width],
        sum_att[:, 2 * local_width : 3 * local_width],
        sum_out,
        sum_gate,
        sum_up,
        sum_down,
    )
    came_back, *sums = lax.optimization_barrier((over_fsdp(sent_back), *sums))
    home = transposed_times(deal_out, came_back).astype(bf16)
    return (home[:, :width], home[:, width:], *sums)


def solution(mesh):
    in_specs = (
        P("fsdp", "tp"),
        P("fsdp", "tp"),
        P("fsdp", "tp"),
        P("fsdp", "tp"),
        P("fsdp", "tp"),
        P(("tp", "fsdp"), None),
        P("fsdp", "tp"),
        P("fsdp", "tp"),
        P(("tp", "fsdp"), None),
        P(),
        P(),
        P("fsdp"),
    )
    out_specs = (
        P("fsdp", "tp"),
        P("fsdp", "tp"),
        P("fsdp", "tp"),
        P("fsdp", "tp"),
        P("fsdp", "tp"),
        P(("tp", "fsdp"), None),
        P("fsdp", "tp"),
        P("fsdp", "tp"),
        P(("tp", "fsdp"), None),
    )
    return jax.shard_map(
        on_device, mesh=mesh, in_specs=in_specs, out_specs=out_specs, check_vma=False
    )
```

time: 780 us -> 744 us (0.954)
  Pallas kernels: 224 us -> 262 us
  matrix products: 41.8 us -> 13.5 us
  waiting for transfers between devices: 308 us -> 283 us
  local copies, waits for them, and re-layouts: 28.3 us -> 8.42 us
    pallas_call x6 -> x11, Pallas kernels: 131 us -> 171 us  [the longest x3 42.4 us: mlp_grads(): pl.pallas_call(body, grid=(model // BLOCK,), in_specs=specs, out_specs=pl...]
    ppermute x12, waiting for transfers between devices: 101 us -> 68.7 us  [line_step(): lax.ppermute(from_high, axis, down)]
    ppermute x0 -> x6, waiting for transfers between devices: none -> 21.8 us  [on_device(): mlp_come = [lax.ppermute(low, 'tp', up), lax.ppermute(high, 'tp', down)]]
    ppermute x12 -> x9, waiting for transfers between devices: 112 us -> 95.8 us  [sent_on(): lax.ppermute(term, axis, [(i, (i + step) % size) for i in range(size)])]
    dot_general x5 -> x4, matrix products: 20.4 us -> 7.62 us  [matmul(): return jnp.dot(left, right, preferred_element_type=f32)]
    ppermute x0 -> x6, starting transfers between devices: none -> 11.5 us  [on_device(): mlp_come = [lax.ppermute(low, 'tp', up), lax.ppermute(high, 'tp', down)]]
    select_n x4 -> x0, other arithmetic: 7.98 us -> none  [line_whole(): piece = jnp.where(me == owner + step, arrived[step - 1][0], piece)]
    all_to_all x4 -> x3, starting transfers between devices: 26.7 us -> 20.5 us  [over_fsdp(): return lax.all_to_all(rows, 'fsdp', split_axis=0, concat_axis=0, tiled=True)]
  transfers between devices with their start and end apart: 45 -> 47, of which waited for: 22 -> 21; matrix products, arithmetic and copies ran while one was open for 10% -> 7% of each run, Pallas kernels for 29% -> 32%
where the time goes in v3:
time: 744 us; the launch traced here: 732 us
  waiting for transfers between devices  283 us (38%)
  Pallas kernels  262 us (35%)
  starting transfers between devices  116 us (16%)
  other arithmetic  32.6 us (4%)
  between operations  16.8 us (2%)
  matrix products  13.5 us (2%)
  local copies, waits for them, and re-layouts  8.42 us (1%)
    ppermute x9, waiting for transfers between devices, sent_on(): lax.ppermute(term, axis, [(i, (i + step) % size) for i in range(size)])  95.8 us
    ppermute x12, waiting for transfers between devices, line_step(): lax.ppermute(from_high, axis, down)  68.7 us
    ppermute x12, waiting for transfers between devices, line_step(): lax.ppermute(from_low, axis, up)  60.9 us
    ppermute x12, starting transfers between devices, line_step(): lax.ppermute(from_low, axis, up)  45.7 us
    pallas_call x3, Pallas kernels, mlp_grads(): pl.pallas_call(body, grid=(model // BLOCK,), in_specs=specs, out_specs=pl...  42.4 us
    pallas_call x2, Pallas kernels, two_grad_pieces(): pl.pallas_call(two_grad_kernel, grid_spec=pltpu.PrefetchScalarGridSpec(nu...  37.7 us
    all_to_all x3, waiting for transfers between devices, over_fsdp(): return lax.all_to_all(rows, 'fsdp', split_axis=0, concat_axis=0, tiled=True)  35 us
    ppermute x12, starting transfers between devices, line_step(): lax.ppermute(from_high, axis, down)  27.6 us
  transfers between devices with their start and end apart: 47, of which 21 were waited for; matrix products, arithmetic and copies ran while one was open for 7% of the time, Pallas kernels for 32%

profile of v3, /device:TPU:16, one launch (start us, length us, event | category | flops | bytes accessed | tf_op | source)
XLA Modules:
  0.0 731.8 jit_solution(18184109371914227809)
XLA Ops:
  13.1 3.9 all-to-all-start
  20.1 3.8 pad_maximum_fusion
  26.1 17.4 %all-to-all-done = bf16[8,128,640]{2,1,0:T(8,128)(2,1)S(1)} async-done(((bf16[8,128,640]{2,1,0:T(8,128)(2,1)}), bf16[8,128,640]{2,1,0:T(8,128)(2,1)S(1)}, u32[]{:S(2)}, u32[]{:S(2)}) %all-to-all-start) | async-done | bytes 1310752 | tf_op jit(solution)/shard_map/all_to_all | solution.py:766
  54.9 20.6 %collective-permute-done.6.refs_4_ = bf16[1024,512]{1,0:T(8,128)(2,1)S(1)} collective-permute-done((bf16[1024,512]{1,0:T(8,128)(2,1)S(1)}, bf16[1024,512]{1,0:T(8,128)(2,1)S(1)}, u32[]{:S(2)}, u32[]{:S(2)}) %collective-permute-start.6) | collective-permute-done | bytes 1048608 | tf_op jit(solution)/shard_map/ppermute | solution.py:682
  81.3 3.8 all-to-all-start.1
  85.1 13.8 %collective-permute-done.7.refs_5_ = bf16[1024,512]{1,0:T(8,128)(2,1)} collective-permute-done((bf16[1024,512]{1,0:T(8,128)(2,1)S(1)}, bf16[1024,512]{1,0:T(8,128)(2,1)}, u32[]{:S(2)}, u32[]{:S(2)}) %collective-permute-start.7) | collective-permute-done | bytes 1048608 | tf_op jit(solution)/shard_map/ppermute | solution.py:682
  100.6 3.7 collective-permute-done.4.refs_2_
  104.3 3.7 collective-permute-start.5
  112.3 15.0 %collective-permute-done.5.refs_3_ = bf16[1024,512]{1,0:T(8,128)(2,1)} collective-permute-done((bf16[1024,512]{1,0:T(8,128)(2,1)}, bf16[1024,512]{1,0:T(8,128)(2,1)}, u32[]{:S(2)}, u32[]{:S(2)}) %collective-permute-start.5) | collective-permute-done | bytes 1048608 | tf_op jit(solution)/shard_map/ppermute | solution.py:682
  127.3 7.7 %gathered_norm.1 = (bf16[1024,2048]{1,0:T(8,128)(2,1)}, bf16[1024,2048]{1,0:T(8,128)(2,1)}) custom-call(s32[1]{0:T(128)} %bitcast.6.me_ref, bf16[1024,512]{1,0:T(8,128)(2,1)} %copy-done.18, bf16[1024,512]{1,0:T(8,128)(2,1)} %collective-permute-done.3.refs_1_, bf16[1024,512]{1,0:T(8,128)(2,1)} %collective-permute-done.4.refs_2_, ...), custom_call_target="tpu_custom_call" | custom-call | flops 41943040 | bytes 16777216 | tf_op jit(solution)/shard_map/gathered_norm/pallas_call | solution.py:116
  136.9 5.2 collective-permute-start.9
  146.3 15.1 %qkv.1 = (bf16[1024,512]{1,0:T(8,128)(2,1)}, bf16[1024,512]{1,0:T(8,128)(2,1)}, bf16[1024,512]{1,0:T(8,128)(2,1)}) custom-call(bf16[1024,2048]{1,0:T(8,128)(2,1)} %get-tuple-element.117.rows_ref.normed_ref, bf16[2048,1536]{1,0:T(8,128)(2,1)} %all-gather.6.cloned.1.call-done.wq_ref.wk_ref.wv_ref.weight_ref, ...), custom_call_target="tpu_custom_call" | custom-call | flops 6442450944 | bytes 10485760 | tf_op jit(solution)/shard_map/qkv/pallas_call | solution.py:155
  161.4 15.5 %attend.1.refs_0_.att_ref = bf16[1024,512]{1,0:T(8,128)(2,1)} custom-call(bf16[1024,512]{1,0:T(8,128)(2,1)} %get-tuple-element.118.q_ref, bf16[1024,512]{1,0:T(8,128)(2,1)} %get-tuple-element.119.k_ref, bf16[1024,512]{1,0:T(8,128)(2,1)} %get-tuple-element.120.v_ref, s32[1024,1]{1,0:T(8,128)} %copy.27.column_ref, s32[1,1024]{1,0:T(1,128)} %bitcast.52), custom_call_target="tpu_custom_call" | custom-call | flops 2147483648 | bytes 4194304 | tf_op jit(solution)/shard_map/attend/pallas_call | solution.py:198
  178.8 4.0 collective-permute-start.11
  182.8 16.0 %collective-permute-done.14.refs_4_ = bf16[1024,512]{1,0:T(8,128)(2,1)S(1)} collective-permute-done((bf16[1024,512]{1,0:T(8,128)(2,1)}, bf16[1024,512]{1,0:T(8,128)(2,1)S(1)}, u32[]{:S(2)}, u32[]{:S(2)}) %collective-permute-start.14) | collective-permute-done | bytes 1048608 | tf_op jit(solution)/shard_map/ppermute | solution.py:682
  202.4 3.8 collective-permute-start.12
  206.2 12.9 %collective-permute-done.15.refs_5_ = bf16[1024,512]{1,0:T(8,128)(2,1)S(1)} collective-permute-done((bf16[1024,512]{1,0:T(8,128)(2,1)S(1)}, bf16[1024,512]{1,0:T(8,128)(2,1)S(1)}, u32[]{:S(2)}, u32[]{:S(2)}) %collective-permute-start.15) | collective-permute-done | bytes 1048608 | tf_op jit(solution)/shard_map/ppermute | solution.py:682
  219.8 5.2 collective-permute-done.12.refs_2_
  225.1 4.4 collective-permute-start.13
  229.5 18.5 %collective-permute-done.13.refs_3_ = bf16[1024,512]{1,0:T(8,128)(2,1)S(1)} collective-permute-done((bf16[1024,512]{1,0:T(8,128)(2,1)S(1)}, bf16[1024,512]{1,0:T(8,128)(2,1)S(1)}, u32[]{:S(2)}, u32[]{:S(2)}) %collective-permute-start.13) | collective-permute-done | bytes 1048608 | tf_op jit(solution)/shard_map/ppermute | solution.py:682
  248.1 4.4 collective-permute-start.17
  254.7 17.6 %hidden.1 = (f32[1024,2048]{1,0:T(8,128)}, bf16[1024,2048]{1,0:T(8,128)(2,1)}) custom-call(s32[1]{0:T(128)} %bitcast.6.me_ref, bf16[2048,2048]{1,0:T(8,128)(2,1)} %bitcast.42, bf16[1024,2048]{1,0:T(8,128)(2,1)} %get-tuple-element.114.rows_ref, bf16[1024,512]{1,0:T(8,128)(2,1)} %attend.1.refs_0_.att_ref, bf16[1024,512]{1,0:T(8,128)(2,1)} %copy-done.28, ...), custom_call_target="tpu_custom_call" | custom-call | flops 8589934592 | bytes 29360128 | tf_op jit(solution)/shard_map/hidden/pallas_call | solution.py:292
  272.3 4.5 collective-permute-start.19
  279.1 24.0 %mlp_up.1 = (bf16[1024,2048]{1,0:T(8,128)(2,1)}, bf16[1024,2048]{1,0:T(8,128)(2,1)}, bf16[1024,2048]{1,0:T(8,128)(2,1)}) custom-call(bf16[1024,2048]{1,0:T(8,128)(2,1)} %get-tuple-element.132.rows_ref.refs_0_, bf16[3,2048,2048]{2,1,0:T(8,128)(2,1)} %all-gather.8.cloned.1.call-done.gate_ref.up_ref.down_ref.refs_3_.refs_4_.refs_9_.refs_10_, ...), custom_call_target="tpu_custom_call" | custom-call | flops 17179869184 | bytes 41943040 | tf_op jit(solution)/shard_map/mlp_up/pallas_call | solution.py:330
  303.1 19.0 %mlp_down_back.1 = (bf16[1024,2048]{1,0:T(8,128)(2,1)}, bf16[1024,2048]{1,0:T(8,128)(2,1)}, bf16[1024,2048]{1,0:T(8,128)(2,1)}) custom-call(s32[1]{0:T(128)} %bitcast.6.me_ref, bf16[3,2048,2048]{2,1,0:T(8,128)(2,1)} %all-gather.8.cloned.1.call-done.gate_ref.up_ref.down_ref.refs_3_.refs_4_.refs_9_.refs_10_, bf16[1024,2048]{1,0:T(8,128)(2,1)} %get-tuple-element.133.gate_in, ...), custom_call_target="tpu_custom_call" | custom-call | flops 8589934592 | bytes 37748736 | tf_op jit(solution)/shard_map/mlp_down_back/pallas_call | solution.py:377
  322.1 11.9 %two_grad.2 = bf16[256,2048]{1,0:T(8,128)(2,1)} custom-call(s32[1]{0:T(128)} %bitcast.19.order_ref, bf16[1024,2048]{1,0:T(8,128)(2,1)} %get-tuple-element.148.refs_0_.refs_3_.refs_6_.refs_1_, bf16[1024,2048]{1,0:T(8,128)(2,1)} %get-tuple-element.143.refs_1_.refs_4_.refs_7_, f32[1024,2048]{1,0:T(8,128)} %get-tuple-element.127.refs_2_.refs_5_.refs_8_, ...), custom_call_target="tpu_custom_call" | custom-call | flops 4294967296 | bytes 16777216 | tf_op jit(solution)/shard_map/two_grad/pallas_call | solution.py:482
  334.2 25.7 %two_grad.3 = (bf16[256,2048]{1,0:T(8,128)(2,1)}, bf16[256,2048]{1,0:T(8,128)(2,1)}, bf16[256,2048]{1,0:T(8,128)(2,1)}) custom-call(s32[3]{0:T(128)} %pad_add_fusion.order_ref, bf16[1024,2048]{1,0:T(8,128)(2,1)} %get-tuple-element.148.refs_0_.refs_3_.refs_6_.refs_1_, bf16[1024,2048]{1,0:T(8,128)(2,1)} %get-tuple-element.143.refs_1_.refs_4_.refs_7_, ...), custom_call_target="tpu_custom_call" | custom-call | flops 12884901888 | bytes 16777216 | tf_op jit(solution)/shard_map/two_grad/pallas_call | solution.py:482
  362.0 14.1 %mlp_grads.3.refs_2_ = bf16[3,2048,2048]{2,1,0:T(8,128)(2,1)} custom-call(bf16[1024,2048]{1,0:T(8,128)(2,1)} %get-tuple-element.132.rows_ref.refs_0_, bf16[1024,2048]{1,0:T(8,128)(2,1)} %get-tuple-element.148.refs_0_.refs_3_.refs_6_.refs_1_), custom_call_target="tpu_custom_call" | custom-call | flops 8589934592 | bytes 16777216 | tf_op jit(solution)/shard_map/mlp_grads/pallas_call | solution.py:659
  376.2 14.1 %mlp_grads.4.refs_2_ = bf16[3,2048,2048]{2,1,0:T(8,128)(2,1)} custom-call(bf16[1024,2048]{1,0:T(8,128)(2,1)} %get-tuple-element.132.rows_ref.refs_0_, bf16[1024,2048]{1,0:T(8,128)(2,1)} %get-tuple-element.143.refs_1_.refs_4_.refs_7_, bf16[3,2048,2048]{2,1,0:T(8,128)(2,1)} %mlp_grads.3.refs_2_), custom_call_target="tpu_custom_call", output_to_operand_aliasing={{}: (2, {})} | custom-call | flops 8589934592 | bytes 16777216 | tf_op jit(solution)/shard_map/mlp_grads/pallas_call | solution.py:659
  390.3 14.2 %mlp_grads.5 = bf16[3,2048,2048]{2,1,0:T(8,128)(2,1)} custom-call(bf16[1024,2048]{1,0:T(8,128)(2,1)} %get-tuple-element.153.refs_0_.act_ref, bf16[1024,2048]{1,0:T(8,128)(2,1)} %get-tuple-element.140.refs_1_, bf16[3,2048,2048]{2,1,0:T(8,128)(2,1)} %mlp_grads.4.refs_2_), custom_call_target="tpu_custom_call", output_to_operand_aliasing={{}: (2, {})} | custom-call | flops 8589934592 | bytes 16777216 | tf_op jit(solution)/shard_map/mlp_grads/pallas_call | solution.py:659
  404.5 11.1 %collective-permute-done.23 = bf16[256,2048]{1,0:T(8,128)(2,1)} collective-permute-done((bf16[256,2048]{1,0:T(8,128)(2,1)}, bf16[256,2048]{1,0:T(8,128)(2,1)}, u32[]{:S(2)}, u32[]{:S(2)}) %collective-permute-start.23) | collective-permute-done | bytes 1048608 | tf_op jit(solution)/shard_map/ppermute | solution.py:697
  418.5 4.4 collective-permute-start.25
  425.8 15.5 %mlp_piece.1 = (bf16[1024,512]{1,0:T(8,128)(2,1)}, bf16[1024,512]{1,0:T(8,128)(2,1)}, bf16[1024,512]{1,0:T(8,128)(2,1)}, bf16[1024,512]{1,0:T(8,128)(2,1)}) custom-call(s32[4]{0:T(128)} %pad_add_fusion.1.order_ref, bf16[1024,2048]{1,0:T(8,128)(2,1)} %get-tuple-element.153.refs_0_.act_ref, ...), custom_call_target="tpu_custom_call" | custom-call | flops 8589934592 | bytes 8388608 | tf_op jit(solution)/shard_map/mlp_piece/pallas_call | solution.py:416
  441.4 4.1 collective-permute-done.25.refs_4_
  447.5 3.8 collective-permute-start.26
  455.8 16.3 %collective-permute-done.26.refs_2_ = bf16[256,2048]{1,0:T(8,128)(2,1)S(1)} collective-permute-done((bf16[256,2048]{1,0:T(8,128)(2,1)S(1)}, bf16[256,2048]{1,0:T(8,128)(2,1)S(1)}, u32[]{:S(2)}, u32[]{:S(2)}) %collective-permute-start.26) | collective-permute-done | bytes 1048608 | tf_op jit(solution)/shard_map/ppermute | solution.py:682
  473.4 5.1 collective-permute-done.29
  488.8 14.8 %collective-permute-done.33 = bf16[1024,512]{1,0:T(8,128)(2,1)S(1)} collective-permute-done((bf16[1024,512]{1,0:T(8,128)(2,1)S(1)}, bf16[1024,512]{1,0:T(8,128)(2,1)S(1)}, u32[]{:S(2)}, u32[]{:S(2)}) %collective-permute-start.33) | collective-permute-done | bytes 1048608 | tf_op jit(solution)/shard_map/ppermute | solution.py:868
  511.7 3.7 collective-permute-start.34
  516.1 11.6 %att_grad.1 = (bf16[1024,2048]{1,0:T(8,128)(2,1)}, bf16[1024,512]{1,0:T(8,128)(2,1)}) custom-call(s32[1]{0:T(128)} %bitcast.6.me_ref, bf16[2048,2048]{1,0:T(8,128)(2,1)} %bitcast.43, bf16[256,2048]{1,0:T(8,128)(2,1)} %copy-done.2, bf16[256,2048]{1,0:T(8,128)(2,1)} %copy-done.6, bf16[256,2048]{1,0:T(8,128)(2,1)} %copy-done.8, bf16[256,2048]{1,0:T(8,128)(2,1)} %copy-done.10, ...), custom_call_target="tpu_custom_call" | custom-call | flops 1000 | bytes 1000 | tf_op jit(solution)/shard_map/att_grad/pallas_call | solution.py:517
  527.6 21.5 %attend_back.1 = (bf16[1024,512]{1,0:T(8,128)(2,1)}, bf16[1024,512]{1,0:T(8,128)(2,1)}, bf16[1024,512]{1,0:T(8,128)(2,1)}) custom-call(bf16[1024,512]{1,0:T(8,128)(2,1)} %get-tuple-element.118.q_ref, bf16[1024,512]{1,0:T(8,128)(2,1)} %get-tuple-element.119.k_ref, bf16[1024,512]{1,0:T(8,128)(2,1)} %get-tuple-element.120.v_ref, ...), custom_call_target="tpu_custom_call" | custom-call | flops 1000 | bytes 1000 | tf_op jit(solution)/shard_map/attend_back/pallas_call | solution.py:257
  549.2 16.3 %one_grad.1 = (bf16[1024,512]{1,0:T(8,128)(2,1)}, bf16[1024,512]{1,0:T(8,128)(2,1)}, bf16[1024,512]{1,0:T(8,128)(2,1)}, bf16[1024,512]{1,0:T(8,128)(2,1)}) custom-call(s32[4]{0:T(128)} %pad_add_fusion.2.place_ref, bf16[1024,512]{1,0:T(8,128)(2,1)} %get-tuple-element.190.dq_ref, bf16[1024,512]{1,0:T(8,128)(2,1)} %get-tuple-element.191.dk_ref, ...), custom_call_target="tpu_custom_call" | custom-call | flops 6442450944 | bytes 15728640 | tf_op jit(solution)/shard_map/one_grad/pallas_call | solution.py:558
  565.5 17.8 %att_grads.1 = bf16[8,256,2048]{2,1,0:T(8,128)(2,1)} custom-call(bf16[1024,2048]{1,0:T(8,128)(2,1)} %get-tuple-element.117.rows_ref.normed_ref, bf16[1024,512]{1,0:T(8,128)(2,1)} %get-tuple-element.190.dq_ref, bf16[1024,512]{1,0:T(8,128)(2,1)} %get-tuple-element.191.dk_ref, bf16[1024,512]{1,0:T(8,128)(2,1)} %get-tuple-element.192.dv_ref, ...), custom_call_target="tpu_custom_call" | custom-call | flops 1000 | bytes 1000 | tf_op jit(solution)/shard_map/att_grads/pallas_call | solution.py:616
  590.8 60.4 %collective-permute-done.36 = bf16[1024,512]{1,0:T(8,128)(2,1)} collective-permute-done((bf16[1024,512]{1,0:T(8,128)(2,1)}, bf16[1024,512]{1,0:T(8,128)(2,1)}, u32[]{:S(2)}, u32[]{:S(2)}) %collective-permute-start.36) | collective-permute-done | bytes 1048608 | tf_op jit(solution)/shard_map/ppermute | solution.py:697
  651.3 24.2 %collective-permute-done.37 = bf16[1024,512]{1,0:T(8,128)(2,1)} collective-permute-done((bf16[1024,512]{1,0:T(8,128)(2,1)}, bf16[1024,512]{1,0:T(8,128)(2,1)}, u32[]{:S(2)}, u32[]{:S(2)}) %collective-permute-start.37) | collective-permute-done | bytes 1048608 | tf_op jit(solution)/shard_map/ppermute | solution.py:697
  678.4 3.7 fusion.15
  682.2 12.8 %all-to-all-start.2 = ((bf16[8,128,1024]{2,1,0:T(8,128)(2,1)}), bf16[8,128,1024]{2,1,0:T(8,128)(2,1)S(1)}, u32[]{:S(2)}, u32[]{:S(2)}) async-start(bf16[8,128,1024]{2,1,0:T(8,128)(2,1)} %bitcast.46), calls=%async_computation.2 | async-start | bytes 4194304 | tf_op jit(solution)/shard_map/all_to_all | solution.py:766
  704.1 17.5 %all-to-all-done.2 = bf16[8,128,1024]{2,1,0:T(8,128)(2,1)S(1)} async-done(((bf16[8,128,1024]{2,1,0:T(8,128)(2,1)}), bf16[8,128,1024]{2,1,0:T(8,128)(2,1)S(1)}, u32[]{:S(2)}, u32[]{:S(2)}) %all-to-all-start.2) | async-done | bytes 2097184 | tf_op jit(solution)/shard_map/all_to_all | solution.py:766
  (180 shorter events, 106.7 us)
Async XLA Ops:
  7.2 139.1 %all-gather.6.cloned.1.call-start = ((), (), s32[]{:S(2)}) async-start(), calls=%async_computation.6 | async-start | bytes 7077888 | tf_op jit(solution)/shard_map/all_gather | solution.py:772
  13.1 30.5 %all-to-all-start = ((bf16[8,128,640]{2,1,0:T(8,128)(2,1)}), bf16[8,128,640]{2,1,0:T(8,128)(2,1)S(1)}, u32[]{:S(2)}, u32[]{:S(2)}) async-start(bf16[8,128,640]{2,1,0:T(8,128)(2,1)} %bitcast), calls=%async_computation | async-start | bytes 2621440 | tf_op jit(solution)/shard_map/all_to_all | solution.py:766
  17.0 237.7 %all-gather.4.cloned.1.call-start = ((), (), s32[]{:S(2)}) async-start(), calls=%async_computation.5 | async-start | bytes 9437184 | tf_op jit(solution)/shard_map/all_gather | solution.py:790
  17.0 27.2 %collective-permute-start.1 = (bf16[64,2048]{1,0:T(8,128)(2,1)}, bf16[64,2048]{1,0:T(8,128)(2,1)}, u32[]{:S(2)}, u32[]{:S(2)}) collective-permute-start(bf16[64,2048]{1,0:T(8,128)(2,1)} %param.17), channel_id=1, source_target_pairs={{0,2},{1,3},{2,0},{3,1},{4,6},{5,7},{6,4},{7,5},{8,10},{9,11},{10,... | collective-permute-start | bytes 786440 | tf_op jit(solution)/shard_map/ppermute | solution.py:697
  17.4 26.8 %collective-permute-start = (bf16[64,2048]{1,0:T(8,128)(2,1)}, bf16[64,2048]{1,0:T(8,128)(2,1)}, u32[]{:S(2)}, u32[]{:S(2)}) collective-permute-start(bf16[64,2048]{1,0:T(8,128)(2,1)} %param.17), channel_id=1, source_target_pairs={{0,1},{1,2},{2,3},{3,0},{4,5},{5,6},{6,7},{7,4},{8,9},{9,10},{10,1... | collective-permute-start | bytes 786440 | tf_op jit(solution)/shard_map/ppermute | solution.py:697
  19.0 25.3 %collective-permute-start.2 = (bf16[64,2048]{1,0:T(8,128)(2,1)}, bf16[64,2048]{1,0:T(8,128)(2,1)}, u32[]{:S(2)}, u32[]{:S(2)}) collective-permute-start(bf16[64,2048]{1,0:T(8,128)(2,1)} %param.17), channel_id=1, source_target_pairs={{0,3},{1,0},{2,1},{3,2},{4,7},{5,4},{6,5},{7,6},{8,11},{9,8},{10,9... | collective-permute-start | bytes 786440 | tf_op jit(solution)/shard_map/ppermute | solution.py:697
  46.7 232.3 %all-gather.8.cloned.1.call-start = ((), (), s32[]{:S(2)}) async-start(), calls=%async_computation.7 | async-start | bytes 28311552 | tf_op jit(solution)/shard_map/all_gather | solution.py:792
  48.9 26.7 %collective-permute-start.6 = (bf16[1024,512]{1,0:T(8,128)(2,1)S(1)}, bf16[1024,512]{1,0:T(8,128)(2,1)S(1)}, u32[]{:S(2)}, u32[]{:S(2)}) collective-permute-start(bf16[1024,512]{1,0:T(8,128)(2,1)S(1)} %fusion.24.refs_0_), channel_id=1, source_target_pairs={{3,2},{2,1},{1,0},{7,6},{6,5},{5,4},{11,10},{10,9},{9,8},{15,14},{... | collective-permute-start | bytes 3145736 | tf_op jit(solution)/shard_map/ppermute | solution.py:682
  51.4 27.3 %collective-permute-start.3 = (bf16[1024,512]{1,0:T(8,128)(2,1)S(1)}, bf16[1024,512]{1,0:T(8,128)(2,1)}, u32[]{:S(2)}, u32[]{:S(2)}) collective-permute-start(bf16[1024,512]{1,0:T(8,128)(2,1)S(1)} %fusion.24.refs_0_), channel_id=1, source_target_pairs={{0,1},{1,2},{2,3},{4,5},{5,6},{6,7},{8,9},{9,10},{10,11},{12,13},{... | collective-permute-start | bytes 3145736 | tf_op jit(solution)/shard_map/ppermute | solution.py:682
  75.5 23.4 %collective-permute-start.7 = (bf16[1024,512]{1,0:T(8,128)(2,1)S(1)}, bf16[1024,512]{1,0:T(8,128)(2,1)}, u32[]{:S(2)}, u32[]{:S(2)}) collective-permute-start(bf16[1024,512]{1,0:T(8,128)(2,1)S(1)} %collective-permute-done.6.refs_4_), channel_id=1, source_target_pairs={{2,1},{1,0},{6,5},{5,4},{10,9},{9,8},{14,13},{13,12},{18,17},{17,1... | collective-permute-start | bytes 3145736 | tf_op jit(solution)/shard_map/ppermute | solution.py:682
  78.7 25.6 %collective-permute-start.4 = (bf16[1024,512]{1,0:T(8,128)(2,1)}, bf16[1024,512]{1,0:T(8,128)(2,1)}, u32[]{:S(2)}, u32[]{:S(2)}) collective-permute-start(bf16[1024,512]{1,0:T(8,128)(2,1)} %collective-permute-done.3.refs_1_), channel_id=1, source_target_pairs={{1,2},{2,3},{5,6},{6,7},{9,10},{10,11},{13,14},{14,15},{17,18},{18... | collective-permute-start | bytes 3145736 | tf_op jit(solution)/shard_map/ppermute | solution.py:682
  81.3 29.7 %all-to-all-start.1 = ((bf16[8,128,512]{2,1,0:T(8,128)(2,1)}), bf16[8,128,512]{2,1,0:T(8,128)(2,1)S(1)}, u32[]{:S(2)}, u32[]{:S(2)}) async-start(bf16[8,128,512]{2,1,0:T(8,128)(2,1)} %bitcast.12), calls=%async_computation.1 | async-start | bytes 2097152 | tf_op jit(solution)/shard_map/all_to_all | solution.py:766
  85.1 498.3 %reduce-scatter.3.cloned.1.call-start = ((), (), s32[]{:S(2)}) async-start(), calls=%async_computation.8 | async-start | bytes 28311552 | tf_op jit(solution)/shard_map/reduce_scatter | solution.py:847
  98.9 13.4 %collective-permute-start.8 = (bf16[1024,512]{1,0:T(8,128)(2,1)}, bf16[1024,512]{1,0:T(8,128)(2,1)}, u32[]{:S(2)}, u32[]{:S(2)}) collective-permute-start(bf16[1024,512]{1,0:T(8,128)(2,1)} %collective-permute-done.7.refs_5_), channel_id=1, source_target_pairs={{1,0},{5,4},{9,8},{13,12},{17,16},{21,20},{25,24},{29,28}} | collective-permute-start | bytes 3145736 | tf_op jit(solution)/shard_map/ppermute | solution.py:682
  104.3 23.0 %collective-permute-start.5 = (bf16[1024,512]{1,0:T(8,128)(2,1)}, bf16[1024,512]{1,0:T(8,128)(2,1)}, u32[]{:S(2)}, u32[]{:S(2)}) collective-permute-start(bf16[1024,512]{1,0:T(8,128)(2,1)} %collective-permute-done.4.refs_2_), channel_id=1, source_target_pairs={{2,3},{6,7},{10,11},{14,15},{18,19},{22,23},{26,27},{30,31}} | collective-permute-start | bytes 3145736 | tf_op jit(solution)/shard_map/ppermute | solution.py:682
  134.9 41.9 %collective-permute-start.10 = (bf16[1024,512]{1,0:T(8,128)(2,1)S(1)}, bf16[1024,512]{1,0:T(8,128)(2,1)}, u32[]{:S(2)}, u32[]{:S(2)}) collective-permute-start(bf16[1024,512]{1,0:T(8,128)(2,1)S(1)} %fusion.25.refs_0_), channel_id=1, source_target_pairs={{3,2},{2,1},{1,0},{7,6},{6,5},{5,4},{11,10},{10,9},{9,8},{15,14},{... | collective-permute-start | bytes 3145736 | tf_op jit(solution)/shard_map/ppermute | solution.py:682
  136.9 40.0 %collective-permute-start.9 = (bf16[1024,512]{1,0:T(8,128)(2,1)S(1)}, bf16[1024,512]{1,0:T(8,128)(2,1)}, u32[]{:S(2)}, u32[]{:S(2)}) collective-permute-start(bf16[1024,512]{1,0:T(8,128)(2,1)S(1)} %fusion.25.refs_0_), channel_id=1, source_target_pairs={{0,1},{1,2},{2,3},{4,5},{5,6},{6,7},{8,9},{9,10},{10,11},{12,13},{... | collective-permute-start | bytes 3145736 | tf_op jit(solution)/shard_map/ppermute | solution.py:682
  176.9 22.0 %collective-permute-start.14 = (bf16[1024,512]{1,0:T(8,128)(2,1)}, bf16[1024,512]{1,0:T(8,128)(2,1)S(1)}, u32[]{:S(2)}, u32[]{:S(2)}) collective-permute-start(bf16[1024,512]{1,0:T(8,128)(2,1)} %attend.1.refs_0_.att_ref), channel_id=1, source_target_pairs={{3,2},{2,1},{1,0},{7,6},{6,5},{5,4},{11,10},{10,9},{9,8},{15,14},{... | collective-permute-start | bytes 3145736 | tf_op jit(solution)/shard_map/ppermute | solution.py:682
  178.8 23.6 %collective-permute-start.11 = (bf16[1024,512]{1,0:T(8,128)(2,1)}, bf16[1024,512]{1,0:T(8,128)(2,1)S(1)}, u32[]{:S(2)}, u32[]{:S(2)}) collective-permute-start(bf16[1024,512]{1,0:T(8,128)(2,1)} %attend.1.refs_0_.att_ref), channel_id=1, source_target_pairs={{0,1},{1,2},{2,3},{4,5},{5,6},{6,7},{8,9},{9,10},{10,11},{12,13},{... | collective-permute-start | bytes 3145736 | tf_op jit(solution)/shard_map/ppermute | solution.py:682
  198.8 20.3 %collective-permute-start.15 = (bf16[1024,512]{1,0:T(8,128)(2,1)S(1)}, bf16[1024,512]{1,0:T(8,128)(2,1)S(1)}, u32[]{:S(2)}, u32[]{:S(2)}) collective-permute-start(bf16[1024,512]{1,0:T(8,128)(2,1)S(1)} %collective-permute-done.14.refs_4_), channel_id=1, source_target_pairs={{2,1},{1,0},{6,5},{5,4},{10,9},{9,8},{14,13},{13,12},{18,17},{17,1... | collective-permute-start | bytes 3145736 | tf_op jit(solution)/shard_map/ppermute | solution.py:682
  202.4 22.6 %collective-permute-start.12 = (bf16[1024,512]{1,0:T(8,128)(2,1)S(1)}, bf16[1024,512]{1,0:T(8,128)(2,1)S(1)}, u32[]{:S(2)}, u32[]{:S(2)}) collective-permute-start(bf16[1024,512]{1,0:T(8,128)(2,1)S(1)} %collective-permute-done.11.refs_1_), channel_id=1, source_target_pairs={{1,2},{2,3},{5,6},{6,7},{9,10},{10,11},{13,14},{14,15},{17,18},{18... | collective-permute-start | bytes 3145736 | tf_op jit(solution)/shard_map/ppermute | solution.py:682
  219.1 10.4 %collective-permute-start.16 = (bf16[1024,512]{1,0:T(8,128)(2,1)S(1)}, bf16[1024,512]{1,0:T(8,128)(2,1)S(1)}, u32[]{:S(2)}, u32[]{:S(2)}) collective-permute-start(bf16[1024,512]{1,0:T(8,128)(2,1)S(1)} %collective-permute-done.15.refs_5_), channel_id=1, source_target_pairs={{1,0},{5,4},{9,8},{13,12},{17,16},{21,20},{25,24},{29,28}} | collective-permute-start | bytes 3145736 | tf_op jit(solution)/shard_map/ppermute | solution.py:682
  225.1 23.0 %collective-permute-start.13 = (bf16[1024,512]{1,0:T(8,128)(2,1)S(1)}, bf16[1024,512]{1,0:T(8,128)(2,1)S(1)}, u32[]{:S(2)}, u32[]{:S(2)}) collective-permute-start(bf16[1024,512]{1,0:T(8,128)(2,1)S(1)} %collective-permute-done.12.refs_2_), channel_id=1, source_target_pairs={{2,3},{6,7},{10,11},{14,15},{18,19},{22,23},{26,27},{30,31}} | collective-permute-start | bytes 3145736 | tf_op jit(solution)/shard_map/ppermute | solution.py:682
  248.1 24.2 %collective-permute-start.17 = (bf16[1024,512]{1,0:T(8,128)(2,1)}, bf16[1024,512]{1,0:T(8,128)(2,1)S(1)}, u32[]{:S(2)}, u32[]{:S(2)}) collective-permute-start(bf16[1024,512]{1,0:T(8,128)(2,1)} %collective-permute-done.9.refs_1_), channel_id=1, source_target_pairs={{1,2},{2,3},{5,6},{6,7},{9,10},{10,11},{13,14},{14,15},{17,18},{18... | collective-permute-start | bytes 3145736 | tf_op jit(solution)/shard_map/ppermute | solution.py:682
  252.5 19.8 %collective-permute-start.18 = (bf16[1024,512]{1,0:T(8,128)(2,1)}, bf16[1024,512]{1,0:T(8,128)(2,1)S(1)}, u32[]{:S(2)}, u32[]{:S(2)}) collective-permute-start(bf16[1024,512]{1,0:T(8,128)(2,1)} %collective-permute-done.10.refs_4_), channel_id=1, source_target_pairs={{2,1},{1,0},{6,5},{5,4},{10,9},{9,8},{14,13},{13,12},{18,17},{17,1... | collective-permute-start | bytes 3145736 | tf_op jit(solution)/shard_map/ppermute | solution.py:682
  272.3 30.7 %collective-permute-start.19 = (bf16[1024,512]{1,0:T(8,128)(2,1)S(1)}, bf16[1024,512]{1,0:T(8,128)(2,1)}, u32[]{:S(2)}, u32[]{:S(2)}) collective-permute-start(bf16[1024,512]{1,0:T(8,128)(2,1)S(1)} %collective-permute-done.17.refs_2_), channel_id=1, source_target_pairs={{2,3},{6,7},{10,11},{14,15},{18,19},{22,23},{26,27},{30,31}} | collective-permute-start | bytes 3145736 | tf_op jit(solution)/shard_map/ppermute | solution.py:682
  276.9 26.2 %collective-permute-start.20 = (bf16[1024,512]{1,0:T(8,128)(2,1)S(1)}, bf16[1024,512]{1,0:T(8,128)(2,1)}, u32[]{:S(2)}, u32[]{:S(2)}) collective-permute-start(bf16[1024,512]{1,0:T(8,128)(2,1)S(1)} %collective-permute-done.18.refs_5_), channel_id=1, source_target_pairs={{1,0},{5,4},{9,8},{13,12},{17,16},{21,20},{25,24},{29,28}} | collective-permute-start | bytes 3145736 | tf_op jit(solution)/shard_map/ppermute | solution.py:682
  334.0 70.5 %collective-permute-start.21 = (bf16[256,2048]{1,0:T(8,128)(2,1)}, bf16[256,2048]{1,0:T(8,128)(2,1)S(1)}, u32[]{:S(2)}, u32[]{:S(2)}) collective-permute-start(bf16[256,2048]{1,0:T(8,128)(2,1)} %two_grad.2), channel_id=1, source_target_pairs={{0,1},{1,2},{2,3},{3,0},{4,5},{5,6},{6,7},{7,4},{8,9},{9,10},{10,1... | collective-permute-start | bytes 3145736 | tf_op jit(solution)/shard_map/ppermute | solution.py:697
  359.9 44.6 %collective-permute-start.22 = (bf16[256,2048]{1,0:T(8,128)(2,1)}, bf16[256,2048]{1,0:T(8,128)(2,1)}, u32[]{:S(2)}, u32[]{:S(2)}) collective-permute-start(bf16[256,2048]{1,0:T(8,128)(2,1)} %get-tuple-element.145), channel_id=1, source_target_pairs={{0,2},{1,3},{2,0},{3,1},{4,6},{5,7},{6,4},{7,5},{8,10},{9,11},{10,... | collective-permute-start | bytes 3145736 | tf_op jit(solution)/shard_map/ppermute | solution.py:697
  359.9 55.7 %collective-permute-start.23 = (bf16[256,2048]{1,0:T(8,128)(2,1)}, bf16[256,2048]{1,0:T(8,128)(2,1)}, u32[]{:S(2)}, u32[]{:S(2)}) collective-permute-start(bf16[256,2048]{1,0:T(8,128)(2,1)} %get-tuple-element.146), channel_id=1, source_target_pairs={{0,3},{1,0},{2,1},{3,2},{4,7},{5,4},{6,5},{7,6},{8,11},{9,8},{10,9... | collective-permute-start | bytes 3145736 | tf_op jit(solution)/shard_map/ppermute | solution.py:697
  415.7 284.9 %reduce-scatter.5.cloned.1.call-start = ((), (), s32[]{:S(2)}) async-start(), calls=%async_computation.9 | async-start | bytes 9437184 | tf_op jit(solution)/shard_map/reduce_scatter | solution.py:882
  418.5 27.0 %collective-permute-start.25 = (bf16[256,2048]{1,0:T(8,128)(2,1)S(1)}, bf16[256,2048]{1,0:T(8,128)(2,1)S(1)}, u32[]{:S(2)}, u32[]{:S(2)}) collective-permute-start(bf16[256,2048]{1,0:T(8,128)(2,1)S(1)} %add_convert_fusion.4.refs_0_), channel_id=1, source_target_pairs={{3,2},{2,1},{1,0},{7,6},{6,5},{5,4},{11,10},{10,9},{9,8},{15,14},{... | collective-permute-start | bytes 3145736 | tf_op jit(solution)/shard_map/ppermute | solution.py:682
  422.9 24.7 %collective-permute-start.24 = (bf16[256,2048]{1,0:T(8,128)(2,1)S(1)}, bf16[256,2048]{1,0:T(8,128)(2,1)S(1)}, u32[]{:S(2)}, u32[]{:S(2)}) collective-permute-start(bf16[256,2048]{1,0:T(8,128)(2,1)S(1)} %add_convert_fusion.4.refs_0_), channel_id=1, source_target_pairs={{0,1},{1,2},{2,3},{4,5},{5,6},{6,7},{8,9},{9,10},{10,11},{12,13},{... | collective-permute-start | bytes 3145736 | tf_op jit(solution)/shard_map/ppermute | solution.py:682
  447.5 24.6 %collective-permute-start.26 = (bf16[256,2048]{1,0:T(8,128)(2,1)S(1)}, bf16[256,2048]{1,0:T(8,128)(2,1)S(1)}, u32[]{:S(2)}, u32[]{:S(2)}) collective-permute-start(bf16[256,2048]{1,0:T(8,128)(2,1)S(1)} %collective-permute-done.24.refs_1_), channel_id=1, source_target_pairs={{1,2},{2,3},{5,6},{6,7},{9,10},{10,11},{13,14},{14,15},{17,18},{18... | collective-permute-start | bytes 3145736 | tf_op jit(solution)/shard_map/ppermute | solution.py:682
  451.4 22.0 %collective-permute-start.27 = (bf16[256,2048]{1,0:T(8,128)(2,1)S(1)}, bf16[256,2048]{1,0:T(8,128)(2,1)S(1)}, u32[]{:S(2)}, u32[]{:S(2)}) collective-permute-start(bf16[256,2048]{1,0:T(8,128)(2,1)S(1)} %collective-permute-done.25.refs_4_), channel_id=1, source_target_pairs={{2,1},{1,0},{6,5},{5,4},{10,9},{9,8},{14,13},{13,12},{18,17},{17,1... | collective-permute-start | bytes 3145736 | tf_op jit(solution)/shard_map/ppermute | solution.py:682
  453.8 19.6 %collective-permute-start.28 = (bf16[1024,512]{1,0:T(8,128)(2,1)}, bf16[1024,512]{1,0:T(8,128)(2,1)S(1)}, u32[]{:S(2)}, u32[]{:S(2)}) collective-permute-start(bf16[1024,512]{1,0:T(8,128)(2,1)} %get-tuple-element.175), channel_id=1, source_target_pairs={{0,1},{4,5},{8,9},{12,13},{16,17},{20,21},{24,25},{28,29}} | collective-permute-start | bytes 3145736 | tf_op jit(solution)/shard_map/ppermute | solution.py:868
  454.5 24.0 %collective-permute-start.29 = (bf16[1024,512]{1,0:T(8,128)(2,1)}, bf16[1024,512]{1,0:T(8,128)(2,1)S(1)}, u32[]{:S(2)}, u32[]{:S(2)}) collective-permute-start(bf16[1024,512]{1,0:T(8,128)(2,1)} %get-tuple-element.173), channel_id=1, source_target_pairs={{3,2},{7,6},{11,10},{15,14},{19,18},{23,22},{27,26},{31,30}} | collective-permute-start | bytes 3145736 | tf_op jit(solution)/shard_map/ppermute | solution.py:868
  480.3 23.3 %collective-permute-start.33 = (bf16[1024,512]{1,0:T(8,128)(2,1)S(1)}, bf16[1024,512]{1,0:T(8,128)(2,1)S(1)}, u32[]{:S(2)}, u32[]{:S(2)}) collective-permute-start(bf16[1024,512]{1,0:T(8,128)(2,1)S(1)} %get-tuple-element.217), channel_id=1, source_target_pairs={{3,2},{2,1},{7,6},{6,5},{11,10},{10,9},{15,14},{14,13},{19,18},{18... | collective-permute-start | bytes 3145736 | tf_op jit(solution)/shard_map/ppermute | solution.py:868
  482.4 23.2 %collective-permute-start.32 = (bf16[1024,512]{1,0:T(8,128)(2,1)S(1)}, bf16[1024,512]{1,0:T(8,128)(2,1)S(1)}, u32[]{:S(2)}, u32[]{:S(2)}) collective-permute-start(bf16[1024,512]{1,0:T(8,128)(2,1)S(1)} %get-tuple-element.218), channel_id=1, source_target_pairs={{0,1},{1,2},{4,5},{5,6},{8,9},{9,10},{12,13},{13,14},{16,17},{17,1... | collective-permute-start | bytes 3145736 | tf_op jit(solution)/shard_map/ppermute | solution.py:868
  483.7 21.9 %collective-permute-start.30 = (bf16[256,2048]{1,0:T(8,128)(2,1)S(1)}, bf16[256,2048]{1,0:T(8,128)(2,1)S(1)}, u32[]{:S(2)}, u32[]{:S(2)}) collective-permute-start(bf16[256,2048]{1,0:T(8,128)(2,1)S(1)} %collective-permute-done.26.refs_2_), channel_id=1, source_target_pairs={{2,3},{6,7},{10,11},{14,15},{18,19},{22,23},{26,27},{30,31}} | collective-permute-start | bytes 3145736 | tf_op jit(solution)/shard_map/ppermute | solution.py:682
  487.2 19.4 %collective-permute-start.31 = (bf16[256,2048]{1,0:T(8,128)(2,1)S(1)}, bf16[256,2048]{1,0:T(8,128)(2,1)}, u32[]{:S(2)}, u32[]{:S(2)}) collective-permute-start(bf16[256,2048]{1,0:T(8,128)(2,1)S(1)} %collective-permute-done.27.refs_5_), channel_id=1, source_target_pairs={{1,0},{5,4},{9,8},{13,12},{17,16},{21,20},{25,24},{29,28}} | collective-permute-start | bytes 3145736 | tf_op jit(solution)/shard_map/ppermute | solution.py:682
  507.9 57.6 %collective-permute-start.35 = (bf16[1024,512]{1,0:T(8,128)(2,1)}, bf16[1024,512]{1,0:T(8,128)(2,1)S(1)}, u32[]{:S(2)}, u32[]{:S(2)}) collective-permute-start(bf16[1024,512]{1,0:T(8,128)(2,1)} %add_convert_fusion.2), channel_id=1, source_target_pairs={{3,2},{2,1},{1,0},{7,6},{6,5},{5,4},{11,10},{10,9},{9,8},{15,14},{... | collective-permute-start | bytes 3145736 | tf_op jit(solution)/shard_map/ppermute | solution.py:868
  511.7 53.8 %collective-permute-start.34 = (bf16[1024,512]{1,0:T(8,128)(2,1)}, bf16[1024,512]{1,0:T(8,128)(2,1)S(1)}, u32[]{:S(2)}, u32[]{:S(2)}) collective-permute-start(bf16[1024,512]{1,0:T(8,128)(2,1)} %add_convert_fusion.3), channel_id=1, source_target_pairs={{0,1},{1,2},{2,3},{4,5},{5,6},{6,7},{8,9},{9,10},{10,11},{12,13},{... | collective-permute-start | bytes 3145736 | tf_op jit(solution)/shard_map/ppermute | solution.py:868
  583.4 67.9 %collective-permute-start.36 = (bf16[1024,512]{1,0:T(8,128)(2,1)}, bf16[1024,512]{1,0:T(8,128)(2,1)}, u32[]{:S(2)}, u32[]{:S(2)}) collective-permute-start(bf16[1024,512]{1,0:T(8,128)(2,1)} %get-tuple-element.183), channel_id=1, source_target_pairs={{0,2},{1,3},{2,0},{3,1},{4,6},{5,7},{6,4},{7,5},{8,10},{9,11},{10,... | collective-permute-start | bytes 3145736 | tf_op jit(solution)/shard_map/ppermute | solution.py:697
  585.8 89.7 %collective-permute-start.37 = (bf16[1024,512]{1,0:T(8,128)(2,1)}, bf16[1024,512]{1,0:T(8,128)(2,1)}, u32[]{:S(2)}, u32[]{:S(2)}) collective-permute-start(bf16[1024,512]{1,0:T(8,128)(2,1)} %get-tuple-element.184), channel_id=1, source_target_pairs={{0,1},{1,2},{2,3},{3,0},{4,5},{5,6},{6,7},{7,4},{8,9},{9,10},{10,1... | collective-permute-start | bytes 3145736 | tf_op jit(solution)/shard_map/ppermute | solution.py:697
  586.1 89.4 %collective-permute-start.38 = (bf16[1024,512]{1,0:T(8,128)(2,1)}, bf16[1024,512]{1,0:T(8,128)(2,1)}, u32[]{:S(2)}, u32[]{:S(2)}) collective-permute-start(bf16[1024,512]{1,0:T(8,128)(2,1)} %get-tuple-element.185), channel_id=1, source_target_pairs={{0,3},{1,0},{2,1},{3,2},{4,7},{5,4},{6,5},{7,6},{8,11},{9,8},{10,9... | collective-permute-start | bytes 3145736 | tf_op jit(solution)/shard_map/ppermute | solution.py:697
  588.3 87.2 %copy-start.15 = (bf16[1024,512]{1,0:T(8,128)(2,1)S(1)}, bf16[1024,512]{1,0:T(8,128)(2,1)}, u32[]{:S(2)}) copy-start(bf16[1024,512]{1,0:T(8,128)(2,1)} %get-tuple-element.189) | copy-start | bytes 3145732
  682.2 39.5 %all-to-all-start.2 = ((bf16[8,128,1024]{2,1,0:T(8,128)(2,1)}), bf16[8,128,1024]{2,1,0:T(8,128)(2,1)S(1)}, u32[]{:S(2)}, u32[]{:S(2)}) async-start(bf16[8,128,1024]{2,1,0:T(8,128)(2,1)} %bitcast.46), calls=%async_computation.2 | async-start | bytes 4194304 | tf_op jit(solution)/shard_map/all_to_all | solution.py:766
  (34 other events, 837.6 us)
Sparse Core Ops, SparseCore 0:
  10.5 58.5 all-gather.5
  71.0 65.6 all-gather.3
  138.6 125.3 all-gather.7
  415.8 166.0 reduce-scatter.2
  585.2 82.3 reduce-scatter.4

commit v4 on v3

--- a/solution.py
+++ b/solution.py
@@ -100,11 +100,12 @@
 
 
 def norm_kernel(me_ref, *refs):
-    *come_refs, rows_ref, normed_ref = refs
+    *come_refs, rows_ref, normed_ref, inverse_ref = refs
     size = len(come_refs) // 2 + 1
     rows = jnp.concatenate([picked(me_ref[0], j, come_refs) for j in range(size)], axis=1)
     rows_ref[...] = rows
-    normed_ref[...] = norm_parts(rows.astype(f32))[0].astype(bf16)
+    unit, inverse_ref[...] = norm_parts(rows.astype(f32))
+    normed_ref[...] = unit.astype(bf16)
 
 
 def gathered_norm(me, own, arrived):
@@ -119,9 +120,13 @@
             num_scalar_prefetch=1,
             grid=(count // BLOCK,),
             in_specs=[pl.BlockSpec((BLOCK, width), here)] * len(operands),
-            out_specs=[pl.BlockSpec((BLOCK, model), here)] * 2,
-        ),
-        out_shape=[out, out],
+            out_specs=[
+                pl.BlockSpec((BLOCK, model), here),
+                pl.BlockSpec((BLOCK, model), here),
+                pl.BlockSpec((BLOCK, 1), here),
+            ],
+        ),
+        out_shape=[out, out, jax.ShapeDtypeStruct((count, 1), f32)],
         compiler_params=params(),
         cost_estimate=cost(20 * count * model, 8 * count * model),
         name="gathered_norm",
@@ -179,6 +184,9 @@
     return exponent * (1.0 / jnp.sum(exponent, axis=-1, keepdims=True))
 
 
+PAIR = 2 * HEAD_DIM
+
+
 def attend_kernel(q_ref, k_ref, v_ref, column_ref, row_ref, out_ref):
     block = pl.program_id(1)
     for index in range(k_ref.shape[0] // BLOCK):
@@ -186,38 +194,43 @@
         @pl.when(block == index)
         def _(index=index):
             seen = (index + 1) * BLOCK
-            prob = masked_softmax(
-                q_ref[...], k_ref[:seen, :], column_ref[...], row_ref[:, :seen], index * BLOCK
-            )
-            out_ref[...] = matmul(prob.astype(bf16), v_ref[:seen, :]).astype(bf16)
+            for first in range(0, PAIR, HEAD_DIM):
+                head = slice(first, first + HEAD_DIM)
+                prob = masked_softmax(
+                    q_ref[:, head],
+                    k_ref[:seen, head],
+                    column_ref[...],
+                    row_ref[:, :seen],
+                    index * BLOCK,
+                )
+                out_ref[:, head] = matmul(prob.astype(bf16), v_ref[:seen, head]).astype(bf16)
 
 
 def attend(qkv, segment):
-    count = qkv[0].shape[0]
-    heads = qkv[0].shape[1] // HEAD_DIM
+    count, local = qkv[0].shape
+    column = lambda h, i: (0, h)
     return pl.pallas_call(
         attend_kernel,
-        grid=(heads, count // BLOCK),
+        grid=(local // PAIR, count // BLOCK),
         in_specs=[
-            pl.BlockSpec((BLOCK, HEAD_DIM), lambda h, i: (i, h)),
-            pl.BlockSpec((count, HEAD_DIM), lambda h, i: (0, h)),
-            pl.BlockSpec((count, HEAD_DIM), lambda h, i: (0, h)),
+            pl.BlockSpec((BLOCK, PAIR), lambda h, i: (i, h)),
+            pl.BlockSpec((count, PAIR), column),
+            pl.BlockSpec((count, PAIR), column),
             pl.BlockSpec((BLOCK, 1), lambda h, i: (i, 0)),
             pl.BlockSpec((1, count), lambda h, i: (0, 0)),
         ],
-        out_specs=pl.BlockSpec((BLOCK, HEAD_DIM), lambda h, i: (i, h)),
-        out_shape=jax.ShapeDtypeStruct((count, heads * HEAD_DIM), bf16),
-        compiler_params=params(),
-        cost_estimate=cost(
-            4 * heads * count * count * HEAD_DIM, 8 * count * heads * HEAD_DIM, heads * count * count
-        ),
+        out_specs=pl.BlockSpec((BLOCK, PAIR), lambda h, i: (i, h)),
+        out_shape=jax.ShapeDtypeStruct((count, local), bf16),
+        compiler_params=params(),
+        cost_estimate=cost(4 * count * count * local, 8 * count * local, count * count * 4),
         name="attend",
-    )(*qkv, segment[:, None], segment[None, :])
+    )(*qkv, *segment)
 
 
 def attend_back_kernel(
-    q_ref, k_ref, v_ref, grad_ref, column_ref, row_ref, cos_ref, sin_ref, dq_ref, dk_ref, dv_ref, total
+    me_ref, q_ref, k_ref, v_ref, column_ref, row_ref, cos_ref, sin_ref, *refs
 ):
+    *grad_refs, dq_ref, dk_ref, dv_ref, total = refs
     block = pl.program_id(1)
     scale = HEAD_DIM ** (-0.5)
     blocks = k_ref.shape[0] // BLOCK
@@ -231,58 +244,72 @@
         @pl.when(block == index)
         def _(index=index):
             seen = (index + 1) * BLOCK
-            q_rows, k_rows, grad = q_ref[...], k_ref[:seen, :], grad_ref[...]
-            prob = masked_softmax(
-                q_rows, k_rows, column_ref[...], row_ref[:, :seen], index * BLOCK
-            )
-            prob_grad = times_transposed(grad, v_ref[:seen, :])
-            delta = jnp.sum(prob_grad * prob, axis=-1, keepdims=True)
-            score_grad = (prob * (prob_grad - delta)).astype(bf16)
-            total[0, index * BLOCK : seen, :] = matmul(score_grad, k_rows) * scale
-            total[1, :seen, :] += transposed_times(score_grad, q_rows) * scale
-            total[2, :seen, :] += transposed_times(prob.astype(bf16), grad)
+            grads = picked(me_ref[0], index, grad_refs)
+            for first in range(0, PAIR, HEAD_DIM):
+                head = slice(first, first + HEAD_DIM)
+                q_rows, k_rows, grad = q_ref[:, head], k_ref[:seen, head], grads[:, head]
+                prob = masked_softmax(
+                    q_rows, k_rows, column_ref[...], row_ref[:, :seen], index * BLOCK
+                )
+                prob_grad = times_transposed(grad, v_ref[:seen, head])
+                delta = jnp.sum(prob_grad * prob, axis=-1, keepdims=True)
+                score_grad = (prob * (prob_grad - delta)).astype(bf16)
+                total[0, index * BLOCK : seen, head] = matmul(score_grad, k_rows) * scale
+                total[1, :seen, head] += transposed_times(score_grad, q_rows) * scale
+                total[2, :seen, head] += transposed_times(prob.astype(bf16), grad)
 
     @pl.when(block == blocks - 1)
     def _():
         for part, out_ref in enumerate((dq_ref, dk_ref, dv_ref)):
-            piece = total[part]
-            if part < 2:
-                piece = piece * cos_ref[...] - half_turn(piece) * sin_ref[...]
-            out_ref[...] = piece.astype(bf16)
-
-
-def attend_back(qkv, grad, segment, cosine, sine):
-    count = qkv[0].shape[0]
-    heads = qkv[0].shape[1] // HEAD_DIM
+            for first in range(0, PAIR, HEAD_DIM):
+                head = slice(first, first + HEAD_DIM)
+                piece = total[part, :, head]
+                if part < 2:
+                    piece = piece * cos_ref[...] - half_turn(piece) * sin_ref[...]
+                out_ref[:, head] = piece.astype(bf16)
+
+
+def attend_back(me, qkv, grads, segment, cosine, sine):
+    count, local = qkv[0].shape
+    whole = lambda h, i, me: (0, 0)
+    column = lambda h, i, me: (0, h)
     return pl.pallas_call(
         attend_back_kernel,
-        grid=(heads, count // BLOCK),
-        in_specs=[
-            pl.BlockSpec((BLOCK, HEAD_DIM), lambda h, i: (i, h)),
-            pl.BlockSpec((count, HEAD_DIM), lambda h, i: (0, h)),
-            pl.BlockSpec((count, HEAD_DIM), lambda h, i: (0, h)),
-            pl.BlockSpec((BLOCK, HEAD_DIM), lambda h, i: (i, h)),
-            pl.BlockSpec((BLOCK, 1), lambda h, i: (i, 0)),
-            pl.BlockSpec((1, count), lambda h, i: (0, 0)),
-            pl.BlockSpec((count, HEAD_DIM), lambda h, i: (0, 0)),
-            pl.BlockSpec((count, HEAD_DIM), lambda h, i: (0, 0)),
-        ],
-        out_specs=[pl.BlockSpec((count, HEAD_DIM), lambda h, i: (0, h))] * 3,
-        out_shape=[jax.ShapeDtypeStruct(qkv[0].shape, bf16)] * 3,
-        scratch_shapes=[pltpu.VMEM((3, count, HEAD_DIM), f32)],
+        grid_spec=pltpu.PrefetchScalarGridSpec(
+            num_scalar_prefetch=1,
+            grid=(local // PAIR, count // BLOCK),
+            in_specs=[
+                pl.BlockSpec((BLOCK, PAIR), lambda h, i, me: (i, h)),
+                pl.BlockSpec((count, PAIR), column),
+                pl.BlockSpec((count, PAIR), column),
+                pl.BlockSpec((BLOCK, 1), lambda h, i, me: (i, 0)),
+                pl.BlockSpec((1, count), whole),
+                pl.BlockSpec((count, HEAD_DIM), whole),
+                pl.BlockSpec((count, HEAD_DIM), whole),
+                *[pl.BlockSpec((BLOCK, PAIR), column)] * len(grads),
+            ],
+            out_specs=[pl.BlockSpec((count, PAIR), column)] * 3,
+            scratch_shapes=[pltpu.VMEM((3, count, PAIR), f32)],
+        ),
+        out_shape=[jax.ShapeDtypeStruct((count, local), bf16)] * 3,
         compiler_params=params(),
         cost_estimate=cost(1000, 1000),
         name="attend_back",
-    )(*qkv, grad, segment[:, None], segment[None, :], cosine, sine)
+    )(me, *qkv, *segment, cosine, sine, *grads)
 
 
 def hidden_kernel(me_ref, weight_ref, rows_ref, *refs):
-    *come_refs, hidden_ref, normed_ref = refs
+    *come_refs, hidden_ref, normed_ref, inverse_ref = refs
     size = len(come_refs) // 2 + 1
     attended = jnp.concatenate([picked(me_ref[0], j, come_refs) for j in range(size)], axis=1)
     hidden = rows_ref[...].astype(f32) + matmul(attended, weight_ref[...])
-    hidden_ref[...] = hidden
-    normed_ref[...] = norm_parts(hidden)[0].astype(bf16)
+    width = hidden_ref.shape[1]
+    own = hidden[:, :width]
+    for piece in range(1, size):
+        own = jnp.where(me_ref[0] == piece, hidden[:, piece * width : (piece + 1) * width], own)
+    hidden_ref[...] = own
+    unit, inverse_ref[...] = norm_parts(hidden)
+    normed_ref[...] = unit.astype(bf16)
 
 
 def hidden_and_norm(me, own, arrived, weight, rows):
@@ -299,11 +326,16 @@
                 pl.BlockSpec((BLOCK, model), here),
                 *[pl.BlockSpec((BLOCK, own.shape[1]), here)] * len(operands),
             ],
-            out_specs=[pl.BlockSpec((BLOCK, model), here)] * 2,
+            out_specs=[
+                pl.BlockSpec((BLOCK, own.shape[1]), here),
+                pl.BlockSpec((BLOCK, model), here),
+                pl.BlockSpec((BLOCK, 1), here),
+            ],
         ),
         out_shape=[
-            jax.ShapeDtypeStruct((count, model), f32),
+            jax.ShapeDtypeStruct(own.shape, f32),
             jax.ShapeDtypeStruct((count, model), bf16),
+            jax.ShapeDtypeStruct((count, 1), f32),
         ],
         compiler_params=params(),
         cost_estimate=cost(2 * count * model * model, 2 * model * model + 10 * count * model),
@@ -433,8 +465,8 @@
     )(order, act, weights)
 
 
-def norm_back(values_in, grad_in):
-    unit_rows, inverse = norm_parts(values_in)
+def norm_back(unit_rows, inverse, grad_in):
+    unit_rows = unit_rows.astype(f32)
     return inverse * (
         grad_in
         - jnp.mean(grad_in, axis=-1, keepdims=True)
@@ -451,26 +483,26 @@
 
 
 def two_grad_kernel(order_ref, *refs):
-    pieces = (len(refs) - 3) // 4
-    row_refs = refs[: 3 * pieces]
-    gate_ref, up_ref = refs[3 * pieces : 3 * pieces + 2]
-    out_refs, total = refs[3 * pieces + 2 : -1], refs[-1]
+    pieces = (len(refs) - 3) // 5
+    row_refs = refs[: 4 * pieces]
+    gate_ref, up_ref = refs[4 * pieces : 4 * pieces + 2]
+    out_refs, total = refs[4 * pieces + 2 : -1], refs[-1]
     step = pl.program_id(0)
     columns = pl.ds(pl.multiple_of(step * WIDE, WIDE), WIDE)
     for piece in range(pieces):
         total[piece, :, columns] = times_transposed(
-            row_refs[3 * piece][...], gate_ref[0]
-        ) + times_transposed(row_refs[3 * piece + 1][...], up_ref[0])
+            row_refs[4 * piece][...], gate_ref[0]
+        ) + times_transposed(row_refs[4 * piece + 1][...], up_ref[0])
 
     @pl.when(step == pl.num_programs(0) - 1)
     def _():
         for piece in range(pieces):
             out_refs[piece][...] = norm_back(
-                row_refs[3 * piece + 2][...], total[piece]
+                row_refs[4 * piece + 2][...], row_refs[4 * piece + 3][...], total[piece]
             ).astype(bf16)
 
 
-def two_grad_pieces(order, dgate, dup, weights, hidden, quarter):
+def two_grad_pieces(order, dgate, dup, weights, normed, inverse, quarter):
     pieces = order.shape[0]
     hidden_units = dgate.shape[1]
     model = weights.shape[1]
@@ -479,6 +511,7 @@
         here = lambda j, order, p=p: (order[p], 0)
         rows += [pl.BlockSpec((quarter, hidden_units), here)] * 2
         rows += [pl.BlockSpec((quarter, model), here, pipeline_mode=pl.Buffered(1))]
+        rows += [pl.BlockSpec((quarter, 1), here, pipeline_mode=pl.Buffered(1))]
     return pl.pallas_call(
         two_grad_kernel,
         grid_spec=pltpu.PrefetchScalarGridSpec(
@@ -498,58 +531,20 @@
             4 * pieces * quarter * model * hidden_units, 4 * model * hidden_units
         ),
         name="two_grad",
-    )(order, *([dgate, dup, hidden] * pieces), weights, weights)
-
-
-def att_grad_kernel(me_ref, weight_ref, *refs):
-    *come_refs, whole_ref, out_ref = refs
-    rows = picked(me_ref[0], pl.program_id(0), come_refs)
-    whole_ref[...] = rows
-    out_ref[...] = times_transposed(rows, weight_ref[...]).astype(bf16)
-
-
-def att_grad_rows(me, own, arrived, weight, local):
-    operands = flat(own, arrived)
-    share, model = own.shape
-    size = len(operands) // 2 + 1
-    here = lambda i, me: (i, 0)
-    once = pl.Buffered(1)
-    return pl.pallas_call(
-        att_grad_kernel,
-        grid_spec=pltpu.PrefetchScalarGridSpec(
-            num_scalar_prefetch=1,
-            grid=(size,),
-            in_specs=[
-                pl.BlockSpec((local, model), lambda i, me: (me[0], 0), pipeline_mode=once),
-                *[pl.BlockSpec((share, model), lambda i, me: (0, 0), pipeline_mode=once)]
-                * len(operands),
-            ],
-            out_specs=[
-                pl.BlockSpec((share, model), here),
-                pl.BlockSpec((share, local), here),
-            ],
-        ),
-        out_shape=[
-            jax.ShapeDtypeStruct((share * size, model), bf16),
-            jax.ShapeDtypeStruct((share * size, local), bf16),
-        ],
-        compiler_params=params(),
-        cost_estimate=cost(1000, 1000),
-        name="att_grad",
-    )(me, weight, *operands)
-
-
-def one_grad_kernel(place_ref, dq_ref, dk_ref, dv_ref, weight_ref, rows_ref, *out_refs):
+    )(order, *([dgate, dup, normed, inverse] * pieces), weights, weights)
+
+
+def one_grad_kernel(place_ref, dq_ref, dk_ref, dv_ref, weight_ref, unit_ref, inv_ref, *out_refs):
     columns = jnp.concatenate([dq_ref[...], dk_ref[...], dv_ref[...]], axis=1)
     grad = norm_back(
-        rows_ref[...].astype(f32), times_transposed(columns, weight_ref[...])
+        unit_ref[...], inv_ref[...], times_transposed(columns, weight_ref[...])
     ).astype(bf16)
     width = out_refs[0].shape[1]
     for piece in range(len(out_refs)):
         put_at(place_ref[piece], grad[:, piece * width : (piece + 1) * width], out_refs)
 
 
-def one_grad_pieces(place, grads, weight, rows):
+def one_grad_pieces(place, grads, weight, rows, inverse):
     count, local = grads[0].shape
     columns = 3 * local
     pieces = place.shape[0]
@@ -566,6 +561,7 @@
                     (model, columns), lambda i, place: (0, 0), pipeline_mode=pl.Buffered(1)
                 ),
                 pl.BlockSpec((BLOCK, model), here),
+                pl.BlockSpec((BLOCK, 1), here),
             ],
             out_specs=[pl.BlockSpec((BLOCK, model // pieces), here)] * pieces,
         ),
@@ -575,7 +571,7 @@
             2 * count * model * columns, 2 * columns * model + 6 * count * columns
         ),
         name="one_grad",
-    )(place, *grads, weight, rows)
+    )(place, *grads, weight, rows, inverse)
 
 
 def att_grads_kernel(normed_ref, dq_ref, dk_ref, dv_ref, att_ref, hidden_ref, out_ref):
@@ -687,6 +683,12 @@
     for step in range(len(arrived) + 1, size):
         arrived.append(line_step(arrived[-1] if arrived else (block, block), axis, size, step))
     return arrived
+
+
+def line_whole(own, arrived, axis, size):
+    me = lax.axis_index(axis)
+    low, high = [pair[0] for pair in arrived], [pair[1] for pair in arrived]
+    return [pick(me, owner, own, low, high) for owner in range(size)]
 
 
 def far_first(size):
@@ -793,16 +795,20 @@
     buffer_rows = matmul(place_in, came_rows[:, :width]).astype(bf16)
     buffer_grads = matmul(place_in, over_fsdp(after(sent_grads, buffer_rows))).astype(bf16)
     rows_come = chain_gather(buffer_rows, "tp", shards)
-    *last, first_grads = lax.optimization_barrier((*rows_come[-1], buffer_grads))
-    rows_come[-1] = tuple(last)
-    me = own_shard[None].astype(jnp.int32)
-
     list_index = jnp.sum(jnp.where(deal == own_group, jnp.arange(groups, dtype=jnp.int32), 0))
     lengths = lax.dynamic_index_in_dim(seq_lengths, list_index, 0, keepdims=False)
     segment, position = segments(lengths)
     cosine, sine = rope_tables(position, head_dim)
-
-    full_rows, normed_one = gathered_norm(me, buffer_rows, rows_come)
+    segment_column, segment_row = segment[:, None], segment[None, :]
+    rows_come[-1], first_grads, segment_column, segment_row, cosine, sine = (
+        lax.optimization_barrier(
+            (rows_come[-1], buffer_grads, segment_column, segment_row, cosine, sine)
+        )
+    )
+    segment = (segment_column, segment_row)
+    me = own_shard[None].astype(jnp.int32)
+
+    full_rows, normed_one, inverse_one = gathered_norm(me, buffer_rows, rows_come)
     first_grads, normed_one = lax.optimization_barrier((first_grads, normed_one))
     grads_begun = line_step((first_grads, first_grads), "tp", shards, 1)
     qkv = project_qkv(normed_one, full_qkv, cosine, sine)
@@ -812,7 +818,7 @@
     *grads_begun, last_low, last_high = lax.optimization_barrier((*grads_begun, *att_come[-1]))
     att_come[-1] = (last_low, last_high)
     grads_come = [grads_begun, line_step(grads_begun, "tp", shards, 2)]
-    hidden, normed_two = hidden_and_norm(me, attended, att_come, full_out, full_rows)
+    hidden, normed_two, inverse_two = hidden_and_norm(me, attended, att_come, full_out, full_rows)
     *grads_come[1], normed_two = lax.optimization_barrier((*grads_come[1], normed_two))
     grads_come = chain_gather(first_grads, "tp", shards, grads_come)
     gate, up, activated = mlp_up(normed_two, full_mlp)
@@ -828,17 +834,15 @@
     def rows_of(rows, owner):
         return lax.dynamic_slice_in_dim(rows, owner * quarter, quarter, 0)
 
-    near = [steps[1], steps[0], *steps[2:], 0]
-    near_order = jnp.stack([lax.rem(own_shard + step, shards) for step in near])
     two_first = two_grad_pieces(
-        near_order[:1], gate_grad, up_grad, full_mlp, hidden, quarter
+        order[:1], gate_grad, up_grad, full_mlp, normed_two, inverse_two, quarter
     )
     two_rest = two_grad_pieces(
-        near_order[1:], gate_grad, after(up_grad, *two_first), full_mlp, hidden, quarter
+        order[1:], gate_grad, after(up_grad, *two_first), full_mlp, normed_two, inverse_two, quarter
     )
     two_came = [
         sent_on(term, "tp", shards, step)
-        for term, step in zip((*two_first, *two_rest), near[:-1])
+        for term, step in zip((*two_first, *two_rest), steps)
     ]
     grad_mlp = mlp_grads(0, [normed_two], [after(gate_grad, *two_rest)])
     grad_mlp = mlp_grads(1, [normed_two], [up_grad], grad_mlp)
@@ -849,6 +853,19 @@
         rows_of(full_grads, own_shard).astype(f32) + two_rest[-1].astype(f32), two_came
     ).astype(bf16)
     back_come = [line_step((back_low, back_low), "tp", shards, 1)]
+    own_out = lax.dynamic_slice_in_dim(full_out, own_shard * local_width, local_width, 0)
+
+    def att_piece(block):
+        return times_transposed(block, own_out).astype(bf16)
+
+    def merged(step):
+        low, high = back_come[step - 1]
+        if 2 * step < shards:
+            return low, high
+        both = jnp.where(own_shard >= step, low, high)
+        return both, both
+
+    att_pieces = [att_piece(back_low)]
     terms = mlp_pieces(around, after(activated, grad_mlp, back_low), full_mlp, width)
     mlp_come = []
     for step in range(1, shards):
@@ -857,6 +874,7 @@
         )
         if step < shards - 1:
             back_come.append(line_step(back_come[-1], "tp", shards, step + 1))
+            att_pieces += [att_piece(block) for block in merged(step)]
         low, high = terms[shards - step], terms[step]
         if mlp_come:
             low, high = (
@@ -866,12 +884,20 @@
         up = [(i, i + 1) for i in range(step)]
         down = [(i, i - 1) for i in range(shards - 1, shards - 1 - step, -1)]
         mlp_come = [lax.ppermute(low, "tp", up), lax.ppermute(high, "tp", down)]
-    full_hidden_grad, attended_grad = att_grad_rows(
-        me, back_low, back_come, full_out, local_width
-    )
-    qkv_grad = attend_back(qkv, attended_grad, segment, cosine, sine)
-    one_terms = one_grad_pieces(place, qkv_grad, full_qkv, full_rows)
+    att_pieces += [att_piece(block) for block in merged(shards - 1)]
+    qkv_grad = attend_back(
+        me,
+        qkv,
+        [att_pieces[0], *att_pieces[1::2], *att_pieces[2::2]],
+        segment,
+        cosine,
+        sine,
+    )
+    one_terms = one_grad_pieces(place, qkv_grad, full_qkv, normed_one, inverse_one)
     one_came = [sent_on(term, "tp", shards, step) for term, step in zip(one_terms, steps)]
+    full_hidden_grad = jnp.concatenate(
+        line_whole(after(back_low, *one_terms[:3]), back_come, "tp", shards), axis=0
+    )
     *mlp_come, late_grad, _ = lax.optimization_barrier(
         (*mlp_come, tuple(qkv_grad), tuple(one_terms[:3]))
     )
@@ -881,9 +907,6 @@
     sum_mlp, grad_att = lax.optimization_barrier((sum_mlp, grad_att))
     sum_att = lax.psum_scatter(grad_att, "fsdp", scatter_dimension=0, tiled=False)
 
-    output_here = added(
-        features_of(hidden, own_shard) + terms[0].astype(f32), mlp_come
-    )
     sum_att = sum_att.astype(f32)
     out_part = sum_att[:, 3 * local_width :]
     out_pieces = model // out_part.shape[1]
@@ -894,6 +917,7 @@
     sum_gate, sum_up, sum_down = sum_mlp.astype(f32)
     back_here = added(one_terms[-1].astype(f32), one_came)
     input_here = features_of(full_hidden_grad, own_shard).astype(f32) + back_here
+    output_here = hidden + added(terms[0].astype(f32), mlp_come)
     here = jnp.concatenate([output_here.astype(bf16), input_here.astype(bf16)], axis=1)
     sent_back = transposed_times(place_in, here).astype(bf16)
     sums = (

time: 744 us -> 725 us (0.974)
  Pallas kernels: 262 us -> 243 us
  matrix products: 13.5 us -> 27.6 us
  waiting for transfers between devices: 283 us -> 269 us
    ppermute x12, waiting for transfers between devices: 68.7 us -> 5.23 us  [line_step(): lax.ppermute(from_high, axis, down)]
    ppermute x12, waiting for transfers between devices: 60.9 us -> 114 us  [line_step(): lax.ppermute(from_low, axis, up)]
    pallas_call x3 -> x2, Pallas kernels: 48.6 us -> 31.9 us  [the longest x1 19.8 us: attend_back(): pl.pallas_call(attend_back_kernel, grid_spec=pltpu.PrefetchScalarGridSpec...]
    ppermute x12, starting transfers between devices: 27.6 us -> 43 us  [line_step(): lax.ppermute(from_high, axis, down)]
    ppermute x12, starting transfers between devices: 45.7 us -> 30.9 us  [line_step(): lax.ppermute(from_low, axis, up)]
    dot_general x0 -> x5, matrix products: none -> 14.2 us  [times_transposed(): lax.dot_general(left, right, (((1,), (1,)), ((), ())), preferred_element_...]
    ppermute x6, waiting for transfers between devices: 21.8 us -> 10.9 us  [on_device(): mlp_come = [lax.ppermute(low, 'tp', up), lax.ppermute(high, 'tp', down)]]
    all_to_all x3, starting transfers between devices: 20.5 us -> 11.3 us  [over_fsdp(): return lax.all_to_all(rows, 'fsdp', split_axis=0, concat_axis=0, tiled=True)]
  transfers between devices with their start and end apart: 47 -> 47, of which waited for: 21 -> 20; matrix products, arithmetic and copies ran while one was open for 7% -> 9% of each run, Pallas kernels for 32% -> 30%
where the time goes in v4:
time: 725 us; the launch traced here: 715 us
  waiting for transfers between devices  269 us (37%)
  Pallas kernels  243 us (34%)
  starting transfers between devices  113 us (16%)
  other arithmetic  35.5 us (5%)
  matrix products  27.6 us (4%)
  between operations  17 us (2%)
  local copies, waits for them, and re-layouts  9.53 us (1%)
    ppermute x12, waiting for transfers between devices, line_step(): lax.ppermute(from_low, axis, up)  114 us
    ppermute x9, waiting for transfers between devices, sent_on(): lax.ppermute(term, axis, [(i, (i + step) % size) for i in range(size)])  103 us
    ppermute x12, starting transfers between devices, line_step(): lax.ppermute(from_high, axis, down)  43 us
    pallas_call x3, Pallas kernels, mlp_grads(): pl.pallas_call(body, grid=(model // BLOCK,), in_specs=specs, out_specs=pl...  42.4 us
    pallas_call x2, Pallas kernels, two_grad_pieces(): pl.pallas_call(two_grad_kernel, grid_spec=pltpu.PrefetchScalarGridSpec(nu...  35.6 us
    all_to_all x3, waiting for transfers between devices, over_fsdp(): return lax.all_to_all(rows, 'fsdp', split_axis=0, concat_axis=0, tiled=True)  34.8 us
    ppermute x12, starting transfers between devices, line_step(): lax.ppermute(from_low, axis, up)  30.9 us
    pallas_call x1, Pallas kernels, mlp_up(): pl.pallas_call(up_kernel, grid=(hidden_units // WIDE,), in_specs=[pl.Bloc...  24 us
  transfers between devices with their start and end apart: 47, of which 20 were waited for; matrix products, arithmetic and copies ran while one was open for 9% of the time, Pallas kernels for 30%

profile of v4, /device:TPU:16, one launch (start us, length us, event | category | flops | bytes accessed | tf_op | source)
XLA Modules:
  0.0 715.2 jit_solution(10044004299310987261)
XLA Ops:
  13.1 3.9 all-to-all-start
  20.3 3.7 pad_maximum_fusion.1
  26.3 17.3 %all-to-all-done = bf16[8,128,640]{2,1,0:T(8,128)(2,1)S(1)} async-done(((bf16[8,128,640]{2,1,0:T(8,128)(2,1)}), bf16[8,128,640]{2,1,0:T(8,128)(2,1)S(1)}, u32[]{:S(2)}, u32[]{:S(2)}) %all-to-all-start) | async-done | bytes 1310752 | tf_op jit(solution)/shard_map/all_to_all | solution.py:768
  48.9 3.5 collective-permute-start.3
  54.7 19.3 %collective-permute-done.3.refs_1_ = bf16[1024,512]{1,0:T(8,128)(2,1)S(1)} collective-permute-done((bf16[1024,512]{1,0:T(8,128)(2,1)S(1)}, bf16[1024,512]{1,0:T(8,128)(2,1)S(1)}, u32[]{:S(2)}, u32[]{:S(2)}) %collective-permute-start.3) | collective-permute-done | bytes 1048608 | tf_op jit(solution)/shard_map/ppermute | solution.py:678
  74.1 3.4 collective-permute-start.4
  77.5 4.4 collective-permute-start.7
  84.6 3.8 all-to-all-start.1
  88.7 10.5 %collective-permute-done.4.refs_2_ = bf16[1024,512]{1,0:T(8,128)(2,1)} collective-permute-done((bf16[1024,512]{1,0:T(8,128)(2,1)S(1)}, bf16[1024,512]{1,0:T(8,128)(2,1)}, u32[]{:S(2)}, u32[]{:S(2)}) %collective-permute-start.4) | collective-permute-done | bytes 1048608 | tf_op jit(solution)/shard_map/ppermute | solution.py:678
  99.2 3.5 collective-permute-start.5
  109.0 11.9 %collective-permute-done.5.refs_3_ = bf16[1024,512]{1,0:T(8,128)(2,1)} collective-permute-done((bf16[1024,512]{1,0:T(8,128)(2,1)}, bf16[1024,512]{1,0:T(8,128)(2,1)}, u32[]{:S(2)}, u32[]{:S(2)}) %collective-permute-start.5) | collective-permute-done | bytes 1048608 | tf_op jit(solution)/shard_map/ppermute | solution.py:678
  120.9 7.8 %gathered_norm.1 = (bf16[1024,2048]{1,0:T(8,128)(2,1)}, bf16[1024,2048]{1,0:T(8,128)(2,1)}, f32[1024,1]{1,0:T(8,128)}) custom-call(s32[1]{0:T(128)} %bitcast.6.me_ref, bf16[1024,512]{1,0:T(8,128)(2,1)} %copy-done.13, bf16[1024,512]{1,0:T(8,128)(2,1)} %copy-done.14, bf16[1024,512]{1,0:T(8,128)(2,1)} %collective-permute-done.4.refs_2_, ...), custom_call_target="tpu_custom_call" | custom-call | flops 41943040 | bytes 16777216 | tf_op jit(solution)/shard_map/gathered_norm/pallas_call | solution.py:117
  128.7 8.4 %collective-permute-start.10 = (bf16[1024,512]{1,0:T(8,128)(2,1)S(1)}, bf16[1024,512]{1,0:T(8,128)(2,1)S(1)}, u32[]{:S(2)}, u32[]{:S(2)}) collective-permute-start(bf16[1024,512]{1,0:T(8,128)(2,1)S(1)} %fusion.25.refs_0_), channel_id=1, source_target_pairs={{3,2},{2,1},{1,0},{7,6},{6,5},{5,4},{11,10},{10,9},{9,8},{15,14},{... | collective-permute-start | bytes 3145736 | tf_op jit(solution)/shard_map/ppermute | solution.py:678
  140.1 13.7 %qkv.1 = (bf16[1024,512]{1,0:T(8,128)(2,1)}, bf16[1024,512]{1,0:T(8,128)(2,1)}, bf16[1024,512]{1,0:T(8,128)(2,1)}) custom-call(bf16[1024,2048]{1,0:T(8,128)(2,1)} %get-tuple-element.122.rows_ref.unit_ref.normed_ref, bf16[2048,1536]{1,0:T(8,128)(2,1)} %all-gather.6.cloned.1.call-done.wq_ref.wk_ref.wv_ref.weight_ref, ...), custom_call_target="tpu_custom_call" | custom-call | flops 6442450944 | bytes 10485760 | tf_op jit(solution)/shard_map/qkv/pallas_call | solution.py:160
  153.8 12.0 %attend.1.refs_0_.att_ref = bf16[1024,512]{1,0:T(8,128)(2,1)} custom-call(bf16[1024,512]{1,0:T(8,128)(2,1)} %get-tuple-element.125.q_ref, bf16[1024,512]{1,0:T(8,128)(2,1)} %get-tuple-element.126.k_ref, bf16[1024,512]{1,0:T(8,128)(2,1)} %get-tuple-element.127.v_ref, s32[1024,1]{1,0:T(8,128)} %copy.27.column_ref, s32[1,1024]{1,0:T(1,128)} %bitcast.53), custom_call_target="tpu_custom_call" | custom-call | flops 2147483648 | bytes 4194304 | tf_op jit(solution)/shard_map/attend/pallas_call | solution.py:212
  167.8 4.3 collective-permute-start.14
  172.1 18.1 %collective-permute-done.11.refs_1_ = bf16[1024,512]{1,0:T(8,128)(2,1)S(1)} collective-permute-done((bf16[1024,512]{1,0:T(8,128)(2,1)}, bf16[1024,512]{1,0:T(8,128)(2,1)S(1)}, u32[]{:S(2)}, u32[]{:S(2)}) %collective-permute-start.11) | collective-permute-done | bytes 1048608 | tf_op jit(solution)/shard_map/ppermute | solution.py:678
  192.2 4.3 collective-permute-start.15
  196.4 16.6 %collective-permute-done.12.refs_2_ = bf16[1024,512]{1,0:T(8,128)(2,1)S(1)} collective-permute-done((bf16[1024,512]{1,0:T(8,128)(2,1)S(1)}, bf16[1024,512]{1,0:T(8,128)(2,1)S(1)}, u32[]{:S(2)}, u32[]{:S(2)}) %collective-permute-start.12) | collective-permute-done | bytes 1048608 | tf_op jit(solution)/shard_map/ppermute | solution.py:678
  216.4 17.6 %collective-permute-done.13.refs_3_ = bf16[1024,512]{1,0:T(8,128)(2,1)S(1)} collective-permute-done((bf16[1024,512]{1,0:T(8,128)(2,1)S(1)}, bf16[1024,512]{1,0:T(8,128)(2,1)S(1)}, u32[]{:S(2)}, u32[]{:S(2)}) %collective-permute-start.13) | collective-permute-done | bytes 1048608 | tf_op jit(solution)/shard_map/ppermute | solution.py:678
  234.0 4.4 collective-permute-start.17
  238.4 5.7 collective-permute-start.18
  244.8 17.9 %hidden.1 = (f32[1024,512]{1,0:T(8,128)}, bf16[1024,2048]{1,0:T(8,128)(2,1)}, f32[1024,1]{1,0:T(8,128)}) custom-call(s32[1]{0:T(128)} %bitcast.6.me_ref, bf16[2048,2048]{1,0:T(8,128)(2,1)} %bitcast.58, bf16[1024,2048]{1,0:T(8,128)(2,1)} %get-tuple-element.119.rows_ref, bf16[1024,512]{1,0:T(8,128)(2,1)} %attend.1.refs_0_.att_ref, ...), custom_call_target="tpu_custom_call" | custom-call | flops 8589934592 | bytes 29360128 | tf_op jit(solution)/shard_map/hidden/pallas_call | solution.py:319
  265.7 24.0 %mlp_up.1 = (bf16[1024,2048]{1,0:T(8,128)(2,1)}, bf16[1024,2048]{1,0:T(8,128)(2,1)}, bf16[1024,2048]{1,0:T(8,128)(2,1)}) custom-call(bf16[1024,2048]{1,0:T(8,128)(2,1)} %get-tuple-element.141.rows_ref.refs_2_.refs_6_.refs_10_.refs_0_, bf16[3,2048,2048]{2,1,0:T(8,128)(2,1)} %all-gather.8.cloned.1.call-done.gate_ref.up_ref.down_ref.refs_4_.refs_5_.refs_12_.refs_13_, ...), custom_call_target="tpu_custom_call" | custom-call | flops 17179869184 | bytes 41943040 | tf_op jit(solution)/shard_map/mlp_up/pallas_call | solution.py:362
  290.8 19.0 %mlp_down_back.1 = (bf16[1024,2048]{1,0:T(8,128)(2,1)}, bf16[1024,2048]{1,0:T(8,128)(2,1)}, bf16[1024,2048]{1,0:T(8,128)(2,1)}) custom-call(s32[1]{0:T(128)} %bitcast.6.me_ref, bf16[3,2048,2048]{2,1,0:T(8,128)(2,1)} %all-gather.8.cloned.1.call-done.gate_ref.up_ref.down_ref.refs_4_.refs_5_.refs_12_.refs_13_, bf16[1024,2048]{1,0:T(8,128)(2,1)} %get-tuple-element.142.gate_in, ...), custom_call_target="tpu_custom_call" | custom-call | flops 8589934592 | bytes 37748736 | tf_op jit(solution)/shard_map/mlp_down_back/pallas_call | solution.py:409
  309.8 11.3 %two_grad.2 = bf16[256,2048]{1,0:T(8,128)(2,1)} custom-call(s32[1]{0:T(128)} %bitcast.19.order_ref, bf16[1024,2048]{1,0:T(8,128)(2,1)} %get-tuple-element.158.refs_0_.refs_4_.refs_8_.refs_1_, bf16[1024,2048]{1,0:T(8,128)(2,1)} %get-tuple-element.153.refs_1_.refs_5_.refs_9_, bf16[1024,2048]{1,0:T(8,128)(2,1)} %get-tuple-element.141.rows_ref.refs_2_.refs_6_.refs_10_.refs_0_, ...), custom_call_target="tpu_custom_call" | custom-call | flops 4294967296 | bytes 16777216 | tf_op jit(solution)/shard_map/two_grad/pallas_call | solution.py:515
  322.5 24.3 %two_grad.3 = (bf16[256,2048]{1,0:T(8,128)(2,1)}, bf16[256,2048]{1,0:T(8,128)(2,1)}, bf16[256,2048]{1,0:T(8,128)(2,1)}) custom-call(s32[3]{0:T(128)} %pad_add_fusion.order_ref, bf16[1024,2048]{1,0:T(8,128)(2,1)} %get-tuple-element.158.refs_0_.refs_4_.refs_8_.refs_1_, bf16[1024,2048]{1,0:T(8,128)(2,1)} %get-tuple-element.153.refs_1_.refs_5_.refs_9_, ...), custom_call_target="tpu_custom_call" | custom-call | flops 12884901888 | bytes 16777216 | tf_op jit(solution)/shard_map/two_grad/pallas_call | solution.py:515
  346.8 3.6 collective-permute-start.22
  350.4 14.2 %mlp_grads.3.refs_2_ = bf16[3,2048,2048]{2,1,0:T(8,128)(2,1)} custom-call(bf16[1024,2048]{1,0:T(8,128)(2,1)} %get-tuple-element.141.rows_ref.refs_2_.refs_6_.refs_10_.refs_0_, bf16[1024,2048]{1,0:T(8,128)(2,1)} %get-tuple-element.158.refs_0_.refs_4_.refs_8_.refs_1_), custom_call_target="tpu_custom_call" | custom-call | flops 8589934592 | bytes 16777216 | tf_op jit(solution)/shard_map/mlp_grads/pallas_call | solution.py:655
  364.5 14.1 %mlp_grads.4.refs_2_ = bf16[3,2048,2048]{2,1,0:T(8,128)(2,1)} custom-call(bf16[1024,2048]{1,0:T(8,128)(2,1)} %get-tuple-element.141.rows_ref.refs_2_.refs_6_.refs_10_.refs_0_, bf16[1024,2048]{1,0:T(8,128)(2,1)} %get-tuple-element.153.refs_1_.refs_5_.refs_9_, bf16[3,2048,2048]{2,1,0:T(8,128)(2,1)} %mlp_grads.3.refs_2_), custom_call_target="tpu_custom_call", output_to_operand_aliasing={{}: (2, {})} | custom-call | flops 8589934592 | bytes 16777216 | tf_op jit(solution)/shard_map/mlp_grads/pallas_call | solution.py:655
  378.6 14.2 %mlp_grads.5 = bf16[3,2048,2048]{2,1,0:T(8,128)(2,1)} custom-call(bf16[1024,2048]{1,0:T(8,128)(2,1)} %get-tuple-element.163.refs_0_.act_ref, bf16[1024,2048]{1,0:T(8,128)(2,1)} %get-tuple-element.149.refs_1_, bf16[3,2048,2048]{2,1,0:T(8,128)(2,1)} %mlp_grads.4.refs_2_), custom_call_target="tpu_custom_call", output_to_operand_aliasing={{}: (2, {})} | custom-call | flops 8589934592 | bytes 16777216 | tf_op jit(solution)/shard_map/mlp_grads/pallas_call | solution.py:655
  392.8 20.4 %collective-permute-done.22 = bf16[256,2048]{1,0:T(8,128)(2,1)S(1)} collective-permute-done((bf16[256,2048]{1,0:T(8,128)(2,1)}, bf16[256,2048]{1,0:T(8,128)(2,1)S(1)}, u32[]{:S(2)}, u32[]{:S(2)}) %collective-permute-start.22) | collective-permute-done | bytes 1048608 | tf_op jit(solution)/shard_map/ppermute | solution.py:699
  423.7 17.2 %mlp_piece.1 = (bf16[1024,512]{1,0:T(8,128)(2,1)}, bf16[1024,512]{1,0:T(8,128)(2,1)}, bf16[1024,512]{1,0:T(8,128)(2,1)}, bf16[1024,512]{1,0:T(8,128)(2,1)}) custom-call(s32[4]{0:T(128)} %pad_add_fusion.1.order_ref, bf16[1024,2048]{1,0:T(8,128)(2,1)} %get-tuple-element.163.refs_0_.act_ref, ...), custom_call_target="tpu_custom_call" | custom-call | flops 8589934592 | bytes 8388608 | tf_op jit(solution)/shard_map/mlp_piece/pallas_call | solution.py:448
  441.0 3.4 collective-permute-done.24
  449.3 5.9 collective-permute-start.27
  457.9 15.6 %collective-permute-done.26 = bf16[256,2048]{1,0:T(8,128)(2,1)} collective-permute-done((bf16[256,2048]{1,0:T(8,128)(2,1)}, bf16[256,2048]{1,0:T(8,128)(2,1)}, u32[]{:S(2)}, u32[]{:S(2)}) %collective-permute-start.26) | collective-permute-done | bytes 1048608 | tf_op jit(solution)/shard_map/ppermute | solution.py:678
  475.7 5.8 collective-permute-done.29
  485.0 4.8 collective-permute-start.33
  498.4 3.4 convolution_convert_fusion.3.refs_1_
  504.7 3.5 collective-permute-done.32
  519.4 19.8 %attend_back.1 = (bf16[1024,512]{1,0:T(8,128)(2,1)}, bf16[1024,512]{1,0:T(8,128)(2,1)}, bf16[1024,512]{1,0:T(8,128)(2,1)}) custom-call(s32[1]{0:T(128)} %bitcast.6.me_ref, bf16[1024,512]{1,0:T(8,128)(2,1)} %get-tuple-element.125.q_ref, bf16[1024,512]{1,0:T(8,128)(2,1)} %get-tuple-element.126.k_ref, bf16[1024,512]{1,0:T(8,128)(2,1)} %get-tuple-element.127.v_ref, ...), custom_call_target="tpu_custom_call" | custom-call | flops 1000 | bytes 1000 | tf_op jit(solution)/shard_map/attend_back/pallas_call | solution.py:276
  539.3 15.9 %one_grad.1 = (bf16[1024,512]{1,0:T(8,128)(2,1)}, bf16[1024,512]{1,0:T(8,128)(2,1)}, bf16[1024,512]{1,0:T(8,128)(2,1)}, bf16[1024,512]{1,0:T(8,128)(2,1)}) custom-call(s32[4]{0:T(128)} %pad_add_fusion.2.place_ref, bf16[1024,512]{1,0:T(8,128)(2,1)} %get-tuple-element.200.dq_ref, bf16[1024,512]{1,0:T(8,128)(2,1)} %get-tuple-element.201.dk_ref, ...), custom_call_target="tpu_custom_call" | custom-call | flops 6442450944 | bytes 15728640 | tf_op jit(solution)/shard_map/one_grad/pallas_call | solution.py:553
  560.8 17.6 %att_grads.1 = bf16[8,256,2048]{2,1,0:T(8,128)(2,1)} custom-call(bf16[1024,2048]{1,0:T(8,128)(2,1)} %get-tuple-element.122.rows_ref.unit_ref.normed_ref, bf16[1024,512]{1,0:T(8,128)(2,1)} %get-tuple-element.200.dq_ref, bf16[1024,512]{1,0:T(8,128)(2,1)} %get-tuple-element.201.dk_ref, bf16[1024,512]{1,0:T(8,128)(2,1)} %get-tuple-element.202.dv_ref, ...), custom_call_target="tpu_custom_call" | custom-call | flops 1000 | bytes 1000 | tf_op jit(solution)/shard_map/att_grads/pallas_call | solution.py:612
  583.9 60.5 %collective-permute-done.36 = bf16[1024,512]{1,0:T(8,128)(2,1)S(1)} collective-permute-done((bf16[1024,512]{1,0:T(8,128)(2,1)}, bf16[1024,512]{1,0:T(8,128)(2,1)S(1)}, u32[]{:S(2)}, u32[]{:S(2)}) %collective-permute-start.36) | collective-permute-done | bytes 1048608 | tf_op jit(solution)/shard_map/ppermute | solution.py:699
  644.3 22.1 %collective-permute-done.37 = bf16[1024,512]{1,0:T(8,128)(2,1)S(1)} collective-permute-done((bf16[1024,512]{1,0:T(8,128)(2,1)}, bf16[1024,512]{1,0:T(8,128)(2,1)S(1)}, u32[]{:S(2)}, u32[]{:S(2)}) %collective-permute-start.37) | collective-permute-done | bytes 1048608 | tf_op jit(solution)/shard_map/ppermute | solution.py:699
  670.8 3.7 fusion.15
  674.5 3.6 all-to-all-start.2
  687.3 17.5 %all-to-all-done.2 = bf16[8,128,1024]{2,1,0:T(8,128)(2,1)S(1)} async-done(((bf16[8,128,1024]{2,1,0:T(8,128)(2,1)}), bf16[8,128,1024]{2,1,0:T(8,128)(2,1)S(1)}, u32[]{:S(2)}, u32[]{:S(2)}) %all-to-all-start.2) | async-done | bytes 2097184 | tf_op jit(solution)/shard_map/all_to_all | solution.py:768
  (185 shorter events, 117.1 us)
Async XLA Ops:
  7.2 132.9 %all-gather.6.cloned.1.call-start = ((), (), s32[]{:S(2)}) async-start(), calls=%async_computation.6 | async-start | bytes 7077888 | tf_op jit(solution)/shard_map/all_gather | solution.py:774
  13.1 30.5 %all-to-all-start = ((bf16[8,128,640]{2,1,0:T(8,128)(2,1)}), bf16[8,128,640]{2,1,0:T(8,128)(2,1)S(1)}, u32[]{:S(2)}, u32[]{:S(2)}) async-start(bf16[8,128,640]{2,1,0:T(8,128)(2,1)} %bitcast), calls=%async_computation | async-start | bytes 2621440 | tf_op jit(solution)/shard_map/all_to_all | solution.py:768
  17.0 227.8 %all-gather.4.cloned.1.call-start = ((), (), s32[]{:S(2)}) async-start(), calls=%async_computation.5 | async-start | bytes 9437184 | tf_op jit(solution)/shard_map/all_gather | solution.py:792
  17.0 27.2 %collective-permute-start = (bf16[64,2048]{1,0:T(8,128)(2,1)}, bf16[64,2048]{1,0:T(8,128)(2,1)}, u32[]{:S(2)}, u32[]{:S(2)}) collective-permute-start(bf16[64,2048]{1,0:T(8,128)(2,1)} %param.17), channel_id=1, source_target_pairs={{0,1},{1,2},{2,3},{3,0},{4,5},{5,6},{6,7},{7,4},{8,9},{9,10},{10,1... | collective-permute-start | bytes 786440 | tf_op jit(solution)/shard_map/ppermute | solution.py:699
  18.6 25.6 %collective-permute-start.1 = (bf16[64,2048]{1,0:T(8,128)(2,1)}, bf16[64,2048]{1,0:T(8,128)(2,1)}, u32[]{:S(2)}, u32[]{:S(2)}) collective-permute-start(bf16[64,2048]{1,0:T(8,128)(2,1)} %param.17), channel_id=1, source_target_pairs={{0,2},{1,3},{2,0},{3,1},{4,6},{5,7},{6,4},{7,5},{8,10},{9,11},{10,... | collective-permute-start | bytes 786440 | tf_op jit(solution)/shard_map/ppermute | solution.py:699
  19.0 25.3 %collective-permute-start.2 = (bf16[64,2048]{1,0:T(8,128)(2,1)}, bf16[64,2048]{1,0:T(8,128)(2,1)}, u32[]{:S(2)}, u32[]{:S(2)}) collective-permute-start(bf16[64,2048]{1,0:T(8,128)(2,1)} %param.17), channel_id=1, source_target_pairs={{0,3},{1,0},{2,1},{3,2},{4,7},{5,4},{6,5},{7,6},{8,11},{9,8},{10,9... | collective-permute-start | bytes 786440 | tf_op jit(solution)/shard_map/ppermute | solution.py:699
  46.7 219.0 %all-gather.8.cloned.1.call-start = ((), (), s32[]{:S(2)}) async-start(), calls=%async_computation.7 | async-start | bytes 28311552 | tf_op jit(solution)/shard_map/all_gather | solution.py:794
  48.9 25.2 %collective-permute-start.3 = (bf16[1024,512]{1,0:T(8,128)(2,1)S(1)}, bf16[1024,512]{1,0:T(8,128)(2,1)S(1)}, u32[]{:S(2)}, u32[]{:S(2)}) collective-permute-start(bf16[1024,512]{1,0:T(8,128)(2,1)S(1)} %fusion.24.refs_0_), channel_id=1, source_target_pairs={{0,1},{1,2},{2,3},{4,5},{5,6},{6,7},{8,9},{9,10},{10,11},{12,13},{... | collective-permute-start | bytes 3145736 | tf_op jit(solution)/shard_map/ppermute | solution.py:678
  52.4 25.1 %collective-permute-start.6 = (bf16[1024,512]{1,0:T(8,128)(2,1)S(1)}, bf16[1024,512]{1,0:T(8,128)(2,1)}, u32[]{:S(2)}, u32[]{:S(2)}) collective-permute-start(bf16[1024,512]{1,0:T(8,128)(2,1)S(1)} %fusion.24.refs_0_), channel_id=1, source_target_pairs={{3,2},{2,1},{1,0},{7,6},{6,5},{5,4},{11,10},{10,9},{9,8},{15,14},{... | collective-permute-start | bytes 3145736 | tf_op jit(solution)/shard_map/ppermute | solution.py:678
  74.1 25.1 %collective-permute-start.4 = (bf16[1024,512]{1,0:T(8,128)(2,1)S(1)}, bf16[1024,512]{1,0:T(8,128)(2,1)}, u32[]{:S(2)}, u32[]{:S(2)}) collective-permute-start(bf16[1024,512]{1,0:T(8,128)(2,1)S(1)} %collective-permute-done.3.refs_1_), channel_id=1, source_target_pairs={{1,2},{2,3},{5,6},{6,7},{9,10},{10,11},{13,14},{14,15},{17,18},{18... | collective-permute-start | bytes 3145736 | tf_op jit(solution)/shard_map/ppermute | solution.py:678
  77.5 25.3 %collective-permute-start.7 = (bf16[1024,512]{1,0:T(8,128)(2,1)}, bf16[1024,512]{1,0:T(8,128)(2,1)}, u32[]{:S(2)}, u32[]{:S(2)}) collective-permute-start(bf16[1024,512]{1,0:T(8,128)(2,1)} %collective-permute-done.6.refs_4_), channel_id=1, source_target_pairs={{2,1},{1,0},{6,5},{5,4},{10,9},{9,8},{14,13},{13,12},{18,17},{17,1... | collective-permute-start | bytes 3145736 | tf_op jit(solution)/shard_map/ppermute | solution.py:678
  84.6 23.1 %all-to-all-start.1 = ((bf16[8,128,512]{2,1,0:T(8,128)(2,1)}), bf16[8,128,512]{2,1,0:T(8,128)(2,1)S(1)}, u32[]{:S(2)}, u32[]{:S(2)}) async-start(bf16[8,128,512]{2,1,0:T(8,128)(2,1)} %bitcast.12), calls=%async_computation.1 | async-start | bytes 2097152 | tf_op jit(solution)/shard_map/all_to_all | solution.py:768
  88.5 489.9 %reduce-scatter.3.cloned.1.call-start = ((), (), s32[]{:S(2)}) async-start(), calls=%async_computation.8 | async-start | bytes 28311552 | tf_op jit(solution)/shard_map/reduce_scatter | solution.py:851
  99.2 21.7 %collective-permute-start.5 = (bf16[1024,512]{1,0:T(8,128)(2,1)}, bf16[1024,512]{1,0:T(8,128)(2,1)}, u32[]{:S(2)}, u32[]{:S(2)}) collective-permute-start(bf16[1024,512]{1,0:T(8,128)(2,1)} %collective-permute-done.4.refs_2_), channel_id=1, source_target_pairs={{2,3},{6,7},{10,11},{14,15},{18,19},{22,23},{26,27},{30,31}} | collective-permute-start | bytes 3145736 | tf_op jit(solution)/shard_map/ppermute | solution.py:678
  102.7 18.2 %collective-permute-start.8 = (bf16[1024,512]{1,0:T(8,128)(2,1)}, bf16[1024,512]{1,0:T(8,128)(2,1)}, u32[]{:S(2)}, u32[]{:S(2)}) collective-permute-start(bf16[1024,512]{1,0:T(8,128)(2,1)} %collective-permute-done.7.refs_5_), channel_id=1, source_target_pairs={{1,0},{5,4},{9,8},{13,12},{17,16},{21,20},{25,24},{29,28}} | collective-permute-start | bytes 3145736 | tf_op jit(solution)/shard_map/ppermute | solution.py:678
  128.7 37.1 %collective-permute-start.10 = (bf16[1024,512]{1,0:T(8,128)(2,1)S(1)}, bf16[1024,512]{1,0:T(8,128)(2,1)S(1)}, u32[]{:S(2)}, u32[]{:S(2)}) collective-permute-start(bf16[1024,512]{1,0:T(8,128)(2,1)S(1)} %fusion.25.refs_0_), channel_id=1, source_target_pairs={{3,2},{2,1},{1,0},{7,6},{6,5},{5,4},{11,10},{10,9},{9,8},{15,14},{... | collective-permute-start | bytes 3145736 | tf_op jit(solution)/shard_map/ppermute | solution.py:678
  137.1 28.7 %collective-permute-start.9 = (bf16[1024,512]{1,0:T(8,128)(2,1)S(1)}, bf16[1024,512]{1,0:T(8,128)(2,1)}, u32[]{:S(2)}, u32[]{:S(2)}) collective-permute-start(bf16[1024,512]{1,0:T(8,128)(2,1)S(1)} %fusion.25.refs_0_), channel_id=1, source_target_pairs={{0,1},{1,2},{2,3},{4,5},{5,6},{6,7},{8,9},{9,10},{10,11},{12,13},{... | collective-permute-start | bytes 3145736 | tf_op jit(solution)/shard_map/ppermute | solution.py:678
  165.8 96.9 %copy-start.6 = (bf16[1024,512]{1,0:T(8,128)(2,1)}, bf16[1024,512]{1,0:T(8,128)(2,1)S(1)}, u32[]{:S(2)}) copy-start(bf16[1024,512]{1,0:T(8,128)(2,1)S(1)} %collective-permute-done.10.refs_4_) | copy-start | bytes 3145732
  165.9 24.4 %collective-permute-start.11 = (bf16[1024,512]{1,0:T(8,128)(2,1)}, bf16[1024,512]{1,0:T(8,128)(2,1)S(1)}, u32[]{:S(2)}, u32[]{:S(2)}) collective-permute-start(bf16[1024,512]{1,0:T(8,128)(2,1)} %attend.1.refs_0_.att_ref), channel_id=1, source_target_pairs={{0,1},{1,2},{2,3},{4,5},{5,6},{6,7},{8,9},{9,10},{10,11},{12,13},{... | collective-permute-start | bytes 3145736 | tf_op jit(solution)/shard_map/ppermute | solution.py:678
  167.8 24.4 %collective-permute-start.14 = (bf16[1024,512]{1,0:T(8,128)(2,1)}, bf16[1024,512]{1,0:T(8,128)(2,1)S(1)}, u32[]{:S(2)}, u32[]{:S(2)}) collective-permute-start(bf16[1024,512]{1,0:T(8,128)(2,1)} %attend.1.refs_0_.att_ref), channel_id=1, source_target_pairs={{3,2},{2,1},{1,0},{7,6},{6,5},{5,4},{11,10},{10,9},{9,8},{15,14},{... | collective-permute-start | bytes 3145736 | tf_op jit(solution)/shard_map/ppermute | solution.py:678
  190.2 22.8 %collective-permute-start.12 = (bf16[1024,512]{1,0:T(8,128)(2,1)S(1)}, bf16[1024,512]{1,0:T(8,128)(2,1)S(1)}, u32[]{:S(2)}, u32[]{:S(2)}) collective-permute-start(bf16[1024,512]{1,0:T(8,128)(2,1)S(1)} %collective-permute-done.11.refs_1_), channel_id=1, source_target_pairs={{1,2},{2,3},{5,6},{6,7},{9,10},{10,11},{13,14},{14,15},{17,18},{18... | collective-permute-start | bytes 3145736 | tf_op jit(solution)/shard_map/ppermute | solution.py:678
  192.2 23.3 %collective-permute-start.15 = (bf16[1024,512]{1,0:T(8,128)(2,1)S(1)}, bf16[1024,512]{1,0:T(8,128)(2,1)S(1)}, u32[]{:S(2)}, u32[]{:S(2)}) collective-permute-start(bf16[1024,512]{1,0:T(8,128)(2,1)S(1)} %collective-permute-done.14.refs_4_), channel_id=1, source_target_pairs={{2,1},{1,0},{6,5},{5,4},{10,9},{9,8},{14,13},{13,12},{18,17},{17,1... | collective-permute-start | bytes 3145736 | tf_op jit(solution)/shard_map/ppermute | solution.py:678
  213.0 20.9 %collective-permute-start.13 = (bf16[1024,512]{1,0:T(8,128)(2,1)S(1)}, bf16[1024,512]{1,0:T(8,128)(2,1)S(1)}, u32[]{:S(2)}, u32[]{:S(2)}) collective-permute-start(bf16[1024,512]{1,0:T(8,128)(2,1)S(1)} %collective-permute-done.12.refs_2_), channel_id=1, source_target_pairs={{2,3},{6,7},{10,11},{14,15},{18,19},{22,23},{26,27},{30,31}} | collective-permute-start | bytes 3145736 | tf_op jit(solution)/shard_map/ppermute | solution.py:678
  215.4 18.5 %collective-permute-start.16 = (bf16[1024,512]{1,0:T(8,128)(2,1)S(1)}, bf16[1024,512]{1,0:T(8,128)(2,1)S(1)}, u32[]{:S(2)}, u32[]{:S(2)}) collective-permute-start(bf16[1024,512]{1,0:T(8,128)(2,1)S(1)} %collective-permute-done.15.refs_5_), channel_id=1, source_target_pairs={{1,0},{5,4},{9,8},{13,12},{17,16},{21,20},{25,24},{29,28}} | collective-permute-start | bytes 3145736 | tf_op jit(solution)/shard_map/ppermute | solution.py:678
  234.0 28.7 %collective-permute-start.17 = (bf16[1024,512]{1,0:T(8,128)(2,1)}, bf16[1024,512]{1,0:T(8,128)(2,1)S(1)}, u32[]{:S(2)}, u32[]{:S(2)}) collective-permute-start(bf16[1024,512]{1,0:T(8,128)(2,1)} %collective-permute-done.9.refs_1_), channel_id=1, source_target_pairs={{1,2},{2,3},{5,6},{6,7},{9,10},{10,11},{13,14},{14,15},{17,18},{18... | collective-permute-start | bytes 3145736 | tf_op jit(solution)/shard_map/ppermute | solution.py:678
  238.4 24.3 %collective-permute-start.18 = (bf16[1024,512]{1,0:T(8,128)(2,1)S(1)}, bf16[1024,512]{1,0:T(8,128)(2,1)}, u32[]{:S(2)}, u32[]{:S(2)}) collective-permute-start(bf16[1024,512]{1,0:T(8,128)(2,1)S(1)} %collective-permute-done.10.refs_4_), channel_id=1, source_target_pairs={{2,1},{1,0},{6,5},{5,4},{10,9},{9,8},{14,13},{13,12},{18,17},{17,1... | collective-permute-start | bytes 3145736 | tf_op jit(solution)/shard_map/ppermute | solution.py:678
  262.7 27.0 %collective-permute-start.19 = (bf16[1024,512]{1,0:T(8,128)(2,1)S(1)}, bf16[1024,512]{1,0:T(8,128)(2,1)S(1)}, u32[]{:S(2)}, u32[]{:S(2)}) collective-permute-start(bf16[1024,512]{1,0:T(8,128)(2,1)S(1)} %collective-permute-done.17.refs_2_), channel_id=1, source_target_pairs={{2,3},{6,7},{10,11},{14,15},{18,19},{22,23},{26,27},{30,31}} | collective-permute-start | bytes 3145736 | tf_op jit(solution)/shard_map/ppermute | solution.py:678
  264.1 25.7 %collective-permute-start.20 = (bf16[1024,512]{1,0:T(8,128)(2,1)}, bf16[1024,512]{1,0:T(8,128)(2,1)}, u32[]{:S(2)}, u32[]{:S(2)}) collective-permute-start(bf16[1024,512]{1,0:T(8,128)(2,1)} %collective-permute-done.18.refs_5_), channel_id=1, source_target_pairs={{1,0},{5,4},{9,8},{13,12},{17,16},{21,20},{25,24},{29,28}} | collective-permute-start | bytes 3145736 | tf_op jit(solution)/shard_map/ppermute | solution.py:678
  321.1 92.1 %collective-permute-start.21 = (bf16[256,2048]{1,0:T(8,128)(2,1)}, bf16[256,2048]{1,0:T(8,128)(2,1)S(1)}, u32[]{:S(2)}, u32[]{:S(2)}) collective-permute-start(bf16[256,2048]{1,0:T(8,128)(2,1)} %two_grad.2), channel_id=1, source_target_pairs={{0,2},{1,3},{2,0},{3,1},{4,6},{5,7},{6,4},{7,5},{8,10},{9,11},{10,... | collective-permute-start | bytes 3145736 | tf_op jit(solution)/shard_map/ppermute | solution.py:699
  346.8 66.4 %collective-permute-start.22 = (bf16[256,2048]{1,0:T(8,128)(2,1)}, bf16[256,2048]{1,0:T(8,128)(2,1)S(1)}, u32[]{:S(2)}, u32[]{:S(2)}) collective-permute-start(bf16[256,2048]{1,0:T(8,128)(2,1)} %get-tuple-element.155), channel_id=1, source_target_pairs={{0,1},{1,2},{2,3},{3,0},{4,5},{5,6},{6,7},{7,4},{8,9},{9,10},{10,1... | collective-permute-start | bytes 3145736 | tf_op jit(solution)/shard_map/ppermute | solution.py:699
  350.4 62.8 %collective-permute-start.23 = (bf16[256,2048]{1,0:T(8,128)(2,1)}, bf16[256,2048]{1,0:T(8,128)(2,1)}, u32[]{:S(2)}, u32[]{:S(2)}) collective-permute-start(bf16[256,2048]{1,0:T(8,128)(2,1)} %get-tuple-element.156), channel_id=1, source_target_pairs={{0,3},{1,0},{2,1},{3,2},{4,7},{5,4},{6,5},{7,6},{8,11},{9,8},{10,9... | collective-permute-start | bytes 3145736 | tf_op jit(solution)/shard_map/ppermute | solution.py:699
  414.2 269.5 %reduce-scatter.5.cloned.1.call-start = ((), (), s32[]{:S(2)}) async-start(), calls=%async_computation.9 | async-start | bytes 9437184 | tf_op jit(solution)/shard_map/reduce_scatter | solution.py:908
  417.3 27.1 %collective-permute-start.24 = (bf16[256,2048]{1,0:T(8,128)(2,1)S(1)}, bf16[256,2048]{1,0:T(8,128)(2,1)}, u32[]{:S(2)}, u32[]{:S(2)}) collective-permute-start(bf16[256,2048]{1,0:T(8,128)(2,1)S(1)} %add_convert_fusion.4), channel_id=1, source_target_pairs={{0,1},{1,2},{2,3},{4,5},{5,6},{6,7},{8,9},{9,10},{10,11},{12,13},{... | collective-permute-start | bytes 3145736 | tf_op jit(solution)/shard_map/ppermute | solution.py:678
  420.6 26.8 %collective-permute-start.25 = (bf16[256,2048]{1,0:T(8,128)(2,1)S(1)}, bf16[256,2048]{1,0:T(8,128)(2,1)}, u32[]{:S(2)}, u32[]{:S(2)}) collective-permute-start(bf16[256,2048]{1,0:T(8,128)(2,1)S(1)} %add_convert_fusion.4), channel_id=1, source_target_pairs={{3,2},{2,1},{1,0},{7,6},{6,5},{5,4},{11,10},{10,9},{9,8},{15,14},{... | collective-permute-start | bytes 3145736 | tf_op jit(solution)/shard_map/ppermute | solution.py:678
  447.4 26.1 %collective-permute-start.26 = (bf16[256,2048]{1,0:T(8,128)(2,1)}, bf16[256,2048]{1,0:T(8,128)(2,1)}, u32[]{:S(2)}, u32[]{:S(2)}) collective-permute-start(bf16[256,2048]{1,0:T(8,128)(2,1)} %collective-permute-done.24), channel_id=1, source_target_pairs={{1,2},{2,3},{5,6},{6,7},{9,10},{10,11},{13,14},{14,15},{17,18},{18... | collective-permute-start | bytes 3145736 | tf_op jit(solution)/shard_map/ppermute | solution.py:678
  449.3 26.3 %collective-permute-start.27 = (bf16[256,2048]{1,0:T(8,128)(2,1)}, bf16[256,2048]{1,0:T(8,128)(2,1)}, u32[]{:S(2)}, u32[]{:S(2)}) collective-permute-start(bf16[256,2048]{1,0:T(8,128)(2,1)} %collective-permute-done.25), channel_id=1, source_target_pairs={{2,1},{1,0},{6,5},{5,4},{10,9},{9,8},{14,13},{13,12},{18,17},{17,1... | collective-permute-start | bytes 3145736 | tf_op jit(solution)/shard_map/ppermute | solution.py:678
  455.2 20.5 %collective-permute-start.28 = (bf16[1024,512]{1,0:T(8,128)(2,1)}, bf16[1024,512]{1,0:T(8,128)(2,1)S(1)}, u32[]{:S(2)}, u32[]{:S(2)}) collective-permute-start(bf16[1024,512]{1,0:T(8,128)(2,1)} %get-tuple-element.185), channel_id=1, source_target_pairs={{0,1},{4,5},{8,9},{12,13},{16,17},{20,21},{24,25},{28,29}} | collective-permute-start | bytes 3145736 | tf_op jit(solution)/shard_map/ppermute | solution.py:886
  455.9 25.6 %collective-permute-start.29 = (bf16[1024,512]{1,0:T(8,128)(2,1)}, bf16[1024,512]{1,0:T(8,128)(2,1)}, u32[]{:S(2)}, u32[]{:S(2)}) collective-permute-start(bf16[1024,512]{1,0:T(8,128)(2,1)} %get-tuple-element.183), channel_id=1, source_target_pairs={{3,2},{7,6},{11,10},{15,14},{19,18},{23,22},{27,26},{31,30}} | collective-permute-start | bytes 3145736 | tf_op jit(solution)/shard_map/ppermute | solution.py:886
  483.7 24.5 %collective-permute-start.32 = (bf16[1024,512]{1,0:T(8,128)(2,1)S(1)}, bf16[1024,512]{1,0:T(8,128)(2,1)S(1)}, u32[]{:S(2)}, u32[]{:S(2)}) collective-permute-start(bf16[1024,512]{1,0:T(8,128)(2,1)S(1)} %get-tuple-element.232), channel_id=1, source_target_pairs={{0,1},{1,2},{4,5},{5,6},{8,9},{9,10},{12,13},{13,14},{16,17},{17,1... | collective-permute-start | bytes 3145736 | tf_op jit(solution)/shard_map/ppermute | solution.py:886
  485.0 24.7 %collective-permute-start.33 = (bf16[1024,512]{1,0:T(8,128)(2,1)S(1)}, bf16[1024,512]{1,0:T(8,128)(2,1)S(1)}, u32[]{:S(2)}, u32[]{:S(2)}) collective-permute-start(bf16[1024,512]{1,0:T(8,128)(2,1)S(1)} %get-tuple-element.231), channel_id=1, source_target_pairs={{3,2},{2,1},{7,6},{6,5},{11,10},{10,9},{15,14},{14,13},{19,18},{18... | collective-permute-start | bytes 3145736 | tf_op jit(solution)/shard_map/ppermute | solution.py:886
  489.9 21.5 %collective-permute-start.30 = (bf16[256,2048]{1,0:T(8,128)(2,1)}, bf16[256,2048]{1,0:T(8,128)(2,1)S(1)}, u32[]{:S(2)}, u32[]{:S(2)}) collective-permute-start(bf16[256,2048]{1,0:T(8,128)(2,1)} %collective-permute-done.26), channel_id=1, source_target_pairs={{2,3},{6,7},{10,11},{14,15},{18,19},{22,23},{26,27},{30,31}} | collective-permute-start | bytes 3145736 | tf_op jit(solution)/shard_map/ppermute | solution.py:678
  491.3 20.0 %collective-permute-start.31 = (bf16[256,2048]{1,0:T(8,128)(2,1)}, bf16[256,2048]{1,0:T(8,128)(2,1)S(1)}, u32[]{:S(2)}, u32[]{:S(2)}) collective-permute-start(bf16[256,2048]{1,0:T(8,128)(2,1)} %collective-permute-done.27), channel_id=1, source_target_pairs={{1,0},{5,4},{9,8},{13,12},{17,16},{21,20},{25,24},{29,28}} | collective-permute-start | bytes 3145736 | tf_op jit(solution)/shard_map/ppermute | solution.py:678
  511.6 49.1 %collective-permute-start.35 = (bf16[1024,512]{1,0:T(8,128)(2,1)S(1)}, bf16[1024,512]{1,0:T(8,128)(2,1)S(1)}, u32[]{:S(2)}, u32[]{:S(2)}) collective-permute-start(bf16[1024,512]{1,0:T(8,128)(2,1)S(1)} %add_convert_fusion.2), channel_id=1, source_target_pairs={{3,2},{2,1},{1,0},{7,6},{6,5},{5,4},{11,10},{10,9},{9,8},{15,14},{... | collective-permute-start | bytes 3145736 | tf_op jit(solution)/shard_map/ppermute | solution.py:886
  516.3 44.5 %collective-permute-start.34 = (bf16[1024,512]{1,0:T(8,128)(2,1)S(1)}, bf16[1024,512]{1,0:T(8,128)(2,1)}, u32[]{:S(2)}, u32[]{:S(2)}) collective-permute-start(bf16[1024,512]{1,0:T(8,128)(2,1)S(1)} %add_convert_fusion.3), channel_id=1, source_target_pairs={{0,1},{1,2},{2,3},{4,5},{5,6},{6,7},{8,9},{9,10},{10,11},{12,13},{... | collective-permute-start | bytes 3145736 | tf_op jit(solution)/shard_map/ppermute | solution.py:886
  578.4 65.9 %collective-permute-start.36 = (bf16[1024,512]{1,0:T(8,128)(2,1)}, bf16[1024,512]{1,0:T(8,128)(2,1)S(1)}, u32[]{:S(2)}, u32[]{:S(2)}) collective-permute-start(bf16[1024,512]{1,0:T(8,128)(2,1)} %get-tuple-element.193), channel_id=1, source_target_pairs={{0,2},{1,3},{2,0},{3,1},{4,6},{5,7},{6,4},{7,5},{8,10},{9,11},{10,... | collective-permute-start | bytes 3145736 | tf_op jit(solution)/shard_map/ppermute | solution.py:699
  581.6 84.8 %collective-permute-start.37 = (bf16[1024,512]{1,0:T(8,128)(2,1)}, bf16[1024,512]{1,0:T(8,128)(2,1)S(1)}, u32[]{:S(2)}, u32[]{:S(2)}) collective-permute-start(bf16[1024,512]{1,0:T(8,128)(2,1)} %get-tuple-element.194), channel_id=1, source_target_pairs={{0,1},{1,2},{2,3},{3,0},{4,5},{5,6},{6,7},{7,4},{8,9},{9,10},{10,1... | collective-permute-start | bytes 3145736 | tf_op jit(solution)/shard_map/ppermute | solution.py:699
  581.6 85.1 %collective-permute-start.38 = (bf16[1024,512]{1,0:T(8,128)(2,1)}, bf16[1024,512]{1,0:T(8,128)(2,1)S(1)}, u32[]{:S(2)}, u32[]{:S(2)}) collective-permute-start(bf16[1024,512]{1,0:T(8,128)(2,1)} %get-tuple-element.195), channel_id=1, source_target_pairs={{0,3},{1,0},{2,1},{3,2},{4,7},{5,4},{6,5},{7,6},{8,11},{9,8},{10,9... | collective-permute-start | bytes 3145736 | tf_op jit(solution)/shard_map/ppermute | solution.py:699
  674.5 30.2 %all-to-all-start.2 = ((bf16[8,128,1024]{2,1,0:T(8,128)(2,1)}), bf16[8,128,1024]{2,1,0:T(8,128)(2,1)S(1)}, u32[]{:S(2)}, u32[]{:S(2)}) async-start(bf16[8,128,1024]{2,1,0:T(8,128)(2,1)} %bitcast.47), calls=%async_computation.2 | async-start | bytes 4194304 | tf_op jit(solution)/shard_map/all_to_all | solution.py:768
  (33 other events, 644.6 us)
Sparse Core Ops, SparseCore 0:
  10.5 58.5 all-gather.5
  71.0 65.6 all-gather.3
  138.6 125.3 all-gather.7
  413.4 156.8 reduce-scatter.2
  578.5 71.1 reduce-scatter.4

commit v5 on v4

--- a/solution.py
+++ b/solution.py
@@ -62,13 +62,13 @@
     return (segment, row_index - begin_row)
 
 
-VMEM_LIMIT = 58 * 1024 * 1024
+MIB = 1024 * 1024
 BLOCK = 256
 WIDE = 512
 
 
-def params():
-    return pltpu.CompilerParams(vmem_limit_bytes=VMEM_LIMIT)
+def params(mib=58):
+    return pltpu.CompilerParams(vmem_limit_bytes=mib * MIB)
 
 
 def cost(flops, read, transcendentals=0):
@@ -292,7 +292,7 @@
             scratch_shapes=[pltpu.VMEM((3, count, PAIR), f32)],
         ),
         out_shape=[jax.ShapeDtypeStruct((count, local), bf16)] * 3,
-        compiler_params=params(),
+        compiler_params=params(32),
         cost_estimate=cost(1000, 1000),
         name="attend_back",
     )(me, *qkv, *segment, cosine, sine, *grads)
@@ -457,7 +457,7 @@
             out_specs=[pl.BlockSpec((count, width), whole)] * pieces,
         ),
         out_shape=[jax.ShapeDtypeStruct((count, width), bf16)] * pieces,
-        compiler_params=params(),
+        compiler_params=params(32),
         cost_estimate=cost(
             2 * pieces * count * width * hidden_units, 2 * pieces * width * hidden_units
         ),
@@ -566,7 +566,7 @@
             out_specs=[pl.BlockSpec((BLOCK, model // pieces), here)] * pieces,
         ),
         out_shape=[jax.ShapeDtypeStruct((count, model // pieces), bf16)] * pieces,
-        compiler_params=params(),
+        compiler_params=params(32),
         cost_estimate=cost(
             2 * count * model * columns, 2 * columns * model + 6 * count * columns
         ),
@@ -620,7 +620,7 @@
         ],
         out_specs=pl.BlockSpec((1, tall, model), lambda i: (i, 0, 0)),
         out_shape=jax.ShapeDtypeStruct((groups, tall, model), bf16),
-        compiler_params=params(),
+        compiler_params=params(32),
         cost_estimate=cost(1000, 1000),
         name="att_grads",
     )(operand, *qkv_grad, attended, hidden_grad)
@@ -659,7 +659,7 @@
         out_specs=pl.BlockSpec((1, BLOCK, hidden_units), lambda i: (which, i, 0)),
         out_shape=jax.ShapeDtypeStruct((3, model, hidden_units), bf16),
         input_output_aliases=aliases,
-        compiler_params=params(),
+        compiler_params=params(32),
         cost_estimate=cost(
             2 * count * model * hidden_units, 2 * model * hidden_units + 4 * count * model
         ),

time: 725 us -> 718 us (level)
  Pallas kernels: 243 us -> 219 us
  waiting for transfers between devices: 269 us -> 285 us
  local copies, waits for them, and re-layouts: 9.53 us -> 20.7 us
    unnamed x68 -> x122, local copies, waits for them, and re-layouts: 2.22 us -> 13.4 us
    ppermute x9, waiting for transfers between devices: 103 us -> 112 us  [sent_on(): lax.ppermute(term, axis, [(i, (i + step) % size) for i in range(size)])]
  transfers between devices with their start and end apart: 47 -> 47, of which waited for: 20 -> 19; matrix products, arithmetic and copies ran while one was open for 9% -> 8% of each run, Pallas kernels for 30% -> 27%
where the time goes in v5:
time: 718 us; the launch traced here: 712 us
  waiting for transfers between devices  285 us (40%)
  Pallas kernels  219 us (31%)
  starting transfers between devices  113 us (16%)
  other arithmetic  32.1 us (4%)
  matrix products  24.4 us (3%)
  local copies, waits for them, and re-layouts  20.7 us (3%)
  between operations  17.4 us (2%)
    ppermute x12, waiting for transfers between devices, line_step(): lax.ppermute(from_low, axis, up)  118 us
    ppermute x9, waiting for transfers between devices, sent_on(): lax.ppermute(term, axis, [(i, (i + step) % size) for i in range(size)])  112 us
    ppermute x12, starting transfers between devices, line_step(): lax.ppermute(from_high, axis, down)  42.8 us
    pallas_call x3, Pallas kernels, mlp_grads(): pl.pallas_call(body, grid=(model // BLOCK,), in_specs=specs, out_specs=pl...  35.8 us
    pallas_call x2, Pallas kernels, two_grad_pieces(): pl.pallas_call(two_grad_kernel, grid_spec=pltpu.PrefetchScalarGridSpec(nu...  35.6 us
    all_to_all x3, waiting for transfers between devices, over_fsdp(): return lax.all_to_all(rows, 'fsdp', split_axis=0, concat_axis=0, tiled=True)  34.7 us
    ppermute x12, starting transfers between devices, line_step(): lax.ppermute(from_low, axis, up)  30.9 us
    pallas_call x1, Pallas kernels, mlp_up(): pl.pallas_call(up_kernel, grid=(hidden_units // WIDE,), in_specs=[pl.Bloc...  24 us
  transfers between devices with their start and end apart: 47, of which 19 were waited for; matrix products, arithmetic and copies ran while one was open for 8% of the time, Pallas kernels for 27%

profile of v5, /device:TPU:16, one launch (start us, length us, event | category | flops | bytes accessed | tf_op | source)
XLA Modules:
  0.0 711.5 jit_solution(16876074396615939296)
XLA Ops:
  13.1 3.9 all-to-all-start
  20.3 3.7 pad_maximum_fusion.1
  26.3 17.3 %all-to-all-done = bf16[8,128,640]{2,1,0:T(8,128)(2,1)S(1)} async-done(((bf16[8,128,640]{2,1,0:T(8,128)(2,1)}), bf16[8,128,640]{2,1,0:T(8,128)(2,1)S(1)}, u32[]{:S(2)}, u32[]{:S(2)}) %all-to-all-start) | async-done | bytes 1310752 | tf_op jit(solution)/shard_map/all_to_all | solution.py:768
  48.8 3.5 collective-permute-start.3
  54.7 19.3 %collective-permute-done.3.refs_1_ = bf16[1024,512]{1,0:T(8,128)(2,1)S(1)} collective-permute-done((bf16[1024,512]{1,0:T(8,128)(2,1)S(1)}, bf16[1024,512]{1,0:T(8,128)(2,1)S(1)}, u32[]{:S(2)}, u32[]{:S(2)}) %collective-permute-start.3) | collective-permute-done | bytes 1048608 | tf_op jit(solution)/shard_map/ppermute | solution.py:678
  77.4 4.3 collective-permute-start.7
  84.5 3.8 all-to-all-start.1
  88.6 10.5 %collective-permute-done.4.refs_2_ = bf16[1024,512]{1,0:T(8,128)(2,1)} collective-permute-done((bf16[1024,512]{1,0:T(8,128)(2,1)S(1)}, bf16[1024,512]{1,0:T(8,128)(2,1)}, u32[]{:S(2)}, u32[]{:S(2)}) %collective-permute-start.4) | collective-permute-done | bytes 1048608 | tf_op jit(solution)/shard_map/ppermute | solution.py:678
  99.2 3.6 collective-permute-start.5
  109.1 11.8 %collective-permute-done.5.refs_3_ = bf16[1024,512]{1,0:T(8,128)(2,1)} collective-permute-done((bf16[1024,512]{1,0:T(8,128)(2,1)}, bf16[1024,512]{1,0:T(8,128)(2,1)}, u32[]{:S(2)}, u32[]{:S(2)}) %collective-permute-start.5) | collective-permute-done | bytes 1048608 | tf_op jit(solution)/shard_map/ppermute | solution.py:678
  120.9 7.8 %gathered_norm.1 = (bf16[1024,2048]{1,0:T(8,128)(2,1)}, bf16[1024,2048]{1,0:T(8,128)(2,1)}, f32[1024,1]{1,0:T(8,128)}) custom-call(s32[1]{0:T(128)} %bitcast.6.me_ref, bf16[1024,512]{1,0:T(8,128)(2,1)} %copy-done.39, bf16[1024,512]{1,0:T(8,128)(2,1)} %copy-done.40, bf16[1024,512]{1,0:T(8,128)(2,1)} %collective-permute-done.4.refs_2_, ...), custom_call_target="tpu_custom_call" | custom-call | flops 41943040 | bytes 16777216 | tf_op jit(solution)/shard_map/gathered_norm/pallas_call | solution.py:117
  128.7 8.4 %collective-permute-start.10 = (bf16[1024,512]{1,0:T(8,128)(2,1)S(1)}, bf16[1024,512]{1,0:T(8,128)(2,1)S(1)}, u32[]{:S(2)}, u32[]{:S(2)}) collective-permute-start(bf16[1024,512]{1,0:T(8,128)(2,1)S(1)} %fusion.25.refs_0_), channel_id=1, source_target_pairs={{3,2},{2,1},{1,0},{7,6},{6,5},{5,4},{11,10},{10,9},{9,8},{15,14},{... | collective-permute-start | bytes 3145736 | tf_op jit(solution)/shard_map/ppermute | solution.py:678
  140.0 13.7 %qkv.1 = (bf16[1024,512]{1,0:T(8,128)(2,1)}, bf16[1024,512]{1,0:T(8,128)(2,1)}, bf16[1024,512]{1,0:T(8,128)(2,1)}) custom-call(bf16[1024,2048]{1,0:T(8,128)(2,1)} %get-tuple-element.122.rows_ref.unit_ref.normed_ref, bf16[2048,1536]{1,0:T(8,128)(2,1)} %all-gather.6.cloned.1.call-done.wq_ref.wk_ref.wv_ref.weight_ref, ...), custom_call_target="tpu_custom_call" | custom-call | flops 6442450944 | bytes 10485760 | tf_op jit(solution)/shard_map/qkv/pallas_call | solution.py:160
  153.8 12.0 %attend.1.refs_0_.att_ref = bf16[1024,512]{1,0:T(8,128)(2,1)} custom-call(bf16[1024,512]{1,0:T(8,128)(2,1)} %get-tuple-element.125.q_ref, bf16[1024,512]{1,0:T(8,128)(2,1)} %get-tuple-element.126.k_ref, bf16[1024,512]{1,0:T(8,128)(2,1)} %get-tuple-element.127.v_ref, s32[1024,1]{1,0:T(8,128)} %copy.27.column_ref, s32[1,1024]{1,0:T(1,128)} %bitcast.48), custom_call_target="tpu_custom_call" | custom-call | flops 2147483648 | bytes 4194304 | tf_op jit(solution)/shard_map/attend/pallas_call | solution.py:212
  167.7 4.3 collective-permute-start.14
  172.1 18.1 %collective-permute-done.11.refs_1_ = bf16[1024,512]{1,0:T(8,128)(2,1)S(1)} collective-permute-done((bf16[1024,512]{1,0:T(8,128)(2,1)}, bf16[1024,512]{1,0:T(8,128)(2,1)S(1)}, u32[]{:S(2)}, u32[]{:S(2)}) %collective-permute-start.11) | collective-permute-done | bytes 1048608 | tf_op jit(solution)/shard_map/ppermute | solution.py:678
  192.1 4.2 collective-permute-start.15
  196.3 16.7 %collective-permute-done.12.refs_2_ = bf16[1024,512]{1,0:T(8,128)(2,1)S(1)} collective-permute-done((bf16[1024,512]{1,0:T(8,128)(2,1)S(1)}, bf16[1024,512]{1,0:T(8,128)(2,1)S(1)}, u32[]{:S(2)}, u32[]{:S(2)}) %collective-permute-start.12) | collective-permute-done | bytes 1048608 | tf_op jit(solution)/shard_map/ppermute | solution.py:678
  216.3 17.6 %collective-permute-done.13.refs_3_ = bf16[1024,512]{1,0:T(8,128)(2,1)S(1)} collective-permute-done((bf16[1024,512]{1,0:T(8,128)(2,1)S(1)}, bf16[1024,512]{1,0:T(8,128)(2,1)S(1)}, u32[]{:S(2)}, u32[]{:S(2)}) %collective-permute-start.13) | collective-permute-done | bytes 1048608 | tf_op jit(solution)/shard_map/ppermute | solution.py:678
  233.9 4.4 collective-permute-start.17
  238.3 5.6 collective-permute-start.18
  244.6 18.0 %hidden.1 = (f32[1024,512]{1,0:T(8,128)}, bf16[1024,2048]{1,0:T(8,128)(2,1)}, f32[1024,1]{1,0:T(8,128)}) custom-call(s32[1]{0:T(128)} %bitcast.6.me_ref, bf16[2048,2048]{1,0:T(8,128)(2,1)} %bitcast.60, bf16[1024,2048]{1,0:T(8,128)(2,1)} %get-tuple-element.119.rows_ref, bf16[1024,512]{1,0:T(8,128)(2,1)} %attend.1.refs_0_.att_ref, ...), custom_call_target="tpu_custom_call" | custom-call | flops 8589934592 | bytes 29360128 | tf_op jit(solution)/shard_map/hidden/pallas_call | solution.py:319
  265.7 24.0 %mlp_up.1 = (bf16[1024,2048]{1,0:T(8,128)(2,1)}, bf16[1024,2048]{1,0:T(8,128)(2,1)}, bf16[1024,2048]{1,0:T(8,128)(2,1)}) custom-call(bf16[1024,2048]{1,0:T(8,128)(2,1)} %get-tuple-element.141.rows_ref.refs_2_.refs_6_.refs_10_.refs_0_, bf16[3,2048,2048]{2,1,0:T(8,128)(2,1)} %all-gather.8.cloned.1.call-done.gate_ref.up_ref.down_ref.refs_4_.refs_5_.refs_12_.refs_13_, ...), custom_call_target="tpu_custom_call" | custom-call | flops 17179869184 | bytes 41943040 | tf_op jit(solution)/shard_map/mlp_up/pallas_call | solution.py:362
  290.7 18.9 %mlp_down_back.1 = (bf16[1024,2048]{1,0:T(8,128)(2,1)}, bf16[1024,2048]{1,0:T(8,128)(2,1)}, bf16[1024,2048]{1,0:T(8,128)(2,1)}) custom-call(s32[1]{0:T(128)} %bitcast.6.me_ref, bf16[3,2048,2048]{2,1,0:T(8,128)(2,1)} %all-gather.8.cloned.1.call-done.gate_ref.up_ref.down_ref.refs_4_.refs_5_.refs_12_.refs_13_, bf16[1024,2048]{1,0:T(8,128)(2,1)} %get-tuple-element.142.gate_in, ...), custom_call_target="tpu_custom_call" | custom-call | flops 8589934592 | bytes 37748736 | tf_op jit(solution)/shard_map/mlp_down_back/pallas_call | solution.py:409
  309.5 11.3 %two_grad.2 = bf16[256,2048]{1,0:T(8,128)(2,1)} custom-call(s32[1]{0:T(128)} %bitcast.19.order_ref, bf16[1024,2048]{1,0:T(8,128)(2,1)} %get-tuple-element.158.refs_0_.refs_4_.refs_8_.refs_1_, bf16[1024,2048]{1,0:T(8,128)(2,1)} %get-tuple-element.153.refs_1_.refs_5_.refs_9_, bf16[1024,2048]{1,0:T(8,128)(2,1)} %get-tuple-element.141.rows_ref.refs_2_.refs_6_.refs_10_.refs_0_, ...), custom_call_target="tpu_custom_call" | custom-call | flops 4294967296 | bytes 16777216 | tf_op jit(solution)/shard_map/two_grad/pallas_call | solution.py:515
  322.2 24.3 %two_grad.3 = (bf16[256,2048]{1,0:T(8,128)(2,1)}, bf16[256,2048]{1,0:T(8,128)(2,1)}, bf16[256,2048]{1,0:T(8,128)(2,1)}) custom-call(s32[3]{0:T(128)} %pad_add_fusion.order_ref, bf16[1024,2048]{1,0:T(8,128)(2,1)} %get-tuple-element.158.refs_0_.refs_4_.refs_8_.refs_1_, bf16[1024,2048]{1,0:T(8,128)(2,1)} %get-tuple-element.153.refs_1_.refs_5_.refs_9_, ...), custom_call_target="tpu_custom_call" | custom-call | flops 12884901888 | bytes 16777216 | tf_op jit(solution)/shard_map/two_grad/pallas_call | solution.py:515
  346.5 3.6 collective-permute-start.22
  352.3 11.9 %mlp_grads.3.refs_2_ = bf16[3,2048,2048]{2,1,0:T(8,128)(2,1)} custom-call(bf16[1024,2048]{1,0:T(8,128)(2,1)S(1)} %copy-done.2, bf16[1024,2048]{1,0:T(8,128)(2,1)S(1)} %copy-done.4), custom_call_target="tpu_custom_call" | custom-call | flops 8589934592 | bytes 16777216 | tf_op jit(solution)/shard_map/mlp_grads/pallas_call | solution.py:655
  364.2 11.9 %mlp_grads.4.refs_2_ = bf16[3,2048,2048]{2,1,0:T(8,128)(2,1)} custom-call(bf16[1024,2048]{1,0:T(8,128)(2,1)S(1)} %copy-done.2, bf16[1024,2048]{1,0:T(8,128)(2,1)S(1)} %copy-done.3, bf16[3,2048,2048]{2,1,0:T(8,128)(2,1)} %mlp_grads.3.refs_2_), custom_call_target="tpu_custom_call", output_to_operand_aliasing={{}: (2, {})} | custom-call | flops 8589934592 | bytes 16777216 | tf_op jit(solution)/shard_map/mlp_grads/pallas_call | solution.py:655
  376.2 11.9 %mlp_grads.5 = bf16[3,2048,2048]{2,1,0:T(8,128)(2,1)} custom-call(bf16[1024,2048]{1,0:T(8,128)(2,1)S(1)} %copy-done.11, bf16[1024,2048]{1,0:T(8,128)(2,1)S(1)} %copy-done.8, bf16[3,2048,2048]{2,1,0:T(8,128)(2,1)} %mlp_grads.4.refs_2_), custom_call_target="tpu_custom_call", output_to_operand_aliasing={{}: (2, {})} | custom-call | flops 8589934592 | bytes 16777216 | tf_op jit(solution)/shard_map/mlp_grads/pallas_call | solution.py:655
  388.1 25.0 %collective-permute-done.22 = bf16[256,2048]{1,0:T(8,128)(2,1)} collective-permute-done((bf16[256,2048]{1,0:T(8,128)(2,1)}, bf16[256,2048]{1,0:T(8,128)(2,1)}, u32[]{:S(2)}, u32[]{:S(2)}) %collective-permute-start.22) | collective-permute-done | bytes 1048608 | tf_op jit(solution)/shard_map/ppermute | solution.py:699
  422.1 12.3 %mlp_piece.1 = (bf16[1024,512]{1,0:T(8,128)(2,1)S(1)}, bf16[1024,512]{1,0:T(8,128)(2,1)S(1)}, bf16[1024,512]{1,0:T(8,128)(2,1)S(1)}, bf16[1024,512]{1,0:T(8,128)(2,1)S(1)}) custom-call(s32[4]{0:T(128)S(1)} %pad_add_fusion.1.order_ref, bf16[1024,2048]{1,0:T(8,128)(2,1)S(1)} %copy-done.12, ...), custom_call_target="tpu_custom_call" | custom-call | flops 8589934592 | bytes 8388608 | tf_op jit(solution)/shard_map/mlp_piece/pallas_call | solution.py:448
  436.3 6.9 collective-permute-done.24
  448.2 5.9 collective-permute-start.27
  457.2 15.2 %collective-permute-done.26 = bf16[256,2048]{1,0:T(8,128)(2,1)} collective-permute-done((bf16[256,2048]{1,0:T(8,128)(2,1)}, bf16[256,2048]{1,0:T(8,128)(2,1)}, u32[]{:S(2)}, u32[]{:S(2)}) %collective-permute-start.26) | collective-permute-done | bytes 1048608 | tf_op jit(solution)/shard_map/ppermute | solution.py:678
  474.5 6.5 collective-permute-done.29
  485.0 4.8 collective-permute-start.33
  502.2 5.9 collective-permute-done.32
  515.4 3.4 collective-permute-start.34
  519.0 17.2 %attend_back.1 = (bf16[1024,512]{1,0:T(8,128)(2,1)S(1)}, bf16[1024,512]{1,0:T(8,128)(2,1)S(1)}, bf16[1024,512]{1,0:T(8,128)(2,1)S(1)}) custom-call(s32[1]{0:T(128)} %bitcast.6.me_ref, bf16[1024,512]{1,0:T(8,128)(2,1)S(1)} %copy-done.16, bf16[1024,512]{1,0:T(8,128)(2,1)S(1)} %copy-done.17, bf16[1024,512]{1,0:T(8,128)(2,1)S(1)} %copy-done.18, ...), custom_call_target="tpu_custom_call" | custom-call | flops 1000 | bytes 1000 | tf_op jit(solution)/shard_map/attend_back/pallas_call | solution.py:276
  536.2 10.5 %one_grad.1 = (bf16[1024,512]{1,0:T(8,128)(2,1)S(1)}, bf16[1024,512]{1,0:T(8,128)(2,1)S(1)}, bf16[1024,512]{1,0:T(8,128)(2,1)S(1)}, bf16[1024,512]{1,0:T(8,128)(2,1)S(1)}) custom-call(s32[4]{0:T(128)S(1)} %pad_add_fusion.2.place_ref, bf16[1024,512]{1,0:T(8,128)(2,1)S(1)} %get-tuple-element.200.dq_ref, bf16[1024,512]{1,0:T(8,128)(2,1)S(1)} %get-tuple-element.201.dk_ref, ...), custom_call_target="tpu_custom_call" | custom-call | flops 6442450944 | bytes 15728640 | tf_op jit(solution)/shard_map/one_grad/pallas_call | solution.py:553
  546.8 3.7 select_select_fusion.3
  553.2 13.6 %att_grads.1 = bf16[8,256,2048]{2,1,0:T(8,128)(2,1)S(1)} custom-call(bf16[1024,2048]{1,0:T(8,128)(2,1)S(1)} %copy-done.7, bf16[1024,512]{1,0:T(8,128)(2,1)S(1)} %get-tuple-element.200.dq_ref, bf16[1024,512]{1,0:T(8,128)(2,1)S(1)} %get-tuple-element.201.dk_ref, bf16[1024,512]{1,0:T(8,128)(2,1)S(1)} %get-tuple-element.202.dv_ref, ...), custom_call_target="tpu_custom_call" | custom-call | flops 1000 | bytes 1000 | tf_op jit(solution)/shard_map/att_grads/pallas_call | solution.py:612
  576.4 63.1 %collective-permute-done.36 = bf16[1024,512]{1,0:T(8,128)(2,1)S(1)} collective-permute-done((bf16[1024,512]{1,0:T(8,128)(2,1)}, bf16[1024,512]{1,0:T(8,128)(2,1)S(1)}, u32[]{:S(2)}, u32[]{:S(2)}) %collective-permute-start.36) | collective-permute-done | bytes 1048608 | tf_op jit(solution)/shard_map/ppermute | solution.py:699
  639.6 24.1 %collective-permute-done.37 = bf16[1024,512]{1,0:T(8,128)(2,1)S(1)} collective-permute-done((bf16[1024,512]{1,0:T(8,128)(2,1)}, bf16[1024,512]{1,0:T(8,128)(2,1)S(1)}, u32[]{:S(2)}, u32[]{:S(2)}) %collective-permute-start.37) | collective-permute-done | bytes 1048608 | tf_op jit(solution)/shard_map/ppermute | solution.py:699
  667.1 3.7 fusion.15
  670.9 3.6 all-to-all-start.2
  683.6 17.5 %all-to-all-done.2 = bf16[8,128,1024]{2,1,0:T(8,128)(2,1)S(1)} async-done(((bf16[8,128,1024]{2,1,0:T(8,128)(2,1)}), bf16[8,128,1024]{2,1,0:T(8,128)(2,1)S(1)}, u32[]{:S(2)}, u32[]{:S(2)}) %all-to-all-start.2) | async-done | bytes 2097184 | tf_op jit(solution)/shard_map/all_to_all | solution.py:768
  (240 shorter events, 120.7 us)
Async XLA Ops:
  7.2 132.8 %all-gather.6.cloned.1.call-start = ((), (), s32[]{:S(2)}) async-start(), calls=%async_computation.6 | async-start | bytes 7077888 | tf_op jit(solution)/shard_map/all_gather | solution.py:774
  13.1 30.5 %all-to-all-start = ((bf16[8,128,640]{2,1,0:T(8,128)(2,1)}), bf16[8,128,640]{2,1,0:T(8,128)(2,1)S(1)}, u32[]{:S(2)}, u32[]{:S(2)}) async-start(bf16[8,128,640]{2,1,0:T(8,128)(2,1)} %bitcast), calls=%async_computation | async-start | bytes 2621440 | tf_op jit(solution)/shard_map/all_to_all | solution.py:768
  17.0 227.6 %all-gather.4.cloned.1.call-start = ((), (), s32[]{:S(2)}) async-start(), calls=%async_computation.5 | async-start | bytes 9437184 | tf_op jit(solution)/shard_map/all_gather | solution.py:792
  17.0 27.2 %collective-permute-start = (bf16[64,2048]{1,0:T(8,128)(2,1)}, bf16[64,2048]{1,0:T(8,128)(2,1)}, u32[]{:S(2)}, u32[]{:S(2)}) collective-permute-start(bf16[64,2048]{1,0:T(8,128)(2,1)} %param.17), channel_id=1, source_target_pairs={{0,1},{1,2},{2,3},{3,0},{4,5},{5,6},{6,7},{7,4},{8,9},{9,10},{10,1... | collective-permute-start | bytes 786440 | tf_op jit(solution)/shard_map/ppermute | solution.py:699
  18.6 25.6 %collective-permute-start.1 = (bf16[64,2048]{1,0:T(8,128)(2,1)}, bf16[64,2048]{1,0:T(8,128)(2,1)}, u32[]{:S(2)}, u32[]{:S(2)}) collective-permute-start(bf16[64,2048]{1,0:T(8,128)(2,1)} %param.17), channel_id=1, source_target_pairs={{0,2},{1,3},{2,0},{3,1},{4,6},{5,7},{6,4},{7,5},{8,10},{9,11},{10,... | collective-permute-start | bytes 786440 | tf_op jit(solution)/shard_map/ppermute | solution.py:699
  19.0 25.3 %collective-permute-start.2 = (bf16[64,2048]{1,0:T(8,128)(2,1)}, bf16[64,2048]{1,0:T(8,128)(2,1)}, u32[]{:S(2)}, u32[]{:S(2)}) collective-permute-start(bf16[64,2048]{1,0:T(8,128)(2,1)} %param.17), channel_id=1, source_target_pairs={{0,3},{1,0},{2,1},{3,2},{4,7},{5,4},{6,5},{7,6},{8,11},{9,8},{10,9... | collective-permute-start | bytes 786440 | tf_op jit(solution)/shard_map/ppermute | solution.py:699
  46.7 219.0 %all-gather.8.cloned.1.call-start = ((), (), s32[]{:S(2)}) async-start(), calls=%async_computation.7 | async-start | bytes 28311552 | tf_op jit(solution)/shard_map/all_gather | solution.py:794
  48.8 25.2 %collective-permute-start.3 = (bf16[1024,512]{1,0:T(8,128)(2,1)S(1)}, bf16[1024,512]{1,0:T(8,128)(2,1)S(1)}, u32[]{:S(2)}, u32[]{:S(2)}) collective-permute-start(bf16[1024,512]{1,0:T(8,128)(2,1)S(1)} %fusion.24.refs_0_), channel_id=1, source_target_pairs={{0,1},{1,2},{2,3},{4,5},{5,6},{6,7},{8,9},{9,10},{10,11},{12,13},{... | collective-permute-start | bytes 3145736 | tf_op jit(solution)/shard_map/ppermute | solution.py:678
  52.3 25.1 %collective-permute-start.6 = (bf16[1024,512]{1,0:T(8,128)(2,1)S(1)}, bf16[1024,512]{1,0:T(8,128)(2,1)}, u32[]{:S(2)}, u32[]{:S(2)}) collective-permute-start(bf16[1024,512]{1,0:T(8,128)(2,1)S(1)} %fusion.24.refs_0_), channel_id=1, source_target_pairs={{3,2},{2,1},{1,0},{7,6},{6,5},{5,4},{11,10},{10,9},{9,8},{15,14},{... | collective-permute-start | bytes 3145736 | tf_op jit(solution)/shard_map/ppermute | solution.py:678
  74.0 25.1 %collective-permute-start.4 = (bf16[1024,512]{1,0:T(8,128)(2,1)S(1)}, bf16[1024,512]{1,0:T(8,128)(2,1)}, u32[]{:S(2)}, u32[]{:S(2)}) collective-permute-start(bf16[1024,512]{1,0:T(8,128)(2,1)S(1)} %collective-permute-done.3.refs_1_), channel_id=1, source_target_pairs={{1,2},{2,3},{5,6},{6,7},{9,10},{10,11},{13,14},{14,15},{17,18},{18... | collective-permute-start | bytes 3145736 | tf_op jit(solution)/shard_map/ppermute | solution.py:678
  77.4 25.3 %collective-permute-start.7 = (bf16[1024,512]{1,0:T(8,128)(2,1)}, bf16[1024,512]{1,0:T(8,128)(2,1)}, u32[]{:S(2)}, u32[]{:S(2)}) collective-permute-start(bf16[1024,512]{1,0:T(8,128)(2,1)} %collective-permute-done.6.refs_4_), channel_id=1, source_target_pairs={{2,1},{1,0},{6,5},{5,4},{10,9},{9,8},{14,13},{13,12},{18,17},{17,1... | collective-permute-start | bytes 3145736 | tf_op jit(solution)/shard_map/ppermute | solution.py:678
  84.5 23.3 %all-to-all-start.1 = ((bf16[8,128,512]{2,1,0:T(8,128)(2,1)}), bf16[8,128,512]{2,1,0:T(8,128)(2,1)S(1)}, u32[]{:S(2)}, u32[]{:S(2)}) async-start(bf16[8,128,512]{2,1,0:T(8,128)(2,1)} %bitcast.12), calls=%async_computation.1 | async-start | bytes 2097152 | tf_op jit(solution)/shard_map/all_to_all | solution.py:768
  88.4 483.8 %reduce-scatter.3.cloned.1.call-start = ((), (), s32[]{:S(2)}) async-start(), calls=%async_computation.8 | async-start | bytes 28311552 | tf_op jit(solution)/shard_map/reduce_scatter | solution.py:851
  99.2 21.7 %collective-permute-start.5 = (bf16[1024,512]{1,0:T(8,128)(2,1)}, bf16[1024,512]{1,0:T(8,128)(2,1)}, u32[]{:S(2)}, u32[]{:S(2)}) collective-permute-start(bf16[1024,512]{1,0:T(8,128)(2,1)} %collective-permute-done.4.refs_2_), channel_id=1, source_target_pairs={{2,3},{6,7},{10,11},{14,15},{18,19},{22,23},{26,27},{30,31}} | collective-permute-start | bytes 3145736 | tf_op jit(solution)/shard_map/ppermute | solution.py:678
  102.7 18.1 %collective-permute-start.8 = (bf16[1024,512]{1,0:T(8,128)(2,1)}, bf16[1024,512]{1,0:T(8,128)(2,1)}, u32[]{:S(2)}, u32[]{:S(2)}) collective-permute-start(bf16[1024,512]{1,0:T(8,128)(2,1)} %collective-permute-done.7.refs_5_), channel_id=1, source_target_pairs={{1,0},{5,4},{9,8},{13,12},{17,16},{21,20},{25,24},{29,28}} | collective-permute-start | bytes 3145736 | tf_op jit(solution)/shard_map/ppermute | solution.py:678
  128.7 37.1 %collective-permute-start.10 = (bf16[1024,512]{1,0:T(8,128)(2,1)S(1)}, bf16[1024,512]{1,0:T(8,128)(2,1)S(1)}, u32[]{:S(2)}, u32[]{:S(2)}) collective-permute-start(bf16[1024,512]{1,0:T(8,128)(2,1)S(1)} %fusion.25.refs_0_), channel_id=1, source_target_pairs={{3,2},{2,1},{1,0},{7,6},{6,5},{5,4},{11,10},{10,9},{9,8},{15,14},{... | collective-permute-start | bytes 3145736 | tf_op jit(solution)/shard_map/ppermute | solution.py:678
  137.1 28.8 %collective-permute-start.9 = (bf16[1024,512]{1,0:T(8,128)(2,1)S(1)}, bf16[1024,512]{1,0:T(8,128)(2,1)}, u32[]{:S(2)}, u32[]{:S(2)}) collective-permute-start(bf16[1024,512]{1,0:T(8,128)(2,1)S(1)} %fusion.25.refs_0_), channel_id=1, source_target_pairs={{0,1},{1,2},{2,3},{4,5},{5,6},{6,7},{8,9},{9,10},{10,11},{12,13},{... | collective-permute-start | bytes 3145736 | tf_op jit(solution)/shard_map/ppermute | solution.py:678
  165.8 96.8 %copy-start.30 = (bf16[1024,512]{1,0:T(8,128)(2,1)}, bf16[1024,512]{1,0:T(8,128)(2,1)S(1)}, u32[]{:S(2)}) copy-start(bf16[1024,512]{1,0:T(8,128)(2,1)S(1)} %collective-permute-done.10.refs_4_) | copy-start | bytes 3145732
  165.8 24.3 %collective-permute-start.11 = (bf16[1024,512]{1,0:T(8,128)(2,1)}, bf16[1024,512]{1,0:T(8,128)(2,1)S(1)}, u32[]{:S(2)}, u32[]{:S(2)}) collective-permute-start(bf16[1024,512]{1,0:T(8,128)(2,1)} %attend.1.refs_0_.att_ref), channel_id=1, source_target_pairs={{0,1},{1,2},{2,3},{4,5},{5,6},{6,7},{8,9},{9,10},{10,11},{12,13},{... | collective-permute-start | bytes 3145736 | tf_op jit(solution)/shard_map/ppermute | solution.py:678
  167.7 24.3 %collective-permute-start.14 = (bf16[1024,512]{1,0:T(8,128)(2,1)}, bf16[1024,512]{1,0:T(8,128)(2,1)S(1)}, u32[]{:S(2)}, u32[]{:S(2)}) collective-permute-start(bf16[1024,512]{1,0:T(8,128)(2,1)} %attend.1.refs_0_.att_ref), channel_id=1, source_target_pairs={{3,2},{2,1},{1,0},{7,6},{6,5},{5,4},{11,10},{10,9},{9,8},{15,14},{... | collective-permute-start | bytes 3145736 | tf_op jit(solution)/shard_map/ppermute | solution.py:678
  190.1 22.9 %collective-permute-start.12 = (bf16[1024,512]{1,0:T(8,128)(2,1)S(1)}, bf16[1024,512]{1,0:T(8,128)(2,1)S(1)}, u32[]{:S(2)}, u32[]{:S(2)}) collective-permute-start(bf16[1024,512]{1,0:T(8,128)(2,1)S(1)} %collective-permute-done.11.refs_1_), channel_id=1, source_target_pairs={{1,2},{2,3},{5,6},{6,7},{9,10},{10,11},{13,14},{14,15},{17,18},{18... | collective-permute-start | bytes 3145736 | tf_op jit(solution)/shard_map/ppermute | solution.py:678
  192.1 23.3 %collective-permute-start.15 = (bf16[1024,512]{1,0:T(8,128)(2,1)S(1)}, bf16[1024,512]{1,0:T(8,128)(2,1)S(1)}, u32[]{:S(2)}, u32[]{:S(2)}) collective-permute-start(bf16[1024,512]{1,0:T(8,128)(2,1)S(1)} %collective-permute-done.14.refs_4_), channel_id=1, source_target_pairs={{2,1},{1,0},{6,5},{5,4},{10,9},{9,8},{14,13},{13,12},{18,17},{17,1... | collective-permute-start | bytes 3145736 | tf_op jit(solution)/shard_map/ppermute | solution.py:678
  213.0 20.9 %collective-permute-start.13 = (bf16[1024,512]{1,0:T(8,128)(2,1)S(1)}, bf16[1024,512]{1,0:T(8,128)(2,1)S(1)}, u32[]{:S(2)}, u32[]{:S(2)}) collective-permute-start(bf16[1024,512]{1,0:T(8,128)(2,1)S(1)} %collective-permute-done.12.refs_2_), channel_id=1, source_target_pairs={{2,3},{6,7},{10,11},{14,15},{18,19},{22,23},{26,27},{30,31}} | collective-permute-start | bytes 3145736 | tf_op jit(solution)/shard_map/ppermute | solution.py:678
  215.4 18.5 %collective-permute-start.16 = (bf16[1024,512]{1,0:T(8,128)(2,1)S(1)}, bf16[1024,512]{1,0:T(8,128)(2,1)S(1)}, u32[]{:S(2)}, u32[]{:S(2)}) collective-permute-start(bf16[1024,512]{1,0:T(8,128)(2,1)S(1)} %collective-permute-done.15.refs_5_), channel_id=1, source_target_pairs={{1,0},{5,4},{9,8},{13,12},{17,16},{21,20},{25,24},{29,28}} | collective-permute-start | bytes 3145736 | tf_op jit(solution)/shard_map/ppermute | solution.py:678
  233.9 28.7 %collective-permute-start.17 = (bf16[1024,512]{1,0:T(8,128)(2,1)}, bf16[1024,512]{1,0:T(8,128)(2,1)S(1)}, u32[]{:S(2)}, u32[]{:S(2)}) collective-permute-start(bf16[1024,512]{1,0:T(8,128)(2,1)} %collective-permute-done.9.refs_1_), channel_id=1, source_target_pairs={{1,2},{2,3},{5,6},{6,7},{9,10},{10,11},{13,14},{14,15},{17,18},{18... | collective-permute-start | bytes 3145736 | tf_op jit(solution)/shard_map/ppermute | solution.py:678
  238.3 24.3 %collective-permute-start.18 = (bf16[1024,512]{1,0:T(8,128)(2,1)S(1)}, bf16[1024,512]{1,0:T(8,128)(2,1)}, u32[]{:S(2)}, u32[]{:S(2)}) collective-permute-start(bf16[1024,512]{1,0:T(8,128)(2,1)S(1)} %collective-permute-done.10.refs_4_), channel_id=1, source_target_pairs={{2,1},{1,0},{6,5},{5,4},{10,9},{9,8},{14,13},{13,12},{18,17},{17,1... | collective-permute-start | bytes 3145736 | tf_op jit(solution)/shard_map/ppermute | solution.py:678
  262.7 27.0 %collective-permute-start.19 = (bf16[1024,512]{1,0:T(8,128)(2,1)S(1)}, bf16[1024,512]{1,0:T(8,128)(2,1)S(1)}, u32[]{:S(2)}, u32[]{:S(2)}) collective-permute-start(bf16[1024,512]{1,0:T(8,128)(2,1)S(1)} %collective-permute-done.17.refs_2_), channel_id=1, source_target_pairs={{2,3},{6,7},{10,11},{14,15},{18,19},{22,23},{26,27},{30,31}} | collective-permute-start | bytes 3145736 | tf_op jit(solution)/shard_map/ppermute | solution.py:678
  264.0 25.7 %collective-permute-start.20 = (bf16[1024,512]{1,0:T(8,128)(2,1)}, bf16[1024,512]{1,0:T(8,128)(2,1)}, u32[]{:S(2)}, u32[]{:S(2)}) collective-permute-start(bf16[1024,512]{1,0:T(8,128)(2,1)} %collective-permute-done.18.refs_5_), channel_id=1, source_target_pairs={{1,0},{5,4},{9,8},{13,12},{17,16},{21,20},{25,24},{29,28}} | collective-permute-start | bytes 3145736 | tf_op jit(solution)/shard_map/ppermute | solution.py:678
  320.8 92.3 %collective-permute-start.21 = (bf16[256,2048]{1,0:T(8,128)(2,1)}, bf16[256,2048]{1,0:T(8,128)(2,1)S(1)}, u32[]{:S(2)}, u32[]{:S(2)}) collective-permute-start(bf16[256,2048]{1,0:T(8,128)(2,1)} %two_grad.2), channel_id=1, source_target_pairs={{0,2},{1,3},{2,0},{3,1},{4,6},{5,7},{6,4},{7,5},{8,10},{9,11},{10,... | collective-permute-start | bytes 3145736 | tf_op jit(solution)/shard_map/ppermute | solution.py:699
  346.5 66.6 %collective-permute-start.22 = (bf16[256,2048]{1,0:T(8,128)(2,1)}, bf16[256,2048]{1,0:T(8,128)(2,1)}, u32[]{:S(2)}, u32[]{:S(2)}) collective-permute-start(bf16[256,2048]{1,0:T(8,128)(2,1)} %get-tuple-element.155), channel_id=1, source_target_pairs={{0,1},{1,2},{2,3},{3,0},{4,5},{5,6},{6,7},{7,4},{8,9},{9,10},{10,1... | collective-permute-start | bytes 3145736 | tf_op jit(solution)/shard_map/ppermute | solution.py:699
  350.1 63.0 %collective-permute-start.23 = (bf16[256,2048]{1,0:T(8,128)(2,1)}, bf16[256,2048]{1,0:T(8,128)(2,1)}, u32[]{:S(2)}, u32[]{:S(2)}) collective-permute-start(bf16[256,2048]{1,0:T(8,128)(2,1)} %get-tuple-element.156), channel_id=1, source_target_pairs={{0,3},{1,0},{2,1},{3,2},{4,7},{5,4},{6,5},{7,6},{8,11},{9,8},{10,9... | collective-permute-start | bytes 3145736 | tf_op jit(solution)/shard_map/ppermute | solution.py:699
  413.1 266.9 %reduce-scatter.5.cloned.1.call-start = ((), (), s32[]{:S(2)}) async-start(), calls=%async_computation.9 | async-start | bytes 9437184 | tf_op jit(solution)/shard_map/reduce_scatter | solution.py:908
  416.1 27.1 %collective-permute-start.24 = (bf16[256,2048]{1,0:T(8,128)(2,1)S(1)}, bf16[256,2048]{1,0:T(8,128)(2,1)}, u32[]{:S(2)}, u32[]{:S(2)}) collective-permute-start(bf16[256,2048]{1,0:T(8,128)(2,1)S(1)} %add_convert_fusion.4), channel_id=1, source_target_pairs={{0,1},{1,2},{2,3},{4,5},{5,6},{6,7},{8,9},{9,10},{10,11},{12,13},{... | collective-permute-start | bytes 3145736 | tf_op jit(solution)/shard_map/ppermute | solution.py:678
  419.5 26.8 %collective-permute-start.25 = (bf16[256,2048]{1,0:T(8,128)(2,1)S(1)}, bf16[256,2048]{1,0:T(8,128)(2,1)}, u32[]{:S(2)}, u32[]{:S(2)}) collective-permute-start(bf16[256,2048]{1,0:T(8,128)(2,1)S(1)} %add_convert_fusion.4), channel_id=1, source_target_pairs={{3,2},{2,1},{1,0},{7,6},{6,5},{5,4},{11,10},{10,9},{9,8},{15,14},{... | collective-permute-start | bytes 3145736 | tf_op jit(solution)/shard_map/ppermute | solution.py:678
  446.3 26.1 %collective-permute-start.26 = (bf16[256,2048]{1,0:T(8,128)(2,1)}, bf16[256,2048]{1,0:T(8,128)(2,1)}, u32[]{:S(2)}, u32[]{:S(2)}) collective-permute-start(bf16[256,2048]{1,0:T(8,128)(2,1)} %collective-permute-done.24), channel_id=1, source_target_pairs={{1,2},{2,3},{5,6},{6,7},{9,10},{10,11},{13,14},{14,15},{17,18},{18... | collective-permute-start | bytes 3145736 | tf_op jit(solution)/shard_map/ppermute | solution.py:678
  448.2 26.3 %collective-permute-start.27 = (bf16[256,2048]{1,0:T(8,128)(2,1)}, bf16[256,2048]{1,0:T(8,128)(2,1)}, u32[]{:S(2)}, u32[]{:S(2)}) collective-permute-start(bf16[256,2048]{1,0:T(8,128)(2,1)} %collective-permute-done.25), channel_id=1, source_target_pairs={{2,1},{1,0},{6,5},{5,4},{10,9},{9,8},{14,13},{13,12},{18,17},{17,1... | collective-permute-start | bytes 3145736 | tf_op jit(solution)/shard_map/ppermute | solution.py:678
  454.1 20.4 %collective-permute-start.28 = (bf16[1024,512]{1,0:T(8,128)(2,1)S(1)}, bf16[1024,512]{1,0:T(8,128)(2,1)}, u32[]{:S(2)}, u32[]{:S(2)}) collective-permute-start(bf16[1024,512]{1,0:T(8,128)(2,1)S(1)} %get-tuple-element.185), channel_id=1, source_target_pairs={{0,1},{4,5},{8,9},{12,13},{16,17},{20,21},{24,25},{28,29}} | collective-permute-start | bytes 3145736 | tf_op jit(solution)/shard_map/ppermute | solution.py:886
  455.7 25.3 %collective-permute-start.29 = (bf16[1024,512]{1,0:T(8,128)(2,1)S(1)}, bf16[1024,512]{1,0:T(8,128)(2,1)}, u32[]{:S(2)}, u32[]{:S(2)}) collective-permute-start(bf16[1024,512]{1,0:T(8,128)(2,1)S(1)} %get-tuple-element.183), channel_id=1, source_target_pairs={{3,2},{7,6},{11,10},{15,14},{19,18},{23,22},{27,26},{31,30}} | collective-permute-start | bytes 3145736 | tf_op jit(solution)/shard_map/ppermute | solution.py:886
  483.7 24.4 %collective-permute-start.32 = (bf16[1024,512]{1,0:T(8,128)(2,1)S(1)}, bf16[1024,512]{1,0:T(8,128)(2,1)S(1)}, u32[]{:S(2)}, u32[]{:S(2)}) collective-permute-start(bf16[1024,512]{1,0:T(8,128)(2,1)S(1)} %get-tuple-element.232), channel_id=1, source_target_pairs={{0,1},{1,2},{4,5},{5,6},{8,9},{9,10},{12,13},{13,14},{16,17},{17,1... | collective-permute-start | bytes 3145736 | tf_op jit(solution)/shard_map/ppermute | solution.py:886
  485.0 24.7 %collective-permute-start.33 = (bf16[1024,512]{1,0:T(8,128)(2,1)S(1)}, bf16[1024,512]{1,0:T(8,128)(2,1)S(1)}, u32[]{:S(2)}, u32[]{:S(2)}) collective-permute-start(bf16[1024,512]{1,0:T(8,128)(2,1)S(1)} %get-tuple-element.231), channel_id=1, source_target_pairs={{3,2},{2,1},{7,6},{6,5},{11,10},{10,9},{15,14},{14,13},{19,18},{18... | collective-permute-start | bytes 3145736 | tf_op jit(solution)/shard_map/ppermute | solution.py:886
  489.8 21.4 %collective-permute-start.30 = (bf16[256,2048]{1,0:T(8,128)(2,1)}, bf16[256,2048]{1,0:T(8,128)(2,1)S(1)}, u32[]{:S(2)}, u32[]{:S(2)}) collective-permute-start(bf16[256,2048]{1,0:T(8,128)(2,1)} %collective-permute-done.26), channel_id=1, source_target_pairs={{2,3},{6,7},{10,11},{14,15},{18,19},{22,23},{26,27},{30,31}} | collective-permute-start | bytes 3145736 | tf_op jit(solution)/shard_map/ppermute | solution.py:678
  491.2 20.0 %collective-permute-start.31 = (bf16[256,2048]{1,0:T(8,128)(2,1)}, bf16[256,2048]{1,0:T(8,128)(2,1)S(1)}, u32[]{:S(2)}, u32[]{:S(2)}) collective-permute-start(bf16[256,2048]{1,0:T(8,128)(2,1)} %collective-permute-done.27), channel_id=1, source_target_pairs={{1,0},{5,4},{9,8},{13,12},{17,16},{21,20},{25,24},{29,28}} | collective-permute-start | bytes 3145736 | tf_op jit(solution)/shard_map/ppermute | solution.py:678
  511.5 39.7 %collective-permute-start.35 = (bf16[1024,512]{1,0:T(8,128)(2,1)S(1)}, bf16[1024,512]{1,0:T(8,128)(2,1)S(1)}, u32[]{:S(2)}, u32[]{:S(2)}) collective-permute-start(bf16[1024,512]{1,0:T(8,128)(2,1)S(1)} %add_convert_fusion.2), channel_id=1, source_target_pairs={{3,2},{2,1},{1,0},{7,6},{6,5},{5,4},{11,10},{10,9},{9,8},{15,14},{... | collective-permute-start | bytes 3145736 | tf_op jit(solution)/shard_map/ppermute | solution.py:886
  515.4 35.8 %collective-permute-start.34 = (bf16[1024,512]{1,0:T(8,128)(2,1)S(1)}, bf16[1024,512]{1,0:T(8,128)(2,1)S(1)}, u32[]{:S(2)}, u32[]{:S(2)}) collective-permute-start(bf16[1024,512]{1,0:T(8,128)(2,1)S(1)} %add_convert_fusion.3), channel_id=1, source_target_pairs={{0,1},{1,2},{2,3},{4,5},{5,6},{6,7},{8,9},{9,10},{10,11},{12,13},{... | collective-permute-start | bytes 3145736 | tf_op jit(solution)/shard_map/ppermute | solution.py:886
  572.2 67.4 %collective-permute-start.36 = (bf16[1024,512]{1,0:T(8,128)(2,1)}, bf16[1024,512]{1,0:T(8,128)(2,1)S(1)}, u32[]{:S(2)}, u32[]{:S(2)}) collective-permute-start(bf16[1024,512]{1,0:T(8,128)(2,1)} %copy-done.24), channel_id=1, source_target_pairs={{0,2},{1,3},{2,0},{3,1},{4,6},{5,7},{6,4},{7,5},{8,10},{9,11},{10,... | collective-permute-start | bytes 3145736 | tf_op jit(solution)/shard_map/ppermute | solution.py:699
  574.1 89.5 %collective-permute-start.37 = (bf16[1024,512]{1,0:T(8,128)(2,1)}, bf16[1024,512]{1,0:T(8,128)(2,1)S(1)}, u32[]{:S(2)}, u32[]{:S(2)}) collective-permute-start(bf16[1024,512]{1,0:T(8,128)(2,1)} %copy-done.23), channel_id=1, source_target_pairs={{0,1},{1,2},{2,3},{3,0},{4,5},{5,6},{6,7},{7,4},{8,9},{9,10},{10,1... | collective-permute-start | bytes 3145736 | tf_op jit(solution)/shard_map/ppermute | solution.py:699
  574.6 89.0 %collective-permute-start.38 = (bf16[1024,512]{1,0:T(8,128)(2,1)S(1)}, bf16[1024,512]{1,0:T(8,128)(2,1)S(1)}, u32[]{:S(2)}, u32[]{:S(2)}) collective-permute-start(bf16[1024,512]{1,0:T(8,128)(2,1)S(1)} %get-tuple-element.195), channel_id=1, source_target_pairs={{0,3},{1,0},{2,1},{3,2},{4,7},{5,4},{6,5},{7,6},{8,11},{9,8},{10,9... | collective-permute-start | bytes 3145736 | tf_op jit(solution)/shard_map/ppermute | solution.py:699
  670.9 30.2 %all-to-all-start.2 = ((bf16[8,128,1024]{2,1,0:T(8,128)(2,1)}), bf16[8,128,1024]{2,1,0:T(8,128)(2,1)S(1)}, u32[]{:S(2)}, u32[]{:S(2)}) async-start(bf16[8,128,1024]{2,1,0:T(8,128)(2,1)} %bitcast.52), calls=%async_computation.2 | async-start | bytes 4194304 | tf_op jit(solution)/shard_map/all_to_all | solution.py:768
  (60 other events, 878.5 us)
Sparse Core Ops, SparseCore 0:
  10.5 58.5 all-gather.5
  71.0 65.6 all-gather.3
  138.6 125.3 all-gather.7
  413.3 156.8 reduce-scatter.2
  573.4 71.2 reduce-scatter.4

commit v6 on v5

--- a/solution.py
+++ b/solution.py
@@ -472,6 +472,80 @@
         - jnp.mean(grad_in, axis=-1, keepdims=True)
         - unit_rows * jnp.mean(grad_in * unit_rows, axis=-1, keepdims=True)
     )
+
+
+def first_two_kernel(at_ref, *refs):
+    (down_ref, gate_ref, up_ref, gate_in, up_in, normed_ref, inverse_ref) = refs[:7]
+    *come_refs, out_ref, grad_ref, dgate_ref, dup_ref, total = refs[7:]
+    step, half = pl.program_id(0), pl.num_programs(0) // 2
+    size = len(come_refs) // 2 + 1
+    width = come_refs[0].shape[1]
+
+    @pl.when(step == 0)
+    def _():
+        for owner in range(size):
+            grad_ref[:, owner * width : (owner + 1) * width] = picked(
+                at_ref[1], owner, come_refs
+            )
+
+    @pl.when(step < half)
+    def _():
+        columns = pl.ds(pl.multiple_of(step * WIDE, WIDE), WIDE)
+        down = times_transposed(grad_ref[...], down_ref[0])
+        dgate_ref[:, columns] = (down * gate_in[...].astype(f32)).astype(bf16)
+        dup_ref[:, columns] = (down * up_in[...].astype(f32)).astype(bf16)
+
+    @pl.when(step >= half)
+    def _():
+        columns = pl.ds(pl.multiple_of((step - half) * WIDE, WIDE), WIDE)
+        total[:, columns] = times_transposed(dgate_ref[...], gate_ref[0]) + times_transposed(
+            dup_ref[...], up_ref[0]
+        )
+
+    @pl.when(step == 2 * half - 1)
+    def _():
+        out_ref[...] = norm_back(normed_ref[...], inverse_ref[...], total[...]).astype(bf16)
+
+
+def first_two_grad(at, own, arrived, weights, gate, up, normed, inverse, quarter):
+    operands = flat(own, arrived)
+    width = own.shape[1]
+    hidden_units = gate.shape[1]
+    model = weights.shape[1]
+    half = hidden_units // WIDE
+    first = lambda j: jnp.minimum(j, half - 1)
+    second = lambda j: jnp.maximum(j - half, 0)
+    rows = lambda j, at: (at[0], 0)
+    part = pl.BlockSpec((quarter, WIDE), lambda j, at: (at[0], first(j)))
+    once = pl.Buffered(1)
+    return pl.pallas_call(
+        first_two_kernel,
+        grid_spec=pltpu.PrefetchScalarGridSpec(
+            num_scalar_prefetch=1,
+            grid=(2 * half,),
+            in_specs=[
+                pl.BlockSpec((1, WIDE, model), lambda j, at: (2, first(j), 0)),
+                pl.BlockSpec((1, WIDE, hidden_units), lambda j, at: (0, second(j), 0)),
+                pl.BlockSpec((1, WIDE, hidden_units), lambda j, at: (1, second(j), 0)),
+                part,
+                part,
+                pl.BlockSpec((quarter, model), rows, pipeline_mode=once),
+                pl.BlockSpec((quarter, 1), rows, pipeline_mode=once),
+                *[pl.BlockSpec((quarter, width), rows, pipeline_mode=once)] * len(operands),
+            ],
+            out_specs=pl.BlockSpec((quarter, model), lambda j, at: (0, 0)),
+            scratch_shapes=[
+                pltpu.VMEM((quarter, model), bf16),
+                pltpu.VMEM((quarter, hidden_units), bf16),
+                pltpu.VMEM((quarter, hidden_units), bf16),
+                pltpu.VMEM((quarter, model), f32),
+            ],
+        ),
+        out_shape=jax.ShapeDtypeStruct((quarter, model), bf16),
+        compiler_params=params(),
+        cost_estimate=cost(6 * quarter * model * hidden_units, 6 * model * hidden_units),
+        name="first_two_grad",
+    )(at, weights, weights, weights, gate, up, normed, inverse, *operands)
 
 
 def put_at(place, value, refs):
@@ -827,22 +901,30 @@
 
     *last, activated = lax.optimization_barrier((*grads_come[-1], activated))
     grads_come[-1] = tuple(last)
+    two_first = first_two_grad(
+        jnp.stack([order[0], own_shard]),
+        first_grads,
+        grads_come,
+        full_mlp,
+        gate,
+        up,
+        normed_two,
+        inverse_two,
+        quarter,
+    )
     full_grads, gate_grad, up_grad = mlp_down_back(
-        me, first_grads, grads_come, full_mlp, gate, up
+        me, first_grads, grads_come, full_mlp, after(gate, two_first), up
     )
 
     def rows_of(rows, owner):
         return lax.dynamic_slice_in_dim(rows, owner * quarter, quarter, 0)
 
-    two_first = two_grad_pieces(
-        order[:1], gate_grad, up_grad, full_mlp, normed_two, inverse_two, quarter
-    )
     two_rest = two_grad_pieces(
-        order[1:], gate_grad, after(up_grad, *two_first), full_mlp, normed_two, inverse_two, quarter
+        order[1:], gate_grad, up_grad, full_mlp, normed_two, inverse_two, quarter
     )
     two_came = [
         sent_on(term, "tp", shards, step)
-        for term, step in zip((*two_first, *two_rest), steps)
+        for term, step in zip((two_first, *two_rest), steps)
     ]
     grad_mlp = mlp_grads(0, [normed_two], [after(gate_grad, *two_rest)])
     grad_mlp = mlp_grads(1, [normed_two], [up_grad], grad_mlp)

time: 718 us -> 707 us (0.985)
  waiting for transfers between devices: 285 us -> 266 us
    pallas_call x0 -> x1, Pallas kernels: none -> 18.2 us  [first_two_grad(): pl.pallas_call(first_two_kernel, grid_spec=pltpu.PrefetchScalarGridSpec(n...]
    ppermute x9, waiting for transfers between devices: 112 us -> 95.9 us  [sent_on(): lax.ppermute(term, axis, [(i, (i + step) % size) for i in range(size)])]
    pallas_call x2 -> x1, Pallas kernels: 35.6 us -> 24.5 us  [two_grad_pieces(): pl.pallas_call(two_grad_kernel, grid_spec=pltpu.PrefetchScalarGridSpec(nu...]
  transfers between devices with their start and end apart: 47 -> 47, of which waited for: 19 -> 20; matrix products, arithmetic and copies ran while one was open for 8% -> 8% of each run, Pallas kernels for 27% -> 30%
where the time goes in v6:
time: 707 us; the launch traced here: 700 us
  waiting for transfers between devices  266 us (38%)
  Pallas kernels  226 us (32%)
  starting transfers between devices  113 us (16%)
  other arithmetic  32.3 us (5%)
  matrix products  24.5 us (3%)
  local copies, waits for them, and re-layouts  20.7 us (3%)
  between operations  17.4 us (2%)
    ppermute x12, waiting for transfers between devices, line_step(): lax.ppermute(from_low, axis, up)  115 us
    ppermute x9, waiting for transfers between devices, sent_on(): lax.ppermute(term, axis, [(i, (i + step) % size) for i in range(size)])  95.9 us
    ppermute x12, starting transfers between devices, line_step(): lax.ppermute(from_high, axis, down)  42.7 us
    pallas_call x3, Pallas kernels, mlp_grads(): pl.pallas_call(body, grid=(model // BLOCK,), in_specs=specs, out_specs=pl...  35.7 us
    all_to_all x3, waiting for transfers between devices, over_fsdp(): return lax.all_to_all(rows, 'fsdp', split_axis=0, concat_axis=0, tiled=True)  34.7 us
    ppermute x12, starting transfers between devices, line_step(): lax.ppermute(from_low, axis, up)  31 us
    pallas_call x1, Pallas kernels, two_grad_pieces(): pl.pallas_call(two_grad_kernel, grid_spec=pltpu.PrefetchScalarGridSpec(nu...  24.5 us
    pallas_call x1, Pallas kernels, mlp_up(): pl.pallas_call(up_kernel, grid=(hidden_units // WIDE,), in_specs=[pl.Bloc...  24 us
  transfers between devices with their start and end apart: 47, of which 20 were waited for; matrix products, arithmetic and copies ran while one was open for 8% of the time, Pallas kernels for 30%

profile of v6, /device:TPU:16, one launch (start us, length us, event | category | flops | bytes accessed | tf_op | source)
XLA Modules:
  0.0 700.3 jit_solution(14275696695793794293)
XLA Ops:
  13.1 3.9 all-to-all-start
  20.3 3.7 pad_maximum_fusion.1
  26.3 17.3 %all-to-all-done = bf16[8,128,640]{2,1,0:T(8,128)(2,1)S(1)} async-done(((bf16[8,128,640]{2,1,0:T(8,128)(2,1)}), bf16[8,128,640]{2,1,0:T(8,128)(2,1)S(1)}, u32[]{:S(2)}, u32[]{:S(2)}) %all-to-all-start) | async-done | bytes 1310752 | tf_op jit(solution)/shard_map/all_to_all | solution.py:842
  48.8 3.5 collective-permute-start.3
  54.7 19.3 %collective-permute-done.3.refs_1_ = bf16[1024,512]{1,0:T(8,128)(2,1)S(1)} collective-permute-done((bf16[1024,512]{1,0:T(8,128)(2,1)S(1)}, bf16[1024,512]{1,0:T(8,128)(2,1)S(1)}, u32[]{:S(2)}, u32[]{:S(2)}) %collective-permute-start.3) | collective-permute-done | bytes 1048608 | tf_op jit(solution)/shard_map/ppermute | solution.py:752
  77.4 4.3 collective-permute-start.7
  84.5 3.8 all-to-all-start.1
  88.6 10.5 %collective-permute-done.4.refs_2_ = bf16[1024,512]{1,0:T(8,128)(2,1)} collective-permute-done((bf16[1024,512]{1,0:T(8,128)(2,1)S(1)}, bf16[1024,512]{1,0:T(8,128)(2,1)}, u32[]{:S(2)}, u32[]{:S(2)}) %collective-permute-start.4) | collective-permute-done | bytes 1048608 | tf_op jit(solution)/shard_map/ppermute | solution.py:752
  99.2 3.6 collective-permute-start.5
  109.1 11.8 %collective-permute-done.5.refs_3_ = bf16[1024,512]{1,0:T(8,128)(2,1)} collective-permute-done((bf16[1024,512]{1,0:T(8,128)(2,1)}, bf16[1024,512]{1,0:T(8,128)(2,1)}, u32[]{:S(2)}, u32[]{:S(2)}) %collective-permute-start.5) | collective-permute-done | bytes 1048608 | tf_op jit(solution)/shard_map/ppermute | solution.py:752
  120.9 7.8 %gathered_norm.1 = (bf16[1024,2048]{1,0:T(8,128)(2,1)}, bf16[1024,2048]{1,0:T(8,128)(2,1)}, f32[1024,1]{1,0:T(8,128)}) custom-call(s32[1]{0:T(128)} %bitcast.6.me_ref, bf16[1024,512]{1,0:T(8,128)(2,1)} %copy-done.39, bf16[1024,512]{1,0:T(8,128)(2,1)} %copy-done.40, bf16[1024,512]{1,0:T(8,128)(2,1)} %collective-permute-done.4.refs_2_, ...), custom_call_target="tpu_custom_call" | custom-call | flops 41943040 | bytes 16777216 | tf_op jit(solution)/shard_map/gathered_norm/pallas_call | solution.py:117
  128.7 8.4 %collective-permute-start.10 = (bf16[1024,512]{1,0:T(8,128)(2,1)S(1)}, bf16[1024,512]{1,0:T(8,128)(2,1)S(1)}, u32[]{:S(2)}, u32[]{:S(2)}) collective-permute-start(bf16[1024,512]{1,0:T(8,128)(2,1)S(1)} %fusion.25.refs_7_.refs_0_), channel_id=1, source_target_pairs={{3,2},{2,1},{1,0},{7,6},{6,5},{5,4},{11,10},{10,9},{9,8},{15,14},{... | collective-permute-start | bytes 3145736 | tf_op jit(solution)/shard_map/ppermute | solution.py:752
  140.0 13.7 %qkv.1 = (bf16[1024,512]{1,0:T(8,128)(2,1)}, bf16[1024,512]{1,0:T(8,128)(2,1)}, bf16[1024,512]{1,0:T(8,128)(2,1)}) custom-call(bf16[1024,2048]{1,0:T(8,128)(2,1)} %get-tuple-element.122.rows_ref.unit_ref.normed_ref, bf16[2048,1536]{1,0:T(8,128)(2,1)} %all-gather.6.cloned.1.call-done.wq_ref.wk_ref.wv_ref.weight_ref, ...), custom_call_target="tpu_custom_call" | custom-call | flops 6442450944 | bytes 10485760 | tf_op jit(solution)/shard_map/qkv/pallas_call | solution.py:160
  153.8 12.0 %attend.1.refs_0_.att_ref = bf16[1024,512]{1,0:T(8,128)(2,1)} custom-call(bf16[1024,512]{1,0:T(8,128)(2,1)} %get-tuple-element.125.q_ref, bf16[1024,512]{1,0:T(8,128)(2,1)} %get-tuple-element.126.k_ref, bf16[1024,512]{1,0:T(8,128)(2,1)} %get-tuple-element.127.v_ref, s32[1024,1]{1,0:T(8,128)} %copy.27.column_ref, s32[1,1024]{1,0:T(1,128)} %bitcast.48), custom_call_target="tpu_custom_call" | custom-call | flops 2147483648 | bytes 4194304 | tf_op jit(solution)/shard_map/attend/pallas_call | solution.py:212
  167.7 4.3 collective-permute-start.14
  172.1 18.1 %collective-permute-done.11.refs_1_ = bf16[1024,512]{1,0:T(8,128)(2,1)S(1)} collective-permute-done((bf16[1024,512]{1,0:T(8,128)(2,1)}, bf16[1024,512]{1,0:T(8,128)(2,1)S(1)}, u32[]{:S(2)}, u32[]{:S(2)}) %collective-permute-start.11) | collective-permute-done | bytes 1048608 | tf_op jit(solution)/shard_map/ppermute | solution.py:752
  192.1 4.2 collective-permute-start.15
  196.3 16.7 %collective-permute-done.12.refs_2_ = bf16[1024,512]{1,0:T(8,128)(2,1)S(1)} collective-permute-done((bf16[1024,512]{1,0:T(8,128)(2,1)S(1)}, bf16[1024,512]{1,0:T(8,128)(2,1)S(1)}, u32[]{:S(2)}, u32[]{:S(2)}) %collective-permute-start.12) | collective-permute-done | bytes 1048608 | tf_op jit(solution)/shard_map/ppermute | solution.py:752
  216.3 17.6 %collective-permute-done.13.refs_3_ = bf16[1024,512]{1,0:T(8,128)(2,1)S(1)} collective-permute-done((bf16[1024,512]{1,0:T(8,128)(2,1)S(1)}, bf16[1024,512]{1,0:T(8,128)(2,1)S(1)}, u32[]{:S(2)}, u32[]{:S(2)}) %collective-permute-start.13) | collective-permute-done | bytes 1048608 | tf_op jit(solution)/shard_map/ppermute | solution.py:752
  233.9 4.4 collective-permute-start.17
  238.3 5.6 collective-permute-start.18
  245.2 17.7 %hidden.1 = (f32[1024,512]{1,0:T(8,128)}, bf16[1024,2048]{1,0:T(8,128)(2,1)}, f32[1024,1]{1,0:T(8,128)}) custom-call(s32[1]{0:T(128)} %bitcast.6.me_ref, bf16[2048,2048]{1,0:T(8,128)(2,1)} %bitcast.60, bf16[1024,2048]{1,0:T(8,128)(2,1)} %get-tuple-element.119.rows_ref, bf16[1024,512]{1,0:T(8,128)(2,1)} %attend.1.refs_0_.att_ref, ...), custom_call_target="tpu_custom_call" | custom-call | flops 8589934592 | bytes 29360128 | tf_op jit(solution)/shard_map/hidden/pallas_call | solution.py:319
  265.9 24.0 %mlp_up.1 = (bf16[1024,2048]{1,0:T(8,128)(2,1)}, bf16[1024,2048]{1,0:T(8,128)(2,1)}, bf16[1024,2048]{1,0:T(8,128)(2,1)}) custom-call(bf16[1024,2048]{1,0:T(8,128)(2,1)} %get-tuple-element.141.rows_ref.refs_5_.refs_2_.refs_6_.refs_10_.refs_0_, ...), custom_call_target="tpu_custom_call" | custom-call | flops 17179869184 | bytes 41943040 | tf_op jit(solution)/shard_map/mlp_up/pallas_call | solution.py:362
  290.9 18.2 %first_two_grad.1 = bf16[256,2048]{1,0:T(8,128)(2,1)} custom-call(s32[2]{0:T(128)} %pad_add_fusion.at_ref, bf16[3,2048,2048]{2,1,0:T(8,128)(2,1)} %all-gather.8.cloned.1.call-done.gate_ref.up_ref.refs_0_.refs_1_.refs_2_.down_ref.refs_12_.refs_13_, ...), custom_call_target="tpu_custom_call" | custom-call | flops 6442450944 | bytes 25165824 | tf_op jit(solution)/shard_map/first_two_grad/pallas_call | solution.py:521
  310.2 18.9 %mlp_down_back.1 = (bf16[1024,2048]{1,0:T(8,128)(2,1)}, bf16[1024,2048]{1,0:T(8,128)(2,1)}, bf16[1024,2048]{1,0:T(8,128)(2,1)}) custom-call(s32[1]{0:T(128)} %bitcast.6.me_ref, bf16[3,2048,2048]{2,1,0:T(8,128)(2,1)} %all-gather.8.cloned.1.call-done.gate_ref.up_ref.refs_0_.refs_1_.refs_2_.down_ref.refs_12_.refs_13_, ...), custom_call_target="tpu_custom_call" | custom-call | flops 8589934592 | bytes 37748736 | tf_op jit(solution)/shard_map/mlp_down_back/pallas_call | solution.py:409
  329.1 24.5 %two_grad.1 = (bf16[256,2048]{1,0:T(8,128)(2,1)}, bf16[256,2048]{1,0:T(8,128)(2,1)}, bf16[256,2048]{1,0:T(8,128)(2,1)}) custom-call(s32[3]{0:T(128)} %pad_add_fusion.1.order_ref, bf16[1024,2048]{1,0:T(8,128)(2,1)} %get-tuple-element.158.refs_0_.refs_4_.refs_8_.refs_1_, bf16[1024,2048]{1,0:T(8,128)(2,1)} %get-tuple-element.153.refs_1_.refs_5_.refs_9_, ...), custom_call_target="tpu_custom_call" | custom-call | flops 12884901888 | bytes 16777216 | tf_op jit(solution)/shard_map/two_grad/pallas_call | solution.py:589
  353.6 4.6 collective-permute-start.22
  360.4 11.9 %mlp_grads.3.refs_2_ = bf16[3,2048,2048]{2,1,0:T(8,128)(2,1)} custom-call(bf16[1024,2048]{1,0:T(8,128)(2,1)S(1)} %copy-done.2, bf16[1024,2048]{1,0:T(8,128)(2,1)S(1)} %copy-done.4), custom_call_target="tpu_custom_call" | custom-call | flops 8589934592 | bytes 16777216 | tf_op jit(solution)/shard_map/mlp_grads/pallas_call | solution.py:729
  372.3 11.9 %mlp_grads.4.refs_2_ = bf16[3,2048,2048]{2,1,0:T(8,128)(2,1)} custom-call(bf16[1024,2048]{1,0:T(8,128)(2,1)S(1)} %copy-done.2, bf16[1024,2048]{1,0:T(8,128)(2,1)S(1)} %copy-done.3, bf16[3,2048,2048]{2,1,0:T(8,128)(2,1)} %mlp_grads.3.refs_2_), custom_call_target="tpu_custom_call", output_to_operand_aliasing={{}: (2, {})} | custom-call | flops 8589934592 | bytes 16777216 | tf_op jit(solution)/shard_map/mlp_grads/pallas_call | solution.py:729
  384.3 11.9 %mlp_grads.5 = bf16[3,2048,2048]{2,1,0:T(8,128)(2,1)} custom-call(bf16[1024,2048]{1,0:T(8,128)(2,1)S(1)} %copy-done.11, bf16[1024,2048]{1,0:T(8,128)(2,1)S(1)} %copy-done.8, bf16[3,2048,2048]{2,1,0:T(8,128)(2,1)} %mlp_grads.4.refs_2_), custom_call_target="tpu_custom_call", output_to_operand_aliasing={{}: (2, {})} | custom-call | flops 8589934592 | bytes 16777216 | tf_op jit(solution)/shard_map/mlp_grads/pallas_call | solution.py:729
  396.2 5.6 collective-permute-done.23
  410.8 12.4 %mlp_piece.1 = (bf16[1024,512]{1,0:T(8,128)(2,1)S(1)}, bf16[1024,512]{1,0:T(8,128)(2,1)S(1)}, bf16[1024,512]{1,0:T(8,128)(2,1)S(1)}, bf16[1024,512]{1,0:T(8,128)(2,1)S(1)}) custom-call(s32[4]{0:T(128)S(1)} %pad_add_fusion.2.order_ref, bf16[1024,2048]{1,0:T(8,128)(2,1)S(1)} %copy-done.12, ...), custom_call_target="tpu_custom_call" | custom-call | flops 8589934592 | bytes 8388608 | tf_op jit(solution)/shard_map/mlp_piece/pallas_call | solution.py:448
  425.1 5.0 collective-permute-done.24
  433.8 5.9 collective-permute-start.27
  442.7 14.1 %collective-permute-done.26 = bf16[256,2048]{1,0:T(8,128)(2,1)} collective-permute-done((bf16[256,2048]{1,0:T(8,128)(2,1)}, bf16[256,2048]{1,0:T(8,128)(2,1)}, u32[]{:S(2)}, u32[]{:S(2)}) %collective-permute-start.26) | collective-permute-done | bytes 1048608 | tf_op jit(solution)/shard_map/ppermute | solution.py:752
  458.9 6.5 collective-permute-done.29
  469.4 4.8 collective-permute-start.33
  486.7 4.5 collective-permute-done.32
  498.6 3.5 collective-permute-start.34
  502.2 17.2 %attend_back.1 = (bf16[1024,512]{1,0:T(8,128)(2,1)S(1)}, bf16[1024,512]{1,0:T(8,128)(2,1)S(1)}, bf16[1024,512]{1,0:T(8,128)(2,1)S(1)}) custom-call(s32[1]{0:T(128)} %bitcast.6.me_ref, bf16[1024,512]{1,0:T(8,128)(2,1)S(1)} %copy-done.16, bf16[1024,512]{1,0:T(8,128)(2,1)S(1)} %copy-done.17, bf16[1024,512]{1,0:T(8,128)(2,1)S(1)} %copy-done.18, ...), custom_call_target="tpu_custom_call" | custom-call | flops 1000 | bytes 1000 | tf_op jit(solution)/shard_map/attend_back/pallas_call | solution.py:276
  519.4 10.5 %one_grad.1 = (bf16[1024,512]{1,0:T(8,128)(2,1)S(1)}, bf16[1024,512]{1,0:T(8,128)(2,1)S(1)}, bf16[1024,512]{1,0:T(8,128)(2,1)S(1)}, bf16[1024,512]{1,0:T(8,128)(2,1)S(1)}) custom-call(s32[4]{0:T(128)S(1)} %pad_add_fusion.3.place_ref, bf16[1024,512]{1,0:T(8,128)(2,1)S(1)} %get-tuple-element.200.dq_ref, bf16[1024,512]{1,0:T(8,128)(2,1)S(1)} %get-tuple-element.201.dk_ref, ...), custom_call_target="tpu_custom_call" | custom-call | flops 6442450944 | bytes 15728640 | tf_op jit(solution)/shard_map/one_grad/pallas_call | solution.py:627
  536.1 13.6 %att_grads.1 = bf16[8,256,2048]{2,1,0:T(8,128)(2,1)S(1)} custom-call(bf16[1024,2048]{1,0:T(8,128)(2,1)S(1)} %copy-done.7, bf16[1024,512]{1,0:T(8,128)(2,1)S(1)} %get-tuple-element.200.dq_ref, bf16[1024,512]{1,0:T(8,128)(2,1)S(1)} %get-tuple-element.201.dk_ref, bf16[1024,512]{1,0:T(8,128)(2,1)S(1)} %get-tuple-element.202.dv_ref, ...), custom_call_target="tpu_custom_call" | custom-call | flops 1000 | bytes 1000 | tf_op jit(solution)/shard_map/att_grads/pallas_call | solution.py:686
  555.0 3.9 reduce-scatter.3.cloned.1.call-done
  562.2 66.1 %collective-permute-done.36 = bf16[1024,512]{1,0:T(8,128)(2,1)S(1)} collective-permute-done((bf16[1024,512]{1,0:T(8,128)(2,1)}, bf16[1024,512]{1,0:T(8,128)(2,1)S(1)}, u32[]{:S(2)}, u32[]{:S(2)}) %collective-permute-start.36) | collective-permute-done | bytes 1048608 | tf_op jit(solution)/shard_map/ppermute | solution.py:773
  628.3 24.1 %collective-permute-done.37 = bf16[1024,512]{1,0:T(8,128)(2,1)S(1)} collective-permute-done((bf16[1024,512]{1,0:T(8,128)(2,1)}, bf16[1024,512]{1,0:T(8,128)(2,1)S(1)}, u32[]{:S(2)}, u32[]{:S(2)}) %collective-permute-start.37) | collective-permute-done | bytes 1048608 | tf_op jit(solution)/shard_map/ppermute | solution.py:773
  655.9 3.7 fusion.15
  659.6 3.6 all-to-all-start.2
  672.4 17.5 %all-to-all-done.2 = bf16[8,128,1024]{2,1,0:T(8,128)(2,1)S(1)} async-done(((bf16[8,128,1024]{2,1,0:T(8,128)(2,1)}), bf16[8,128,1024]{2,1,0:T(8,128)(2,1)S(1)}, u32[]{:S(2)}, u32[]{:S(2)}) %all-to-all-start.2) | async-done | bytes 2097184 | tf_op jit(solution)/shard_map/all_to_all | solution.py:842
  (241 shorter events, 122.3 us)
Async XLA Ops:
  7.2 132.8 %all-gather.6.cloned.1.call-start = ((), (), s32[]{:S(2)}) async-start(), calls=%async_computation.6 | async-start | bytes 7077888 | tf_op jit(solution)/shard_map/all_gather | solution.py:848
  13.1 30.5 %all-to-all-start = ((bf16[8,128,640]{2,1,0:T(8,128)(2,1)}), bf16[8,128,640]{2,1,0:T(8,128)(2,1)S(1)}, u32[]{:S(2)}, u32[]{:S(2)}) async-start(bf16[8,128,640]{2,1,0:T(8,128)(2,1)} %bitcast), calls=%async_computation | async-start | bytes 2621440 | tf_op jit(solution)/shard_map/all_to_all | solution.py:842
  17.0 228.2 %all-gather.4.cloned.1.call-start = ((), (), s32[]{:S(2)}) async-start(), calls=%async_computation.5 | async-start | bytes 9437184 | tf_op jit(solution)/shard_map/all_gather | solution.py:866
  17.0 27.2 %collective-permute-start = (bf16[64,2048]{1,0:T(8,128)(2,1)}, bf16[64,2048]{1,0:T(8,128)(2,1)}, u32[]{:S(2)}, u32[]{:S(2)}) collective-permute-start(bf16[64,2048]{1,0:T(8,128)(2,1)} %param.17), channel_id=1, source_target_pairs={{0,1},{1,2},{2,3},{3,0},{4,5},{5,6},{6,7},{7,4},{8,9},{9,10},{10,1... | collective-permute-start | bytes 786440 | tf_op jit(solution)/shard_map/ppermute | solution.py:773
  18.6 25.6 %collective-permute-start.1 = (bf16[64,2048]{1,0:T(8,128)(2,1)}, bf16[64,2048]{1,0:T(8,128)(2,1)}, u32[]{:S(2)}, u32[]{:S(2)}) collective-permute-start(bf16[64,2048]{1,0:T(8,128)(2,1)} %param.17), channel_id=1, source_target_pairs={{0,2},{1,3},{2,0},{3,1},{4,6},{5,7},{6,4},{7,5},{8,10},{9,11},{10,... | collective-permute-start | bytes 786440 | tf_op jit(solution)/shard_map/ppermute | solution.py:773
  19.0 25.3 %collective-permute-start.2 = (bf16[64,2048]{1,0:T(8,128)(2,1)}, bf16[64,2048]{1,0:T(8,128)(2,1)}, u32[]{:S(2)}, u32[]{:S(2)}) collective-permute-start(bf16[64,2048]{1,0:T(8,128)(2,1)} %param.17), channel_id=1, source_target_pairs={{0,3},{1,0},{2,1},{3,2},{4,7},{5,4},{6,5},{7,6},{8,11},{9,8},{10,9... | collective-permute-start | bytes 786440 | tf_op jit(solution)/shard_map/ppermute | solution.py:773
  46.7 219.2 %all-gather.8.cloned.1.call-start = ((), (), s32[]{:S(2)}) async-start(), calls=%async_computation.7 | async-start | bytes 28311552 | tf_op jit(solution)/shard_map/all_gather | solution.py:868
  48.8 25.2 %collective-permute-start.3 = (bf16[1024,512]{1,0:T(8,128)(2,1)S(1)}, bf16[1024,512]{1,0:T(8,128)(2,1)S(1)}, u32[]{:S(2)}, u32[]{:S(2)}) collective-permute-start(bf16[1024,512]{1,0:T(8,128)(2,1)S(1)} %fusion.24.refs_0_), channel_id=1, source_target_pairs={{0,1},{1,2},{2,3},{4,5},{5,6},{6,7},{8,9},{9,10},{10,11},{12,13},{... | collective-permute-start | bytes 3145736 | tf_op jit(solution)/shard_map/ppermute | solution.py:752
  52.3 25.1 %collective-permute-start.6 = (bf16[1024,512]{1,0:T(8,128)(2,1)S(1)}, bf16[1024,512]{1,0:T(8,128)(2,1)}, u32[]{:S(2)}, u32[]{:S(2)}) collective-permute-start(bf16[1024,512]{1,0:T(8,128)(2,1)S(1)} %fusion.24.refs_0_), channel_id=1, source_target_pairs={{3,2},{2,1},{1,0},{7,6},{6,5},{5,4},{11,10},{10,9},{9,8},{15,14},{... | collective-permute-start | bytes 3145736 | tf_op jit(solution)/shard_map/ppermute | solution.py:752
  74.0 25.1 %collective-permute-start.4 = (bf16[1024,512]{1,0:T(8,128)(2,1)S(1)}, bf16[1024,512]{1,0:T(8,128)(2,1)}, u32[]{:S(2)}, u32[]{:S(2)}) collective-permute-start(bf16[1024,512]{1,0:T(8,128)(2,1)S(1)} %collective-permute-done.3.refs_1_), channel_id=1, source_target_pairs={{1,2},{2,3},{5,6},{6,7},{9,10},{10,11},{13,14},{14,15},{17,18},{18... | collective-permute-start | bytes 3145736 | tf_op jit(solution)/shard_map/ppermute | solution.py:752
  77.4 25.3 %collective-permute-start.7 = (bf16[1024,512]{1,0:T(8,128)(2,1)}, bf16[1024,512]{1,0:T(8,128)(2,1)}, u32[]{:S(2)}, u32[]{:S(2)}) collective-permute-start(bf16[1024,512]{1,0:T(8,128)(2,1)} %collective-permute-done.6.refs_4_), channel_id=1, source_target_pairs={{2,1},{1,0},{6,5},{5,4},{10,9},{9,8},{14,13},{13,12},{18,17},{17,1... | collective-permute-start | bytes 3145736 | tf_op jit(solution)/shard_map/ppermute | solution.py:752
  84.5 23.3 %all-to-all-start.1 = ((bf16[8,128,512]{2,1,0:T(8,128)(2,1)}), bf16[8,128,512]{2,1,0:T(8,128)(2,1)S(1)}, u32[]{:S(2)}, u32[]{:S(2)}) async-start(bf16[8,128,512]{2,1,0:T(8,128)(2,1)} %bitcast.12), calls=%async_computation.1 | async-start | bytes 2097152 | tf_op jit(solution)/shard_map/all_to_all | solution.py:842
  88.4 470.5 %reduce-scatter.3.cloned.1.call-start = ((), (), s32[]{:S(2)}) async-start(), calls=%async_computation.8 | async-start | bytes 28311552 | tf_op jit(solution)/shard_map/reduce_scatter | solution.py:933
  99.2 21.7 %collective-permute-start.5 = (bf16[1024,512]{1,0:T(8,128)(2,1)}, bf16[1024,512]{1,0:T(8,128)(2,1)}, u32[]{:S(2)}, u32[]{:S(2)}) collective-permute-start(bf16[1024,512]{1,0:T(8,128)(2,1)} %collective-permute-done.4.refs_2_), channel_id=1, source_target_pairs={{2,3},{6,7},{10,11},{14,15},{18,19},{22,23},{26,27},{30,31}} | collective-permute-start | bytes 3145736 | tf_op jit(solution)/shard_map/ppermute | solution.py:752
  102.7 18.1 %collective-permute-start.8 = (bf16[1024,512]{1,0:T(8,128)(2,1)}, bf16[1024,512]{1,0:T(8,128)(2,1)}, u32[]{:S(2)}, u32[]{:S(2)}) collective-permute-start(bf16[1024,512]{1,0:T(8,128)(2,1)} %collective-permute-done.7.refs_5_), channel_id=1, source_target_pairs={{1,0},{5,4},{9,8},{13,12},{17,16},{21,20},{25,24},{29,28}} | collective-permute-start | bytes 3145736 | tf_op jit(solution)/shard_map/ppermute | solution.py:752
  128.7 37.1 %collective-permute-start.10 = (bf16[1024,512]{1,0:T(8,128)(2,1)S(1)}, bf16[1024,512]{1,0:T(8,128)(2,1)S(1)}, u32[]{:S(2)}, u32[]{:S(2)}) collective-permute-start(bf16[1024,512]{1,0:T(8,128)(2,1)S(1)} %fusion.25.refs_7_.refs_0_), channel_id=1, source_target_pairs={{3,2},{2,1},{1,0},{7,6},{6,5},{5,4},{11,10},{10,9},{9,8},{15,14},{... | collective-permute-start | bytes 3145736 | tf_op jit(solution)/shard_map/ppermute | solution.py:752
  137.1 28.8 %collective-permute-start.9 = (bf16[1024,512]{1,0:T(8,128)(2,1)S(1)}, bf16[1024,512]{1,0:T(8,128)(2,1)}, u32[]{:S(2)}, u32[]{:S(2)}) collective-permute-start(bf16[1024,512]{1,0:T(8,128)(2,1)S(1)} %fusion.25.refs_7_.refs_0_), channel_id=1, source_target_pairs={{0,1},{1,2},{2,3},{4,5},{5,6},{6,7},{8,9},{9,10},{10,11},{12,13},{... | collective-permute-start | bytes 3145736 | tf_op jit(solution)/shard_map/ppermute | solution.py:752
  165.8 97.0 %copy-start.27 = (bf16[1024,512]{1,0:T(8,128)(2,1)}, bf16[1024,512]{1,0:T(8,128)(2,1)S(1)}, u32[]{:S(2)}) copy-start(bf16[1024,512]{1,0:T(8,128)(2,1)S(1)} %collective-permute-done.10.refs_11_.refs_4_) | copy-start | bytes 3145732
  165.8 24.3 %collective-permute-start.11 = (bf16[1024,512]{1,0:T(8,128)(2,1)}, bf16[1024,512]{1,0:T(8,128)(2,1)S(1)}, u32[]{:S(2)}, u32[]{:S(2)}) collective-permute-start(bf16[1024,512]{1,0:T(8,128)(2,1)} %attend.1.refs_0_.att_ref), channel_id=1, source_target_pairs={{0,1},{1,2},{2,3},{4,5},{5,6},{6,7},{8,9},{9,10},{10,11},{12,13},{... | collective-permute-start | bytes 3145736 | tf_op jit(solution)/shard_map/ppermute | solution.py:752
  167.7 24.3 %collective-permute-start.14 = (bf16[1024,512]{1,0:T(8,128)(2,1)}, bf16[1024,512]{1,0:T(8,128)(2,1)S(1)}, u32[]{:S(2)}, u32[]{:S(2)}) collective-permute-start(bf16[1024,512]{1,0:T(8,128)(2,1)} %attend.1.refs_0_.att_ref), channel_id=1, source_target_pairs={{3,2},{2,1},{1,0},{7,6},{6,5},{5,4},{11,10},{10,9},{9,8},{15,14},{... | collective-permute-start | bytes 3145736 | tf_op jit(solution)/shard_map/ppermute | solution.py:752
  190.1 22.9 %collective-permute-start.12 = (bf16[1024,512]{1,0:T(8,128)(2,1)S(1)}, bf16[1024,512]{1,0:T(8,128)(2,1)S(1)}, u32[]{:S(2)}, u32[]{:S(2)}) collective-permute-start(bf16[1024,512]{1,0:T(8,128)(2,1)S(1)} %collective-permute-done.11.refs_1_), channel_id=1, source_target_pairs={{1,2},{2,3},{5,6},{6,7},{9,10},{10,11},{13,14},{14,15},{17,18},{18... | collective-permute-start | bytes 3145736 | tf_op jit(solution)/shard_map/ppermute | solution.py:752
  192.1 23.3 %collective-permute-start.15 = (bf16[1024,512]{1,0:T(8,128)(2,1)S(1)}, bf16[1024,512]{1,0:T(8,128)(2,1)S(1)}, u32[]{:S(2)}, u32[]{:S(2)}) collective-permute-start(bf16[1024,512]{1,0:T(8,128)(2,1)S(1)} %collective-permute-done.14.refs_4_), channel_id=1, source_target_pairs={{2,1},{1,0},{6,5},{5,4},{10,9},{9,8},{14,13},{13,12},{18,17},{17,1... | collective-permute-start | bytes 3145736 | tf_op jit(solution)/shard_map/ppermute | solution.py:752
  213.0 20.9 %collective-permute-start.13 = (bf16[1024,512]{1,0:T(8,128)(2,1)S(1)}, bf16[1024,512]{1,0:T(8,128)(2,1)S(1)}, u32[]{:S(2)}, u32[]{:S(2)}) collective-permute-start(bf16[1024,512]{1,0:T(8,128)(2,1)S(1)} %collective-permute-done.12.refs_2_), channel_id=1, source_target_pairs={{2,3},{6,7},{10,11},{14,15},{18,19},{22,23},{26,27},{30,31}} | collective-permute-start | bytes 3145736 | tf_op jit(solution)/shard_map/ppermute | solution.py:752
  215.4 18.5 %collective-permute-start.16 = (bf16[1024,512]{1,0:T(8,128)(2,1)S(1)}, bf16[1024,512]{1,0:T(8,128)(2,1)S(1)}, u32[]{:S(2)}, u32[]{:S(2)}) collective-permute-start(bf16[1024,512]{1,0:T(8,128)(2,1)S(1)} %collective-permute-done.15.refs_5_), channel_id=1, source_target_pairs={{1,0},{5,4},{9,8},{13,12},{17,16},{21,20},{25,24},{29,28}} | collective-permute-start | bytes 3145736 | tf_op jit(solution)/shard_map/ppermute | solution.py:752
  233.9 29.0 %collective-permute-start.17 = (bf16[1024,512]{1,0:T(8,128)(2,1)}, bf16[1024,512]{1,0:T(8,128)(2,1)S(1)}, u32[]{:S(2)}, u32[]{:S(2)}) collective-permute-start(bf16[1024,512]{1,0:T(8,128)(2,1)} %collective-permute-done.9.refs_8_.refs_1_), channel_id=1, source_target_pairs={{1,2},{2,3},{5,6},{6,7},{9,10},{10,11},{13,14},{14,15},{17,18},{18... | collective-permute-start | bytes 3145736 | tf_op jit(solution)/shard_map/ppermute | solution.py:752
  238.3 24.5 %collective-permute-start.18 = (bf16[1024,512]{1,0:T(8,128)(2,1)S(1)}, bf16[1024,512]{1,0:T(8,128)(2,1)}, u32[]{:S(2)}, u32[]{:S(2)}) collective-permute-start(bf16[1024,512]{1,0:T(8,128)(2,1)S(1)} %collective-permute-done.10.refs_11_.refs_4_), channel_id=1, source_target_pairs={{2,1},{1,0},{6,5},{5,4},{10,9},{9,8},{14,13},{13,12},{18,17},{17,1... | collective-permute-start | bytes 3145736 | tf_op jit(solution)/shard_map/ppermute | solution.py:752
  262.9 27.0 %collective-permute-start.19 = (bf16[1024,512]{1,0:T(8,128)(2,1)S(1)}, bf16[1024,512]{1,0:T(8,128)(2,1)S(1)}, u32[]{:S(2)}, u32[]{:S(2)}) collective-permute-start(bf16[1024,512]{1,0:T(8,128)(2,1)S(1)} %collective-permute-done.17.refs_9_.refs_2_), channel_id=1, source_target_pairs={{2,3},{6,7},{10,11},{14,15},{18,19},{22,23},{26,27},{30,31}} | collective-permute-start | bytes 3145736 | tf_op jit(solution)/shard_map/ppermute | solution.py:752
  264.2 25.7 %collective-permute-start.20 = (bf16[1024,512]{1,0:T(8,128)(2,1)}, bf16[1024,512]{1,0:T(8,128)(2,1)}, u32[]{:S(2)}, u32[]{:S(2)}) collective-permute-start(bf16[1024,512]{1,0:T(8,128)(2,1)} %collective-permute-done.18.refs_12_.refs_5_), channel_id=1, source_target_pairs={{1,0},{5,4},{9,8},{13,12},{17,16},{21,20},{25,24},{29,28}} | collective-permute-start | bytes 3145736 | tf_op jit(solution)/shard_map/ppermute | solution.py:752
  309.1 92.7 %collective-permute-start.21 = (bf16[256,2048]{1,0:T(8,128)(2,1)}, bf16[256,2048]{1,0:T(8,128)(2,1)S(1)}, u32[]{:S(2)}, u32[]{:S(2)}) collective-permute-start(bf16[256,2048]{1,0:T(8,128)(2,1)} %first_two_grad.1), channel_id=1, source_target_pairs={{0,2},{1,3},{2,0},{3,1},{4,6},{5,7},{6,4},{7,5},{8,10},{9,11},{10,... | collective-permute-start | bytes 3145736 | tf_op jit(solution)/shard_map/ppermute | solution.py:773
  353.6 42.6 %collective-permute-start.22 = (bf16[256,2048]{1,0:T(8,128)(2,1)}, bf16[256,2048]{1,0:T(8,128)(2,1)}, u32[]{:S(2)}, u32[]{:S(2)}) collective-permute-start(bf16[256,2048]{1,0:T(8,128)(2,1)} %get-tuple-element.155), channel_id=1, source_target_pairs={{0,1},{1,2},{2,3},{3,0},{4,5},{5,6},{6,7},{7,4},{8,9},{9,10},{10,1... | collective-permute-start | bytes 3145736 | tf_op jit(solution)/shard_map/ppermute | solution.py:773
  358.2 43.6 %collective-permute-start.23 = (bf16[256,2048]{1,0:T(8,128)(2,1)}, bf16[256,2048]{1,0:T(8,128)(2,1)}, u32[]{:S(2)}, u32[]{:S(2)}) collective-permute-start(bf16[256,2048]{1,0:T(8,128)(2,1)} %get-tuple-element.156), channel_id=1, source_target_pairs={{0,3},{1,0},{2,1},{3,2},{4,7},{5,4},{6,5},{7,6},{8,11},{9,8},{10,9... | collective-permute-start | bytes 3145736 | tf_op jit(solution)/shard_map/ppermute | solution.py:773
  401.8 267.0 %reduce-scatter.5.cloned.1.call-start = ((), (), s32[]{:S(2)}) async-start(), calls=%async_computation.9 | async-start | bytes 9437184 | tf_op jit(solution)/shard_map/reduce_scatter | solution.py:990
  404.8 25.2 %collective-permute-start.24 = (bf16[256,2048]{1,0:T(8,128)(2,1)S(1)}, bf16[256,2048]{1,0:T(8,128)(2,1)}, u32[]{:S(2)}, u32[]{:S(2)}) collective-permute-start(bf16[256,2048]{1,0:T(8,128)(2,1)S(1)} %add_convert_fusion.4), channel_id=1, source_target_pairs={{0,1},{1,2},{2,3},{4,5},{5,6},{6,7},{8,9},{9,10},{10,11},{12,13},{... | collective-permute-start | bytes 3145736 | tf_op jit(solution)/shard_map/ppermute | solution.py:752
  408.3 23.6 %collective-permute-start.25 = (bf16[256,2048]{1,0:T(8,128)(2,1)S(1)}, bf16[256,2048]{1,0:T(8,128)(2,1)}, u32[]{:S(2)}, u32[]{:S(2)}) collective-permute-start(bf16[256,2048]{1,0:T(8,128)(2,1)S(1)} %add_convert_fusion.4), channel_id=1, source_target_pairs={{3,2},{2,1},{1,0},{7,6},{6,5},{5,4},{11,10},{10,9},{9,8},{15,14},{... | collective-permute-start | bytes 3145736 | tf_op jit(solution)/shard_map/ppermute | solution.py:752
  431.8 24.9 %collective-permute-start.26 = (bf16[256,2048]{1,0:T(8,128)(2,1)}, bf16[256,2048]{1,0:T(8,128)(2,1)}, u32[]{:S(2)}, u32[]{:S(2)}) collective-permute-start(bf16[256,2048]{1,0:T(8,128)(2,1)} %collective-permute-done.24), channel_id=1, source_target_pairs={{1,2},{2,3},{5,6},{6,7},{9,10},{10,11},{13,14},{14,15},{17,18},{18... | collective-permute-start | bytes 3145736 | tf_op jit(solution)/shard_map/ppermute | solution.py:752
  433.8 25.2 %collective-permute-start.27 = (bf16[256,2048]{1,0:T(8,128)(2,1)}, bf16[256,2048]{1,0:T(8,128)(2,1)}, u32[]{:S(2)}, u32[]{:S(2)}) collective-permute-start(bf16[256,2048]{1,0:T(8,128)(2,1)} %collective-permute-done.25), channel_id=1, source_target_pairs={{2,1},{1,0},{6,5},{5,4},{10,9},{9,8},{14,13},{13,12},{18,17},{17,1... | collective-permute-start | bytes 3145736 | tf_op jit(solution)/shard_map/ppermute | solution.py:752
  439.7 19.3 %collective-permute-start.28 = (bf16[1024,512]{1,0:T(8,128)(2,1)S(1)}, bf16[1024,512]{1,0:T(8,128)(2,1)}, u32[]{:S(2)}, u32[]{:S(2)}) collective-permute-start(bf16[1024,512]{1,0:T(8,128)(2,1)S(1)} %get-tuple-element.185), channel_id=1, source_target_pairs={{0,1},{4,5},{8,9},{12,13},{16,17},{20,21},{24,25},{28,29}} | collective-permute-start | bytes 3145736 | tf_op jit(solution)/shard_map/ppermute | solution.py:968
  441.3 24.2 %collective-permute-start.29 = (bf16[1024,512]{1,0:T(8,128)(2,1)S(1)}, bf16[1024,512]{1,0:T(8,128)(2,1)}, u32[]{:S(2)}, u32[]{:S(2)}) collective-permute-start(bf16[1024,512]{1,0:T(8,128)(2,1)S(1)} %get-tuple-element.183), channel_id=1, source_target_pairs={{3,2},{7,6},{11,10},{15,14},{19,18},{23,22},{27,26},{31,30}} | collective-permute-start | bytes 3145736 | tf_op jit(solution)/shard_map/ppermute | solution.py:968
  468.1 23.1 %collective-permute-start.32 = (bf16[1024,512]{1,0:T(8,128)(2,1)S(1)}, bf16[1024,512]{1,0:T(8,128)(2,1)S(1)}, u32[]{:S(2)}, u32[]{:S(2)}) collective-permute-start(bf16[1024,512]{1,0:T(8,128)(2,1)S(1)} %get-tuple-element.232), channel_id=1, source_target_pairs={{0,1},{1,2},{4,5},{5,6},{8,9},{9,10},{12,13},{13,14},{16,17},{17,1... | collective-permute-start | bytes 3145736 | tf_op jit(solution)/shard_map/ppermute | solution.py:968
  469.4 23.4 %collective-permute-start.33 = (bf16[1024,512]{1,0:T(8,128)(2,1)S(1)}, bf16[1024,512]{1,0:T(8,128)(2,1)S(1)}, u32[]{:S(2)}, u32[]{:S(2)}) collective-permute-start(bf16[1024,512]{1,0:T(8,128)(2,1)S(1)} %get-tuple-element.231), channel_id=1, source_target_pairs={{3,2},{2,1},{7,6},{6,5},{11,10},{10,9},{15,14},{14,13},{19,18},{18... | collective-permute-start | bytes 3145736 | tf_op jit(solution)/shard_map/ppermute | solution.py:968
  474.2 20.1 %collective-permute-start.30 = (bf16[256,2048]{1,0:T(8,128)(2,1)}, bf16[256,2048]{1,0:T(8,128)(2,1)S(1)}, u32[]{:S(2)}, u32[]{:S(2)}) collective-permute-start(bf16[256,2048]{1,0:T(8,128)(2,1)} %collective-permute-done.26), channel_id=1, source_target_pairs={{2,3},{6,7},{10,11},{14,15},{18,19},{22,23},{26,27},{30,31}} | collective-permute-start | bytes 3145736 | tf_op jit(solution)/shard_map/ppermute | solution.py:752
  475.6 18.7 %collective-permute-start.31 = (bf16[256,2048]{1,0:T(8,128)(2,1)}, bf16[256,2048]{1,0:T(8,128)(2,1)S(1)}, u32[]{:S(2)}, u32[]{:S(2)}) collective-permute-start(bf16[256,2048]{1,0:T(8,128)(2,1)} %collective-permute-done.27), channel_id=1, source_target_pairs={{1,0},{5,4},{9,8},{13,12},{17,16},{21,20},{25,24},{29,28}} | collective-permute-start | bytes 3145736 | tf_op jit(solution)/shard_map/ppermute | solution.py:752
  494.6 39.5 %collective-permute-start.35 = (bf16[1024,512]{1,0:T(8,128)(2,1)S(1)}, bf16[1024,512]{1,0:T(8,128)(2,1)S(1)}, u32[]{:S(2)}, u32[]{:S(2)}) collective-permute-start(bf16[1024,512]{1,0:T(8,128)(2,1)S(1)} %add_convert_fusion.2), channel_id=1, source_target_pairs={{3,2},{2,1},{1,0},{7,6},{6,5},{5,4},{11,10},{10,9},{9,8},{15,14},{... | collective-permute-start | bytes 3145736 | tf_op jit(solution)/shard_map/ppermute | solution.py:968
  498.6 35.5 %collective-permute-start.34 = (bf16[1024,512]{1,0:T(8,128)(2,1)S(1)}, bf16[1024,512]{1,0:T(8,128)(2,1)S(1)}, u32[]{:S(2)}, u32[]{:S(2)}) collective-permute-start(bf16[1024,512]{1,0:T(8,128)(2,1)S(1)} %add_convert_fusion.3), channel_id=1, source_target_pairs={{0,1},{1,2},{2,3},{4,5},{5,6},{6,7},{8,9},{9,10},{10,11},{12,13},{... | collective-permute-start | bytes 3145736 | tf_op jit(solution)/shard_map/ppermute | solution.py:968
  558.9 69.3 %collective-permute-start.36 = (bf16[1024,512]{1,0:T(8,128)(2,1)}, bf16[1024,512]{1,0:T(8,128)(2,1)S(1)}, u32[]{:S(2)}, u32[]{:S(2)}) collective-permute-start(bf16[1024,512]{1,0:T(8,128)(2,1)} %copy-done.24), channel_id=1, source_target_pairs={{0,2},{1,3},{2,0},{3,1},{4,6},{5,7},{6,4},{7,5},{8,10},{9,11},{10,... | collective-permute-start | bytes 3145736 | tf_op jit(solution)/shard_map/ppermute | solution.py:773
  559.5 92.9 %collective-permute-start.37 = (bf16[1024,512]{1,0:T(8,128)(2,1)}, bf16[1024,512]{1,0:T(8,128)(2,1)S(1)}, u32[]{:S(2)}, u32[]{:S(2)}) collective-permute-start(bf16[1024,512]{1,0:T(8,128)(2,1)} %copy-done.23), channel_id=1, source_target_pairs={{0,1},{1,2},{2,3},{3,0},{4,5},{5,6},{6,7},{7,4},{8,9},{9,10},{10,1... | collective-permute-start | bytes 3145736 | tf_op jit(solution)/shard_map/ppermute | solution.py:773
  561.0 91.4 %collective-permute-start.38 = (bf16[1024,512]{1,0:T(8,128)(2,1)S(1)}, bf16[1024,512]{1,0:T(8,128)(2,1)S(1)}, u32[]{:S(2)}, u32[]{:S(2)}) collective-permute-start(bf16[1024,512]{1,0:T(8,128)(2,1)S(1)} %get-tuple-element.195), channel_id=1, source_target_pairs={{0,3},{1,0},{2,1},{3,2},{4,7},{5,4},{6,5},{7,6},{8,11},{9,8},{10,9... | collective-permute-start | bytes 3145736 | tf_op jit(solution)/shard_map/ppermute | solution.py:773
  659.6 30.2 %all-to-all-start.2 = ((bf16[8,128,1024]{2,1,0:T(8,128)(2,1)}), bf16[8,128,1024]{2,1,0:T(8,128)(2,1)S(1)}, u32[]{:S(2)}, u32[]{:S(2)}) async-start(bf16[8,128,1024]{2,1,0:T(8,128)(2,1)} %bitcast.52), calls=%async_computation.2 | async-start | bytes 4194304 | tf_op jit(solution)/shard_map/all_to_all | solution.py:842
  (60 other events, 854.0 us)
Sparse Core Ops, SparseCore 0:
  10.5 58.5 all-gather.5
  71.0 65.6 all-gather.3
  138.6 125.3 all-gather.7
  401.9 156.9 reduce-scatter.2
  562.2 71.2 reduce-scatter.4

commit v7 on v6

--- a/solution.py
+++ b/solution.py
@@ -976,7 +976,9 @@
         sine,
     )
     one_terms = one_grad_pieces(place, qkv_grad, full_qkv, normed_one, inverse_one)
-    one_came = [sent_on(term, "tp", shards, step) for term, step in zip(one_terms, steps)]
+    one_came = [
+        sent_on(term, "tp", shards, step) for term, step in list(zip(one_terms, steps))[::-1]
+    ]
     full_hidden_grad = jnp.concatenate(
         line_whole(after(back_low, *one_terms[:3]), back_come, "tp", shards), axis=0
     )
@@ -999,9 +1001,12 @@
     sum_gate, sum_up, sum_down = sum_mlp.astype(f32)
     back_here = added(one_terms[-1].astype(f32), one_came)
     input_here = features_of(full_hidden_grad, own_shard).astype(f32) + back_here
-    output_here = hidden + added(terms[0].astype(f32), mlp_come)
-    here = jnp.concatenate([output_here.astype(bf16), input_here.astype(bf16)], axis=1)
-    sent_back = transposed_times(place_in, here).astype(bf16)
+    output_here = (hidden + added(terms[0].astype(f32), mlp_come)).astype(bf16)
+    out_came = over_fsdp(
+        transposed_times(place_in, after(output_here, grad_att)).astype(bf16)
+    )
+    output = transposed_times(deal_out, out_came).astype(bf16)
+    sent_back = transposed_times(place_in, input_here.astype(bf16)).astype(bf16)
     sums = (
         sum_att[:, : local_width],
         sum_att[:, local_width : 2 * local_width],
@@ -1012,8 +1017,8 @@
         sum_down,
     )
     came_back, *sums = lax.optimization_barrier((over_fsdp(sent_back), *sums))
-    home = transposed_times(deal_out, came_back).astype(bf16)
-    return (home[:, :width], home[:, width:], *sums)
+    input_grad = transposed_times(deal_out, came_back).astype(bf16)
+    return (output, input_grad, *sums)
 
 
 def solution(mesh):

time: 707 us -> 697 us (0.986)
  waiting for transfers between devices: 266 us -> 249 us
    all_to_all x3 -> x4, waiting for transfers between devices: 34.7 us -> 25.8 us  [over_fsdp(): return lax.all_to_all(rows, 'fsdp', split_axis=0, concat_axis=0, tiled=True)]
    ppermute x9, waiting for transfers between devices: 95.9 us -> 88.3 us  [sent_on(): lax.ppermute(term, axis, [(i, (i + step) % size) for i in range(size)])]
    all_to_all x3 -> x4, starting transfers between devices: 11.3 us -> 15.6 us  [over_fsdp(): return lax.all_to_all(rows, 'fsdp', split_axis=0, concat_axis=0, tiled=True)]
  transfers between devices with their start and end apart: 47 -> 48, of which waited for: 20 -> 19; matrix products, arithmetic and copies ran while one was open for 8% -> 9% of each run, Pallas kernels for 30% -> 30%
where the time goes in v7:
time: 697 us; the launch traced here: 690 us
  waiting for transfers between devices  249 us (36%)
  Pallas kernels  227 us (33%)
  starting transfers between devices  115 us (16%)
  other arithmetic  31.2 us (4%)
  matrix products  31.1 us (4%)
  local copies, waits for them, and re-layouts  18.5 us (3%)
  between operations  17.4 us (2%)
    ppermute x12, waiting for transfers between devices, line_step(): lax.ppermute(from_low, axis, up)  113 us
    ppermute x9, waiting for transfers between devices, sent_on(): lax.ppermute(term, axis, [(i, (i + step) % size) for i in range(size)])  88.3 us
    ppermute x12, starting transfers between devices, line_step(): lax.ppermute(from_high, axis, down)  38.5 us
    pallas_call x3, Pallas kernels, mlp_grads(): pl.pallas_call(body, grid=(model // BLOCK,), in_specs=specs, out_specs=pl...  35.8 us
    ppermute x12, starting transfers between devices, line_step(): lax.ppermute(from_low, axis, up)  33.6 us
    all_to_all x4, waiting for transfers between devices, over_fsdp(): return lax.all_to_all(rows, 'fsdp', split_axis=0, concat_axis=0, tiled=True)  25.8 us
    pallas_call x1, Pallas kernels, two_grad_pieces(): pl.pallas_call(two_grad_kernel, grid_spec=pltpu.PrefetchScalarGridSpec(nu...  24.5 us
    pallas_call x1, Pallas kernels, mlp_up(): pl.pallas_call(up_kernel, grid=(hidden_units // WIDE,), in_specs=[pl.Bloc...  24 us
  transfers between devices with their start and end apart: 48, of which 19 were waited for; matrix products, arithmetic and copies ran while one was open for 9% of the time, Pallas kernels for 30%

profile of v7, /device:TPU:16, one launch (start us, length us, event | category | flops | bytes accessed | tf_op | source)
XLA Modules:
  0.0 689.6 jit_solution(12525392062548718282)
XLA Ops:
  13.1 3.9 all-to-all-start
  20.3 3.7 pad_maximum_fusion.1
  26.3 17.3 %all-to-all-done = bf16[8,128,640]{2,1,0:T(8,128)(2,1)S(1)} async-done(((bf16[8,128,640]{2,1,0:T(8,128)(2,1)}), bf16[8,128,640]{2,1,0:T(8,128)(2,1)S(1)}, u32[]{:S(2)}, u32[]{:S(2)}) %all-to-all-start) | async-done | bytes 1310752 | tf_op jit(solution)/shard_map/all_to_all | solution.py:842
  54.7 19.3 %collective-permute-done.3.refs_1_ = bf16[1024,512]{1,0:T(8,128)(2,1)S(1)} collective-permute-done((bf16[1024,512]{1,0:T(8,128)(2,1)S(1)}, bf16[1024,512]{1,0:T(8,128)(2,1)S(1)}, u32[]{:S(2)}, u32[]{:S(2)}) %collective-permute-start.3) | collective-permute-done | bytes 1048608 | tf_op jit(solution)/shard_map/ppermute | solution.py:752
  77.4 4.4 collective-permute-start.7
  84.6 3.8 all-to-all-start.1
  88.6 10.5 %collective-permute-done.4.refs_2_ = bf16[1024,512]{1,0:T(8,128)(2,1)} collective-permute-done((bf16[1024,512]{1,0:T(8,128)(2,1)S(1)}, bf16[1024,512]{1,0:T(8,128)(2,1)}, u32[]{:S(2)}, u32[]{:S(2)}) %collective-permute-start.4) | collective-permute-done | bytes 1048608 | tf_op jit(solution)/shard_map/ppermute | solution.py:752
  109.1 11.8 %collective-permute-done.5.refs_3_ = bf16[1024,512]{1,0:T(8,128)(2,1)} collective-permute-done((bf16[1024,512]{1,0:T(8,128)(2,1)}, bf16[1024,512]{1,0:T(8,128)(2,1)}, u32[]{:S(2)}, u32[]{:S(2)}) %collective-permute-start.5) | collective-permute-done | bytes 1048608 | tf_op jit(solution)/shard_map/ppermute | solution.py:752
  120.9 7.8 %gathered_norm.1 = (bf16[1024,2048]{1,0:T(8,128)(2,1)}, bf16[1024,2048]{1,0:T(8,128)(2,1)}, f32[1024,1]{1,0:T(8,128)}) custom-call(s32[1]{0:T(128)} %bitcast.6.me_ref, bf16[1024,512]{1,0:T(8,128)(2,1)} %copy-done.39, bf16[1024,512]{1,0:T(8,128)(2,1)} %copy-done.40, bf16[1024,512]{1,0:T(8,128)(2,1)} %collective-permute-done.4.refs_2_, ...), custom_call_target="tpu_custom_call" | custom-call | flops 41943040 | bytes 16777216 | tf_op jit(solution)/shard_map/gathered_norm/pallas_call | solution.py:117
  128.6 4.4 collective-permute-start.9
  133.0 5.9 collective-permute-start.10
  140.0 13.7 %qkv.1 = (bf16[1024,512]{1,0:T(8,128)(2,1)}, bf16[1024,512]{1,0:T(8,128)(2,1)}, bf16[1024,512]{1,0:T(8,128)(2,1)}) custom-call(bf16[1024,2048]{1,0:T(8,128)(2,1)} %get-tuple-element.123.rows_ref.unit_ref.normed_ref, bf16[2048,1536]{1,0:T(8,128)(2,1)} %all-gather.6.cloned.1.call-done.wq_ref.wk_ref.wv_ref.weight_ref, ...), custom_call_target="tpu_custom_call" | custom-call | flops 6442450944 | bytes 10485760 | tf_op jit(solution)/shard_map/qkv/pallas_call | solution.py:160
  153.7 12.0 %attend.1.refs_0_.att_ref = bf16[1024,512]{1,0:T(8,128)(2,1)} custom-call(bf16[1024,512]{1,0:T(8,128)(2,1)} %get-tuple-element.126.q_ref, bf16[1024,512]{1,0:T(8,128)(2,1)} %get-tuple-element.127.k_ref, bf16[1024,512]{1,0:T(8,128)(2,1)} %get-tuple-element.128.v_ref, s32[1024,1]{1,0:T(8,128)} %copy.27.column_ref, s32[1,1024]{1,0:T(1,128)} %bitcast.52), custom_call_target="tpu_custom_call" | custom-call | flops 2147483648 | bytes 4194304 | tf_op jit(solution)/shard_map/attend/pallas_call | solution.py:212
  167.7 4.0 collective-permute-start.14
  171.7 18.0 %collective-permute-done.11.refs_1_ = bf16[1024,512]{1,0:T(8,128)(2,1)S(1)} collective-permute-done((bf16[1024,512]{1,0:T(8,128)(2,1)}, bf16[1024,512]{1,0:T(8,128)(2,1)S(1)}, u32[]{:S(2)}, u32[]{:S(2)}) %collective-permute-start.11) | collective-permute-done | bytes 1048608 | tf_op jit(solution)/shard_map/ppermute | solution.py:752
  191.6 4.0 collective-permute-start.15
  195.7 16.8 %collective-permute-done.12.refs_2_ = bf16[1024,512]{1,0:T(8,128)(2,1)S(1)} collective-permute-done((bf16[1024,512]{1,0:T(8,128)(2,1)S(1)}, bf16[1024,512]{1,0:T(8,128)(2,1)S(1)}, u32[]{:S(2)}, u32[]{:S(2)}) %collective-permute-start.12) | collective-permute-done | bytes 1048608 | tf_op jit(solution)/shard_map/ppermute | solution.py:752
  215.8 17.8 %collective-permute-done.13.refs_3_ = bf16[1024,512]{1,0:T(8,128)(2,1)S(1)} collective-permute-done((bf16[1024,512]{1,0:T(8,128)(2,1)S(1)}, bf16[1024,512]{1,0:T(8,128)(2,1)S(1)}, u32[]{:S(2)}, u32[]{:S(2)}) %collective-permute-start.13) | collective-permute-done | bytes 1048608 | tf_op jit(solution)/shard_map/ppermute | solution.py:752
  233.6 4.4 collective-permute-start.17
  238.1 4.4 collective-permute-start.18
  243.7 18.0 %hidden.1 = (f32[1024,512]{1,0:T(8,128)}, bf16[1024,2048]{1,0:T(8,128)(2,1)}, f32[1024,1]{1,0:T(8,128)}) custom-call(s32[1]{0:T(128)} %bitcast.6.me_ref, bf16[2048,2048]{1,0:T(8,128)(2,1)} %bitcast.65, bf16[1024,2048]{1,0:T(8,128)(2,1)} %get-tuple-element.120.rows_ref, bf16[1024,512]{1,0:T(8,128)(2,1)} %attend.1.refs_0_.att_ref, ...), custom_call_target="tpu_custom_call" | custom-call | flops 8589934592 | bytes 29360128 | tf_op jit(solution)/shard_map/hidden/pallas_call | solution.py:319
  264.8 24.0 %mlp_up.1 = (bf16[1024,2048]{1,0:T(8,128)(2,1)}, bf16[1024,2048]{1,0:T(8,128)(2,1)}, bf16[1024,2048]{1,0:T(8,128)(2,1)}) custom-call(bf16[1024,2048]{1,0:T(8,128)(2,1)} %get-tuple-element.142.rows_ref.refs_5_.refs_2_.refs_6_.refs_10_.refs_0_, ...), custom_call_target="tpu_custom_call" | custom-call | flops 17179869184 | bytes 41943040 | tf_op jit(solution)/shard_map/mlp_up/pallas_call | solution.py:362
  289.8 18.2 %first_two_grad.1 = bf16[256,2048]{1,0:T(8,128)(2,1)} custom-call(s32[2]{0:T(128)} %pad_add_fusion.at_ref, bf16[3,2048,2048]{2,1,0:T(8,128)(2,1)} %all-gather.8.cloned.1.call-done.gate_ref.up_ref.refs_0_.refs_1_.refs_2_.down_ref.refs_12_.refs_13_, ...), custom_call_target="tpu_custom_call" | custom-call | flops 6442450944 | bytes 25165824 | tf_op jit(solution)/shard_map/first_two_grad/pallas_call | solution.py:521
  308.9 18.9 %mlp_down_back.1 = (bf16[1024,2048]{1,0:T(8,128)(2,1)}, bf16[1024,2048]{1,0:T(8,128)(2,1)}, bf16[1024,2048]{1,0:T(8,128)(2,1)}) custom-call(s32[1]{0:T(128)} %bitcast.6.me_ref, bf16[3,2048,2048]{2,1,0:T(8,128)(2,1)} %all-gather.8.cloned.1.call-done.gate_ref.up_ref.refs_0_.refs_1_.refs_2_.down_ref.refs_12_.refs_13_, ...), custom_call_target="tpu_custom_call" | custom-call | flops 8589934592 | bytes 37748736 | tf_op jit(solution)/shard_map/mlp_down_back/pallas_call | solution.py:409
  327.9 24.5 %two_grad.1 = (bf16[256,2048]{1,0:T(8,128)(2,1)}, bf16[256,2048]{1,0:T(8,128)(2,1)}, bf16[256,2048]{1,0:T(8,128)(2,1)}) custom-call(s32[3]{0:T(128)} %pad_add_fusion.1.order_ref, bf16[1024,2048]{1,0:T(8,128)(2,1)} %get-tuple-element.159.refs_0_.refs_4_.refs_8_.refs_1_, bf16[1024,2048]{1,0:T(8,128)(2,1)} %get-tuple-element.154.refs_1_.refs_5_.refs_9_, ...), custom_call_target="tpu_custom_call" | custom-call | flops 12884901888 | bytes 16777216 | tf_op jit(solution)/shard_map/two_grad/pallas_call | solution.py:589
  352.3 4.6 collective-permute-start.22
  359.2 11.9 %mlp_grads.3.refs_2_ = bf16[3,2048,2048]{2,1,0:T(8,128)(2,1)} custom-call(bf16[1024,2048]{1,0:T(8,128)(2,1)S(1)} %copy-done.2, bf16[1024,2048]{1,0:T(8,128)(2,1)S(1)} %copy-done.4), custom_call_target="tpu_custom_call" | custom-call | flops 8589934592 | bytes 16777216 | tf_op jit(solution)/shard_map/mlp_grads/pallas_call | solution.py:729
  371.1 11.9 %mlp_grads.4.refs_2_ = bf16[3,2048,2048]{2,1,0:T(8,128)(2,1)} custom-call(bf16[1024,2048]{1,0:T(8,128)(2,1)S(1)} %copy-done.2, bf16[1024,2048]{1,0:T(8,128)(2,1)S(1)} %copy-done.3, bf16[3,2048,2048]{2,1,0:T(8,128)(2,1)} %mlp_grads.3.refs_2_), custom_call_target="tpu_custom_call", output_to_operand_aliasing={{}: (2, {})} | custom-call | flops 8589934592 | bytes 16777216 | tf_op jit(solution)/shard_map/mlp_grads/pallas_call | solution.py:729
  383.0 11.9 %mlp_grads.5 = bf16[3,2048,2048]{2,1,0:T(8,128)(2,1)} custom-call(bf16[1024,2048]{1,0:T(8,128)(2,1)S(1)} %copy-done.11, bf16[1024,2048]{1,0:T(8,128)(2,1)S(1)} %copy-done.8, bf16[3,2048,2048]{2,1,0:T(8,128)(2,1)} %mlp_grads.4.refs_2_), custom_call_target="tpu_custom_call", output_to_operand_aliasing={{}: (2, {})} | custom-call | flops 8589934592 | bytes 16777216 | tf_op jit(solution)/shard_map/mlp_grads/pallas_call | solution.py:729
  394.9 7.4 %collective-permute-done.23 = bf16[256,2048]{1,0:T(8,128)(2,1)} collective-permute-done((bf16[256,2048]{1,0:T(8,128)(2,1)}, bf16[256,2048]{1,0:T(8,128)(2,1)}, u32[]{:S(2)}, u32[]{:S(2)}) %collective-permute-start.23) | collective-permute-done | bytes 1048608 | tf_op jit(solution)/shard_map/ppermute | solution.py:773
  411.3 12.3 %mlp_piece.1 = (bf16[1024,512]{1,0:T(8,128)(2,1)S(1)}, bf16[1024,512]{1,0:T(8,128)(2,1)S(1)}, bf16[1024,512]{1,0:T(8,128)(2,1)S(1)}, bf16[1024,512]{1,0:T(8,128)(2,1)S(1)}) custom-call(s32[4]{0:T(128)S(1)} %pad_add_fusion.2.order_ref, bf16[1024,2048]{1,0:T(8,128)(2,1)S(1)} %copy-done.12, ...), custom_call_target="tpu_custom_call" | custom-call | flops 8589934592 | bytes 8388608 | tf_op jit(solution)/shard_map/mlp_piece/pallas_call | solution.py:448
  425.6 5.4 collective-permute-done.24
  436.1 5.9 collective-permute-start.27
  445.1 13.8 %collective-permute-done.26 = bf16[256,2048]{1,0:T(8,128)(2,1)} collective-permute-done((bf16[256,2048]{1,0:T(8,128)(2,1)}, bf16[256,2048]{1,0:T(8,128)(2,1)}, u32[]{:S(2)}, u32[]{:S(2)}) %collective-permute-start.26) | collective-permute-done | bytes 1048608 | tf_op jit(solution)/shard_map/ppermute | solution.py:752
  461.1 6.5 collective-permute-done.29
  473.8 4.8 collective-permute-start.33
  488.9 6.3 collective-permute-done.32
  500.2 4.5 collective-permute-start.35
  504.8 17.2 %attend_back.1 = (bf16[1024,512]{1,0:T(8,128)(2,1)S(1)}, bf16[1024,512]{1,0:T(8,128)(2,1)S(1)}, bf16[1024,512]{1,0:T(8,128)(2,1)S(1)}) custom-call(s32[1]{0:T(128)} %bitcast.6.me_ref, bf16[1024,512]{1,0:T(8,128)(2,1)S(1)} %copy-done.16, bf16[1024,512]{1,0:T(8,128)(2,1)S(1)} %copy-done.17, bf16[1024,512]{1,0:T(8,128)(2,1)S(1)} %copy-done.18, ...), custom_call_target="tpu_custom_call" | custom-call | flops 1000 | bytes 1000 | tf_op jit(solution)/shard_map/attend_back/pallas_call | solution.py:276
  522.0 10.5 %one_grad.1 = (bf16[1024,512]{1,0:T(8,128)(2,1)S(1)}, bf16[1024,512]{1,0:T(8,128)(2,1)S(1)}, bf16[1024,512]{1,0:T(8,128)(2,1)S(1)}, bf16[1024,512]{1,0:T(8,128)(2,1)S(1)}) custom-call(s32[4]{0:T(128)S(1)} %pad_add_fusion.3.place_ref, bf16[1024,512]{1,0:T(8,128)(2,1)S(1)} %get-tuple-element.199.dq_ref, bf16[1024,512]{1,0:T(8,128)(2,1)S(1)} %get-tuple-element.200.dk_ref, ...), custom_call_target="tpu_custom_call" | custom-call | flops 6442450944 | bytes 15728640 | tf_op jit(solution)/shard_map/one_grad/pallas_call | solution.py:627
  532.6 3.9 select_select_fusion.3
  539.2 13.6 %att_grads.1 = bf16[8,256,2048]{2,1,0:T(8,128)(2,1)S(1)} custom-call(bf16[1024,2048]{1,0:T(8,128)(2,1)S(1)} %copy-done.7, bf16[1024,512]{1,0:T(8,128)(2,1)S(1)} %get-tuple-element.199.dq_ref, bf16[1024,512]{1,0:T(8,128)(2,1)S(1)} %get-tuple-element.200.dk_ref, bf16[1024,512]{1,0:T(8,128)(2,1)S(1)} %get-tuple-element.201.dv_ref, ...), custom_call_target="tpu_custom_call" | custom-call | flops 1000 | bytes 1000 | tf_op jit(solution)/shard_map/att_grads/pallas_call | solution.py:686
  567.8 4.4 all-to-all-start.2
  572.1 56.6 %collective-permute-done.38 = bf16[1024,512]{1,0:T(8,128)(2,1)} collective-permute-done((bf16[1024,512]{1,0:T(8,128)(2,1)}, bf16[1024,512]{1,0:T(8,128)(2,1)}, u32[]{:S(2)}, u32[]{:S(2)}) %collective-permute-start.38) | collective-permute-done | bytes 1048608 | tf_op jit(solution)/shard_map/ppermute | solution.py:773
  628.8 24.2 %collective-permute-done.37 = bf16[1024,512]{1,0:T(8,128)(2,1)} collective-permute-done((bf16[1024,512]{1,0:T(8,128)(2,1)}, bf16[1024,512]{1,0:T(8,128)(2,1)}, u32[]{:S(2)}, u32[]{:S(2)}) %collective-permute-start.37) | collective-permute-done | bytes 1048608 | tf_op jit(solution)/shard_map/ppermute | solution.py:773
  653.1 4.9 fusion.24
  661.7 3.6 all-to-all-start.3
  672.1 8.5 %all-to-all-done.3 = bf16[8,128,512]{2,1,0:T(8,128)(2,1)S(1)} async-done(((bf16[8,128,512]{2,1,0:T(8,128)(2,1)}), bf16[8,128,512]{2,1,0:T(8,128)(2,1)S(1)}, u32[]{:S(2)}, u32[]{:S(2)}) %all-to-all-start.3) | async-done | bytes 1048608 | tf_op jit(solution)/shard_map/all_to_all | solution.py:842
  (239 shorter events, 125.8 us)
Async XLA Ops:
  7.2 132.8 %all-gather.6.cloned.1.call-start = ((), (), s32[]{:S(2)}) async-start(), calls=%async_computation.7 | async-start | bytes 7077888 | tf_op jit(solution)/shard_map/all_gather | solution.py:848
  13.1 30.5 %all-to-all-start = ((bf16[8,128,640]{2,1,0:T(8,128)(2,1)}), bf16[8,128,640]{2,1,0:T(8,128)(2,1)S(1)}, u32[]{:S(2)}, u32[]{:S(2)}) async-start(bf16[8,128,640]{2,1,0:T(8,128)(2,1)} %bitcast), calls=%async_computation | async-start | bytes 2621440 | tf_op jit(solution)/shard_map/all_to_all | solution.py:842
  17.0 226.8 %all-gather.4.cloned.1.call-start = ((), (), s32[]{:S(2)}) async-start(), calls=%async_computation.6 | async-start | bytes 9437184 | tf_op jit(solution)/shard_map/all_gather | solution.py:866
  17.0 27.2 %collective-permute-start = (bf16[64,2048]{1,0:T(8,128)(2,1)}, bf16[64,2048]{1,0:T(8,128)(2,1)}, u32[]{:S(2)}, u32[]{:S(2)}) collective-permute-start(bf16[64,2048]{1,0:T(8,128)(2,1)} %param.17), channel_id=1, source_target_pairs={{0,1},{1,2},{2,3},{3,0},{4,5},{5,6},{6,7},{7,4},{8,9},{9,10},{10,1... | collective-permute-start | bytes 786440 | tf_op jit(solution)/shard_map/ppermute | solution.py:773
  18.6 25.6 %collective-permute-start.1 = (bf16[64,2048]{1,0:T(8,128)(2,1)}, bf16[64,2048]{1,0:T(8,128)(2,1)}, u32[]{:S(2)}, u32[]{:S(2)}) collective-permute-start(bf16[64,2048]{1,0:T(8,128)(2,1)} %param.17), channel_id=1, source_target_pairs={{0,2},{1,3},{2,0},{3,1},{4,6},{5,7},{6,4},{7,5},{8,10},{9,11},{10,... | collective-permute-start | bytes 786440 | tf_op jit(solution)/shard_map/ppermute | solution.py:773
  19.0 25.3 %collective-permute-start.2 = (bf16[64,2048]{1,0:T(8,128)(2,1)}, bf16[64,2048]{1,0:T(8,128)(2,1)}, u32[]{:S(2)}, u32[]{:S(2)}) collective-permute-start(bf16[64,2048]{1,0:T(8,128)(2,1)} %param.17), channel_id=1, source_target_pairs={{0,3},{1,0},{2,1},{3,2},{4,7},{5,4},{6,5},{7,6},{8,11},{9,8},{10,9... | collective-permute-start | bytes 786440 | tf_op jit(solution)/shard_map/ppermute | solution.py:773
  46.7 218.1 %all-gather.8.cloned.1.call-start = ((), (), s32[]{:S(2)}) async-start(), calls=%async_computation.8 | async-start | bytes 28311552 | tf_op jit(solution)/shard_map/all_gather | solution.py:868
  48.8 25.2 %collective-permute-start.3 = (bf16[1024,512]{1,0:T(8,128)(2,1)S(1)}, bf16[1024,512]{1,0:T(8,128)(2,1)S(1)}, u32[]{:S(2)}, u32[]{:S(2)}) collective-permute-start(bf16[1024,512]{1,0:T(8,128)(2,1)S(1)} %fusion.21.refs_0_), channel_id=1, source_target_pairs={{0,1},{1,2},{2,3},{4,5},{5,6},{6,7},{8,9},{9,10},{10,11},{12,13},{... | collective-permute-start | bytes 3145736 | tf_op jit(solution)/shard_map/ppermute | solution.py:752
  52.3 25.1 %collective-permute-start.6 = (bf16[1024,512]{1,0:T(8,128)(2,1)S(1)}, bf16[1024,512]{1,0:T(8,128)(2,1)}, u32[]{:S(2)}, u32[]{:S(2)}) collective-permute-start(bf16[1024,512]{1,0:T(8,128)(2,1)S(1)} %fusion.21.refs_0_), channel_id=1, source_target_pairs={{3,2},{2,1},{1,0},{7,6},{6,5},{5,4},{11,10},{10,9},{9,8},{15,14},{... | collective-permute-start | bytes 3145736 | tf_op jit(solution)/shard_map/ppermute | solution.py:752
  74.0 25.1 %collective-permute-start.4 = (bf16[1024,512]{1,0:T(8,128)(2,1)S(1)}, bf16[1024,512]{1,0:T(8,128)(2,1)}, u32[]{:S(2)}, u32[]{:S(2)}) collective-permute-start(bf16[1024,512]{1,0:T(8,128)(2,1)S(1)} %collective-permute-done.3.refs_1_), channel_id=1, source_target_pairs={{1,2},{2,3},{5,6},{6,7},{9,10},{10,11},{13,14},{14,15},{17,18},{18... | collective-permute-start | bytes 3145736 | tf_op jit(solution)/shard_map/ppermute | solution.py:752
  77.4 25.3 %collective-permute-start.7 = (bf16[1024,512]{1,0:T(8,128)(2,1)}, bf16[1024,512]{1,0:T(8,128)(2,1)}, u32[]{:S(2)}, u32[]{:S(2)}) collective-permute-start(bf16[1024,512]{1,0:T(8,128)(2,1)} %collective-permute-done.6.refs_4_), channel_id=1, source_target_pairs={{2,1},{1,0},{6,5},{5,4},{10,9},{9,8},{14,13},{13,12},{18,17},{17,1... | collective-permute-start | bytes 3145736 | tf_op jit(solution)/shard_map/ppermute | solution.py:752
  84.6 23.2 %all-to-all-start.1 = ((bf16[8,128,512]{2,1,0:T(8,128)(2,1)}), bf16[8,128,512]{2,1,0:T(8,128)(2,1)S(1)}, u32[]{:S(2)}, u32[]{:S(2)}) async-start(bf16[8,128,512]{2,1,0:T(8,128)(2,1)} %bitcast.12), calls=%async_computation.1 | async-start | bytes 2097152 | tf_op jit(solution)/shard_map/all_to_all | solution.py:842
  88.4 471.1 %reduce-scatter.3.cloned.1.call-start = ((), (), s32[]{:S(2)}) async-start(), calls=%async_computation.9 | async-start | bytes 28311552 | tf_op jit(solution)/shard_map/reduce_scatter | solution.py:933
  99.2 21.7 %collective-permute-start.5 = (bf16[1024,512]{1,0:T(8,128)(2,1)}, bf16[1024,512]{1,0:T(8,128)(2,1)}, u32[]{:S(2)}, u32[]{:S(2)}) collective-permute-start(bf16[1024,512]{1,0:T(8,128)(2,1)} %collective-permute-done.4.refs_2_), channel_id=1, source_target_pairs={{2,3},{6,7},{10,11},{14,15},{18,19},{22,23},{26,27},{30,31}} | collective-permute-start | bytes 3145736 | tf_op jit(solution)/shard_map/ppermute | solution.py:752
  102.7 18.1 %collective-permute-start.8 = (bf16[1024,512]{1,0:T(8,128)(2,1)}, bf16[1024,512]{1,0:T(8,128)(2,1)}, u32[]{:S(2)}, u32[]{:S(2)}) collective-permute-start(bf16[1024,512]{1,0:T(8,128)(2,1)} %collective-permute-done.7.refs_5_), channel_id=1, source_target_pairs={{1,0},{5,4},{9,8},{13,12},{17,16},{21,20},{25,24},{29,28}} | collective-permute-start | bytes 3145736 | tf_op jit(solution)/shard_map/ppermute | solution.py:752
  128.6 37.2 %collective-permute-start.9 = (bf16[1024,512]{1,0:T(8,128)(2,1)S(1)}, bf16[1024,512]{1,0:T(8,128)(2,1)S(1)}, u32[]{:S(2)}, u32[]{:S(2)}) collective-permute-start(bf16[1024,512]{1,0:T(8,128)(2,1)S(1)} %fusion.22.refs_7_.refs_0_), channel_id=1, source_target_pairs={{0,1},{1,2},{2,3},{4,5},{5,6},{6,7},{8,9},{9,10},{10,11},{12,13},{... | collective-permute-start | bytes 3145736 | tf_op jit(solution)/shard_map/ppermute | solution.py:752
  133.0 32.7 %collective-permute-start.10 = (bf16[1024,512]{1,0:T(8,128)(2,1)S(1)}, bf16[1024,512]{1,0:T(8,128)(2,1)}, u32[]{:S(2)}, u32[]{:S(2)}) collective-permute-start(bf16[1024,512]{1,0:T(8,128)(2,1)S(1)} %fusion.22.refs_7_.refs_0_), channel_id=1, source_target_pairs={{3,2},{2,1},{1,0},{7,6},{6,5},{5,4},{11,10},{10,9},{9,8},{15,14},{... | collective-permute-start | bytes 3145736 | tf_op jit(solution)/shard_map/ppermute | solution.py:752
  165.8 23.9 %collective-permute-start.11 = (bf16[1024,512]{1,0:T(8,128)(2,1)}, bf16[1024,512]{1,0:T(8,128)(2,1)S(1)}, u32[]{:S(2)}, u32[]{:S(2)}) collective-permute-start(bf16[1024,512]{1,0:T(8,128)(2,1)} %attend.1.refs_0_.att_ref), channel_id=1, source_target_pairs={{0,1},{1,2},{2,3},{4,5},{5,6},{6,7},{8,9},{9,10},{10,11},{12,13},{... | collective-permute-start | bytes 3145736 | tf_op jit(solution)/shard_map/ppermute | solution.py:752
  167.7 23.9 %collective-permute-start.14 = (bf16[1024,512]{1,0:T(8,128)(2,1)}, bf16[1024,512]{1,0:T(8,128)(2,1)S(1)}, u32[]{:S(2)}, u32[]{:S(2)}) collective-permute-start(bf16[1024,512]{1,0:T(8,128)(2,1)} %attend.1.refs_0_.att_ref), channel_id=1, source_target_pairs={{3,2},{2,1},{1,0},{7,6},{6,5},{5,4},{11,10},{10,9},{9,8},{15,14},{... | collective-permute-start | bytes 3145736 | tf_op jit(solution)/shard_map/ppermute | solution.py:752
  189.7 22.8 %collective-permute-start.12 = (bf16[1024,512]{1,0:T(8,128)(2,1)S(1)}, bf16[1024,512]{1,0:T(8,128)(2,1)S(1)}, u32[]{:S(2)}, u32[]{:S(2)}) collective-permute-start(bf16[1024,512]{1,0:T(8,128)(2,1)S(1)} %collective-permute-done.11.refs_1_), channel_id=1, source_target_pairs={{1,2},{2,3},{5,6},{6,7},{9,10},{10,11},{13,14},{14,15},{17,18},{18... | collective-permute-start | bytes 3145736 | tf_op jit(solution)/shard_map/ppermute | solution.py:752
  191.6 23.3 %collective-permute-start.15 = (bf16[1024,512]{1,0:T(8,128)(2,1)S(1)}, bf16[1024,512]{1,0:T(8,128)(2,1)S(1)}, u32[]{:S(2)}, u32[]{:S(2)}) collective-permute-start(bf16[1024,512]{1,0:T(8,128)(2,1)S(1)} %collective-permute-done.14.refs_4_), channel_id=1, source_target_pairs={{2,1},{1,0},{6,5},{5,4},{10,9},{9,8},{14,13},{13,12},{18,17},{17,1... | collective-permute-start | bytes 3145736 | tf_op jit(solution)/shard_map/ppermute | solution.py:752
  212.4 21.2 %collective-permute-start.13 = (bf16[1024,512]{1,0:T(8,128)(2,1)S(1)}, bf16[1024,512]{1,0:T(8,128)(2,1)S(1)}, u32[]{:S(2)}, u32[]{:S(2)}) collective-permute-start(bf16[1024,512]{1,0:T(8,128)(2,1)S(1)} %collective-permute-done.12.refs_2_), channel_id=1, source_target_pairs={{2,3},{6,7},{10,11},{14,15},{18,19},{22,23},{26,27},{30,31}} | collective-permute-start | bytes 3145736 | tf_op jit(solution)/shard_map/ppermute | solution.py:752
  214.9 18.7 %collective-permute-start.16 = (bf16[1024,512]{1,0:T(8,128)(2,1)S(1)}, bf16[1024,512]{1,0:T(8,128)(2,1)S(1)}, u32[]{:S(2)}, u32[]{:S(2)}) collective-permute-start(bf16[1024,512]{1,0:T(8,128)(2,1)S(1)} %collective-permute-done.15.refs_5_), channel_id=1, source_target_pairs={{1,0},{5,4},{9,8},{13,12},{17,16},{21,20},{25,24},{29,28}} | collective-permute-start | bytes 3145736 | tf_op jit(solution)/shard_map/ppermute | solution.py:752
  233.6 28.2 %collective-permute-start.17 = (bf16[1024,512]{1,0:T(8,128)(2,1)S(1)}, bf16[1024,512]{1,0:T(8,128)(2,1)S(1)}, u32[]{:S(2)}, u32[]{:S(2)}) collective-permute-start(bf16[1024,512]{1,0:T(8,128)(2,1)S(1)} %collective-permute-done.9.refs_8_.refs_1_), channel_id=1, source_target_pairs={{1,2},{2,3},{5,6},{6,7},{9,10},{10,11},{13,14},{14,15},{17,18},{18... | collective-permute-start | bytes 3145736 | tf_op jit(solution)/shard_map/ppermute | solution.py:752
  238.1 23.7 %collective-permute-start.18 = (bf16[1024,512]{1,0:T(8,128)(2,1)}, bf16[1024,512]{1,0:T(8,128)(2,1)}, u32[]{:S(2)}, u32[]{:S(2)}) collective-permute-start(bf16[1024,512]{1,0:T(8,128)(2,1)} %collective-permute-done.10.refs_11_.refs_4_), channel_id=1, source_target_pairs={{2,1},{1,0},{6,5},{5,4},{10,9},{9,8},{14,13},{13,12},{18,17},{17,1... | collective-permute-start | bytes 3145736 | tf_op jit(solution)/shard_map/ppermute | solution.py:752
  261.8 27.0 %collective-permute-start.19 = (bf16[1024,512]{1,0:T(8,128)(2,1)S(1)}, bf16[1024,512]{1,0:T(8,128)(2,1)S(1)}, u32[]{:S(2)}, u32[]{:S(2)}) collective-permute-start(bf16[1024,512]{1,0:T(8,128)(2,1)S(1)} %collective-permute-done.17.refs_9_.refs_2_), channel_id=1, source_target_pairs={{2,3},{6,7},{10,11},{14,15},{18,19},{22,23},{26,27},{30,31}} | collective-permute-start | bytes 3145736 | tf_op jit(solution)/shard_map/ppermute | solution.py:752
  263.2 25.7 %collective-permute-start.20 = (bf16[1024,512]{1,0:T(8,128)(2,1)}, bf16[1024,512]{1,0:T(8,128)(2,1)}, u32[]{:S(2)}, u32[]{:S(2)}) collective-permute-start(bf16[1024,512]{1,0:T(8,128)(2,1)} %collective-permute-done.18.refs_12_.refs_5_), channel_id=1, source_target_pairs={{1,0},{5,4},{9,8},{13,12},{17,16},{21,20},{25,24},{29,28}} | collective-permute-start | bytes 3145736 | tf_op jit(solution)/shard_map/ppermute | solution.py:752
  308.0 86.9 %collective-permute-start.21 = (bf16[256,2048]{1,0:T(8,128)(2,1)}, bf16[256,2048]{1,0:T(8,128)(2,1)S(1)}, u32[]{:S(2)}, u32[]{:S(2)}) collective-permute-start(bf16[256,2048]{1,0:T(8,128)(2,1)} %first_two_grad.1), channel_id=1, source_target_pairs={{0,2},{1,3},{2,0},{3,1},{4,6},{5,7},{6,4},{7,5},{8,10},{9,11},{10,... | collective-permute-start | bytes 3145736 | tf_op jit(solution)/shard_map/ppermute | solution.py:773
  352.3 42.6 %collective-permute-start.22 = (bf16[256,2048]{1,0:T(8,128)(2,1)}, bf16[256,2048]{1,0:T(8,128)(2,1)}, u32[]{:S(2)}, u32[]{:S(2)}) collective-permute-start(bf16[256,2048]{1,0:T(8,128)(2,1)} %get-tuple-element.156), channel_id=1, source_target_pairs={{0,1},{1,2},{2,3},{3,0},{4,5},{5,6},{6,7},{7,4},{8,9},{9,10},{10,1... | collective-permute-start | bytes 3145736 | tf_op jit(solution)/shard_map/ppermute | solution.py:773
  357.0 45.3 %collective-permute-start.23 = (bf16[256,2048]{1,0:T(8,128)(2,1)}, bf16[256,2048]{1,0:T(8,128)(2,1)}, u32[]{:S(2)}, u32[]{:S(2)}) collective-permute-start(bf16[256,2048]{1,0:T(8,128)(2,1)} %get-tuple-element.157), channel_id=1, source_target_pairs={{0,3},{1,0},{2,1},{3,2},{4,7},{5,4},{6,5},{7,6},{8,11},{9,8},{10,9... | collective-permute-start | bytes 3145736 | tf_op jit(solution)/shard_map/ppermute | solution.py:773
  402.3 266.2 %reduce-scatter.5.cloned.1.call-start = ((), (), s32[]{:S(2)}) async-start(), calls=%async_computation.10 | async-start | bytes 9437184 | tf_op jit(solution)/shard_map/reduce_scatter | solution.py:992
  405.3 25.7 %collective-permute-start.24 = (bf16[256,2048]{1,0:T(8,128)(2,1)S(1)}, bf16[256,2048]{1,0:T(8,128)(2,1)}, u32[]{:S(2)}, u32[]{:S(2)}) collective-permute-start(bf16[256,2048]{1,0:T(8,128)(2,1)S(1)} %add_convert_fusion.4), channel_id=1, source_target_pairs={{0,1},{1,2},{2,3},{4,5},{5,6},{6,7},{8,9},{9,10},{10,11},{12,13},{... | collective-permute-start | bytes 3145736 | tf_op jit(solution)/shard_map/ppermute | solution.py:752
  408.8 25.4 %collective-permute-start.25 = (bf16[256,2048]{1,0:T(8,128)(2,1)S(1)}, bf16[256,2048]{1,0:T(8,128)(2,1)}, u32[]{:S(2)}, u32[]{:S(2)}) collective-permute-start(bf16[256,2048]{1,0:T(8,128)(2,1)S(1)} %add_convert_fusion.4), channel_id=1, source_target_pairs={{3,2},{2,1},{1,0},{7,6},{6,5},{5,4},{11,10},{10,9},{9,8},{15,14},{... | collective-permute-start | bytes 3145736 | tf_op jit(solution)/shard_map/ppermute | solution.py:752
  434.2 24.7 %collective-permute-start.26 = (bf16[256,2048]{1,0:T(8,128)(2,1)}, bf16[256,2048]{1,0:T(8,128)(2,1)}, u32[]{:S(2)}, u32[]{:S(2)}) collective-permute-start(bf16[256,2048]{1,0:T(8,128)(2,1)} %collective-permute-done.24), channel_id=1, source_target_pairs={{1,2},{2,3},{5,6},{6,7},{9,10},{10,11},{13,14},{14,15},{17,18},{18... | collective-permute-start | bytes 3145736 | tf_op jit(solution)/shard_map/ppermute | solution.py:752
  436.1 24.9 %collective-permute-start.27 = (bf16[256,2048]{1,0:T(8,128)(2,1)}, bf16[256,2048]{1,0:T(8,128)(2,1)}, u32[]{:S(2)}, u32[]{:S(2)}) collective-permute-start(bf16[256,2048]{1,0:T(8,128)(2,1)} %collective-permute-done.25), channel_id=1, source_target_pairs={{2,1},{1,0},{6,5},{5,4},{10,9},{9,8},{14,13},{13,12},{18,17},{17,1... | collective-permute-start | bytes 3145736 | tf_op jit(solution)/shard_map/ppermute | solution.py:752
  442.0 19.0 %collective-permute-start.28 = (bf16[1024,512]{1,0:T(8,128)(2,1)S(1)}, bf16[1024,512]{1,0:T(8,128)(2,1)}, u32[]{:S(2)}, u32[]{:S(2)}) collective-permute-start(bf16[1024,512]{1,0:T(8,128)(2,1)S(1)} %get-tuple-element.186), channel_id=1, source_target_pairs={{0,1},{4,5},{8,9},{12,13},{16,17},{20,21},{24,25},{28,29}} | collective-permute-start | bytes 3145736 | tf_op jit(solution)/shard_map/ppermute | solution.py:968
  443.7 23.9 %collective-permute-start.29 = (bf16[1024,512]{1,0:T(8,128)(2,1)S(1)}, bf16[1024,512]{1,0:T(8,128)(2,1)}, u32[]{:S(2)}, u32[]{:S(2)}) collective-permute-start(bf16[1024,512]{1,0:T(8,128)(2,1)S(1)} %get-tuple-element.184), channel_id=1, source_target_pairs={{3,2},{7,6},{11,10},{15,14},{19,18},{23,22},{27,26},{31,30}} | collective-permute-start | bytes 3145736 | tf_op jit(solution)/shard_map/ppermute | solution.py:968
  467.6 21.2 %collective-permute-start.30 = (bf16[256,2048]{1,0:T(8,128)(2,1)}, bf16[256,2048]{1,0:T(8,128)(2,1)S(1)}, u32[]{:S(2)}, u32[]{:S(2)}) collective-permute-start(bf16[256,2048]{1,0:T(8,128)(2,1)} %collective-permute-done.26), channel_id=1, source_target_pairs={{2,3},{6,7},{10,11},{14,15},{18,19},{22,23},{26,27},{30,31}} | collective-permute-start | bytes 3145736 | tf_op jit(solution)/shard_map/ppermute | solution.py:752
  469.0 19.9 %collective-permute-start.31 = (bf16[256,2048]{1,0:T(8,128)(2,1)}, bf16[256,2048]{1,0:T(8,128)(2,1)S(1)}, u32[]{:S(2)}, u32[]{:S(2)}) collective-permute-start(bf16[256,2048]{1,0:T(8,128)(2,1)} %collective-permute-done.27), channel_id=1, source_target_pairs={{1,0},{5,4},{9,8},{13,12},{17,16},{21,20},{25,24},{29,28}} | collective-permute-start | bytes 3145736 | tf_op jit(solution)/shard_map/ppermute | solution.py:752
  472.5 22.7 %collective-permute-start.32 = (bf16[1024,512]{1,0:T(8,128)(2,1)S(1)}, bf16[1024,512]{1,0:T(8,128)(2,1)S(1)}, u32[]{:S(2)}, u32[]{:S(2)}) collective-permute-start(bf16[1024,512]{1,0:T(8,128)(2,1)S(1)} %get-tuple-element.232), channel_id=1, source_target_pairs={{0,1},{1,2},{4,5},{5,6},{8,9},{9,10},{12,13},{13,14},{16,17},{17,1... | collective-permute-start | bytes 3145736 | tf_op jit(solution)/shard_map/ppermute | solution.py:968
  473.8 23.0 %collective-permute-start.33 = (bf16[1024,512]{1,0:T(8,128)(2,1)S(1)}, bf16[1024,512]{1,0:T(8,128)(2,1)S(1)}, u32[]{:S(2)}, u32[]{:S(2)}) collective-permute-start(bf16[1024,512]{1,0:T(8,128)(2,1)S(1)} %get-tuple-element.231), channel_id=1, source_target_pairs={{3,2},{2,1},{7,6},{6,5},{11,10},{10,9},{15,14},{14,13},{19,18},{18... | collective-permute-start | bytes 3145736 | tf_op jit(solution)/shard_map/ppermute | solution.py:968
  497.1 40.2 %collective-permute-start.34 = (bf16[1024,512]{1,0:T(8,128)(2,1)S(1)}, bf16[1024,512]{1,0:T(8,128)(2,1)S(1)}, u32[]{:S(2)}, u32[]{:S(2)}) collective-permute-start(bf16[1024,512]{1,0:T(8,128)(2,1)S(1)} %add_convert_fusion.3), channel_id=1, source_target_pairs={{0,1},{1,2},{2,3},{4,5},{5,6},{6,7},{8,9},{9,10},{10,11},{12,13},{... | collective-permute-start | bytes 3145736 | tf_op jit(solution)/shard_map/ppermute | solution.py:968
  500.2 37.1 %collective-permute-start.35 = (bf16[1024,512]{1,0:T(8,128)(2,1)S(1)}, bf16[1024,512]{1,0:T(8,128)(2,1)S(1)}, u32[]{:S(2)}, u32[]{:S(2)}) collective-permute-start(bf16[1024,512]{1,0:T(8,128)(2,1)S(1)} %add_convert_fusion.2), channel_id=1, source_target_pairs={{3,2},{2,1},{1,0},{7,6},{6,5},{5,4},{11,10},{10,9},{9,8},{15,14},{... | collective-permute-start | bytes 3145736 | tf_op jit(solution)/shard_map/ppermute | solution.py:968
  559.5 69.3 %collective-permute-start.38 = (bf16[1024,512]{1,0:T(8,128)(2,1)}, bf16[1024,512]{1,0:T(8,128)(2,1)}, u32[]{:S(2)}, u32[]{:S(2)}) collective-permute-start(bf16[1024,512]{1,0:T(8,128)(2,1)} %copy-done.24), channel_id=1, source_target_pairs={{0,2},{1,3},{2,0},{3,1},{4,6},{5,7},{6,4},{7,5},{8,10},{9,11},{10,... | collective-permute-start | bytes 3145736 | tf_op jit(solution)/shard_map/ppermute | solution.py:773
  560.0 93.0 %collective-permute-start.37 = (bf16[1024,512]{1,0:T(8,128)(2,1)}, bf16[1024,512]{1,0:T(8,128)(2,1)}, u32[]{:S(2)}, u32[]{:S(2)}) collective-permute-start(bf16[1024,512]{1,0:T(8,128)(2,1)} %copy-done.23), channel_id=1, source_target_pairs={{0,1},{1,2},{2,3},{3,0},{4,5},{5,6},{6,7},{7,4},{8,9},{9,10},{10,1... | collective-permute-start | bytes 3145736 | tf_op jit(solution)/shard_map/ppermute | solution.py:773
  561.6 91.4 %collective-permute-start.36 = (bf16[1024,512]{1,0:T(8,128)(2,1)S(1)}, bf16[1024,512]{1,0:T(8,128)(2,1)}, u32[]{:S(2)}, u32[]{:S(2)}) collective-permute-start(bf16[1024,512]{1,0:T(8,128)(2,1)S(1)} %get-tuple-element.196), channel_id=1, source_target_pairs={{0,3},{1,0},{2,1},{3,2},{4,7},{5,4},{6,5},{7,6},{8,11},{9,8},{10,9... | collective-permute-start | bytes 3145736 | tf_op jit(solution)/shard_map/ppermute | solution.py:773
  567.8 93.9 %all-to-all-start.2 = ((bf16[8,128,512]{2,1,0:T(8,128)(2,1)}), bf16[8,128,512]{2,1,0:T(8,128)(2,1)}, u32[]{:S(2)}, u32[]{:S(2)}) async-start(bf16[8,128,512]{2,1,0:T(8,128)(2,1)} %bitcast.57), calls=%async_computation.3 | async-start | bytes 2097152 | tf_op jit(solution)/shard_map/all_to_all | solution.py:842
  661.7 18.9 %all-to-all-start.3 = ((bf16[8,128,512]{2,1,0:T(8,128)(2,1)}), bf16[8,128,512]{2,1,0:T(8,128)(2,1)S(1)}, u32[]{:S(2)}, u32[]{:S(2)}) async-start(bf16[8,128,512]{2,1,0:T(8,128)(2,1)} %bitcast.26), calls=%async_computation.4 | async-start | bytes 2097152 | tf_op jit(solution)/shard_map/all_to_all | solution.py:842
  (59 other events, 1010.6 us)
Sparse Core Ops, SparseCore 0:
  10.5 58.5 all-gather.5
  71.6 65.6 all-gather.3
  139.2 125.3 all-gather.7
  402.4 156.9 reduce-scatter.2
  562.7 71.2 reduce-scatter.4

commit v8 on v7

--- a/solution.py
+++ b/solution.py
@@ -694,7 +694,7 @@
         ],
         out_specs=pl.BlockSpec((1, tall, model), lambda i: (i, 0, 0)),
         out_shape=jax.ShapeDtypeStruct((groups, tall, model), bf16),
-        compiler_params=params(32),
+        compiler_params=params(),
         cost_estimate=cost(1000, 1000),
         name="att_grads",
     )(operand, *qkv_grad, attended, hidden_grad)

time: 697 us -> 697 us (level)
  transfers between devices with their start and end apart: 48 -> 48, of which waited for: 19 -> 19; matrix products, arithmetic and copies ran while one was open for 9% -> 10% of each run, Pallas kernels for 30% -> 31%
where the time goes in v8:
time: 697 us; the launch traced here: 690 us
  waiting for transfers between devices  250 us (36%)
  Pallas kernels  230 us (33%)
  starting transfers between devices  116 us (17%)
  other arithmetic  32.8 us (5%)
  matrix products  31.1 us (4%)
  between operations  17.4 us (2%)
  local copies, waits for them, and re-layouts  12.3 us (2%)
    ppermute x12, waiting for transfers between devices, line_step(): lax.ppermute(from_low, axis, up)  113 us
    ppermute x9, waiting for transfers between devices, sent_on(): lax.ppermute(term, axis, [(i, (i + step) % size) for i in range(size)])  88.4 us
    ppermute x12, starting transfers between devices, line_step(): lax.ppermute(from_high, axis, down)  38.4 us
    pallas_call x3, Pallas kernels, mlp_grads(): pl.pallas_call(body, grid=(model // BLOCK,), in_specs=specs, out_specs=pl...  35.6 us
    ppermute x12, starting transfers between devices, line_step(): lax.ppermute(from_low, axis, up)  33.6 us
    all_to_all x4, waiting for transfers between devices, over_fsdp(): return lax.all_to_all(rows, 'fsdp', split_axis=0, concat_axis=0, tiled=True)  25.7 us
    pallas_call x1, Pallas kernels, two_grad_pieces(): pl.pallas_call(two_grad_kernel, grid_spec=pltpu.PrefetchScalarGridSpec(nu...  24.4 us
    pallas_call x1, Pallas kernels, mlp_up(): pl.pallas_call(up_kernel, grid=(hidden_units // WIDE,), in_specs=[pl.Bloc...  24 us
  transfers between devices with their start and end apart: 48, of which 19 were waited for; matrix products, arithmetic and copies ran while one was open for 10% of the time, Pallas kernels for 31%

profile of v8, /device:TPU:16, one launch (start us, length us, event | category | flops | bytes accessed | tf_op | source)
XLA Modules:
  0.0 689.6 jit_solution(13028074280371911219)
XLA Ops:
  13.1 3.9 all-to-all-start
  20.3 3.8 pad_maximum_fusion.1
  26.3 17.3 %all-to-all-done = bf16[8,128,640]{2,1,0:T(8,128)(2,1)S(1)} async-done(((bf16[8,128,640]{2,1,0:T(8,128)(2,1)}), bf16[8,128,640]{2,1,0:T(8,128)(2,1)S(1)}, u32[]{:S(2)}, u32[]{:S(2)}) %all-to-all-start) | async-done | bytes 1310752 | tf_op jit(solution)/shard_map/all_to_all | solution.py:842
  54.7 19.3 %collective-permute-done.3.refs_1_ = bf16[1024,512]{1,0:T(8,128)(2,1)S(1)} collective-permute-done((bf16[1024,512]{1,0:T(8,128)(2,1)S(1)}, bf16[1024,512]{1,0:T(8,128)(2,1)S(1)}, u32[]{:S(2)}, u32[]{:S(2)}) %collective-permute-start.3) | collective-permute-done | bytes 1048608 | tf_op jit(solution)/shard_map/ppermute | solution.py:752
  77.4 4.4 collective-permute-start.7
  84.6 3.8 all-to-all-start.1
  88.6 10.5 %collective-permute-done.4.refs_2_ = bf16[1024,512]{1,0:T(8,128)(2,1)} collective-permute-done((bf16[1024,512]{1,0:T(8,128)(2,1)S(1)}, bf16[1024,512]{1,0:T(8,128)(2,1)}, u32[]{:S(2)}, u32[]{:S(2)}) %collective-permute-start.4) | collective-permute-done | bytes 1048608 | tf_op jit(solution)/shard_map/ppermute | solution.py:752
  109.1 11.8 %collective-permute-done.5.refs_3_ = bf16[1024,512]{1,0:T(8,128)(2,1)} collective-permute-done((bf16[1024,512]{1,0:T(8,128)(2,1)}, bf16[1024,512]{1,0:T(8,128)(2,1)}, u32[]{:S(2)}, u32[]{:S(2)}) %collective-permute-start.5) | collective-permute-done | bytes 1048608 | tf_op jit(solution)/shard_map/ppermute | solution.py:752
  120.9 7.8 %gathered_norm.1 = (bf16[1024,2048]{1,0:T(8,128)(2,1)}, bf16[1024,2048]{1,0:T(8,128)(2,1)}, f32[1024,1]{1,0:T(8,128)}) custom-call(s32[1]{0:T(128)} %bitcast.6.me_ref, bf16[1024,512]{1,0:T(8,128)(2,1)} %copy-done.38, bf16[1024,512]{1,0:T(8,128)(2,1)} %copy-done.39, bf16[1024,512]{1,0:T(8,128)(2,1)} %collective-permute-done.4.refs_2_, ...), custom_call_target="tpu_custom_call" | custom-call | flops 41943040 | bytes 16777216 | tf_op jit(solution)/shard_map/gathered_norm/pallas_call | solution.py:117
  128.6 4.4 collective-permute-start.9
  133.0 5.9 collective-permute-start.10
  140.0 13.7 %qkv.1 = (bf16[1024,512]{1,0:T(8,128)(2,1)}, bf16[1024,512]{1,0:T(8,128)(2,1)}, bf16[1024,512]{1,0:T(8,128)(2,1)}) custom-call(bf16[1024,2048]{1,0:T(8,128)(2,1)} %get-tuple-element.123.rows_ref.unit_ref.normed_ref, bf16[2048,1536]{1,0:T(8,128)(2,1)} %all-gather.6.cloned.1.call-done.wq_ref.wk_ref.wv_ref.weight_ref, ...), custom_call_target="tpu_custom_call" | custom-call | flops 6442450944 | bytes 10485760 | tf_op jit(solution)/shard_map/qkv/pallas_call | solution.py:160
  153.7 12.0 %attend.1.refs_0_.att_ref = bf16[1024,512]{1,0:T(8,128)(2,1)} custom-call(bf16[1024,512]{1,0:T(8,128)(2,1)} %get-tuple-element.126.q_ref, bf16[1024,512]{1,0:T(8,128)(2,1)} %get-tuple-element.127.k_ref, bf16[1024,512]{1,0:T(8,128)(2,1)} %get-tuple-element.128.v_ref, s32[1024,1]{1,0:T(8,128)} %copy.27.column_ref, s32[1,1024]{1,0:T(1,128)} %bitcast.52), custom_call_target="tpu_custom_call" | custom-call | flops 2147483648 | bytes 4194304 | tf_op jit(solution)/shard_map/attend/pallas_call | solution.py:212
  167.7 4.0 collective-permute-start.14
  171.7 18.0 %collective-permute-done.11.refs_1_ = bf16[1024,512]{1,0:T(8,128)(2,1)S(1)} collective-permute-done((bf16[1024,512]{1,0:T(8,128)(2,1)}, bf16[1024,512]{1,0:T(8,128)(2,1)S(1)}, u32[]{:S(2)}, u32[]{:S(2)}) %collective-permute-start.11) | collective-permute-done | bytes 1048608 | tf_op jit(solution)/shard_map/ppermute | solution.py:752
  191.6 4.0 collective-permute-start.15
  195.6 16.8 %collective-permute-done.12.refs_2_ = bf16[1024,512]{1,0:T(8,128)(2,1)S(1)} collective-permute-done((bf16[1024,512]{1,0:T(8,128)(2,1)S(1)}, bf16[1024,512]{1,0:T(8,128)(2,1)S(1)}, u32[]{:S(2)}, u32[]{:S(2)}) %collective-permute-start.12) | collective-permute-done | bytes 1048608 | tf_op jit(solution)/shard_map/ppermute | solution.py:752
  215.8 17.8 %collective-permute-done.13.refs_3_ = bf16[1024,512]{1,0:T(8,128)(2,1)S(1)} collective-permute-done((bf16[1024,512]{1,0:T(8,128)(2,1)S(1)}, bf16[1024,512]{1,0:T(8,128)(2,1)S(1)}, u32[]{:S(2)}, u32[]{:S(2)}) %collective-permute-start.13) | collective-permute-done | bytes 1048608 | tf_op jit(solution)/shard_map/ppermute | solution.py:752
  233.6 4.4 collective-permute-start.17
  238.1 4.4 collective-permute-start.18
  243.7 18.0 %hidden.1 = (f32[1024,512]{1,0:T(8,128)}, bf16[1024,2048]{1,0:T(8,128)(2,1)}, f32[1024,1]{1,0:T(8,128)}) custom-call(s32[1]{0:T(128)} %bitcast.6.me_ref, bf16[2048,2048]{1,0:T(8,128)(2,1)} %bitcast.65, bf16[1024,2048]{1,0:T(8,128)(2,1)} %get-tuple-element.120.rows_ref, bf16[1024,512]{1,0:T(8,128)(2,1)} %attend.1.refs_0_.att_ref, ...), custom_call_target="tpu_custom_call" | custom-call | flops 8589934592 | bytes 29360128 | tf_op jit(solution)/shard_map/hidden/pallas_call | solution.py:319
  264.7 24.0 %mlp_up.1 = (bf16[1024,2048]{1,0:T(8,128)(2,1)}, bf16[1024,2048]{1,0:T(8,128)(2,1)}, bf16[1024,2048]{1,0:T(8,128)(2,1)}) custom-call(bf16[1024,2048]{1,0:T(8,128)(2,1)} %get-tuple-element.142.rows_ref.refs_5_.refs_2_.refs_6_.refs_10_.refs_0_, ...), custom_call_target="tpu_custom_call" | custom-call | flops 17179869184 | bytes 41943040 | tf_op jit(solution)/shard_map/mlp_up/pallas_call | solution.py:362
  289.7 18.2 %first_two_grad.1 = bf16[256,2048]{1,0:T(8,128)(2,1)} custom-call(s32[2]{0:T(128)} %pad_add_fusion.at_ref, bf16[3,2048,2048]{2,1,0:T(8,128)(2,1)} %all-gather.8.cloned.1.call-done.gate_ref.up_ref.refs_0_.refs_1_.refs_2_.down_ref.refs_12_.refs_13_, ...), custom_call_target="tpu_custom_call" | custom-call | flops 6442450944 | bytes 25165824 | tf_op jit(solution)/shard_map/first_two_grad/pallas_call | solution.py:521
  308.9 18.9 %mlp_down_back.1 = (bf16[1024,2048]{1,0:T(8,128)(2,1)}, bf16[1024,2048]{1,0:T(8,128)(2,1)}, bf16[1024,2048]{1,0:T(8,128)(2,1)}) custom-call(s32[1]{0:T(128)} %bitcast.6.me_ref, bf16[3,2048,2048]{2,1,0:T(8,128)(2,1)} %all-gather.8.cloned.1.call-done.gate_ref.up_ref.refs_0_.refs_1_.refs_2_.down_ref.refs_12_.refs_13_, ...), custom_call_target="tpu_custom_call" | custom-call | flops 8589934592 | bytes 37748736 | tf_op jit(solution)/shard_map/mlp_down_back/pallas_call | solution.py:409
  327.8 24.4 %two_grad.1 = (bf16[256,2048]{1,0:T(8,128)(2,1)}, bf16[256,2048]{1,0:T(8,128)(2,1)}, bf16[256,2048]{1,0:T(8,128)(2,1)}) custom-call(s32[3]{0:T(128)} %pad_add_fusion.1.order_ref, bf16[1024,2048]{1,0:T(8,128)(2,1)} %get-tuple-element.159.refs_0_.refs_4_.refs_8_.refs_1_, bf16[1024,2048]{1,0:T(8,128)(2,1)} %get-tuple-element.154.refs_1_.refs_5_.refs_9_, ...), custom_call_target="tpu_custom_call" | custom-call | flops 12884901888 | bytes 16777216 | tf_op jit(solution)/shard_map/two_grad/pallas_call | solution.py:589
  352.3 4.7 collective-permute-start.22
  359.1 11.9 %mlp_grads.3.refs_2_ = bf16[3,2048,2048]{2,1,0:T(8,128)(2,1)} custom-call(bf16[1024,2048]{1,0:T(8,128)(2,1)S(1)} %copy-done.2, bf16[1024,2048]{1,0:T(8,128)(2,1)S(1)} %copy-done.4), custom_call_target="tpu_custom_call" | custom-call | flops 8589934592 | bytes 16777216 | tf_op jit(solution)/shard_map/mlp_grads/pallas_call | solution.py:729
  371.0 11.9 %mlp_grads.4.refs_2_ = bf16[3,2048,2048]{2,1,0:T(8,128)(2,1)} custom-call(bf16[1024,2048]{1,0:T(8,128)(2,1)S(1)} %copy-done.2, bf16[1024,2048]{1,0:T(8,128)(2,1)S(1)} %copy-done.3, bf16[3,2048,2048]{2,1,0:T(8,128)(2,1)} %mlp_grads.3.refs_2_), custom_call_target="tpu_custom_call", output_to_operand_aliasing={{}: (2, {})} | custom-call | flops 8589934592 | bytes 16777216 | tf_op jit(solution)/shard_map/mlp_grads/pallas_call | solution.py:729
  382.9 11.8 %mlp_grads.5 = bf16[3,2048,2048]{2,1,0:T(8,128)(2,1)} custom-call(bf16[1024,2048]{1,0:T(8,128)(2,1)S(1)} %copy-done.9, bf16[1024,2048]{1,0:T(8,128)(2,1)S(1)} %copy-done.6, bf16[3,2048,2048]{2,1,0:T(8,128)(2,1)} %mlp_grads.4.refs_2_), custom_call_target="tpu_custom_call", output_to_operand_aliasing={{}: (2, {})} | custom-call | flops 8589934592 | bytes 16777216 | tf_op jit(solution)/shard_map/mlp_grads/pallas_call | solution.py:729
  394.8 7.5 %collective-permute-done.23 = bf16[256,2048]{1,0:T(8,128)(2,1)} collective-permute-done((bf16[256,2048]{1,0:T(8,128)(2,1)}, bf16[256,2048]{1,0:T(8,128)(2,1)}, u32[]{:S(2)}, u32[]{:S(2)}) %collective-permute-start.23) | collective-permute-done | bytes 1048608 | tf_op jit(solution)/shard_map/ppermute | solution.py:773
  411.2 12.3 %mlp_piece.1 = (bf16[1024,512]{1,0:T(8,128)(2,1)S(1)}, bf16[1024,512]{1,0:T(8,128)(2,1)S(1)}, bf16[1024,512]{1,0:T(8,128)(2,1)S(1)}, bf16[1024,512]{1,0:T(8,128)(2,1)S(1)}) custom-call(s32[4]{0:T(128)S(1)} %pad_add_fusion.2.order_ref, bf16[1024,2048]{1,0:T(8,128)(2,1)S(1)} %copy-done.10, ...), custom_call_target="tpu_custom_call" | custom-call | flops 8589934592 | bytes 8388608 | tf_op jit(solution)/shard_map/mlp_piece/pallas_call | solution.py:448
  425.5 5.4 collective-permute-done.24
  436.1 5.9 collective-permute-start.27
  445.1 13.8 %collective-permute-done.26 = bf16[256,2048]{1,0:T(8,128)(2,1)} collective-permute-done((bf16[256,2048]{1,0:T(8,128)(2,1)}, bf16[256,2048]{1,0:T(8,128)(2,1)}, u32[]{:S(2)}, u32[]{:S(2)}) %collective-permute-start.26) | collective-permute-done | bytes 1048608 | tf_op jit(solution)/shard_map/ppermute | solution.py:752
  461.1 6.5 collective-permute-done.29
  473.8 4.8 collective-permute-start.33
  488.9 6.4 collective-permute-done.32
  500.2 4.5 collective-permute-start.35
  504.8 17.2 %attend_back.1 = (bf16[1024,512]{1,0:T(8,128)(2,1)S(1)}, bf16[1024,512]{1,0:T(8,128)(2,1)S(1)}, bf16[1024,512]{1,0:T(8,128)(2,1)S(1)}) custom-call(s32[1]{0:T(128)} %bitcast.6.me_ref, bf16[1024,512]{1,0:T(8,128)(2,1)S(1)} %copy-done.16, bf16[1024,512]{1,0:T(8,128)(2,1)S(1)} %copy-done.17, bf16[1024,512]{1,0:T(8,128)(2,1)S(1)} %copy-done.18, ...), custom_call_target="tpu_custom_call" | custom-call | flops 1000 | bytes 1000 | tf_op jit(solution)/shard_map/attend_back/pallas_call | solution.py:276
  522.1 10.5 %one_grad.1 = (bf16[1024,512]{1,0:T(8,128)(2,1)S(1)}, bf16[1024,512]{1,0:T(8,128)(2,1)S(1)}, bf16[1024,512]{1,0:T(8,128)(2,1)S(1)}, bf16[1024,512]{1,0:T(8,128)(2,1)S(1)}) custom-call(s32[4]{0:T(128)S(1)} %pad_add_fusion.3.place_ref, bf16[1024,512]{1,0:T(8,128)(2,1)S(1)} %get-tuple-element.199.dq_ref, bf16[1024,512]{1,0:T(8,128)(2,1)S(1)} %get-tuple-element.200.dk_ref, ...), custom_call_target="tpu_custom_call" | custom-call | flops 6442450944 | bytes 15728640 | tf_op jit(solution)/shard_map/one_grad/pallas_call | solution.py:627
  532.7 3.9 select_select_fusion.3
  539.9 17.7 %att_grads.1 = bf16[8,256,2048]{2,1,0:T(8,128)(2,1)} custom-call(bf16[1024,2048]{1,0:T(8,128)(2,1)} %get-tuple-element.123.rows_ref.unit_ref.normed_ref, bf16[1024,512]{1,0:T(8,128)(2,1)} %copy-done.13, bf16[1024,512]{1,0:T(8,128)(2,1)} %copy-done.14, bf16[1024,512]{1,0:T(8,128)(2,1)} %copy-done.15, bf16[1024,512]{1,0:T(8,128)(2,1)} %attend.1.refs_0_.att_ref, ...), custom_call_target="tpu_custom_call" | custom-call | flops 1000 | bytes 1000 | tf_op jit(solution)/shard_map/att_grads/pallas_call | solution.py:686
  567.8 4.4 all-to-all-start.2
  572.2 56.6 %collective-permute-done.38 = bf16[1024,512]{1,0:T(8,128)(2,1)} collective-permute-done((bf16[1024,512]{1,0:T(8,128)(2,1)}, bf16[1024,512]{1,0:T(8,128)(2,1)}, u32[]{:S(2)}, u32[]{:S(2)}) %collective-permute-start.38) | collective-permute-done | bytes 1048608 | tf_op jit(solution)/shard_map/ppermute | solution.py:773
  628.8 24.3 %collective-permute-done.37 = bf16[1024,512]{1,0:T(8,128)(2,1)} collective-permute-done((bf16[1024,512]{1,0:T(8,128)(2,1)}, bf16[1024,512]{1,0:T(8,128)(2,1)}, u32[]{:S(2)}, u32[]{:S(2)}) %collective-permute-start.37) | collective-permute-done | bytes 1048608 | tf_op jit(solution)/shard_map/ppermute | solution.py:773
  653.1 4.9 fusion.24
  661.7 3.6 all-to-all-start.3
  672.1 8.5 %all-to-all-done.3 = bf16[8,128,512]{2,1,0:T(8,128)(2,1)S(1)} async-done(((bf16[8,128,512]{2,1,0:T(8,128)(2,1)}), bf16[8,128,512]{2,1,0:T(8,128)(2,1)S(1)}, u32[]{:S(2)}, u32[]{:S(2)}) %all-to-all-start.3) | async-done | bytes 1048608 | tf_op jit(solution)/shard_map/all_to_all | solution.py:842
  (237 shorter events, 121.8 us)
Async XLA Ops:
  7.2 132.8 %all-gather.6.cloned.1.call-start = ((), (), s32[]{:S(2)}) async-start(), calls=%async_computation.7 | async-start | bytes 7077888 | tf_op jit(solution)/shard_map/all_gather | solution.py:848
  13.1 30.5 %all-to-all-start = ((bf16[8,128,640]{2,1,0:T(8,128)(2,1)}), bf16[8,128,640]{2,1,0:T(8,128)(2,1)S(1)}, u32[]{:S(2)}, u32[]{:S(2)}) async-start(bf16[8,128,640]{2,1,0:T(8,128)(2,1)} %bitcast), calls=%async_computation | async-start | bytes 2621440 | tf_op jit(solution)/shard_map/all_to_all | solution.py:842
  17.0 226.7 %all-gather.4.cloned.1.call-start = ((), (), s32[]{:S(2)}) async-start(), calls=%async_computation.6 | async-start | bytes 9437184 | tf_op jit(solution)/shard_map/all_gather | solution.py:866
  17.0 27.2 %collective-permute-start = (bf16[64,2048]{1,0:T(8,128)(2,1)}, bf16[64,2048]{1,0:T(8,128)(2,1)}, u32[]{:S(2)}, u32[]{:S(2)}) collective-permute-start(bf16[64,2048]{1,0:T(8,128)(2,1)} %param.17), channel_id=1, source_target_pairs={{0,1},{1,2},{2,3},{3,0},{4,5},{5,6},{6,7},{7,4},{8,9},{9,10},{10,1... | collective-permute-start | bytes 786440 | tf_op jit(solution)/shard_map/ppermute | solution.py:773
  18.6 25.6 %collective-permute-start.1 = (bf16[64,2048]{1,0:T(8,128)(2,1)}, bf16[64,2048]{1,0:T(8,128)(2,1)}, u32[]{:S(2)}, u32[]{:S(2)}) collective-permute-start(bf16[64,2048]{1,0:T(8,128)(2,1)} %param.17), channel_id=1, source_target_pairs={{0,2},{1,3},{2,0},{3,1},{4,6},{5,7},{6,4},{7,5},{8,10},{9,11},{10,... | collective-permute-start | bytes 786440 | tf_op jit(solution)/shard_map/ppermute | solution.py:773
  19.0 25.3 %collective-permute-start.2 = (bf16[64,2048]{1,0:T(8,128)(2,1)}, bf16[64,2048]{1,0:T(8,128)(2,1)}, u32[]{:S(2)}, u32[]{:S(2)}) collective-permute-start(bf16[64,2048]{1,0:T(8,128)(2,1)} %param.17), channel_id=1, source_target_pairs={{0,3},{1,0},{2,1},{3,2},{4,7},{5,4},{6,5},{7,6},{8,11},{9,8},{10,9... | collective-permute-start | bytes 786440 | tf_op jit(solution)/shard_map/ppermute | solution.py:773
  46.7 218.0 %all-gather.8.cloned.1.call-start = ((), (), s32[]{:S(2)}) async-start(), calls=%async_computation.8 | async-start | bytes 28311552 | tf_op jit(solution)/shard_map/all_gather | solution.py:868
  48.8 25.2 %collective-permute-start.3 = (bf16[1024,512]{1,0:T(8,128)(2,1)S(1)}, bf16[1024,512]{1,0:T(8,128)(2,1)S(1)}, u32[]{:S(2)}, u32[]{:S(2)}) collective-permute-start(bf16[1024,512]{1,0:T(8,128)(2,1)S(1)} %fusion.21.refs_0_), channel_id=1, source_target_pairs={{0,1},{1,2},{2,3},{4,5},{5,6},{6,7},{8,9},{9,10},{10,11},{12,13},{... | collective-permute-start | bytes 3145736 | tf_op jit(solution)/shard_map/ppermute | solution.py:752
  52.3 25.1 %collective-permute-start.6 = (bf16[1024,512]{1,0:T(8,128)(2,1)S(1)}, bf16[1024,512]{1,0:T(8,128)(2,1)}, u32[]{:S(2)}, u32[]{:S(2)}) collective-permute-start(bf16[1024,512]{1,0:T(8,128)(2,1)S(1)} %fusion.21.refs_0_), channel_id=1, source_target_pairs={{3,2},{2,1},{1,0},{7,6},{6,5},{5,4},{11,10},{10,9},{9,8},{15,14},{... | collective-permute-start | bytes 3145736 | tf_op jit(solution)/shard_map/ppermute | solution.py:752
  74.0 25.1 %collective-permute-start.4 = (bf16[1024,512]{1,0:T(8,128)(2,1)S(1)}, bf16[1024,512]{1,0:T(8,128)(2,1)}, u32[]{:S(2)}, u32[]{:S(2)}) collective-permute-start(bf16[1024,512]{1,0:T(8,128)(2,1)S(1)} %collective-permute-done.3.refs_1_), channel_id=1, source_target_pairs={{1,2},{2,3},{5,6},{6,7},{9,10},{10,11},{13,14},{14,15},{17,18},{18... | collective-permute-start | bytes 3145736 | tf_op jit(solution)/shard_map/ppermute | solution.py:752
  77.4 25.3 %collective-permute-start.7 = (bf16[1024,512]{1,0:T(8,128)(2,1)}, bf16[1024,512]{1,0:T(8,128)(2,1)}, u32[]{:S(2)}, u32[]{:S(2)}) collective-permute-start(bf16[1024,512]{1,0:T(8,128)(2,1)} %collective-permute-done.6.refs_4_), channel_id=1, source_target_pairs={{2,1},{1,0},{6,5},{5,4},{10,9},{9,8},{14,13},{13,12},{18,17},{17,1... | collective-permute-start | bytes 3145736 | tf_op jit(solution)/shard_map/ppermute | solution.py:752
  84.6 23.2 %all-to-all-start.1 = ((bf16[8,128,512]{2,1,0:T(8,128)(2,1)}), bf16[8,128,512]{2,1,0:T(8,128)(2,1)S(1)}, u32[]{:S(2)}, u32[]{:S(2)}) async-start(bf16[8,128,512]{2,1,0:T(8,128)(2,1)} %bitcast.12), calls=%async_computation.1 | async-start | bytes 2097152 | tf_op jit(solution)/shard_map/all_to_all | solution.py:842
  88.4 471.1 %reduce-scatter.3.cloned.1.call-start = ((), (), s32[]{:S(2)}) async-start(), calls=%async_computation.9 | async-start | bytes 28311552 | tf_op jit(solution)/shard_map/reduce_scatter | solution.py:933
  99.2 21.7 %collective-permute-start.5 = (bf16[1024,512]{1,0:T(8,128)(2,1)}, bf16[1024,512]{1,0:T(8,128)(2,1)}, u32[]{:S(2)}, u32[]{:S(2)}) collective-permute-start(bf16[1024,512]{1,0:T(8,128)(2,1)} %collective-permute-done.4.refs_2_), channel_id=1, source_target_pairs={{2,3},{6,7},{10,11},{14,15},{18,19},{22,23},{26,27},{30,31}} | collective-permute-start | bytes 3145736 | tf_op jit(solution)/shard_map/ppermute | solution.py:752
  102.7 18.1 %collective-permute-start.8 = (bf16[1024,512]{1,0:T(8,128)(2,1)}, bf16[1024,512]{1,0:T(8,128)(2,1)}, u32[]{:S(2)}, u32[]{:S(2)}) collective-permute-start(bf16[1024,512]{1,0:T(8,128)(2,1)} %collective-permute-done.7.refs_5_), channel_id=1, source_target_pairs={{1,0},{5,4},{9,8},{13,12},{17,16},{21,20},{25,24},{29,28}} | collective-permute-start | bytes 3145736 | tf_op jit(solution)/shard_map/ppermute | solution.py:752
  128.6 37.1 %collective-permute-start.9 = (bf16[1024,512]{1,0:T(8,128)(2,1)S(1)}, bf16[1024,512]{1,0:T(8,128)(2,1)S(1)}, u32[]{:S(2)}, u32[]{:S(2)}) collective-permute-start(bf16[1024,512]{1,0:T(8,128)(2,1)S(1)} %fusion.22.refs_7_.refs_0_), channel_id=1, source_target_pairs={{0,1},{1,2},{2,3},{4,5},{5,6},{6,7},{8,9},{9,10},{10,11},{12,13},{... | collective-permute-start | bytes 3145736 | tf_op jit(solution)/shard_map/ppermute | solution.py:752
  133.0 32.7 %collective-permute-start.10 = (bf16[1024,512]{1,0:T(8,128)(2,1)S(1)}, bf16[1024,512]{1,0:T(8,128)(2,1)}, u32[]{:S(2)}, u32[]{:S(2)}) collective-permute-start(bf16[1024,512]{1,0:T(8,128)(2,1)S(1)} %fusion.22.refs_7_.refs_0_), channel_id=1, source_target_pairs={{3,2},{2,1},{1,0},{7,6},{6,5},{5,4},{11,10},{10,9},{9,8},{15,14},{... | collective-permute-start | bytes 3145736 | tf_op jit(solution)/shard_map/ppermute | solution.py:752
  165.8 23.9 %collective-permute-start.11 = (bf16[1024,512]{1,0:T(8,128)(2,1)}, bf16[1024,512]{1,0:T(8,128)(2,1)S(1)}, u32[]{:S(2)}, u32[]{:S(2)}) collective-permute-start(bf16[1024,512]{1,0:T(8,128)(2,1)} %attend.1.refs_0_.att_ref), channel_id=1, source_target_pairs={{0,1},{1,2},{2,3},{4,5},{5,6},{6,7},{8,9},{9,10},{10,11},{12,13},{... | collective-permute-start | bytes 3145736 | tf_op jit(solution)/shard_map/ppermute | solution.py:752
  167.7 23.9 %collective-permute-start.14 = (bf16[1024,512]{1,0:T(8,128)(2,1)}, bf16[1024,512]{1,0:T(8,128)(2,1)S(1)}, u32[]{:S(2)}, u32[]{:S(2)}) collective-permute-start(bf16[1024,512]{1,0:T(8,128)(2,1)} %attend.1.refs_0_.att_ref), channel_id=1, source_target_pairs={{3,2},{2,1},{1,0},{7,6},{6,5},{5,4},{11,10},{10,9},{9,8},{15,14},{... | collective-permute-start | bytes 3145736 | tf_op jit(solution)/shard_map/ppermute | solution.py:752
  189.7 22.8 %collective-permute-start.12 = (bf16[1024,512]{1,0:T(8,128)(2,1)S(1)}, bf16[1024,512]{1,0:T(8,128)(2,1)S(1)}, u32[]{:S(2)}, u32[]{:S(2)}) collective-permute-start(bf16[1024,512]{1,0:T(8,128)(2,1)S(1)} %collective-permute-done.11.refs_1_), channel_id=1, source_target_pairs={{1,2},{2,3},{5,6},{6,7},{9,10},{10,11},{13,14},{14,15},{17,18},{18... | collective-permute-start | bytes 3145736 | tf_op jit(solution)/shard_map/ppermute | solution.py:752
  191.6 23.3 %collective-permute-start.15 = (bf16[1024,512]{1,0:T(8,128)(2,1)S(1)}, bf16[1024,512]{1,0:T(8,128)(2,1)S(1)}, u32[]{:S(2)}, u32[]{:S(2)}) collective-permute-start(bf16[1024,512]{1,0:T(8,128)(2,1)S(1)} %collective-permute-done.14.refs_4_), channel_id=1, source_target_pairs={{2,1},{1,0},{6,5},{5,4},{10,9},{9,8},{14,13},{13,12},{18,17},{17,1... | collective-permute-start | bytes 3145736 | tf_op jit(solution)/shard_map/ppermute | solution.py:752
  212.4 21.2 %collective-permute-start.13 = (bf16[1024,512]{1,0:T(8,128)(2,1)S(1)}, bf16[1024,512]{1,0:T(8,128)(2,1)S(1)}, u32[]{:S(2)}, u32[]{:S(2)}) collective-permute-start(bf16[1024,512]{1,0:T(8,128)(2,1)S(1)} %collective-permute-done.12.refs_2_), channel_id=1, source_target_pairs={{2,3},{6,7},{10,11},{14,15},{18,19},{22,23},{26,27},{30,31}} | collective-permute-start | bytes 3145736 | tf_op jit(solution)/shard_map/ppermute | solution.py:752
  214.9 18.7 %collective-permute-start.16 = (bf16[1024,512]{1,0:T(8,128)(2,1)S(1)}, bf16[1024,512]{1,0:T(8,128)(2,1)S(1)}, u32[]{:S(2)}, u32[]{:S(2)}) collective-permute-start(bf16[1024,512]{1,0:T(8,128)(2,1)S(1)} %collective-permute-done.15.refs_5_), channel_id=1, source_target_pairs={{1,0},{5,4},{9,8},{13,12},{17,16},{21,20},{25,24},{29,28}} | collective-permute-start | bytes 3145736 | tf_op jit(solution)/shard_map/ppermute | solution.py:752
  233.6 28.1 %collective-permute-start.17 = (bf16[1024,512]{1,0:T(8,128)(2,1)S(1)}, bf16[1024,512]{1,0:T(8,128)(2,1)S(1)}, u32[]{:S(2)}, u32[]{:S(2)}) collective-permute-start(bf16[1024,512]{1,0:T(8,128)(2,1)S(1)} %collective-permute-done.9.refs_8_.refs_1_), channel_id=1, source_target_pairs={{1,2},{2,3},{5,6},{6,7},{9,10},{10,11},{13,14},{14,15},{17,18},{18... | collective-permute-start | bytes 3145736 | tf_op jit(solution)/shard_map/ppermute | solution.py:752
  238.1 23.6 %collective-permute-start.18 = (bf16[1024,512]{1,0:T(8,128)(2,1)}, bf16[1024,512]{1,0:T(8,128)(2,1)}, u32[]{:S(2)}, u32[]{:S(2)}) collective-permute-start(bf16[1024,512]{1,0:T(8,128)(2,1)} %collective-permute-done.10.refs_11_.refs_4_), channel_id=1, source_target_pairs={{2,1},{1,0},{6,5},{5,4},{10,9},{9,8},{14,13},{13,12},{18,17},{17,1... | collective-permute-start | bytes 3145736 | tf_op jit(solution)/shard_map/ppermute | solution.py:752
  261.7 27.0 %collective-permute-start.19 = (bf16[1024,512]{1,0:T(8,128)(2,1)S(1)}, bf16[1024,512]{1,0:T(8,128)(2,1)S(1)}, u32[]{:S(2)}, u32[]{:S(2)}) collective-permute-start(bf16[1024,512]{1,0:T(8,128)(2,1)S(1)} %collective-permute-done.17.refs_9_.refs_2_), channel_id=1, source_target_pairs={{2,3},{6,7},{10,11},{14,15},{18,19},{22,23},{26,27},{30,31}} | collective-permute-start | bytes 3145736 | tf_op jit(solution)/shard_map/ppermute | solution.py:752
  263.1 25.7 %collective-permute-start.20 = (bf16[1024,512]{1,0:T(8,128)(2,1)}, bf16[1024,512]{1,0:T(8,128)(2,1)}, u32[]{:S(2)}, u32[]{:S(2)}) collective-permute-start(bf16[1024,512]{1,0:T(8,128)(2,1)} %collective-permute-done.18.refs_12_.refs_5_), channel_id=1, source_target_pairs={{1,0},{5,4},{9,8},{13,12},{17,16},{21,20},{25,24},{29,28}} | collective-permute-start | bytes 3145736 | tf_op jit(solution)/shard_map/ppermute | solution.py:752
  307.9 86.8 %collective-permute-start.21 = (bf16[256,2048]{1,0:T(8,128)(2,1)}, bf16[256,2048]{1,0:T(8,128)(2,1)S(1)}, u32[]{:S(2)}, u32[]{:S(2)}) collective-permute-start(bf16[256,2048]{1,0:T(8,128)(2,1)} %first_two_grad.1), channel_id=1, source_target_pairs={{0,2},{1,3},{2,0},{3,1},{4,6},{5,7},{6,4},{7,5},{8,10},{9,11},{10,... | collective-permute-start | bytes 3145736 | tf_op jit(solution)/shard_map/ppermute | solution.py:773
  352.3 42.5 %collective-permute-start.22 = (bf16[256,2048]{1,0:T(8,128)(2,1)}, bf16[256,2048]{1,0:T(8,128)(2,1)}, u32[]{:S(2)}, u32[]{:S(2)}) collective-permute-start(bf16[256,2048]{1,0:T(8,128)(2,1)} %get-tuple-element.156), channel_id=1, source_target_pairs={{0,1},{1,2},{2,3},{3,0},{4,5},{5,6},{6,7},{7,4},{8,9},{9,10},{10,1... | collective-permute-start | bytes 3145736 | tf_op jit(solution)/shard_map/ppermute | solution.py:773
  356.9 45.3 %collective-permute-start.23 = (bf16[256,2048]{1,0:T(8,128)(2,1)}, bf16[256,2048]{1,0:T(8,128)(2,1)}, u32[]{:S(2)}, u32[]{:S(2)}) collective-permute-start(bf16[256,2048]{1,0:T(8,128)(2,1)} %get-tuple-element.157), channel_id=1, source_target_pairs={{0,3},{1,0},{2,1},{3,2},{4,7},{5,4},{6,5},{7,6},{8,11},{9,8},{10,9... | collective-permute-start | bytes 3145736 | tf_op jit(solution)/shard_map/ppermute | solution.py:773
  402.3 266.3 %reduce-scatter.5.cloned.1.call-start = ((), (), s32[]{:S(2)}) async-start(), calls=%async_computation.10 | async-start | bytes 9437184 | tf_op jit(solution)/shard_map/reduce_scatter | solution.py:992
  405.3 25.6 %collective-permute-start.24 = (bf16[256,2048]{1,0:T(8,128)(2,1)S(1)}, bf16[256,2048]{1,0:T(8,128)(2,1)}, u32[]{:S(2)}, u32[]{:S(2)}) collective-permute-start(bf16[256,2048]{1,0:T(8,128)(2,1)S(1)} %add_convert_fusion.4), channel_id=1, source_target_pairs={{0,1},{1,2},{2,3},{4,5},{5,6},{6,7},{8,9},{9,10},{10,11},{12,13},{... | collective-permute-start | bytes 3145736 | tf_op jit(solution)/shard_map/ppermute | solution.py:752
  408.8 25.4 %collective-permute-start.25 = (bf16[256,2048]{1,0:T(8,128)(2,1)S(1)}, bf16[256,2048]{1,0:T(8,128)(2,1)}, u32[]{:S(2)}, u32[]{:S(2)}) collective-permute-start(bf16[256,2048]{1,0:T(8,128)(2,1)S(1)} %add_convert_fusion.4), channel_id=1, source_target_pairs={{3,2},{2,1},{1,0},{7,6},{6,5},{5,4},{11,10},{10,9},{9,8},{15,14},{... | collective-permute-start | bytes 3145736 | tf_op jit(solution)/shard_map/ppermute | solution.py:752
  434.2 24.7 %collective-permute-start.26 = (bf16[256,2048]{1,0:T(8,128)(2,1)}, bf16[256,2048]{1,0:T(8,128)(2,1)}, u32[]{:S(2)}, u32[]{:S(2)}) collective-permute-start(bf16[256,2048]{1,0:T(8,128)(2,1)} %collective-permute-done.24), channel_id=1, source_target_pairs={{1,2},{2,3},{5,6},{6,7},{9,10},{10,11},{13,14},{14,15},{17,18},{18... | collective-permute-start | bytes 3145736 | tf_op jit(solution)/shard_map/ppermute | solution.py:752
  436.1 24.9 %collective-permute-start.27 = (bf16[256,2048]{1,0:T(8,128)(2,1)}, bf16[256,2048]{1,0:T(8,128)(2,1)}, u32[]{:S(2)}, u32[]{:S(2)}) collective-permute-start(bf16[256,2048]{1,0:T(8,128)(2,1)} %collective-permute-done.25), channel_id=1, source_target_pairs={{2,1},{1,0},{6,5},{5,4},{10,9},{9,8},{14,13},{13,12},{18,17},{17,1... | collective-permute-start | bytes 3145736 | tf_op jit(solution)/shard_map/ppermute | solution.py:752
  442.0 19.1 %collective-permute-start.28 = (bf16[1024,512]{1,0:T(8,128)(2,1)S(1)}, bf16[1024,512]{1,0:T(8,128)(2,1)}, u32[]{:S(2)}, u32[]{:S(2)}) collective-permute-start(bf16[1024,512]{1,0:T(8,128)(2,1)S(1)} %get-tuple-element.186), channel_id=1, source_target_pairs={{0,1},{4,5},{8,9},{12,13},{16,17},{20,21},{24,25},{28,29}} | collective-permute-start | bytes 3145736 | tf_op jit(solution)/shard_map/ppermute | solution.py:968
  443.7 23.9 %collective-permute-start.29 = (bf16[1024,512]{1,0:T(8,128)(2,1)S(1)}, bf16[1024,512]{1,0:T(8,128)(2,1)}, u32[]{:S(2)}, u32[]{:S(2)}) collective-permute-start(bf16[1024,512]{1,0:T(8,128)(2,1)S(1)} %get-tuple-element.184), channel_id=1, source_target_pairs={{3,2},{7,6},{11,10},{15,14},{19,18},{23,22},{27,26},{31,30}} | collective-permute-start | bytes 3145736 | tf_op jit(solution)/shard_map/ppermute | solution.py:968
  467.6 21.2 %collective-permute-start.30 = (bf16[256,2048]{1,0:T(8,128)(2,1)}, bf16[256,2048]{1,0:T(8,128)(2,1)S(1)}, u32[]{:S(2)}, u32[]{:S(2)}) collective-permute-start(bf16[256,2048]{1,0:T(8,128)(2,1)} %collective-permute-done.26), channel_id=1, source_target_pairs={{2,3},{6,7},{10,11},{14,15},{18,19},{22,23},{26,27},{30,31}} | collective-permute-start | bytes 3145736 | tf_op jit(solution)/shard_map/ppermute | solution.py:752
  469.0 19.8 %collective-permute-start.31 = (bf16[256,2048]{1,0:T(8,128)(2,1)}, bf16[256,2048]{1,0:T(8,128)(2,1)S(1)}, u32[]{:S(2)}, u32[]{:S(2)}) collective-permute-start(bf16[256,2048]{1,0:T(8,128)(2,1)} %collective-permute-done.27), channel_id=1, source_target_pairs={{1,0},{5,4},{9,8},{13,12},{17,16},{21,20},{25,24},{29,28}} | collective-permute-start | bytes 3145736 | tf_op jit(solution)/shard_map/ppermute | solution.py:752
  472.5 22.7 %collective-permute-start.32 = (bf16[1024,512]{1,0:T(8,128)(2,1)S(1)}, bf16[1024,512]{1,0:T(8,128)(2,1)S(1)}, u32[]{:S(2)}, u32[]{:S(2)}) collective-permute-start(bf16[1024,512]{1,0:T(8,128)(2,1)S(1)} %get-tuple-element.232), channel_id=1, source_target_pairs={{0,1},{1,2},{4,5},{5,6},{8,9},{9,10},{12,13},{13,14},{16,17},{17,1... | collective-permute-start | bytes 3145736 | tf_op jit(solution)/shard_map/ppermute | solution.py:968
  473.8 23.0 %collective-permute-start.33 = (bf16[1024,512]{1,0:T(8,128)(2,1)S(1)}, bf16[1024,512]{1,0:T(8,128)(2,1)S(1)}, u32[]{:S(2)}, u32[]{:S(2)}) collective-permute-start(bf16[1024,512]{1,0:T(8,128)(2,1)S(1)} %get-tuple-element.231), channel_id=1, source_target_pairs={{3,2},{2,1},{7,6},{6,5},{11,10},{10,9},{15,14},{14,13},{19,18},{18... | collective-permute-start | bytes 3145736 | tf_op jit(solution)/shard_map/ppermute | solution.py:968
  497.1 41.9 %collective-permute-start.34 = (bf16[1024,512]{1,0:T(8,128)(2,1)S(1)}, bf16[1024,512]{1,0:T(8,128)(2,1)S(1)}, u32[]{:S(2)}, u32[]{:S(2)}) collective-permute-start(bf16[1024,512]{1,0:T(8,128)(2,1)S(1)} %add_convert_fusion.3), channel_id=1, source_target_pairs={{0,1},{1,2},{2,3},{4,5},{5,6},{6,7},{8,9},{9,10},{10,11},{12,13},{... | collective-permute-start | bytes 3145736 | tf_op jit(solution)/shard_map/ppermute | solution.py:968
  500.2 39.8 %collective-permute-start.35 = (bf16[1024,512]{1,0:T(8,128)(2,1)S(1)}, bf16[1024,512]{1,0:T(8,128)(2,1)}, u32[]{:S(2)}, u32[]{:S(2)}) collective-permute-start(bf16[1024,512]{1,0:T(8,128)(2,1)S(1)} %add_convert_fusion.2), channel_id=1, source_target_pairs={{3,2},{2,1},{1,0},{7,6},{6,5},{5,4},{11,10},{10,9},{9,8},{15,14},{... | collective-permute-start | bytes 3145736 | tf_op jit(solution)/shard_map/ppermute | solution.py:968
  559.5 69.3 %collective-permute-start.38 = (bf16[1024,512]{1,0:T(8,128)(2,1)}, bf16[1024,512]{1,0:T(8,128)(2,1)}, u32[]{:S(2)}, u32[]{:S(2)}) collective-permute-start(bf16[1024,512]{1,0:T(8,128)(2,1)} %copy-done.24), channel_id=1, source_target_pairs={{0,2},{1,3},{2,0},{3,1},{4,6},{5,7},{6,4},{7,5},{8,10},{9,11},{10,... | collective-permute-start | bytes 3145736 | tf_op jit(solution)/shard_map/ppermute | solution.py:773
  560.0 93.0 %collective-permute-start.37 = (bf16[1024,512]{1,0:T(8,128)(2,1)}, bf16[1024,512]{1,0:T(8,128)(2,1)}, u32[]{:S(2)}, u32[]{:S(2)}) collective-permute-start(bf16[1024,512]{1,0:T(8,128)(2,1)} %copy-done.23), channel_id=1, source_target_pairs={{0,1},{1,2},{2,3},{3,0},{4,5},{5,6},{6,7},{7,4},{8,9},{9,10},{10,1... | collective-permute-start | bytes 3145736 | tf_op jit(solution)/shard_map/ppermute | solution.py:773
  561.5 91.5 %collective-permute-start.36 = (bf16[1024,512]{1,0:T(8,128)(2,1)S(1)}, bf16[1024,512]{1,0:T(8,128)(2,1)}, u32[]{:S(2)}, u32[]{:S(2)}) collective-permute-start(bf16[1024,512]{1,0:T(8,128)(2,1)S(1)} %get-tuple-element.196), channel_id=1, source_target_pairs={{0,3},{1,0},{2,1},{3,2},{4,7},{5,4},{6,5},{7,6},{8,11},{9,8},{10,9... | collective-permute-start | bytes 3145736 | tf_op jit(solution)/shard_map/ppermute | solution.py:773
  567.8 93.9 %all-to-all-start.2 = ((bf16[8,128,512]{2,1,0:T(8,128)(2,1)}), bf16[8,128,512]{2,1,0:T(8,128)(2,1)}, u32[]{:S(2)}, u32[]{:S(2)}) async-start(bf16[8,128,512]{2,1,0:T(8,128)(2,1)} %bitcast.57), calls=%async_computation.3 | async-start | bytes 2097152 | tf_op jit(solution)/shard_map/all_to_all | solution.py:842
  661.7 18.9 %all-to-all-start.3 = ((bf16[8,128,512]{2,1,0:T(8,128)(2,1)}), bf16[8,128,512]{2,1,0:T(8,128)(2,1)S(1)}, u32[]{:S(2)}, u32[]{:S(2)}) async-start(bf16[8,128,512]{2,1,0:T(8,128)(2,1)} %bitcast.26), calls=%async_computation.4 | async-start | bytes 2097152 | tf_op jit(solution)/shard_map/all_to_all | solution.py:842
  (58 other events, 1034.2 us)
Sparse Core Ops, SparseCore 0:
  10.5 58.5 all-gather.5
  71.6 65.6 all-gather.3
  139.2 125.3 all-gather.7
  402.4 156.9 reduce-scatter.2
  562.7 71.2 reduce-scatter.4

commit v9 on v7

--- a/solution.py
+++ b/solution.py
@@ -184,7 +184,7 @@
     return exponent * (1.0 / jnp.sum(exponent, axis=-1, keepdims=True))
 
 
-PAIR = 2 * HEAD_DIM
+PAIR = 4 * HEAD_DIM
 
 
 def attend_kernel(q_ref, k_ref, v_ref, column_ref, row_ref, out_ref):

time: 697 us -> 697 us (level)
  transfers between devices with their start and end apart: 48 -> 48, of which waited for: 19 -> 20; matrix products, arithmetic and copies ran while one was open for 9% -> 9% of each run, Pallas kernels for 30% -> 30%
where the time goes in v9:
time: 697 us; the launch traced here: 690 us
  waiting for transfers between devices  253 us (36%)
  Pallas kernels  224 us (32%)
  starting transfers between devices  114 us (16%)
  matrix products  31.2 us (4%)
  other arithmetic  31.1 us (4%)
  local copies, waits for them, and re-layouts  18.5 us (3%)
  between operations  17.3 us (2%)
    ppermute x12, waiting for transfers between devices, line_step(): lax.ppermute(from_low, axis, up)  115 us
    ppermute x9, waiting for transfers between devices, sent_on(): lax.ppermute(term, axis, [(i, (i + step) % size) for i in range(size)])  89.7 us
    ppermute x12, starting transfers between devices, line_step(): lax.ppermute(from_high, axis, down)  38.5 us
    pallas_call x3, Pallas kernels, mlp_grads(): pl.pallas_call(body, grid=(model // BLOCK,), in_specs=specs, out_specs=pl...  35.7 us
    ppermute x12, starting transfers between devices, line_step(): lax.ppermute(from_low, axis, up)  33.3 us
    all_to_all x4, waiting for transfers between devices, over_fsdp(): return lax.all_to_all(rows, 'fsdp', split_axis=0, concat_axis=0, tiled=True)  25.8 us
    pallas_call x1, Pallas kernels, two_grad_pieces(): pl.pallas_call(two_grad_kernel, grid_spec=pltpu.PrefetchScalarGridSpec(nu...  24.4 us
    pallas_call x1, Pallas kernels, mlp_up(): pl.pallas_call(up_kernel, grid=(hidden_units // WIDE,), in_specs=[pl.Bloc...  24 us
  transfers between devices with their start and end apart: 48, of which 20 were waited for; matrix products, arithmetic and copies ran while one was open for 9% of the time, Pallas kernels for 30%

profile of v9, /device:TPU:16, one launch (start us, length us, event | category | flops | bytes accessed | tf_op | source)
XLA Modules:
  0.0 689.5 jit_solution(17273467406443971243)
XLA Ops:
  13.1 3.9 all-to-all-start
  20.3 3.7 pad_maximum_fusion.1
  26.3 17.3 %all-to-all-done = bf16[8,128,640]{2,1,0:T(8,128)(2,1)S(1)} async-done(((bf16[8,128,640]{2,1,0:T(8,128)(2,1)}), bf16[8,128,640]{2,1,0:T(8,128)(2,1)S(1)}, u32[]{:S(2)}, u32[]{:S(2)}) %all-to-all-start) | async-done | bytes 1310752 | tf_op jit(solution)/shard_map/all_to_all | solution.py:842
  54.7 19.3 %collective-permute-done.3.refs_1_ = bf16[1024,512]{1,0:T(8,128)(2,1)S(1)} collective-permute-done((bf16[1024,512]{1,0:T(8,128)(2,1)S(1)}, bf16[1024,512]{1,0:T(8,128)(2,1)S(1)}, u32[]{:S(2)}, u32[]{:S(2)}) %collective-permute-start.3) | collective-permute-done | bytes 1048608 | tf_op jit(solution)/shard_map/ppermute | solution.py:752
  77.4 4.4 collective-permute-start.7
  84.5 3.8 all-to-all-start.1
  88.6 10.5 %collective-permute-done.4.refs_2_ = bf16[1024,512]{1,0:T(8,128)(2,1)} collective-permute-done((bf16[1024,512]{1,0:T(8,128)(2,1)S(1)}, bf16[1024,512]{1,0:T(8,128)(2,1)}, u32[]{:S(2)}, u32[]{:S(2)}) %collective-permute-start.4) | collective-permute-done | bytes 1048608 | tf_op jit(solution)/shard_map/ppermute | solution.py:752
  109.4 11.4 %collective-permute-done.5.refs_3_ = bf16[1024,512]{1,0:T(8,128)(2,1)} collective-permute-done((bf16[1024,512]{1,0:T(8,128)(2,1)}, bf16[1024,512]{1,0:T(8,128)(2,1)}, u32[]{:S(2)}, u32[]{:S(2)}) %collective-permute-start.5) | collective-permute-done | bytes 1048608 | tf_op jit(solution)/shard_map/ppermute | solution.py:752
  120.9 7.8 %gathered_norm.1 = (bf16[1024,2048]{1,0:T(8,128)(2,1)}, bf16[1024,2048]{1,0:T(8,128)(2,1)}, f32[1024,1]{1,0:T(8,128)}) custom-call(s32[1]{0:T(128)} %bitcast.6.me_ref, bf16[1024,512]{1,0:T(8,128)(2,1)} %copy-done.39, bf16[1024,512]{1,0:T(8,128)(2,1)} %copy-done.40, bf16[1024,512]{1,0:T(8,128)(2,1)} %collective-permute-done.4.refs_2_, ...), custom_call_target="tpu_custom_call" | custom-call | flops 41943040 | bytes 16777216 | tf_op jit(solution)/shard_map/gathered_norm/pallas_call | solution.py:117
  128.6 4.4 collective-permute-start.9
  133.0 5.9 collective-permute-start.10
  140.0 13.7 %qkv.1 = (bf16[1024,512]{1,0:T(8,128)(2,1)}, bf16[1024,512]{1,0:T(8,128)(2,1)}, bf16[1024,512]{1,0:T(8,128)(2,1)}) custom-call(bf16[1024,2048]{1,0:T(8,128)(2,1)} %get-tuple-element.123.rows_ref.unit_ref.normed_ref, bf16[2048,1536]{1,0:T(8,128)(2,1)} %all-gather.6.cloned.1.call-done.wq_ref.wk_ref.wv_ref.weight_ref, ...), custom_call_target="tpu_custom_call" | custom-call | flops 6442450944 | bytes 10485760 | tf_op jit(solution)/shard_map/qkv/pallas_call | solution.py:160
  153.7 11.0 %attend.1.refs_0_.att_ref = bf16[1024,512]{1,0:T(8,128)(2,1)} custom-call(bf16[1024,512]{1,0:T(8,128)(2,1)} %get-tuple-element.126.q_ref, bf16[1024,512]{1,0:T(8,128)(2,1)} %get-tuple-element.127.k_ref, bf16[1024,512]{1,0:T(8,128)(2,1)} %get-tuple-element.128.v_ref, s32[1024,1]{1,0:T(8,128)} %copy.27.column_ref, s32[1,1024]{1,0:T(1,128)} %bitcast.52), custom_call_target="tpu_custom_call" | custom-call | flops 2147483648 | bytes 4194304 | tf_op jit(solution)/shard_map/attend/pallas_call | solution.py:212
  166.7 4.0 collective-permute-start.14
  170.7 18.2 %collective-permute-done.11.refs_1_ = bf16[1024,512]{1,0:T(8,128)(2,1)S(1)} collective-permute-done((bf16[1024,512]{1,0:T(8,128)(2,1)}, bf16[1024,512]{1,0:T(8,128)(2,1)S(1)}, u32[]{:S(2)}, u32[]{:S(2)}) %collective-permute-start.11) | collective-permute-done | bytes 1048608 | tf_op jit(solution)/shard_map/ppermute | solution.py:752
  190.8 4.0 collective-permute-start.15
  194.9 17.0 %collective-permute-done.12.refs_2_ = bf16[1024,512]{1,0:T(8,128)(2,1)S(1)} collective-permute-done((bf16[1024,512]{1,0:T(8,128)(2,1)S(1)}, bf16[1024,512]{1,0:T(8,128)(2,1)S(1)}, u32[]{:S(2)}, u32[]{:S(2)}) %collective-permute-start.12) | collective-permute-done | bytes 1048608 | tf_op jit(solution)/shard_map/ppermute | solution.py:752
  214.9 18.0 %collective-permute-done.13.refs_3_ = bf16[1024,512]{1,0:T(8,128)(2,1)S(1)} collective-permute-done((bf16[1024,512]{1,0:T(8,128)(2,1)S(1)}, bf16[1024,512]{1,0:T(8,128)(2,1)S(1)}, u32[]{:S(2)}, u32[]{:S(2)}) %collective-permute-start.13) | collective-permute-done | bytes 1048608 | tf_op jit(solution)/shard_map/ppermute | solution.py:752
  232.9 4.4 collective-permute-start.17
  237.4 4.2 collective-permute-start.18
  242.9 18.0 %hidden.1 = (f32[1024,512]{1,0:T(8,128)}, bf16[1024,2048]{1,0:T(8,128)(2,1)}, f32[1024,1]{1,0:T(8,128)}) custom-call(s32[1]{0:T(128)} %bitcast.6.me_ref, bf16[2048,2048]{1,0:T(8,128)(2,1)} %bitcast.65, bf16[1024,2048]{1,0:T(8,128)(2,1)} %get-tuple-element.120.rows_ref, bf16[1024,512]{1,0:T(8,128)(2,1)} %attend.1.refs_0_.att_ref, ...), custom_call_target="tpu_custom_call" | custom-call | flops 8589934592 | bytes 29360128 | tf_op jit(solution)/shard_map/hidden/pallas_call | solution.py:319
  264.5 24.0 %mlp_up.1 = (bf16[1024,2048]{1,0:T(8,128)(2,1)}, bf16[1024,2048]{1,0:T(8,128)(2,1)}, bf16[1024,2048]{1,0:T(8,128)(2,1)}) custom-call(bf16[1024,2048]{1,0:T(8,128)(2,1)} %get-tuple-element.142.rows_ref.refs_5_.refs_2_.refs_6_.refs_10_.refs_0_, ...), custom_call_target="tpu_custom_call" | custom-call | flops 17179869184 | bytes 41943040 | tf_op jit(solution)/shard_map/mlp_up/pallas_call | solution.py:362
  289.5 18.2 %first_two_grad.1 = bf16[256,2048]{1,0:T(8,128)(2,1)} custom-call(s32[2]{0:T(128)} %pad_add_fusion.at_ref, bf16[3,2048,2048]{2,1,0:T(8,128)(2,1)} %all-gather.8.cloned.1.call-done.gate_ref.up_ref.refs_0_.refs_1_.refs_2_.down_ref.refs_12_.refs_13_, ...), custom_call_target="tpu_custom_call" | custom-call | flops 6442450944 | bytes 25165824 | tf_op jit(solution)/shard_map/first_two_grad/pallas_call | solution.py:521
  308.3 18.9 %mlp_down_back.1 = (bf16[1024,2048]{1,0:T(8,128)(2,1)}, bf16[1024,2048]{1,0:T(8,128)(2,1)}, bf16[1024,2048]{1,0:T(8,128)(2,1)}) custom-call(s32[1]{0:T(128)} %bitcast.6.me_ref, bf16[3,2048,2048]{2,1,0:T(8,128)(2,1)} %all-gather.8.cloned.1.call-done.gate_ref.up_ref.refs_0_.refs_1_.refs_2_.down_ref.refs_12_.refs_13_, ...), custom_call_target="tpu_custom_call" | custom-call | flops 8589934592 | bytes 37748736 | tf_op jit(solution)/shard_map/mlp_down_back/pallas_call | solution.py:409
  327.2 24.4 %two_grad.1 = (bf16[256,2048]{1,0:T(8,128)(2,1)}, bf16[256,2048]{1,0:T(8,128)(2,1)}, bf16[256,2048]{1,0:T(8,128)(2,1)}) custom-call(s32[3]{0:T(128)} %pad_add_fusion.1.order_ref, bf16[1024,2048]{1,0:T(8,128)(2,1)} %get-tuple-element.159.refs_0_.refs_4_.refs_8_.refs_1_, bf16[1024,2048]{1,0:T(8,128)(2,1)} %get-tuple-element.154.refs_1_.refs_5_.refs_9_, ...), custom_call_target="tpu_custom_call" | custom-call | flops 12884901888 | bytes 16777216 | tf_op jit(solution)/shard_map/two_grad/pallas_call | solution.py:589
  351.6 4.1 collective-permute-start.22
  357.9 11.9 %mlp_grads.3.refs_2_ = bf16[3,2048,2048]{2,1,0:T(8,128)(2,1)} custom-call(bf16[1024,2048]{1,0:T(8,128)(2,1)S(1)} %copy-done.2, bf16[1024,2048]{1,0:T(8,128)(2,1)S(1)} %copy-done.4), custom_call_target="tpu_custom_call" | custom-call | flops 8589934592 | bytes 16777216 | tf_op jit(solution)/shard_map/mlp_grads/pallas_call | solution.py:729
  369.8 11.9 %mlp_grads.4.refs_2_ = bf16[3,2048,2048]{2,1,0:T(8,128)(2,1)} custom-call(bf16[1024,2048]{1,0:T(8,128)(2,1)S(1)} %copy-done.2, bf16[1024,2048]{1,0:T(8,128)(2,1)S(1)} %copy-done.3, bf16[3,2048,2048]{2,1,0:T(8,128)(2,1)} %mlp_grads.3.refs_2_), custom_call_target="tpu_custom_call", output_to_operand_aliasing={{}: (2, {})} | custom-call | flops 8589934592 | bytes 16777216 | tf_op jit(solution)/shard_map/mlp_grads/pallas_call | solution.py:729
  381.7 11.9 %mlp_grads.5 = bf16[3,2048,2048]{2,1,0:T(8,128)(2,1)} custom-call(bf16[1024,2048]{1,0:T(8,128)(2,1)S(1)} %copy-done.11, bf16[1024,2048]{1,0:T(8,128)(2,1)S(1)} %copy-done.8, bf16[3,2048,2048]{2,1,0:T(8,128)(2,1)} %mlp_grads.4.refs_2_), custom_call_target="tpu_custom_call", output_to_operand_aliasing={{}: (2, {})} | custom-call | flops 8589934592 | bytes 16777216 | tf_op jit(solution)/shard_map/mlp_grads/pallas_call | solution.py:729
  393.6 8.6 %collective-permute-done.23 = bf16[256,2048]{1,0:T(8,128)(2,1)} collective-permute-done((bf16[256,2048]{1,0:T(8,128)(2,1)}, bf16[256,2048]{1,0:T(8,128)(2,1)}, u32[]{:S(2)}, u32[]{:S(2)}) %collective-permute-start.23) | collective-permute-done | bytes 1048608 | tf_op jit(solution)/shard_map/ppermute | solution.py:773
  411.2 12.4 %mlp_piece.1 = (bf16[1024,512]{1,0:T(8,128)(2,1)S(1)}, bf16[1024,512]{1,0:T(8,128)(2,1)S(1)}, bf16[1024,512]{1,0:T(8,128)(2,1)S(1)}, bf16[1024,512]{1,0:T(8,128)(2,1)S(1)}) custom-call(s32[4]{0:T(128)S(1)} %pad_add_fusion.2.order_ref, bf16[1024,2048]{1,0:T(8,128)(2,1)S(1)} %copy-done.12, ...), custom_call_target="tpu_custom_call" | custom-call | flops 8589934592 | bytes 8388608 | tf_op jit(solution)/shard_map/mlp_piece/pallas_call | solution.py:448
  425.6 5.9 collective-permute-done.24
  436.4 5.9 collective-permute-start.27
  445.4 14.3 %collective-permute-done.26 = bf16[256,2048]{1,0:T(8,128)(2,1)} collective-permute-done((bf16[256,2048]{1,0:T(8,128)(2,1)}, bf16[256,2048]{1,0:T(8,128)(2,1)}, u32[]{:S(2)}, u32[]{:S(2)}) %collective-permute-start.26) | collective-permute-done | bytes 1048608 | tf_op jit(solution)/shard_map/ppermute | solution.py:752
  461.8 6.5 collective-permute-done.29
  474.4 4.8 collective-permute-start.33
  489.5 6.9 collective-permute-done.32
  501.4 4.5 collective-permute-start.35
  506.0 15.8 %attend_back.1 = (bf16[1024,512]{1,0:T(8,128)(2,1)S(1)}, bf16[1024,512]{1,0:T(8,128)(2,1)S(1)}, bf16[1024,512]{1,0:T(8,128)(2,1)S(1)}) custom-call(s32[1]{0:T(128)} %bitcast.6.me_ref, bf16[1024,512]{1,0:T(8,128)(2,1)S(1)} %copy-done.16, bf16[1024,512]{1,0:T(8,128)(2,1)S(1)} %copy-done.17, bf16[1024,512]{1,0:T(8,128)(2,1)S(1)} %copy-done.18, ...), custom_call_target="tpu_custom_call" | custom-call | flops 1000 | bytes 1000 | tf_op jit(solution)/shard_map/attend_back/pallas_call | solution.py:276
  521.8 10.5 %one_grad.1 = (bf16[1024,512]{1,0:T(8,128)(2,1)S(1)}, bf16[1024,512]{1,0:T(8,128)(2,1)S(1)}, bf16[1024,512]{1,0:T(8,128)(2,1)S(1)}, bf16[1024,512]{1,0:T(8,128)(2,1)S(1)}) custom-call(s32[4]{0:T(128)S(1)} %pad_add_fusion.3.place_ref, bf16[1024,512]{1,0:T(8,128)(2,1)S(1)} %get-tuple-element.199.dq_ref, bf16[1024,512]{1,0:T(8,128)(2,1)S(1)} %get-tuple-element.200.dk_ref, ...), custom_call_target="tpu_custom_call" | custom-call | flops 6442450944 | bytes 15728640 | tf_op jit(solution)/shard_map/one_grad/pallas_call | solution.py:627
  532.4 3.9 select_select_fusion.3
  539.0 13.6 %att_grads.1 = bf16[8,256,2048]{2,1,0:T(8,128)(2,1)S(1)} custom-call(bf16[1024,2048]{1,0:T(8,128)(2,1)S(1)} %copy-done.7, bf16[1024,512]{1,0:T(8,128)(2,1)S(1)} %get-tuple-element.199.dq_ref, bf16[1024,512]{1,0:T(8,128)(2,1)S(1)} %get-tuple-element.200.dk_ref, bf16[1024,512]{1,0:T(8,128)(2,1)S(1)} %get-tuple-element.201.dv_ref, ...), custom_call_target="tpu_custom_call" | custom-call | flops 1000 | bytes 1000 | tf_op jit(solution)/shard_map/att_grads/pallas_call | solution.py:686
  567.3 4.4 all-to-all-start.2
  571.7 56.9 %collective-permute-done.38 = bf16[1024,512]{1,0:T(8,128)(2,1)} collective-permute-done((bf16[1024,512]{1,0:T(8,128)(2,1)}, bf16[1024,512]{1,0:T(8,128)(2,1)}, u32[]{:S(2)}, u32[]{:S(2)}) %collective-permute-start.38) | collective-permute-done | bytes 1048608 | tf_op jit(solution)/shard_map/ppermute | solution.py:773
  628.6 24.3 %collective-permute-done.37 = bf16[1024,512]{1,0:T(8,128)(2,1)} collective-permute-done((bf16[1024,512]{1,0:T(8,128)(2,1)}, bf16[1024,512]{1,0:T(8,128)(2,1)}, u32[]{:S(2)}, u32[]{:S(2)}) %collective-permute-start.37) | collective-permute-done | bytes 1048608 | tf_op jit(solution)/shard_map/ppermute | solution.py:773
  652.9 4.9 fusion.24
  661.5 3.8 all-to-all-start.3
  672.1 8.5 %all-to-all-done.3 = bf16[8,128,512]{2,1,0:T(8,128)(2,1)S(1)} async-done(((bf16[8,128,512]{2,1,0:T(8,128)(2,1)}), bf16[8,128,512]{2,1,0:T(8,128)(2,1)S(1)}, u32[]{:S(2)}, u32[]{:S(2)}) %all-to-all-start.3) | async-done | bytes 1048608 | tf_op jit(solution)/shard_map/all_to_all | solution.py:842
  (239 shorter events, 125.5 us)
Async XLA Ops:
  7.2 132.8 %all-gather.6.cloned.1.call-start = ((), (), s32[]{:S(2)}) async-start(), calls=%async_computation.7 | async-start | bytes 7077888 | tf_op jit(solution)/shard_map/all_gather | solution.py:848
  13.1 30.5 %all-to-all-start = ((bf16[8,128,640]{2,1,0:T(8,128)(2,1)}), bf16[8,128,640]{2,1,0:T(8,128)(2,1)S(1)}, u32[]{:S(2)}, u32[]{:S(2)}) async-start(bf16[8,128,640]{2,1,0:T(8,128)(2,1)} %bitcast), calls=%async_computation | async-start | bytes 2621440 | tf_op jit(solution)/shard_map/all_to_all | solution.py:842
  17.0 225.9 %all-gather.4.cloned.1.call-start = ((), (), s32[]{:S(2)}) async-start(), calls=%async_computation.6 | async-start | bytes 9437184 | tf_op jit(solution)/shard_map/all_gather | solution.py:866
  17.0 27.2 %collective-permute-start = (bf16[64,2048]{1,0:T(8,128)(2,1)}, bf16[64,2048]{1,0:T(8,128)(2,1)}, u32[]{:S(2)}, u32[]{:S(2)}) collective-permute-start(bf16[64,2048]{1,0:T(8,128)(2,1)} %param.17), channel_id=1, source_target_pairs={{0,1},{1,2},{2,3},{3,0},{4,5},{5,6},{6,7},{7,4},{8,9},{9,10},{10,1... | collective-permute-start | bytes 786440 | tf_op jit(solution)/shard_map/ppermute | solution.py:773
  18.6 25.6 %collective-permute-start.1 = (bf16[64,2048]{1,0:T(8,128)(2,1)}, bf16[64,2048]{1,0:T(8,128)(2,1)}, u32[]{:S(2)}, u32[]{:S(2)}) collective-permute-start(bf16[64,2048]{1,0:T(8,128)(2,1)} %param.17), channel_id=1, source_target_pairs={{0,2},{1,3},{2,0},{3,1},{4,6},{5,7},{6,4},{7,5},{8,10},{9,11},{10,... | collective-permute-start | bytes 786440 | tf_op jit(solution)/shard_map/ppermute | solution.py:773
  19.0 25.3 %collective-permute-start.2 = (bf16[64,2048]{1,0:T(8,128)(2,1)}, bf16[64,2048]{1,0:T(8,128)(2,1)}, u32[]{:S(2)}, u32[]{:S(2)}) collective-permute-start(bf16[64,2048]{1,0:T(8,128)(2,1)} %param.17), channel_id=1, source_target_pairs={{0,3},{1,0},{2,1},{3,2},{4,7},{5,4},{6,5},{7,6},{8,11},{9,8},{10,9... | collective-permute-start | bytes 786440 | tf_op jit(solution)/shard_map/ppermute | solution.py:773
  46.7 217.8 %all-gather.8.cloned.1.call-start = ((), (), s32[]{:S(2)}) async-start(), calls=%async_computation.8 | async-start | bytes 28311552 | tf_op jit(solution)/shard_map/all_gather | solution.py:868
  48.8 25.2 %collective-permute-start.3 = (bf16[1024,512]{1,0:T(8,128)(2,1)S(1)}, bf16[1024,512]{1,0:T(8,128)(2,1)S(1)}, u32[]{:S(2)}, u32[]{:S(2)}) collective-permute-start(bf16[1024,512]{1,0:T(8,128)(2,1)S(1)} %fusion.21.refs_0_), channel_id=1, source_target_pairs={{0,1},{1,2},{2,3},{4,5},{5,6},{6,7},{8,9},{9,10},{10,11},{12,13},{... | collective-permute-start | bytes 3145736 | tf_op jit(solution)/shard_map/ppermute | solution.py:752
  52.3 25.1 %collective-permute-start.6 = (bf16[1024,512]{1,0:T(8,128)(2,1)S(1)}, bf16[1024,512]{1,0:T(8,128)(2,1)}, u32[]{:S(2)}, u32[]{:S(2)}) collective-permute-start(bf16[1024,512]{1,0:T(8,128)(2,1)S(1)} %fusion.21.refs_0_), channel_id=1, source_target_pairs={{3,2},{2,1},{1,0},{7,6},{6,5},{5,4},{11,10},{10,9},{9,8},{15,14},{... | collective-permute-start | bytes 3145736 | tf_op jit(solution)/shard_map/ppermute | solution.py:752
  74.0 25.1 %collective-permute-start.4 = (bf16[1024,512]{1,0:T(8,128)(2,1)S(1)}, bf16[1024,512]{1,0:T(8,128)(2,1)}, u32[]{:S(2)}, u32[]{:S(2)}) collective-permute-start(bf16[1024,512]{1,0:T(8,128)(2,1)S(1)} %collective-permute-done.3.refs_1_), channel_id=1, source_target_pairs={{1,2},{2,3},{5,6},{6,7},{9,10},{10,11},{13,14},{14,15},{17,18},{18... | collective-permute-start | bytes 3145736 | tf_op jit(solution)/shard_map/ppermute | solution.py:752
  77.4 25.3 %collective-permute-start.7 = (bf16[1024,512]{1,0:T(8,128)(2,1)}, bf16[1024,512]{1,0:T(8,128)(2,1)}, u32[]{:S(2)}, u32[]{:S(2)}) collective-permute-start(bf16[1024,512]{1,0:T(8,128)(2,1)} %collective-permute-done.6.refs_4_), channel_id=1, source_target_pairs={{2,1},{1,0},{6,5},{5,4},{10,9},{9,8},{14,13},{13,12},{18,17},{17,1... | collective-permute-start | bytes 3145736 | tf_op jit(solution)/shard_map/ppermute | solution.py:752
  84.5 23.6 %all-to-all-start.1 = ((bf16[8,128,512]{2,1,0:T(8,128)(2,1)}), bf16[8,128,512]{2,1,0:T(8,128)(2,1)S(1)}, u32[]{:S(2)}, u32[]{:S(2)}) async-start(bf16[8,128,512]{2,1,0:T(8,128)(2,1)} %bitcast.12), calls=%async_computation.1 | async-start | bytes 2097152 | tf_op jit(solution)/shard_map/all_to_all | solution.py:842
  88.4 470.8 %reduce-scatter.3.cloned.1.call-start = ((), (), s32[]{:S(2)}) async-start(), calls=%async_computation.9 | async-start | bytes 28311552 | tf_op jit(solution)/shard_map/reduce_scatter | solution.py:933
  99.2 21.7 %collective-permute-start.5 = (bf16[1024,512]{1,0:T(8,128)(2,1)}, bf16[1024,512]{1,0:T(8,128)(2,1)}, u32[]{:S(2)}, u32[]{:S(2)}) collective-permute-start(bf16[1024,512]{1,0:T(8,128)(2,1)} %collective-permute-done.4.refs_2_), channel_id=1, source_target_pairs={{2,3},{6,7},{10,11},{14,15},{18,19},{22,23},{26,27},{30,31}} | collective-permute-start | bytes 3145736 | tf_op jit(solution)/shard_map/ppermute | solution.py:752
  102.7 18.1 %collective-permute-start.8 = (bf16[1024,512]{1,0:T(8,128)(2,1)}, bf16[1024,512]{1,0:T(8,128)(2,1)}, u32[]{:S(2)}, u32[]{:S(2)}) collective-permute-start(bf16[1024,512]{1,0:T(8,128)(2,1)} %collective-permute-done.7.refs_5_), channel_id=1, source_target_pairs={{1,0},{5,4},{9,8},{13,12},{17,16},{21,20},{25,24},{29,28}} | collective-permute-start | bytes 3145736 | tf_op jit(solution)/shard_map/ppermute | solution.py:752
  128.6 36.1 %collective-permute-start.9 = (bf16[1024,512]{1,0:T(8,128)(2,1)S(1)}, bf16[1024,512]{1,0:T(8,128)(2,1)S(1)}, u32[]{:S(2)}, u32[]{:S(2)}) collective-permute-start(bf16[1024,512]{1,0:T(8,128)(2,1)S(1)} %fusion.22.refs_7_.refs_0_), channel_id=1, source_target_pairs={{0,1},{1,2},{2,3},{4,5},{5,6},{6,7},{8,9},{9,10},{10,11},{12,13},{... | collective-permute-start | bytes 3145736 | tf_op jit(solution)/shard_map/ppermute | solution.py:752
  133.0 31.7 %collective-permute-start.10 = (bf16[1024,512]{1,0:T(8,128)(2,1)S(1)}, bf16[1024,512]{1,0:T(8,128)(2,1)}, u32[]{:S(2)}, u32[]{:S(2)}) collective-permute-start(bf16[1024,512]{1,0:T(8,128)(2,1)S(1)} %fusion.22.refs_7_.refs_0_), channel_id=1, source_target_pairs={{3,2},{2,1},{1,0},{7,6},{6,5},{5,4},{11,10},{10,9},{9,8},{15,14},{... | collective-permute-start | bytes 3145736 | tf_op jit(solution)/shard_map/ppermute | solution.py:752
  164.8 24.1 %collective-permute-start.11 = (bf16[1024,512]{1,0:T(8,128)(2,1)}, bf16[1024,512]{1,0:T(8,128)(2,1)S(1)}, u32[]{:S(2)}, u32[]{:S(2)}) collective-permute-start(bf16[1024,512]{1,0:T(8,128)(2,1)} %attend.1.refs_0_.att_ref), channel_id=1, source_target_pairs={{0,1},{1,2},{2,3},{4,5},{5,6},{6,7},{8,9},{9,10},{10,11},{12,13},{... | collective-permute-start | bytes 3145736 | tf_op jit(solution)/shard_map/ppermute | solution.py:752
  166.7 24.1 %collective-permute-start.14 = (bf16[1024,512]{1,0:T(8,128)(2,1)}, bf16[1024,512]{1,0:T(8,128)(2,1)S(1)}, u32[]{:S(2)}, u32[]{:S(2)}) collective-permute-start(bf16[1024,512]{1,0:T(8,128)(2,1)} %attend.1.refs_0_.att_ref), channel_id=1, source_target_pairs={{3,2},{2,1},{1,0},{7,6},{6,5},{5,4},{11,10},{10,9},{9,8},{15,14},{... | collective-permute-start | bytes 3145736 | tf_op jit(solution)/shard_map/ppermute | solution.py:752
  188.9 23.0 %collective-permute-start.12 = (bf16[1024,512]{1,0:T(8,128)(2,1)S(1)}, bf16[1024,512]{1,0:T(8,128)(2,1)S(1)}, u32[]{:S(2)}, u32[]{:S(2)}) collective-permute-start(bf16[1024,512]{1,0:T(8,128)(2,1)S(1)} %collective-permute-done.11.refs_1_), channel_id=1, source_target_pairs={{1,2},{2,3},{5,6},{6,7},{9,10},{10,11},{13,14},{14,15},{17,18},{18... | collective-permute-start | bytes 3145736 | tf_op jit(solution)/shard_map/ppermute | solution.py:752
  190.8 23.4 %collective-permute-start.15 = (bf16[1024,512]{1,0:T(8,128)(2,1)S(1)}, bf16[1024,512]{1,0:T(8,128)(2,1)S(1)}, u32[]{:S(2)}, u32[]{:S(2)}) collective-permute-start(bf16[1024,512]{1,0:T(8,128)(2,1)S(1)} %collective-permute-done.14.refs_4_), channel_id=1, source_target_pairs={{2,1},{1,0},{6,5},{5,4},{10,9},{9,8},{14,13},{13,12},{18,17},{17,1... | collective-permute-start | bytes 3145736 | tf_op jit(solution)/shard_map/ppermute | solution.py:752
  211.9 21.0 %collective-permute-start.13 = (bf16[1024,512]{1,0:T(8,128)(2,1)S(1)}, bf16[1024,512]{1,0:T(8,128)(2,1)S(1)}, u32[]{:S(2)}, u32[]{:S(2)}) collective-permute-start(bf16[1024,512]{1,0:T(8,128)(2,1)S(1)} %collective-permute-done.12.refs_2_), channel_id=1, source_target_pairs={{2,3},{6,7},{10,11},{14,15},{18,19},{22,23},{26,27},{30,31}} | collective-permute-start | bytes 3145736 | tf_op jit(solution)/shard_map/ppermute | solution.py:752
  214.2 18.7 %collective-permute-start.16 = (bf16[1024,512]{1,0:T(8,128)(2,1)S(1)}, bf16[1024,512]{1,0:T(8,128)(2,1)S(1)}, u32[]{:S(2)}, u32[]{:S(2)}) collective-permute-start(bf16[1024,512]{1,0:T(8,128)(2,1)S(1)} %collective-permute-done.15.refs_5_), channel_id=1, source_target_pairs={{1,0},{5,4},{9,8},{13,12},{17,16},{21,20},{25,24},{29,28}} | collective-permute-start | bytes 3145736 | tf_op jit(solution)/shard_map/ppermute | solution.py:752
  232.9 28.0 %collective-permute-start.17 = (bf16[1024,512]{1,0:T(8,128)(2,1)S(1)}, bf16[1024,512]{1,0:T(8,128)(2,1)S(1)}, u32[]{:S(2)}, u32[]{:S(2)}) collective-permute-start(bf16[1024,512]{1,0:T(8,128)(2,1)S(1)} %collective-permute-done.9.refs_8_.refs_1_), channel_id=1, source_target_pairs={{1,2},{2,3},{5,6},{6,7},{9,10},{10,11},{13,14},{14,15},{17,18},{18... | collective-permute-start | bytes 3145736 | tf_op jit(solution)/shard_map/ppermute | solution.py:752
  237.4 23.6 %collective-permute-start.18 = (bf16[1024,512]{1,0:T(8,128)(2,1)}, bf16[1024,512]{1,0:T(8,128)(2,1)}, u32[]{:S(2)}, u32[]{:S(2)}) collective-permute-start(bf16[1024,512]{1,0:T(8,128)(2,1)} %collective-permute-done.10.refs_11_.refs_4_), channel_id=1, source_target_pairs={{2,1},{1,0},{6,5},{5,4},{10,9},{9,8},{14,13},{13,12},{18,17},{17,1... | collective-permute-start | bytes 3145736 | tf_op jit(solution)/shard_map/ppermute | solution.py:752
  260.9 27.6 %collective-permute-start.19 = (bf16[1024,512]{1,0:T(8,128)(2,1)S(1)}, bf16[1024,512]{1,0:T(8,128)(2,1)S(1)}, u32[]{:S(2)}, u32[]{:S(2)}) collective-permute-start(bf16[1024,512]{1,0:T(8,128)(2,1)S(1)} %collective-permute-done.17.refs_9_.refs_2_), channel_id=1, source_target_pairs={{2,3},{6,7},{10,11},{14,15},{18,19},{22,23},{26,27},{30,31}} | collective-permute-start | bytes 3145736 | tf_op jit(solution)/shard_map/ppermute | solution.py:752
  262.3 26.2 %collective-permute-start.20 = (bf16[1024,512]{1,0:T(8,128)(2,1)}, bf16[1024,512]{1,0:T(8,128)(2,1)}, u32[]{:S(2)}, u32[]{:S(2)}) collective-permute-start(bf16[1024,512]{1,0:T(8,128)(2,1)} %collective-permute-done.18.refs_12_.refs_5_), channel_id=1, source_target_pairs={{1,0},{5,4},{9,8},{13,12},{17,16},{21,20},{25,24},{29,28}} | collective-permute-start | bytes 3145736 | tf_op jit(solution)/shard_map/ppermute | solution.py:752
  307.7 85.9 %collective-permute-start.21 = (bf16[256,2048]{1,0:T(8,128)(2,1)}, bf16[256,2048]{1,0:T(8,128)(2,1)S(1)}, u32[]{:S(2)}, u32[]{:S(2)}) collective-permute-start(bf16[256,2048]{1,0:T(8,128)(2,1)} %first_two_grad.1), channel_id=1, source_target_pairs={{0,2},{1,3},{2,0},{3,1},{4,6},{5,7},{6,4},{7,5},{8,10},{9,11},{10,... | collective-permute-start | bytes 3145736 | tf_op jit(solution)/shard_map/ppermute | solution.py:773
  351.6 42.0 %collective-permute-start.22 = (bf16[256,2048]{1,0:T(8,128)(2,1)}, bf16[256,2048]{1,0:T(8,128)(2,1)}, u32[]{:S(2)}, u32[]{:S(2)}) collective-permute-start(bf16[256,2048]{1,0:T(8,128)(2,1)} %get-tuple-element.156), channel_id=1, source_target_pairs={{0,1},{1,2},{2,3},{3,0},{4,5},{5,6},{6,7},{7,4},{8,9},{9,10},{10,1... | collective-permute-start | bytes 3145736 | tf_op jit(solution)/shard_map/ppermute | solution.py:773
  355.7 46.5 %collective-permute-start.23 = (bf16[256,2048]{1,0:T(8,128)(2,1)}, bf16[256,2048]{1,0:T(8,128)(2,1)}, u32[]{:S(2)}, u32[]{:S(2)}) collective-permute-start(bf16[256,2048]{1,0:T(8,128)(2,1)} %get-tuple-element.157), channel_id=1, source_target_pairs={{0,3},{1,0},{2,1},{3,2},{4,7},{5,4},{6,5},{7,6},{8,11},{9,8},{10,9... | collective-permute-start | bytes 3145736 | tf_op jit(solution)/shard_map/ppermute | solution.py:773
  402.2 266.4 %reduce-scatter.5.cloned.1.call-start = ((), (), s32[]{:S(2)}) async-start(), calls=%async_computation.10 | async-start | bytes 9437184 | tf_op jit(solution)/shard_map/reduce_scatter | solution.py:992
  405.2 26.2 %collective-permute-start.24 = (bf16[256,2048]{1,0:T(8,128)(2,1)S(1)}, bf16[256,2048]{1,0:T(8,128)(2,1)}, u32[]{:S(2)}, u32[]{:S(2)}) collective-permute-start(bf16[256,2048]{1,0:T(8,128)(2,1)S(1)} %add_convert_fusion.4), channel_id=1, source_target_pairs={{0,1},{1,2},{2,3},{4,5},{5,6},{6,7},{8,9},{9,10},{10,11},{12,13},{... | collective-permute-start | bytes 3145736 | tf_op jit(solution)/shard_map/ppermute | solution.py:752
  408.6 25.9 %collective-permute-start.25 = (bf16[256,2048]{1,0:T(8,128)(2,1)S(1)}, bf16[256,2048]{1,0:T(8,128)(2,1)}, u32[]{:S(2)}, u32[]{:S(2)}) collective-permute-start(bf16[256,2048]{1,0:T(8,128)(2,1)S(1)} %add_convert_fusion.4), channel_id=1, source_target_pairs={{3,2},{2,1},{1,0},{7,6},{6,5},{5,4},{11,10},{10,9},{9,8},{15,14},{... | collective-permute-start | bytes 3145736 | tf_op jit(solution)/shard_map/ppermute | solution.py:752
  434.5 25.2 %collective-permute-start.26 = (bf16[256,2048]{1,0:T(8,128)(2,1)}, bf16[256,2048]{1,0:T(8,128)(2,1)}, u32[]{:S(2)}, u32[]{:S(2)}) collective-permute-start(bf16[256,2048]{1,0:T(8,128)(2,1)} %collective-permute-done.24), channel_id=1, source_target_pairs={{1,2},{2,3},{5,6},{6,7},{9,10},{10,11},{13,14},{14,15},{17,18},{18... | collective-permute-start | bytes 3145736 | tf_op jit(solution)/shard_map/ppermute | solution.py:752
  436.4 25.4 %collective-permute-start.27 = (bf16[256,2048]{1,0:T(8,128)(2,1)}, bf16[256,2048]{1,0:T(8,128)(2,1)}, u32[]{:S(2)}, u32[]{:S(2)}) collective-permute-start(bf16[256,2048]{1,0:T(8,128)(2,1)} %collective-permute-done.25), channel_id=1, source_target_pairs={{2,1},{1,0},{6,5},{5,4},{10,9},{9,8},{14,13},{13,12},{18,17},{17,1... | collective-permute-start | bytes 3145736 | tf_op jit(solution)/shard_map/ppermute | solution.py:752
  442.3 19.5 %collective-permute-start.28 = (bf16[1024,512]{1,0:T(8,128)(2,1)S(1)}, bf16[1024,512]{1,0:T(8,128)(2,1)}, u32[]{:S(2)}, u32[]{:S(2)}) collective-permute-start(bf16[1024,512]{1,0:T(8,128)(2,1)S(1)} %get-tuple-element.186), channel_id=1, source_target_pairs={{0,1},{4,5},{8,9},{12,13},{16,17},{20,21},{24,25},{28,29}} | collective-permute-start | bytes 3145736 | tf_op jit(solution)/shard_map/ppermute | solution.py:968
  443.9 24.4 %collective-permute-start.29 = (bf16[1024,512]{1,0:T(8,128)(2,1)S(1)}, bf16[1024,512]{1,0:T(8,128)(2,1)}, u32[]{:S(2)}, u32[]{:S(2)}) collective-permute-start(bf16[1024,512]{1,0:T(8,128)(2,1)S(1)} %get-tuple-element.184), channel_id=1, source_target_pairs={{3,2},{7,6},{11,10},{15,14},{19,18},{23,22},{27,26},{31,30}} | collective-permute-start | bytes 3145736 | tf_op jit(solution)/shard_map/ppermute | solution.py:968
  468.3 21.2 %collective-permute-start.30 = (bf16[256,2048]{1,0:T(8,128)(2,1)}, bf16[256,2048]{1,0:T(8,128)(2,1)S(1)}, u32[]{:S(2)}, u32[]{:S(2)}) collective-permute-start(bf16[256,2048]{1,0:T(8,128)(2,1)} %collective-permute-done.26), channel_id=1, source_target_pairs={{2,3},{6,7},{10,11},{14,15},{18,19},{22,23},{26,27},{30,31}} | collective-permute-start | bytes 3145736 | tf_op jit(solution)/shard_map/ppermute | solution.py:752
  469.8 19.8 %collective-permute-start.31 = (bf16[256,2048]{1,0:T(8,128)(2,1)}, bf16[256,2048]{1,0:T(8,128)(2,1)S(1)}, u32[]{:S(2)}, u32[]{:S(2)}) collective-permute-start(bf16[256,2048]{1,0:T(8,128)(2,1)} %collective-permute-done.27), channel_id=1, source_target_pairs={{1,0},{5,4},{9,8},{13,12},{17,16},{21,20},{25,24},{29,28}} | collective-permute-start | bytes 3145736 | tf_op jit(solution)/shard_map/ppermute | solution.py:752
  473.1 23.4 %collective-permute-start.32 = (bf16[1024,512]{1,0:T(8,128)(2,1)S(1)}, bf16[1024,512]{1,0:T(8,128)(2,1)S(1)}, u32[]{:S(2)}, u32[]{:S(2)}) collective-permute-start(bf16[1024,512]{1,0:T(8,128)(2,1)S(1)} %get-tuple-element.232), channel_id=1, source_target_pairs={{0,1},{1,2},{4,5},{5,6},{8,9},{9,10},{12,13},{13,14},{16,17},{17,1... | collective-permute-start | bytes 3145736 | tf_op jit(solution)/shard_map/ppermute | solution.py:968
  474.4 23.6 %collective-permute-start.33 = (bf16[1024,512]{1,0:T(8,128)(2,1)S(1)}, bf16[1024,512]{1,0:T(8,128)(2,1)S(1)}, u32[]{:S(2)}, u32[]{:S(2)}) collective-permute-start(bf16[1024,512]{1,0:T(8,128)(2,1)S(1)} %get-tuple-element.231), channel_id=1, source_target_pairs={{3,2},{2,1},{7,6},{6,5},{11,10},{10,9},{15,14},{14,13},{19,18},{18... | collective-permute-start | bytes 3145736 | tf_op jit(solution)/shard_map/ppermute | solution.py:968
  498.3 38.8 %collective-permute-start.34 = (bf16[1024,512]{1,0:T(8,128)(2,1)S(1)}, bf16[1024,512]{1,0:T(8,128)(2,1)S(1)}, u32[]{:S(2)}, u32[]{:S(2)}) collective-permute-start(bf16[1024,512]{1,0:T(8,128)(2,1)S(1)} %add_convert_fusion.3), channel_id=1, source_target_pairs={{0,1},{1,2},{2,3},{4,5},{5,6},{6,7},{8,9},{9,10},{10,11},{12,13},{... | collective-permute-start | bytes 3145736 | tf_op jit(solution)/shard_map/ppermute | solution.py:968
  501.4 35.7 %collective-permute-start.35 = (bf16[1024,512]{1,0:T(8,128)(2,1)S(1)}, bf16[1024,512]{1,0:T(8,128)(2,1)S(1)}, u32[]{:S(2)}, u32[]{:S(2)}) collective-permute-start(bf16[1024,512]{1,0:T(8,128)(2,1)S(1)} %add_convert_fusion.2), channel_id=1, source_target_pairs={{3,2},{2,1},{1,0},{7,6},{6,5},{5,4},{11,10},{10,9},{9,8},{15,14},{... | collective-permute-start | bytes 3145736 | tf_op jit(solution)/shard_map/ppermute | solution.py:968
  559.2 69.3 %collective-permute-start.38 = (bf16[1024,512]{1,0:T(8,128)(2,1)}, bf16[1024,512]{1,0:T(8,128)(2,1)}, u32[]{:S(2)}, u32[]{:S(2)}) collective-permute-start(bf16[1024,512]{1,0:T(8,128)(2,1)} %copy-done.24), channel_id=1, source_target_pairs={{0,2},{1,3},{2,0},{3,1},{4,6},{5,7},{6,4},{7,5},{8,10},{9,11},{10,... | collective-permute-start | bytes 3145736 | tf_op jit(solution)/shard_map/ppermute | solution.py:773
  559.8 93.0 %collective-permute-start.37 = (bf16[1024,512]{1,0:T(8,128)(2,1)}, bf16[1024,512]{1,0:T(8,128)(2,1)}, u32[]{:S(2)}, u32[]{:S(2)}) collective-permute-start(bf16[1024,512]{1,0:T(8,128)(2,1)} %copy-done.23), channel_id=1, source_target_pairs={{0,1},{1,2},{2,3},{3,0},{4,5},{5,6},{6,7},{7,4},{8,9},{9,10},{10,1... | collective-permute-start | bytes 3145736 | tf_op jit(solution)/shard_map/ppermute | solution.py:773
  561.5 91.4 %collective-permute-start.36 = (bf16[1024,512]{1,0:T(8,128)(2,1)S(1)}, bf16[1024,512]{1,0:T(8,128)(2,1)}, u32[]{:S(2)}, u32[]{:S(2)}) collective-permute-start(bf16[1024,512]{1,0:T(8,128)(2,1)S(1)} %get-tuple-element.196), channel_id=1, source_target_pairs={{0,3},{1,0},{2,1},{3,2},{4,7},{5,4},{6,5},{7,6},{8,11},{9,8},{10,9... | collective-permute-start | bytes 3145736 | tf_op jit(solution)/shard_map/ppermute | solution.py:773
  567.3 94.2 %all-to-all-start.2 = ((bf16[8,128,512]{2,1,0:T(8,128)(2,1)}), bf16[8,128,512]{2,1,0:T(8,128)(2,1)}, u32[]{:S(2)}, u32[]{:S(2)}) async-start(bf16[8,128,512]{2,1,0:T(8,128)(2,1)} %bitcast.57), calls=%async_computation.3 | async-start | bytes 2097152 | tf_op jit(solution)/shard_map/all_to_all | solution.py:842
  661.5 19.2 %all-to-all-start.3 = ((bf16[8,128,512]{2,1,0:T(8,128)(2,1)}), bf16[8,128,512]{2,1,0:T(8,128)(2,1)S(1)}, u32[]{:S(2)}, u32[]{:S(2)}) async-start(bf16[8,128,512]{2,1,0:T(8,128)(2,1)} %bitcast.26), calls=%async_computation.4 | async-start | bytes 2097152 | tf_op jit(solution)/shard_map/all_to_all | solution.py:842
  (59 other events, 1008.9 us)
Sparse Core Ops, SparseCore 0:
  10.5 58.5 all-gather.5
  71.6 65.6 all-gather.3
  139.2 125.3 all-gather.7
  402.3 156.8 reduce-scatter.2
  562.5 71.2 reduce-scatter.4
